TPU v7x, 32 devices: a whole 2x2x4 slice. The times are simulated.
32 devices in a mesh: expert: 8 (over z, y), inner: 2 (over x), outer: 2 (over core).
Axes of the slice: x: 2, y: 2, z: 4, core: 2. Of those that a mesh axis runs over, the one named last changes fastest.
Arguments:
- token_grads: bfloat16 [4096, 8192], P(('expert', 'inner', 'outer')), may hold values from -6 to 6
- router_gates: bfloat16 [4096, 2], P(('expert', 'inner', 'outer')), may hold values from 0.099609375 to 1
- expert_ids: int32 [4096, 2], P(('expert', 'inner', 'outer')), may hold values from 0 to 15, all different within a row; in each aligned block of 128 rows (0 to 127, 128 to 255, ...) at most 20 rows name the same one
- saved_hidden: bfloat16 [4096, 128], P(('expert', 'inner', 'outer')), may hold values from -6 to 6
- up_weight: bfloat16 [16, 64, 8192], P('expert', None, ('inner', 'outer')), may hold values from -0.75 to 0.75
- down_weight: bfloat16 [16, 64, 8192], P('expert', None, ('inner', 'outer')), may hold values from -0.0625 to 0.0625
Outputs:
- input_grads: bfloat16 [4096, 8192], P(('expert', 'inner', 'outer'))
- gate_grads: bfloat16 [4096, 2], P(('expert', 'inner', 'outer'))
- down_grads: bfloat16 [16, 64, 8192], P('expert', None, ('inner', 'outer'))
Inputs may be any that keep to these rules, and one draw needn't show every extreme that they name: `expert_ids`: each row names 2 different experts; within the rows of one device (aligned blocks of 128 rows) no expert is named more than 20 times.
All inputs are finite; a program needn't handle non-finite values.
Results may differ from a plain program's by a relative error of at most 0.0067.
Values may be sent and summed in bfloat16 or wider, within the bound.
No kernel may reach another device: no remote copies, remote signals or barrier semaphores. Data moves between devices by JAX's collectives and lax.ppermute only.
A program may use at most 128 MiB of HBM per device.

v0:
```python
import jax
import jax.numpy as jnp
from jax import lax
from jax.sharding import PartitionSpec as P

root_half = 0.7071067811865476
inv_root_tau = 0.3989422804014327


def gelu_parts(preact):
    cumulative = 0.5 * (1.0 + lax.erf(preact * root_half))
    density = inv_root_tau * jnp.exp(-0.5 * preact * preact)
    return (preact * cumulative, cumulative + preact * density)


def slot_numbers(route_ids, expert_total, capacity):
    flat_ids = route_ids.reshape(-1)
    matches = (flat_ids[:, None] == lax.iota(jnp.int32, expert_total)[None, :]).astype(jnp.int32)
    earlier = jnp.cumsum(matches, axis=0) - matches
    return flat_ids * capacity + jnp.sum(earlier * matches, axis=1)


def expert_pass(slot_grads, slot_hidden, slot_gates, up_full, down_full):
    projected = jnp.einsum(
        "secd,efd->secf", slot_grads, down_full, preferred_element_type=jnp.float32
    )
    activation, gelu_slope = gelu_parts(slot_hidden.astype(jnp.float32))
    gate_values = slot_gates.astype(jnp.float32)[..., None]
    gate_grad = jnp.sum(activation * projected, axis=-1).astype(jnp.bfloat16)
    hidden_grad = (gate_values * projected * gelu_slope).astype(jnp.bfloat16)
    route_rows = jnp.einsum(
        "secf,efd->secd", hidden_grad, up_full, preferred_element_type=jnp.float32
    ).astype(jnp.bfloat16)
    weighted = (gate_values * activation).astype(jnp.bfloat16)
    partial_value = jnp.einsum(
        "secf,secd->efd", weighted, slot_grads, preferred_element_type=jnp.float32
    )
    return (route_rows, gate_grad, partial_value)


def body(token_grads, router_gates, expert_ids, saved_hidden, up_weight, down_weight):
    tok_count, model_width = token_grads.shape
    top_count = expert_ids.shape[1]
    local_experts, hidden_width = (up_weight.shape[0], up_weight.shape[1])
    senders = lax.axis_size("expert")
    expert_total = local_experts * senders
    capacity = max(2, 5 * tok_count * top_count // (4 * expert_total))
    slot_ids = slot_numbers(expert_ids, expert_total, capacity)
    route_tokens = lax.iota(jnp.int32, tok_count * top_count) // top_count
    send_grads = (
        jnp.zeros((expert_total * capacity, model_width), jnp.bfloat16)
        .at[slot_ids]
        .set(token_grads[route_tokens])
    )
    send_hidden = (
        jnp.zeros((expert_total * capacity, hidden_width), jnp.bfloat16)
        .at[slot_ids]
        .set(saved_hidden.reshape(tok_count * top_count, hidden_width))
    )
    send_gates = (
        jnp.zeros((expert_total * capacity,), jnp.bfloat16)
        .at[slot_ids]
        .set(router_gates.reshape(-1))
    )
    send_grads = send_grads.reshape(senders, local_experts, capacity, model_width)
    send_hidden = send_hidden.reshape(senders, local_experts, capacity, hidden_width)
    send_gates = send_gates.reshape(senders, local_experts, capacity)
    up_full, down_full = (
        lax.all_gather(up_weight, ("inner", "outer"), axis=2, tiled=True),
        lax.all_gather(down_weight, ("inner", "outer"), axis=2, tiled=True),
    )
    received = (
        lax.all_to_all(send_grads, "expert", split_axis=0, concat_axis=0, tiled=True),
        lax.all_to_all(send_hidden, "expert", split_axis=0, concat_axis=0, tiled=True),
        lax.all_to_all(send_gates, "expert", split_axis=0, concat_axis=0, tiled=True),
    )
    route_rows, gate_grad, partial_value = expert_pass(
        received[0], received[1], received[2], up_full, down_full
    )
    back_rows, back_gates = (
        lax.all_to_all(route_rows, "expert", split_axis=0, concat_axis=0, tiled=True),
        lax.all_to_all(gate_grad, "expert", split_axis=0, concat_axis=0, tiled=True),
    )
    flat_rows = back_rows.reshape(expert_total * capacity, model_width)
    picked = flat_rows[slot_ids].reshape(tok_count, top_count, model_width)
    input_grads = jnp.sum(picked, axis=1, dtype=jnp.float32).astype(jnp.bfloat16)
    gate_grads = back_gates.reshape(-1)[slot_ids].reshape(tok_count, top_count)
    inner_terms = lax.optimization_barrier(partial_value.astype(jnp.bfloat16)).astype(jnp.float32)
    pair_sum = lax.psum_scatter(
        inner_terms.astype(jnp.bfloat16), "inner", scatter_dimension=2, tiled=True
    )
    outer_terms = lax.optimization_barrier(pair_sum).astype(jnp.float32)
    down_grads = lax.psum_scatter(
        outer_terms.astype(jnp.bfloat16), "outer", scatter_dimension=2, tiled=True
    )
    return (input_grads, gate_grads, down_grads)


def solution(mesh):
    return jax.shard_map(
        body,
        mesh=mesh,
        in_specs=(
            P(("expert", "inner", "outer"), None),
            P(("expert", "inner", "outer"), None),
            P(("expert", "inner", "outer"), None),
            P(("expert", "inner", "outer"), None),
            P("expert", None, ("inner", "outer")),
            P("expert", None, ("inner", "outer")),
        ),
        out_specs=(
            P(("expert", "inner", "outer"), None),
            P(("expert", "inner", "outer"), None),
            P("expert", None, ("inner", "outer")),
        ),
        check_vma=False,
    )
```

profile of v0, /device:TPU:0, one launch (start us, length us, event | category | flops | bytes accessed | tf_op | source)
XLA Modules:
  0.0 395.8 jit_solution(7910703824125257710)
XLA Ops:
  8.0 0.0 copy-start
  8.0 0.8 broadcast_multiply_fusion
  8.8 0.8 copy.79
  9.6 0.1 eq.29
  9.8 0.1 eq.25
  9.9 0.8 copy.82
  10.7 0.1 reshape.161
  10.8 0.1 copy.78
  11.0 0.1 mul.74
  11.1 0.6 reduce-window.6
  11.7 0.2 slice_reduce_fusion
  11.9 0.1 fusion.34
  12.0 2.2 scatter_custom_fusion
  14.2 0.7 reshape.125
  14.9 7.3 %all-to-all-start = ((bf16[8,2,20]{2,1,0:T(2,128)(2,1)}), bf16[8,2,20]{2,1,0:T(2,128)(2,1)S(1)}, u32[]{:S(2)}, u32[]{:S(2)}) async-start(bf16[8,2,20]{2,1,0:T(2,128)(2,1)} %reshape.125), calls=%async_computation | async-start | bytes 8192 | tf_op jit(solution)/shard_map/all_to_all | solution.py:75
  22.2 0.8 reshape.177
  23.0 1.2 scatter_custom_fusion.2
  24.3 0.1 copy.126
  24.3 0.7 reshape.195
  25.1 3.5 all-to-all-done
  28.6 3.5 all-to-all-start.2
  32.1 0.0 copy-done
  32.1 21.2 %scatter_custom_fusion.1 = bf16[320,8192]{1,0:T(8,128)(2,1)} fusion(s32[256]{0:T(256)S(1)} %bitcast.58, bf16[128,8192]{1,0:T(8,128)(2,1)S(1)} %copy-done, s32[1024]{0:T(1024)S(1)} %pad_clamp_fusion.1, bf16[]{:T(256)} %constant.14.clone.1), kind=kCustom, calls=%fused_computation.13 | custom fusion | bytes 5242882 | tf_op jit(solution)/shard_map/scatter | solution.py:53
  53.3 7.7 %reshape.126 = bf16[8,2,20,8192]{3,2,1,0:T(8,128)(2,1)} reshape(bf16[320,8192]{1,0:T(8,128)(2,1)} %scatter_custom_fusion.1) | data formatting | bytes 10485760 | tf_op jit(solution)/shard_map/reshape | solution.py:65
  61.0 9.1 %copy.84 = bf16[8,2,20,8192]{3,1,2,0:T(2,128)(2,1)} copy(bf16[8,2,20,8192]{3,2,1,0:T(8,128)(2,1)} %reshape.126) | data formatting | bytes 10485760 | tf_op jit(solution)/shard_map/reshape | solution.py:65
  70.1 0.0 all-to-all-done.2
  70.1 5.9 %all-to-all-start.1 = ((bf16[8,2,20,8192]{3,1,2,0:T(2,128)(2,1)}), bf16[8,2,20,8192]{3,1,2,0:T(2,128)(2,1)}, u32[]{:S(2)}, u32[]{:S(2)}) async-start(bf16[8,2,20,8192]{3,1,2,0:T(2,128)(2,1)} %copy.84), calls=%async_computation.1 | async-start | bytes 10485760 | tf_op jit(solution)/shard_map/all_to_all | solution.py:73
  76.0 0.0 all-gather.3.cloned.1.call-start
  76.1 0.7 all-gather.3.cloned.1.call-update
  76.7 0.4 all-gather.5.cloned.1.call-start
  77.2 0.3 all-gather.5.cloned.1.call-update
  77.5 0.1 reshape.196
  77.6 24.8 %all-gather.3.cloned.1.call-done = bf16[2,64,8192]{2,1,0:T(8,128)(2,1)} async-done(((bf16[2,64,2048]{2,1,0:T(8,128)(2,1)}), bf16[2,64,8192]{2,1,0:T(8,128)(2,1)}) %all-gather.3.cloned.1.call-update) | async-done | bytes 2097168 | tf_op jit(solution)/shard_map/all_gather | solution.py:70
  102.4 87.6 %all-to-all-done.1 = bf16[8,2,20,8192]{3,1,2,0:T(2,128)(2,1)} async-done(((bf16[8,2,20,8192]{3,1,2,0:T(2,128)(2,1)}), bf16[8,2,20,8192]{3,1,2,0:T(2,128)(2,1)}, u32[]{:S(2)}, u32[]{:S(2)}) %all-to-all-start.1) | async-done | bytes 5242912 | tf_op jit(solution)/shard_map/all_to_all | solution.py:73
  190.1 7.3 %multiply_reduce_fusion = (bf16[8,2,20]{2,0,1:T(8,128)(2,1)S(1)}, f32[8,2,20,64]{3,2,0,1:T(8,128)S(1)}) fusion(bf16[8,2,20,64]{3,1,2,0:T(2,128)(2,1)S(1)} %bitcast.52, bf16[2,64,8192]{2,1,0:T(8,128)(2,1)} %all-gather.3.cloned.1.call-done, bf16[8,2,20,8192]{3,1,2,0:T(2,128)(2,1)} %all-to-all-done.1), kind=kOutput, calls=%fused_computation.33 | convolution fusion | flops 335687360 | bytes 7463552 | tf_op jit(solution)/shard_map/secd,efd->secf/dot_general | solution.py:24
  197.4 0.6 copy.90
  198.0 3.6 all-to-all-start.4
  201.6 0.0 all-gather.5.cloned.1.call-done
  201.6 3.4 fusion
  205.1 11.8 %copy.88 = bf16[8,2,20,8192]{3,1,2,0:T(2,128)(2,1)} copy(bf16[8,2,20,8192]{3,2,0,1:T(8,128)(2,1)S(1)} %fusion) | data formatting | bytes 10485760 | tf_op jit(solution)/shard_map/convert_element_type | solution.py:33
  216.9 0.0 all-to-all-done.4
  216.9 6.0 %all-to-all-start.3 = ((bf16[8,2,20,8192]{3,1,2,0:T(2,128)(2,1)}), bf16[8,2,20,8192]{3,1,2,0:T(2,128)(2,1)}, u32[]{:S(2)}, u32[]{:S(2)}) async-start(bf16[8,2,20,8192]{3,1,2,0:T(2,128)(2,1)} %copy.88), calls=%async_computation.3 | async-start | bytes 10485760 | tf_op jit(solution)/shard_map/all_to_all | solution.py:81
  222.9 0.2 reduce-scatter.3.cloned.1.call-start
  223.1 10.0 %fusion.1 = bf16[2,64,8192]{2,1,0:T(8,128)(2,1)} fusion(bf16[8,2,20,8192]{3,1,2,0:T(2,128)(2,1)} %all-to-all-done.1, f32[8,2,20]{2,0,1:T(8,128)S(1)} %copy_convert_fusion, bf16[8,2,20,64]{3,1,2,0:T(2,128)(2,1)S(1)} %bitcast.54), kind=kOutput, calls=%fused_computation.9 | convolution fusion | flops 336736256 | bytes 7382272 | tf_op jit(solution)/shard_map/secf,secd->efd/dot_general | solution.py:35
  233.0 0.0 reduce-scatter.3.cloned.1.call-update
  233.1 0.0 reduce-scatter.5.cloned.1.call-start
  233.1 33.1 %reduce-scatter.3.cloned.1.call-done = bf16[2,64,4096]{2,1,0:T(8,128)(2,1)} async-done(((bf16[2,64,8192]{2,1,0:T(8,128)(2,1)}), bf16[2,64,4096]{2,1,0:T(8,128)(2,1)}) %reduce-scatter.3.cloned.1.call-update) | async-done | bytes 1048592 | tf_op jit(solution)/shard_map/reduce_scatter | solution.py:89
  266.3 0.0 reduce-scatter.5.cloned.1.call-update
  266.3 0.1 reshape.131
  266.4 1.9 gather_fusion.1
  268.3 0.2 reshape.132
  268.5 0.6 copy.92
  269.1 69.1 %all-to-all-done.3 = bf16[8,2,20,8192]{3,1,2,0:T(2,128)(2,1)} async-done(((bf16[8,2,20,8192]{3,1,2,0:T(2,128)(2,1)}), bf16[8,2,20,8192]{3,1,2,0:T(2,128)(2,1)}, u32[]{:S(2)}, u32[]{:S(2)}) %all-to-all-start.3) | async-done | bytes 5242912 | tf_op jit(solution)/shard_map/all_to_all | solution.py:81
  338.2 8.9 %copy.89 = bf16[8,2,20,8192]{3,2,1,0:T(8,128)(2,1)} copy(bf16[8,2,20,8192]{3,1,2,0:T(2,128)(2,1)} %all-to-all-done.3) | data formatting | bytes 10485760 | tf_op jit(solution)/shard_map/all_to_all | solution.py:81
  347.2 8.0 %reshape.129 = bf16[320,8192]{1,0:T(8,128)(2,1)} reshape(bf16[8,2,20,8192]{3,2,1,0:T(8,128)(2,1)} %copy.89) | data formatting | bytes 10485760 | tf_op jit(solution)/shard_map/reshape | solution.py:84
  355.2 12.2 %gather_fusion = bf16[256,8192]{1,0:T(8,128)(2,1)} fusion(bf16[320,8192]{1,0:T(8,128)(2,1)} %reshape.129, s32[1024]{0:T(1024)S(1)} %pad_clamp_fusion), kind=kCustom, calls=%fused_computation.1 | custom fusion | bytes 8389632 | tf_op jit(solution)/shard_map/gather | solution.py:85
  367.4 0.0 copy-start.1
  367.4 7.8 %reshape.130 = bf16[128,2,8192]{2,1,0:T(2,128)(2,1)} reshape(bf16[256,8192]{1,0:T(8,128)(2,1)} %gather_fusion) | data formatting | bytes 8388608 | tf_op jit(solution)/shard_map/reshape | solution.py:85
  375.2 12.9 %reduce_sum.34 = bf16[128,8192]{1,0:T(8,128)(2,1)} reduce(bf16[128,2,8192]{2,1,0:T(2,128)(2,1)} %reshape.130, bf16[]{:T(256)} %constant.14.clone.1), dimensions={1}, to_apply=%region_6.7 | reduce | flops 1048576 | bytes 6291458 | tf_op jit(solution)/shard_map/reduce_sum | solution.py:86
  388.2 0.0 reduce-scatter.5.cloned.1.call-done
  388.2 0.0 copy-done.1
  (9 shorter events, 0.1 us)
Async XLA Ops:
  8.0 24.1 %copy-start = (bf16[128,8192]{1,0:T(8,128)(2,1)S(1)}, bf16[128,8192]{1,0:T(8,128)(2,1)}, u32[]{:S(2)}) copy-start(bf16[128,8192]{1,0:T(8,128)(2,1)} %param.6) | copy-start | bytes 6291460
  14.9 13.7 %all-to-all-start = ((bf16[8,2,20]{2,1,0:T(2,128)(2,1)}), bf16[8,2,20]{2,1,0:T(2,128)(2,1)S(1)}, u32[]{:S(2)}, u32[]{:S(2)}) async-start(bf16[8,2,20]{2,1,0:T(2,128)(2,1)} %reshape.125), calls=%async_computation | async-start | bytes 8192 | tf_op jit(solution)/shard_map/all_to_all | solution.py:75
  28.6 41.5 %all-to-all-start.2 = ((bf16[8,2,1280]{2,1,0:T(2,128)(2,1)}), bf16[8,2,1280]{2,1,0:T(2,128)(2,1)S(1)}, u32[]{:S(2)}, u32[]{:S(2)}) async-start(bf16[8,2,1280]{2,1,0:T(2,128)(2,1)} %reshape.195), calls=%async_computation.2 | async-start | bytes 81920 | tf_op jit(solution)/shard_map/all_to_all | solution.py:74
  70.1 120.0 %all-to-all-start.1 = ((bf16[8,2,20,8192]{3,1,2,0:T(2,128)(2,1)}), bf16[8,2,20,8192]{3,1,2,0:T(2,128)(2,1)}, u32[]{:S(2)}, u32[]{:S(2)}) async-start(bf16[8,2,20,8192]{3,1,2,0:T(2,128)(2,1)} %copy.84), calls=%async_computation.1 | async-start | bytes 10485760 | tf_op jit(solution)/shard_map/all_to_all | solution.py:73
  76.0 26.4 %all-gather.3.cloned.1.call-start = ((), (), s32[]{:S(2)}) async-start(), calls=%async_computation.7 | async-start | bytes 2621440 | tf_op jit(solution)/shard_map/all_gather | solution.py:70
  76.7 124.9 %all-gather.5.cloned.1.call-start = ((), (), s32[]{:S(2)}) async-start(), calls=%async_computation.8 | async-start | bytes 2621440 | tf_op jit(solution)/shard_map/all_gather | solution.py:69
  198.0 18.9 %all-to-all-start.4 = ((bf16[8,2,20]{2,1,0:T(2,128)(2,1)}), bf16[8,2,20]{2,1,0:T(2,128)(2,1)S(1)}, u32[]{:S(2)}, u32[]{:S(2)}) async-start(bf16[8,2,20]{2,1,0:T(2,128)(2,1)} %copy.90), calls=%async_computation.4 | async-start | bytes 8192 | tf_op jit(solution)/shard_map/all_to_all | solution.py:82
  216.9 121.4 %all-to-all-start.3 = ((bf16[8,2,20,8192]{3,1,2,0:T(2,128)(2,1)}), bf16[8,2,20,8192]{3,1,2,0:T(2,128)(2,1)}, u32[]{:S(2)}, u32[]{:S(2)}) async-start(bf16[8,2,20,8192]{3,1,2,0:T(2,128)(2,1)} %copy.88), calls=%async_computation.3 | async-start | bytes 10485760 | tf_op jit(solution)/shard_map/all_to_all | solution.py:81
  222.9 43.4 %reduce-scatter.3.cloned.1.call-start = ((), (), s32[]{:S(2)}) async-start(), calls=%async_computation.9 | async-start | bytes 3145728 | tf_op jit(solution)/shard_map/reduce_scatter | solution.py:89
  233.1 155.1 %reduce-scatter.5.cloned.1.call-start = ((), (), s32[]{:S(2)}) async-start(), calls=%async_computation.10 | async-start | bytes 1572864 | tf_op jit(solution)/shard_map/reduce_scatter | solution.py:93
  367.4 20.8 %copy-start.1 = (bf16[128,8192]{1,0:T(8,128)(2,1)S(1)}, bf16[128,8192]{1,0:T(8,128)(2,1)}, u32[]{:S(2)}) copy-start(bf16[128,8192]{1,0:T(8,128)(2,1)} %param.6) | copy-start | bytes 6291460
Sparse Core Ops, SparseCore 0:
  78.4 23.9 all-gather.2
  104.0 22.5 all-gather.4
Sparse Core Ops, SparseCore 1:
  233.1 33.1 reduce-scatter.2
  269.0 8.5 reduce-scatter.4
where the time goes:
time: 400 us; the launch traced here: 396 us
  waiting for transfers between devices  219 us (55%)
  local copies, waits for them, and re-layouts  98.4 us (25%)
  starting transfers between devices  27.1 us (7%)
  matrix products  20.7 us (5%)
  between operations  15.9 us (4%)
  other arithmetic  14.5 us (4%)
    all_to_all x1, waiting for transfers between devices, body(): lax.all_to_all(send_grads, 'expert', split_axis=0, concat_axis=0, tiled=T...  87.6 us
    all_to_all x1, waiting for transfers between devices, body(): lax.all_to_all(route_rows, 'expert', split_axis=0, concat_axis=0, tiled=T...  69.1 us
    reduce_scatter x1, waiting for transfers between devices, body(): lax.psum_scatter(inner_terms.astype(jnp.bfloat16), 'inner', scatter_dimen...  33.1 us
    all_gather x1, waiting for transfers between devices, body(): lax.all_gather(down_weight, ('inner', 'outer'), axis=2, tiled=True)  24.8 us
    scatter x1, local copies, waits for them, and re-layouts, body(): send_grads = jnp.zeros((expert_total * capacity, model_width), jnp.bfloat...  21.2 us
    reshape x2, local copies, waits for them, and re-layouts, body(): send_grads.reshape(senders, local_experts, capacity, model_width)  16.8 us
    reduce_sum x1, other arithmetic, body(): jnp.sum(picked, axis=1, dtype=jnp.float32).astype(jnp.bfloat16)  12.9 us
    gather x1, local copies, waits for them, and re-layouts, body(): picked = flat_rows[slot_ids].reshape(tok_count, top_count, model_width)  12.2 us
  transfers between devices with their start and end apart: 9, of which 5 were waited for; matrix products, arithmetic and copies ran while one was open for 32% of the time, Pallas kernels for 0%

commit v1 on v0

v1 whole, which is shorter than its diff:
```python
import functools
import jax
import jax.numpy as jnp
from jax import lax
from jax.experimental import pallas as pl
from jax.experimental.pallas import tpu as pltpu
from jax.sharding import Mesh, PartitionSpec as P

root_half = 0.7071067811865476
inv_root_tau = 0.3989422804014327
GROUP = ("inner", "outer", "near")
BLOCK = 256
MIB = 1 << 20


def gelu_parts(preact):
    cumulative = 0.5 * (1.0 + lax.erf(preact * root_half))
    density = inv_root_tau * jnp.exp(-0.5 * preact * preact)
    return (preact * cumulative, cumulative + preact * density)


def params():
    return pltpu.CompilerParams(vmem_limit_bytes=40 * MIB)


def low_half(shape):
    return lax.broadcasted_iota(jnp.int32, shape, len(shape) - 1) < shape[-1] // 2


def down_kernel(hidden, ids_ref, weighted_ref, tokens_ref, out_ref, spread):
    first = pl.program_id(0) * (out_ref.shape[0] // hidden)
    for expert in range(out_ref.shape[0] // hidden):
        number = first + expert
        spread[expert * hidden : (expert + 1) * hidden, :] = jnp.where(
            ids_ref[0:1, :] == number,
            weighted_ref[0:hidden, :],
            jnp.where(ids_ref[1:2, :] == number, weighted_ref[hidden:, :], 0.0),
        ).astype(jnp.bfloat16)
    out_ref[...] = jnp.dot(
        spread[...], tokens_ref[...], preferred_element_type=jnp.float32
    ).astype(out_ref.dtype)


def down_partial(ids_t, weighted_t, tokens, experts, hidden):
    total, features = tokens.shape
    return pl.pallas_call(
        functools.partial(down_kernel, hidden),
        grid=(experts * hidden // BLOCK,),
        in_specs=[
            pl.BlockSpec((2, total), lambda i: (0, 0)),
            pl.BlockSpec((2 * hidden, total), lambda i: (0, 0)),
            pl.BlockSpec((total, features), lambda i: (0, 0)),
        ],
        out_specs=pl.BlockSpec((BLOCK, features), lambda i: (i, 0)),
        out_shape=jax.ShapeDtypeStruct((experts * hidden, features), jnp.bfloat16),
        scratch_shapes=[pltpu.VMEM((BLOCK, total), jnp.bfloat16)],
        compiler_params=params(),
        cost_estimate=pl.CostEstimate(
            flops=2 * experts * hidden * features * total,
            bytes_accessed=2 * features * (total + experts * hidden),
            transcendentals=0,
        ),
    )(ids_t, weighted_t, tokens)


def project_kernel(ids_ref, tokens_ref, weight_ref, out_ref):
    rows, wide = out_ref.shape
    odd = jnp.where(low_half((rows, wide)), 0, 1)
    first = ids_ref[:, 0:1] - odd
    second = ids_ref[:, 1:2] - odd
    sums = [jnp.zeros((rows, wide), jnp.float32) for _ in range(2)]
    for start in range(0, weight_ref.shape[0], BLOCK):
        product = lax.dot_general(
            tokens_ref[...],
            weight_ref[start : start + BLOCK, :],
            (((1,), (1,)), ((), ())),
            preferred_element_type=jnp.float32,
        )
        for at in range(0, BLOCK, wide):
            part = product[:, at : at + wide]
            number = (start + at) // wide * 2
            sums[0] = jnp.where(first == number, part, sums[0])
            sums[1] = jnp.where(second == number, part, sums[1])
    folded = [value + pltpu.roll(value, wide // 2, 1) for value in sums]
    out_ref[...] = jnp.where(odd == 0, folded[0], folded[1])


def project(ids, tokens, weight, hidden):
    total, features = tokens.shape
    return pl.pallas_call(
        project_kernel,
        grid=(total // BLOCK,),
        in_specs=[
            pl.BlockSpec((BLOCK, 2), lambda i: (i, 0)),
            pl.BlockSpec((BLOCK, features), lambda i: (i, 0)),
            pl.BlockSpec(weight.shape, lambda i: (0, 0)),
        ],
        out_specs=pl.BlockSpec((BLOCK, 2 * hidden), lambda i: (i, 0)),
        out_shape=jax.ShapeDtypeStruct((total, 2 * hidden), jnp.float32),
        compiler_params=params(),
        cost_estimate=pl.CostEstimate(
            flops=2 * weight.shape[0] * features * total,
            bytes_accessed=2 * features * (total + weight.shape[0]),
            transcendentals=0,
        ),
    )(ids, tokens, weight)


def hidden_kernel(parts_ref, gates_ref, activation_ref, slope_ref, hidden_ref, gate_ref):
    projected = parts_ref[0]
    for source in range(1, parts_ref.shape[0]):
        projected = projected + parts_ref[source]
    low = low_half(projected.shape)
    gate_terms = activation_ref[...] * projected
    first = jnp.sum(jnp.where(low, gate_terms, 0.0), axis=1, keepdims=True)
    second = jnp.sum(jnp.where(low, 0.0, gate_terms), axis=1, keepdims=True)
    gate_ref[:, 0:1] = first.astype(gate_ref.dtype)
    gate_ref[:, 1:2] = second.astype(gate_ref.dtype)
    hidden_ref[...] = (gates_ref[...] * projected * slope_ref[...]).astype(hidden_ref.dtype)


def input_kernel(ids_ref, hidden_ref, weight_ref, out_ref, spread):
    rows, wide = hidden_ref.shape
    low = low_half((rows, wide))
    odd = jnp.where(low, 0, 1)
    first = ids_ref[:, 0:1] - odd
    second = ids_ref[:, 1:2] - odd
    values = hidden_ref[...].astype(jnp.float32)
    swapped = pltpu.roll(values, wide // 2, 1)
    one = jnp.where(low, values, swapped)
    two = jnp.where(low, swapped, values)
    for start in range(0, weight_ref.shape[0], wide):
        number = start // wide * 2
        spread[:, start : start + wide] = jnp.where(
            first == number, one, jnp.where(second == number, two, 0.0)
        ).astype(jnp.bfloat16)
    out_ref[...] = jnp.dot(
        spread[...], weight_ref[...], preferred_element_type=jnp.float32
    ).astype(out_ref.dtype)


def input_rows(ids, hidden_grad, weight):
    total, wide = hidden_grad.shape
    features = weight.shape[1]
    return pl.pallas_call(
        input_kernel,
        grid=(total // BLOCK,),
        in_specs=[
            pl.BlockSpec((BLOCK, 2), lambda i: (i, 0)),
            pl.BlockSpec((BLOCK, wide), lambda i: (i, 0)),
            pl.BlockSpec(weight.shape, lambda i: (0, 0)),
        ],
        out_specs=pl.BlockSpec((BLOCK, features), lambda i: (i, 0)),
        out_shape=jax.ShapeDtypeStruct((total, features), jnp.bfloat16),
        scratch_shapes=[pltpu.VMEM((BLOCK, weight.shape[0]), jnp.bfloat16)],
        compiler_params=params(),
        cost_estimate=pl.CostEstimate(
            flops=2 * weight.shape[0] * features * total,
            bytes_accessed=2 * features * (total + weight.shape[0]),
            transcendentals=0,
        ),
    )(ids, hidden_grad, weight)


def body(token_grads, router_gates, expert_ids, saved_hidden, up_weight, down_weight):
    tok_count, model_width = token_grads.shape
    local_experts, hidden = up_weight.shape[:2]
    experts = local_experts * lax.axis_size("far") * lax.axis_size("near")
    members = lax.axis_size(GROUP)
    wide = 2 * hidden

    def everywhere(weight):
        mine = lax.all_to_all(weight, "near", split_axis=2, concat_axis=0, tiled=True)
        full = lax.all_gather(mine, "far", axis=0, tiled=True)
        return full.reshape(experts * hidden, full.shape[2])

    gates = router_gates.astype(jnp.float32)
    gates = jnp.where(low_half((tok_count, wide)), gates[:, 0:1], gates[:, 1:2])
    activation, slope = gelu_parts(saved_hidden.astype(jnp.float32))
    weighted = (gates * activation).astype(jnp.bfloat16)
    tokens = lax.all_to_all(token_grads, GROUP, split_axis=1, concat_axis=0, tiled=True)
    ids = lax.all_gather(expert_ids, GROUP, axis=0, tiled=True)
    weighted = lax.all_gather(weighted, GROUP, axis=0, tiled=True)
    down_full = everywhere(down_weight)
    up_full = everywhere(up_weight)

    partial_value = down_partial(
        ids.T, weighted.T.astype(jnp.float32), tokens, experts, hidden
    ).reshape(experts, hidden, tokens.shape[1])
    far_sum = lax.psum_scatter(partial_value, "far", scatter_dimension=0, tiled=True)
    down_grads = lax.all_to_all(far_sum, "near", split_axis=0, concat_axis=2, tiled=True)

    parts = project(ids, tokens, down_full, hidden).reshape(members, tok_count, wide)
    parts = lax.all_to_all(parts, GROUP, split_axis=0, concat_axis=0, tiled=True)
    hidden_grad, gate_grads = pl.pallas_call(
        hidden_kernel,
        out_shape=(
            jax.ShapeDtypeStruct((tok_count, wide), jnp.bfloat16),
            jax.ShapeDtypeStruct(router_gates.shape, jnp.bfloat16),
        ),
        compiler_params=params(),
    )(parts, gates, activation, slope)
    hidden_grad = lax.all_gather(hidden_grad, GROUP, axis=0, tiled=True)
    rows = input_rows(ids, hidden_grad, up_full)
    input_grads = lax.all_to_all(rows, GROUP, split_axis=0, concat_axis=1, tiled=True)
    return (input_grads, gate_grads, down_grads)


def solution(mesh):
    sizes = [mesh.shape[name] for name in ("expert", "inner", "outer")]
    split = Mesh(
        mesh.devices.reshape(sizes[0] // 2, 2, *sizes[1:]), ("far", "near", "inner", "outer")
    )
    rows = P(("far", "near", "inner", "outer"), None)
    weights = P(("far", "near"), None, ("inner", "outer"))
    return jax.shard_map(
        body,
        mesh=split,
        in_specs=(rows, rows, rows, rows, weights, weights),
        out_specs=(rows, rows, weights),
        check_vma=False,
    )
```

time: 400 us -> 190 us (0.47)
  waiting for transfers between devices: 219 us -> 15.2 us
  blocking collectives: 0 us -> 118 us
  local copies, waits for them, and re-layouts: 98.4 us -> 19.2 us
  matrix products: 20.7 us -> 0 us
  starting transfers between devices: 27.1 us -> 10.8 us
  other arithmetic: 14.5 us -> 0.14 us
  Pallas kernels: 0 us -> 11.8 us
    all_to_all x5 -> x3, waiting for transfers between devices: 160 us -> 15.1 us  [the longest x1 8.47 us: body(): lax.all_to_all(parts, GROUP, split_axis=0, concat_axis=0, tiled=True)]
    all_gather x0 -> x3, blocking collectives: none -> 67.7 us  [the longest x1 34 us: body(): ids = lax.all_gather(expert_ids, GROUP, axis=0, tiled=True)]
    all_to_all x0 -> x3, blocking collectives: none -> 50.2 us  [the longest x1 28.7 us: body(): lax.all_to_all(rows, GROUP, split_axis=0, concat_axis=1, tiled=True)]
    reshape x11 -> x0, local copies, waits for them, and re-layouts: 34.6 us -> none  [the longest x2 16.8 us: body(): send_grads.reshape(senders, local_experts, capacity, model_width)]
    reduce_scatter x2 -> x1, waiting for transfers between devices: 33.1 us -> 0.01 us  [body(): lax.psum_scatter(partial_value, 'far', scatter_dimension=0, tiled=True)]
    all_gather x2, waiting for transfers between devices: 24.8 us -> 0.02 us  [everywhere(): full = lax.all_gather(mine, 'far', axis=0, tiled=True)]
    scatter x3 -> x0, local copies, waits for them, and re-layouts: 24.5 us -> none  [the longest x1 21.2 us: body(): send_grads = jnp.zeros((expert_total * capacity, model_width), jnp.bfloat...]
    dot_general x3 -> x0, matrix products: 20.7 us -> none  [the longest x1 9.96 us: expert_pass(): jnp.einsum('secf,secd->efd', weighted, slot_grads, preferred_element_type...]
  transfers between devices with their start and end apart: 9 -> 6, of which waited for: 5 -> 2; matrix products, arithmetic and copies ran while one was open for 32% -> 5% of each run, Pallas kernels for 0% -> 6%
where the time goes in v1:
time: 190 us; the launch traced here: 189 us
  blocking collectives  118 us (62%)
  local copies, waits for them, and re-layouts  19.2 us (10%)
  waiting for transfers between devices  15.2 us (8%)
  between operations  14 us (7%)
  Pallas kernels  11.8 us (6%)
  starting transfers between devices  10.8 us (6%)
    all_gather x1, blocking collectives, body(): ids = lax.all_gather(expert_ids, GROUP, axis=0, tiled=True)  34 us
    all_to_all x1, blocking collectives, body(): lax.all_to_all(rows, GROUP, split_axis=0, concat_axis=1, tiled=True)  28.7 us
    all_to_all x2, blocking collectives, everywhere(): lax.all_to_all(weight, 'near', split_axis=2, concat_axis=0, tiled=True)  21.5 us
    all_gather x1, blocking collectives, body(): weighted = lax.all_gather(weighted, GROUP, axis=0, tiled=True)  17 us
    all_gather x1, blocking collectives, body(): hidden_grad = lax.all_gather(hidden_grad, GROUP, axis=0, tiled=True)  16.7 us
    unnamed x22, local copies, waits for them, and re-layouts  10.2 us
    all_to_all x1, waiting for transfers between devices, body(): lax.all_to_all(parts, GROUP, split_axis=0, concat_axis=0, tiled=True)  8.47 us
    all_to_all x1, waiting for transfers between devices, body(): lax.all_to_all(far_sum, 'near', split_axis=0, concat_axis=2, tiled=True)  6.61 us
  transfers between devices with their start and end apart: 6, of which 2 were waited for; matrix products, arithmetic and copies ran while one was open for 5% of the time, Pallas kernels for 6%

profile of v1, /device:TPU:0, one launch (start us, length us, event | category | flops | bytes accessed | tf_op | source)
XLA Modules:
  0.0 189.0 jit_solution(13812415143592963084)
XLA Ops:
  7.2 0.0 all-gather.3.cloned.1.call-start
  7.2 2.4 %copy.22 = bf16[2,64,2048]{1,0,2:T(2,128)(2,1)S(1)} copy(bf16[2,64,2048]{2,1,0:T(8,128)(2,1)} %param.11) | data formatting | bytes 1048576 | tf_op args[5]
  9.6 0.8 reshape.28
  10.4 12.0 %all_to_all.97 = bf16[2,2,65536]{2,1,0:T(2,128)(2,1)S(1)} all-to-all(bf16[2,2,65536]{2,1,0:T(2,128)(2,1)S(1)} %reshape.28), channel_id=1, replica_groups=mesh['far'=4,'near'=2,'inner'=2,'outer'=2] {'near'}, dimensions={0} | all-to-all | bytes 1048576 | tf_op jit(solution)/shard_map/all_to_all | solution.py:173
  22.4 0.0 copy-start.3
  22.4 0.7 reshape.29
  23.2 1.9 copy.23
  25.0 0.0 all-gather.3.cloned.1.call-update
  25.0 0.0 all-gather.5.cloned.1.call-start
  25.1 0.0 copy-done.3
  25.1 0.8 copy.29
  25.9 0.8 reshape.30
  26.7 9.5 %all_to_all.98 = bf16[2,2,65536]{2,1,0:T(2,128)(2,1)S(1)} all-to-all(bf16[2,2,65536]{2,1,0:T(2,128)(2,1)S(1)} %reshape.30), channel_id=1, replica_groups=mesh['far'=4,'near'=2,'inner'=2,'outer'=2] {'near'}, dimensions={0} | all-to-all | bytes 1048576 | tf_op jit(solution)/shard_map/all_to_all | solution.py:173
  36.2 0.7 reshape.31
  36.9 0.0 copy-start.2
  36.9 1.9 copy.30
  38.8 0.0 all-gather.5.cloned.1.call-update
  38.8 0.0 copy-done.2
  38.8 1.6 copy.39
  40.4 0.0 copy-start.6
  40.4 0.0 copy-start.4
  40.4 0.0 copy-start.5
  40.4 3.7 %all-to-all-start = ((bf16[128,8,1024]{2,0,1:T(8,128)(2,1)}), bf16[128,8,1024]{2,0,1:T(8,128)(2,1)S(1)}, u32[]{:S(2)}, u32[]{:S(2)}) async-start(bf16[128,8,1024]{2,0,1:T(8,128)(2,1)} %bitcast.44), calls=%async_computation | async-start | bytes 4194304 | tf_op jit(solution)/shard_map/all_to_all | solution.py:181
  44.1 0.0 reduce-scatter.2.cloned.1.call-start
  44.2 0.0 copy-done.6
  44.2 0.0 copy-done.4
  44.2 0.1 copy.25
  44.3 0.0 copy-done.5
  44.3 34.0 %all_gather.15 = s32[1024,2]{0,1:T(2,128)S(1)} all-gather(s32[128,2]{0,1:T(2,128)S(1)} %copy-done.5), channel_id=1, replica_groups=mesh['far'=4,'near'=2,'inner'=2,'outer'=2] {'inner','outer','near'}, dimensions={0}, use_global_device_ids=true | all-gather | bytes 9216 | tf_op jit(solution)/shard_map/all_gather | solution.py:182
  78.4 0.1 multiply_convert_fusion
  78.5 17.0 %all_gather.19 = bf16[1024,128]{0,1:T(8,128)(2,1)S(1)} all-gather(bf16[128,128]{0,1:T(8,128)(2,1)S(1)} %get-tuple-element.13), channel_id=1, replica_groups=mesh['far'=4,'near'=2,'inner'=2,'outer'=2] {'inner','outer','near'}, dimensions={0}, use_global_device_ids=true | all-gather | bytes 294912 | tf_op jit(solution)/shard_map/all_gather | solution.py:183
  95.5 0.0 all-to-all-done
  95.5 3.8 %shard_map.88 = bf16[1024,1024]{1,0:T(8,128)(2,1)} custom-call(s32[2,1024]{1,0:T(2,128)S(1)} %bitcast.41, f32[128,1024]{1,0:T(8,128)S(1)} %convert_bitcast_fusion.weighted_ref, bf16[1024,1024]{1,0:T(8,128)(2,1)S(1)} %bitcast.38), custom_call_target="tpu_custom_call" | custom-call | flops 2147483648 | bytes 4194304 | tf_op jit(solution)/shard_map/pallas_call | solution.py:46
  99.3 0.0 reduce-scatter.2.cloned.1.call-update
  99.3 0.2 copy.31.ids_ref
  99.5 0.0 all-gather.3.cloned.1.call-done
  99.5 0.0 copy-start.1
  99.6 1.6 copy-done.1
  101.1 4.0 %shard_map.85 = f32[1024,128]{1,0:T(8,128)} custom-call(s32[1024,2]{1,0:T(8,128)S(1)} %copy.31.ids_ref, bf16[1024,1024]{1,0:T(8,128)(2,1)S(1)} %bitcast.39, bf16[1024,1024]{1,0:T(8,128)(2,1)S(1)} %bitcast.43), custom_call_target="tpu_custom_call" | custom-call | flops 2147483648 | bytes 4194304 | tf_op jit(solution)/shard_map/pallas_call | solution.py:90
  105.1 3.5 %all-to-all-start.2 = ((f32[8,128,128]{2,1,0:T(8,128)}), f32[8,128,128]{2,1,0:T(8,128)S(1)}, u32[]{:S(2)}, u32[]{:S(2)}) async-start(f32[8,128,128]{2,1,0:T(8,128)} %bitcast.6), calls=%async_computation.2 | async-start | bytes 1048576 | tf_op jit(solution)/shard_map/all_to_all | solution.py:194
  108.6 0.1 copy.26.gates_ref
  108.7 0.1 copy.27.activation_ref
  108.8 0.1 copy.28.slope_ref
  108.9 8.5 %all-to-all-done.2.parts_ref = f32[8,128,128]{2,1,0:T(8,128)S(1)} async-done(((f32[8,128,128]{2,1,0:T(8,128)}), f32[8,128,128]{2,1,0:T(8,128)S(1)}, u32[]{:S(2)}, u32[]{:S(2)}) %all-to-all-start.2) | async-done | bytes 524320 | tf_op jit(solution)/shard_map/all_to_all | solution.py:194
  117.4 0.1 shard_map.86
  117.5 16.7 %all_gather.17.hidden_ref = bf16[1024,128]{1,0:T(8,128)(2,1)S(1)} all-gather(bf16[128,128]{1,0:T(8,128)(2,1)S(1)} %get-tuple-element.5), channel_id=1, replica_groups=mesh['far'=4,'near'=2,'inner'=2,'outer'=2] {'inner','outer','near'}, dimensions={0}, use_global_device_ids=true | all-gather | bytes 294912 | tf_op jit(solution)/shard_map/all_gather | solution.py:203
  134.2 0.0 all-gather.5.cloned.1.call-done
  134.2 0.0 copy-start
  134.2 1.6 copy-done
  135.9 3.9 %shard_map.87 = bf16[1024,1024]{1,0:T(8,128)(2,1)S(1)} custom-call(s32[1024,2]{1,0:T(8,128)S(1)} %copy.31.ids_ref, bf16[1024,128]{1,0:T(8,128)(2,1)S(1)} %all_gather.17.hidden_ref, bf16[1024,1024]{1,0:T(8,128)(2,1)S(1)} %bitcast.42), custom_call_target="tpu_custom_call" | custom-call | flops 2147483648 | bytes 4194304 | tf_op jit(solution)/shard_map/pallas_call | solution.py:145
  139.8 28.7 %all_to_all.99 = bf16[8,128,1024]{2,1,0:T(8,128)(2,1)S(1)} all-to-all(bf16[8,128,1024]{2,1,0:T(8,128)(2,1)S(1)} %bitcast.40), channel_id=1, replica_groups=mesh['far'=4,'near'=2,'inner'=2,'outer'=2] {'inner','outer','near'}, dimensions={0} | all-to-all | bytes 4194304 | tf_op jit(solution)/shard_map/all_to_all | solution.py:205
  168.5 0.0 reduce-scatter.2.cloned.1.call-done
  168.5 3.5 %all-to-all-start.5 = ((bf16[4,64,1024]{2,1,0:T(8,128)(2,1)}), bf16[4,64,1024]{2,1,0:T(8,128)(2,1)S(1)}, u32[]{:S(2)}, u32[]{:S(2)}) async-start(bf16[4,64,1024]{2,1,0:T(8,128)(2,1)} %reduce-scatter.2.cloned.1.call-done), calls=%async_computation.6 | async-start | bytes 1048576 | tf_op jit(solution)/shard_map/all_to_all | solution.py:191
  172.0 0.6 copy.34
  172.6 1.6 copy.36
  174.1 6.6 %all-to-all-done.5 = bf16[4,64,1024]{2,1,0:T(8,128)(2,1)S(1)} async-done(((bf16[4,64,1024]{2,1,0:T(8,128)(2,1)}), bf16[4,64,1024]{2,1,0:T(8,128)(2,1)S(1)}, u32[]{:S(2)}, u32[]{:S(2)}) %all-to-all-start.5) | async-done | bytes 524320 | tf_op jit(solution)/shard_map/all_to_all | solution.py:191
  180.7 0.5 copy.40
  181.3 1.2 all_to_all.90
  (4 shorter events, 0.1 us)
Async XLA Ops:
  7.2 92.4 %all-gather.3.cloned.1.call-start = ((), (), s32[]{:S(2)}) async-start(), calls=%async_computation.7 | async-start | bytes 2621440 | tf_op jit(solution)/shard_map/all_gather | solution.py:174
  22.4 2.7 %copy-start.3 = (bf16[2,64,2048]{2,1,0:T(8,128)(2,1)S(1)}, bf16[2,64,2048]{2,1,0:T(8,128)(2,1)}, u32[]{:S(2)}) copy-start(bf16[2,64,2048]{2,1,0:T(8,128)(2,1)} %param.10) | copy-start | bytes 1572868
  25.0 109.2 %all-gather.5.cloned.1.call-start = ((), (), s32[]{:S(2)}) async-start(), calls=%async_computation.8 | async-start | bytes 2621440 | tf_op jit(solution)/shard_map/all_gather | solution.py:174
  36.9 1.9 %copy-start.2 = (bf16[128,8192]{1,0:T(8,128)(2,1)S(1)}, bf16[128,8192]{1,0:T(8,128)(2,1)}, u32[]{:S(2)}) copy-start(bf16[128,8192]{1,0:T(8,128)(2,1)} %param.6) | copy-start | bytes 6291460
  40.4 3.8 %copy-start.6 = (bf16[128,2]{0,1:T(2,128)(2,1)S(1)}, bf16[128,2]{0,1:T(2,128)(2,1)}, u32[]{:S(2)}) copy-start(bf16[128,2]{0,1:T(2,128)(2,1)} %param.7) | copy-start | bytes 1540
  40.4 3.8 %copy-start.4 = (bf16[128,128]{1,0:T(8,128)(2,1)S(1)}, bf16[128,128]{1,0:T(8,128)(2,1)}, u32[]{:S(2)}) copy-start(bf16[128,128]{1,0:T(8,128)(2,1)} %param.9) | copy-start | bytes 98308
  40.4 3.9 %copy-start.5 = (s32[128,2]{0,1:T(2,128)S(1)}, s32[128,2]{0,1:T(2,128)}, u32[]{:S(2)}) copy-start(s32[128,2]{0,1:T(2,128)} %param.8) | copy-start | bytes 3076
  40.4 55.1 %all-to-all-start = ((bf16[128,8,1024]{2,0,1:T(8,128)(2,1)}), bf16[128,8,1024]{2,0,1:T(8,128)(2,1)S(1)}, u32[]{:S(2)}, u32[]{:S(2)}) async-start(bf16[128,8,1024]{2,0,1:T(8,128)(2,1)} %bitcast.44), calls=%async_computation | async-start | bytes 4194304 | tf_op jit(solution)/shard_map/all_to_all | solution.py:181
  44.1 124.3 %reduce-scatter.2.cloned.1.call-start = ((), (), s32[]{:S(2)}) async-start(), calls=%async_computation.9 | async-start | bytes 2621440 | tf_op jit(solution)/shard_map/reduce_scatter | solution.py:190
  99.5 1.6 copy-start.1
  105.1 12.3 %all-to-all-start.2 = ((f32[8,128,128]{2,1,0:T(8,128)}), f32[8,128,128]{2,1,0:T(8,128)S(1)}, u32[]{:S(2)}, u32[]{:S(2)}) async-start(f32[8,128,128]{2,1,0:T(8,128)} %bitcast.6), calls=%async_computation.2 | async-start | bytes 1048576 | tf_op jit(solution)/shard_map/all_to_all | solution.py:194
  134.2 1.6 copy-start
  168.5 12.3 %all-to-all-start.5 = ((bf16[4,64,1024]{2,1,0:T(8,128)(2,1)}), bf16[4,64,1024]{2,1,0:T(8,128)(2,1)S(1)}, u32[]{:S(2)}, u32[]{:S(2)}) async-start(bf16[4,64,1024]{2,1,0:T(8,128)(2,1)} %reduce-scatter.2.cloned.1.call-done), calls=%async_computation.6 | async-start | bytes 1048576 | tf_op jit(solution)/shard_map/all_to_all | solution.py:191
Sparse Core Ops, SparseCore 0:
  25.2 46.3 all-gather.2
  73.1 44.6 all-gather.4
  120.7 42.5 reduce-scatter.1

commit v2 on v1

v2 whole, which is shorter than its diff:
```python
import functools
import jax
import jax.numpy as jnp
from jax import lax
from jax.experimental import pallas as pl
from jax.experimental.pallas import tpu as pltpu
from jax.sharding import Mesh, PartitionSpec as P

root_half = 0.7071067811865476
inv_root_tau = 0.3989422804014327
GROUP = ("inner", "outer", "near")
BLOCK = 256
MIB = 1 << 20
CHAIN = ((0, 1, 2, 3), (1, 0, 2, 3), (3, 2, 0, 1), (3, 2, 1, 0))
SIDES = ((0, 1), (1, 0), (2, 3), (3, 2))
MIDDLE = ((1, 2), (2, 1))
OUTWARD = ((1, 0), (2, 3))
INWARD = ((0, 1), (3, 2))
SWAP = ((0, 1), (1, 0))


def gelu_parts(preact):
    cumulative = 0.5 * (1.0 + lax.erf(preact * root_half))
    density = inv_root_tau * jnp.exp(-0.5 * preact * preact)
    return (preact * cumulative, cumulative + preact * density)


def params():
    return pltpu.CompilerParams(vmem_limit_bytes=40 * MIB)


def cost(rows, inner, columns):
    return pl.CostEstimate(
        flops=2 * rows * inner * columns,
        bytes_accessed=2 * (rows * inner + inner * columns + rows * columns),
        transcendentals=0,
    )


def low_half(shape):
    return lax.broadcasted_iota(jnp.int32, shape, len(shape) - 1) < shape[-1] // 2


def columns_of(pair, wide):
    wanted = lax.broadcasted_iota(jnp.int32, (2, wide), 0)
    return [
        lax.dot_general(
            pair.astype(jnp.bfloat16),
            jnp.where(wanted == k, 1.0, 0.0).astype(jnp.bfloat16),
            (((0,), (0,)), ((), ())),
            preferred_element_type=jnp.float32,
        )
        for k in range(2)
    ]


def prepare_kernel(ids_ref, gates_ref, preact_ref, sent_ref, activation_ref, scaled_ref):
    rows, wide = preact_ref.shape
    activation, slope = gelu_parts(preact_ref[...].astype(jnp.float32))
    gates = jnp.where(low_half((rows, wide)), *columns_of(gates_ref[...], wide))
    activation_ref[...] = activation
    scaled_ref[...] = gates * slope
    sent_ref[0:rows, :] = (gates * activation).astype(jnp.bfloat16)
    sent_ref[rows:, :] = jnp.zeros((sent_ref.shape[0] - rows, wide), jnp.bfloat16)
    sent_ref[rows : rows + 2, :] = ids_ref[...].astype(jnp.bfloat16)


def down_kernel(hidden, ids_ref, weighted_ref, tokens_ref, *refs):
    out_refs, spread = refs[:-1], refs[-1]
    turned = weighted_ref[...].astype(jnp.float32).T
    each = BLOCK // hidden
    at = 0
    for out_ref in out_refs:
        for start in range(0, out_ref.shape[0], BLOCK):
            for expert in range(each):
                spread[expert * hidden : (expert + 1) * hidden, :] = jnp.where(
                    ids_ref[0:1, :] == at + expert,
                    turned[0:hidden, :],
                    jnp.where(ids_ref[1:2, :] == at + expert, turned[hidden:, :], 0.0),
                ).astype(jnp.bfloat16)
            at += each
            out_ref[start : start + BLOCK, :] = jnp.dot(
                spread[...], tokens_ref[...], preferred_element_type=jnp.float32
            ).astype(out_ref.dtype)


def down_partial(ids, weighted, tokens, rows, count):
    total, features = tokens.shape
    return pl.pallas_call(
        functools.partial(down_kernel, weighted.shape[1] // 2),
        out_shape=[jax.ShapeDtypeStruct((rows // count, features), jnp.bfloat16)] * count,
        scratch_shapes=[pltpu.VMEM((BLOCK, total), jnp.bfloat16)],
        compiler_params=params(),
        cost_estimate=cost(rows, total, features),
    )(ids, weighted, tokens)


def join(pieces, piece_refs, full):
    at = start = 0
    for terms in pieces:
        value = piece_refs[at][...]
        for ref in piece_refs[at + 1 : at + terms]:
            value = value + ref[...]
        full[start : start + value.shape[0], :] = value
        at, start = at + terms, start + value.shape[0]


def project_kernel(pieces, ids_ref, tokens_ref, *refs):
    piece_refs, out_ref, full = refs[:-2], refs[-2], refs[-1]
    pl.when(pl.program_id(0) == 0)(lambda: join(pieces, piece_refs, full))
    rows, wide = out_ref.shape
    low = low_half((rows, wide))
    odd = jnp.where(low, 0.0, 1.0)
    first, second = [value - odd for value in columns_of(ids_ref[...], wide)]
    sums = [jnp.zeros((rows, wide), jnp.float32) for _ in range(2)]
    for start in range(0, full.shape[0], BLOCK):
        product = lax.dot_general(
            tokens_ref[...],
            full[start : start + BLOCK, :],
            (((1,), (1,)), ((), ())),
            preferred_element_type=jnp.float32,
        )
        for at in range(0, BLOCK, wide):
            part = product[:, at : at + wide]
            number = (start + at) // wide * 2.0
            sums[0] = jnp.where(first == number, part, sums[0])
            sums[1] = jnp.where(second == number, part, sums[1])
    folded = [value + pltpu.roll(value, wide // 2, 1) for value in sums]
    out_ref[...] = jnp.where(low, folded[0], folded[1])


def whole_block(array):
    return pl.BlockSpec(array.shape, lambda i: (0, 0))


def project(ids, tokens, pieces, hidden):
    total, features = tokens.shape
    flat = [term for terms in pieces for term in terms]
    rows = sum(terms[0].shape[0] for terms in pieces)
    return pl.pallas_call(
        functools.partial(project_kernel, [len(terms) for terms in pieces]),
        grid=(total // BLOCK,),
        in_specs=[
            pl.BlockSpec((2, BLOCK), lambda i: (0, i)),
            pl.BlockSpec((BLOCK, features), lambda i: (i, 0)),
            *map(whole_block, flat),
        ],
        out_specs=pl.BlockSpec((BLOCK, 2 * hidden), lambda i: (i, 0)),
        out_shape=jax.ShapeDtypeStruct((total, 2 * hidden), jnp.float32),
        scratch_shapes=[pltpu.VMEM((rows, features), jnp.bfloat16)],
        compiler_params=params(),
        cost_estimate=cost(total, features, rows),
    )(ids, tokens, *flat)


def hidden_kernel(parts_ref, activation_ref, scaled_ref, hidden_ref, gate_ref):
    projected = parts_ref[0]
    for source in range(1, parts_ref.shape[0]):
        projected = projected + parts_ref[source]
    wide = projected.shape[1]
    half = lax.broadcasted_iota(jnp.int32, (8, wide), 1) // (wide // 2)
    wanted = lax.broadcasted_iota(jnp.int32, (8, wide), 0)
    sums = lax.dot_general(
        jnp.where(wanted == half, 1.0, 0.0),
        activation_ref[...] * projected,
        (((1,), (1,)), ((), ())),
        precision=lax.Precision.HIGHEST,
        preferred_element_type=jnp.float32,
    )
    gate_ref[...] = sums[0:2, :].astype(gate_ref.dtype)
    hidden_ref[...] = (projected * scaled_ref[...]).astype(hidden_ref.dtype)


def input_kernel(pieces, ids_ref, hidden_ref, *refs):
    piece_refs, out_ref, full, spread = refs[:-3], refs[-3], refs[-2], refs[-1]
    pl.when(pl.program_id(0) == 0)(lambda: join(pieces, piece_refs, full))
    rows, wide = hidden_ref.shape
    low = low_half((rows, wide))
    odd = jnp.where(low, 0.0, 1.0)
    first, second = [value - odd for value in columns_of(ids_ref[...], wide)]
    values = hidden_ref[...].astype(jnp.float32)
    swapped = pltpu.roll(values, wide // 2, 1)
    one = jnp.where(low, values, swapped)
    two = jnp.where(low, swapped, values)
    for start in range(0, full.shape[0], wide):
        number = start // wide * 2.0
        spread[:, start : start + wide] = jnp.where(
            first == number, one, jnp.where(second == number, two, 0.0)
        ).astype(jnp.bfloat16)
    out_ref[...] = jnp.dot(
        spread[...], full[...], preferred_element_type=jnp.float32
    ).astype(out_ref.dtype)


def input_rows(ids, hidden_grad, pieces):
    total, wide = hidden_grad.shape
    flat = [term for terms in pieces for term in terms]
    rows, features = sum(terms[0].shape[0] for terms in pieces), flat[0].shape[1]
    return pl.pallas_call(
        functools.partial(input_kernel, [len(terms) for terms in pieces]),
        grid=(total // BLOCK,),
        in_specs=[
            pl.BlockSpec((2, BLOCK), lambda i: (0, i)),
            pl.BlockSpec((BLOCK, wide), lambda i: (i, 0)),
            *map(whole_block, flat),
        ],
        out_specs=pl.BlockSpec((BLOCK, features), lambda i: (i, 0)),
        out_shape=jax.ShapeDtypeStruct((total, features), jnp.bfloat16),
        scratch_shapes=[
            pltpu.VMEM((rows, features), jnp.bfloat16),
            pltpu.VMEM((BLOCK, rows), jnp.bfloat16),
        ],
        compiler_params=params(),
        cost_estimate=cost(total, rows, features),
    )(ids, hidden_grad, *flat)


def gather_far(mine):
    if lax.axis_size("far") != len(CHAIN):
        return [(lax.all_gather(mine, "far", axis=0, tiled=True),)]
    beside = lax.ppermute(mine, "far", SIDES)
    across = lax.ppermute(mine, "far", MIDDLE)
    across_far = lax.ppermute(beside, "far", MIDDLE)
    second = lax.ppermute(across, "far", OUTWARD)
    third = lax.ppermute(across_far, "far", OUTWARD)
    return [(mine,), (beside,), (across, second), (across_far, third)]


def add(*terms):
    return sum(term.astype(jnp.float32) for term in terms).astype(jnp.bfloat16)


def scatter_far(blocks):
    if lax.axis_size("far") != len(CHAIN):
        return lax.psum_scatter(blocks[0], "far", scatter_dimension=0, tiled=True)
    own, beside, second, third = blocks
    third = add(third, lax.ppermute(third, "far", INWARD))
    second = add(second, lax.ppermute(second, "far", INWARD))
    beside = add(beside, lax.ppermute(third, "far", MIDDLE))
    across = lax.ppermute(second, "far", MIDDLE)
    return add(own, across, lax.ppermute(beside, "far", SIDES))


def gather_group(value):
    value = value[None]
    for axis in reversed(GROUP):
        if lax.axis_size(axis) == 2:
            other = lax.ppermute(value, axis, SWAP)
            swapped = lax.axis_index(axis) == 1
            value = jnp.concatenate(
                [jnp.where(swapped, other, value), jnp.where(swapped, value, other)], axis=0
            )
        else:
            value = lax.all_gather(value, axis, axis=0, tiled=True)
    return value


def body(token_grads, router_gates, expert_ids, saved_hidden, up_weight, down_weight):
    tok_count, model_width = token_grads.shape
    local_experts, hidden, width = up_weight.shape
    far_count, near_count = lax.axis_size("far"), lax.axis_size("near")
    experts = local_experts * far_count * near_count
    members = lax.axis_size(GROUP)
    total, wide, half = members * tok_count, 2 * hidden, width // near_count
    rows = local_experts * hidden
    far, near = lax.axis_index("far"), lax.axis_index("near")

    def halves(weight):
        flat = weight.reshape(rows, width)
        own = lax.dynamic_slice_in_dim(flat, near * half, half, axis=1)
        other = lax.dynamic_slice_in_dim(flat, (1 - near) * half, half, axis=1)
        return own, lax.ppermute(other, "near", SWAP)

    down_own, down_other = halves(down_weight)
    up_own, up_other = halves(up_weight)
    down_pieces = gather_far(down_own) + gather_far(down_other)
    up_pieces = gather_far(up_own) + gather_far(up_other)

    sent, activation, scaled = pl.pallas_call(
        prepare_kernel,
        out_shape=(
            jax.ShapeDtypeStruct((tok_count + 16, wide), jnp.bfloat16),
            jax.ShapeDtypeStruct((tok_count, wide), jnp.float32),
            jax.ShapeDtypeStruct((tok_count, wide), jnp.float32),
        ),
        compiler_params=params(),
    )(expert_ids.T, router_gates.T, saved_hidden)
    tokens = lax.all_to_all(token_grads, GROUP, split_axis=1, concat_axis=0, tiled=True)
    sent = gather_group(sent)
    weighted = sent[:, :tok_count].reshape(total, wide)
    ids = sent[:, tok_count : tok_count + 2].astype(jnp.int32)
    ids = jnp.swapaxes(ids, 0, 1).reshape(2, total)
    far_place = ids // (near_count * local_experts)
    if far_count == len(CHAIN):
        places = jnp.asarray(CHAIN, jnp.int32)[far]
        far_place = sum(jnp.where(far_place == at, places[at], 0) for at in range(len(CHAIN)))
    near_place = (ids // local_experts % near_count) ^ near
    local = ids % local_experts
    place = (near_place * far_count + far_place) * local_experts + local
    grad_place = (far_place * near_count + near_place) * local_experts + local

    blocks = down_partial(
        grad_place, weighted, tokens, experts * hidden,
        len(CHAIN) if far_count == len(CHAIN) else 1,
    )
    sums = scatter_far(blocks)
    kept, passed = sums[:rows], lax.ppermute(sums[rows:], "near", SWAP)
    down_grads = jnp.concatenate(
        [jnp.where(near == 0, kept, passed), jnp.where(near == 0, passed, kept)], axis=1
    ).reshape(down_weight.shape)

    parts = project(place, tokens, down_pieces, hidden).reshape(members, tok_count, wide)
    parts = lax.all_to_all(parts, GROUP, split_axis=0, concat_axis=0, tiled=True)
    hidden_grad, gate_grads = pl.pallas_call(
        hidden_kernel,
        out_shape=(
            jax.ShapeDtypeStruct((tok_count, wide), jnp.bfloat16),
            jax.ShapeDtypeStruct((2, tok_count), jnp.bfloat16),
        ),
        compiler_params=params(),
    )(parts, activation, scaled)
    hidden_grad = gather_group(hidden_grad).reshape(total, wide)
    rows_back = input_rows(place, hidden_grad, up_pieces)
    input_grads = lax.all_to_all(rows_back, GROUP, split_axis=0, concat_axis=1, tiled=True)
    return (input_grads, gate_grads.T, down_grads)


def solution(mesh):
    sizes = [mesh.shape[name] for name in ("expert", "inner", "outer")]
    split = Mesh(
        mesh.devices.reshape(sizes[0] // 2, 2, *sizes[1:]), ("far", "near", "inner", "outer")
    )
    rows = P(("far", "near", "inner", "outer"), None)
    weights = P(("far", "near"), None, ("inner", "outer"))
    return jax.shard_map(
        body,
        mesh=split,
        in_specs=(rows, rows, rows, rows, weights, weights),
        out_specs=(rows, rows, weights),
        check_vma=False,
    )
```

time: 190 us -> 196 us (1.032)
  blocking collectives: 118 us -> 0 us
  waiting for transfers between devices: 15.2 us -> 87.4 us
  starting transfers between devices: 10.8 us -> 61.9 us
  between operations: 14 us -> 1.08 us
  other arithmetic: 0.14 us -> 10.7 us
  Pallas kernels: 11.8 us -> 16 us
    ppermute x0 -> x34, waiting for transfers between devices: none -> 87.3 us  [the longest x6 23.5 us: gather_group(): other = lax.ppermute(value, axis, SWAP)]
    all_gather x3 -> x0, blocking collectives: 67.7 us -> none  [the longest x1 34 us: body(): ids = lax.all_gather(expert_ids, GROUP, axis=0, tiled=True)]
    all_to_all x3 -> x0, blocking collectives: 50.2 us -> none  [the longest x1 28.7 us: body(): lax.all_to_all(rows, GROUP, split_axis=0, concat_axis=1, tiled=True)]
    ppermute x0 -> x34, starting transfers between devices: none -> 48.8 us  [the longest x6 6.8 us: gather_group(): other = lax.ppermute(value, axis, SWAP)]
    all_to_all x1, waiting for transfers between devices: 8.47 us -> 0.01 us  [body(): lax.all_to_all(parts, GROUP, split_axis=0, concat_axis=0, tiled=True)]
    all_to_all x1, waiting for transfers between devices: 6.61 us -> 0.01 us  [body(): lax.all_to_all(rows_back, GROUP, split_axis=0, concat_axis=1, tiled=True)]
    all_to_all x5 -> x1, local copies, waits for them, and re-layouts: 6.99 us -> 3.15 us  [body(): lax.all_to_all(rows_back, GROUP, split_axis=0, concat_axis=1, tiled=True)]
    convert_element_type x3 -> x4, other arithmetic: 0.14 us -> 3.77 us  [add(): sum((term.astype(jnp.float32) for term in terms)).astype(jnp.bfloat16)]
  transfers between devices with their start and end apart: 6 -> 37, of which waited for: 2 -> 15; matrix products, arithmetic and copies ran while one was open for 5% -> 7% of each run, Pallas kernels for 6% -> 8%
where the time goes in v2:
time: 196 us; the launch traced here: 195 us
  waiting for transfers between devices  87.4 us (45%)
  starting transfers between devices  61.9 us (32%)
  local copies, waits for them, and re-layouts  17.7 us (9%)
  Pallas kernels  16 us (8%)
  other arithmetic  10.7 us (5%)
    ppermute x6, waiting for transfers between devices, gather_group(): other = lax.ppermute(value, axis, SWAP)  23.5 us
    ppermute x4, waiting for transfers between devices, gather_far(): third = lax.ppermute(across_far, 'far', OUTWARD)  13.9 us
    ppermute x1, waiting for transfers between devices, scatter_far(): return add(own, across, lax.ppermute(beside, 'far', SIDES))  12.2 us
    ppermute x1, waiting for transfers between devices, body(): kept, passed = (sums[:rows], lax.ppermute(sums[rows:], 'near', SWAP))  11.3 us
    ppermute x4, waiting for transfers between devices, gather_far(): second = lax.ppermute(across, 'far', OUTWARD)  10.8 us
    unnamed x36, local copies, waits for them, and re-layouts  7.59 us
    ppermute x4, waiting for transfers between devices, gather_far(): beside = lax.ppermute(mine, 'far', SIDES)  7.38 us
    pallas_call x1, Pallas kernels, input_rows(): pl.pallas_call(functools.partial(input_kernel, [len(terms) for terms in p...  6.81 us
  transfers between devices with their start and end apart: 37, of which 15 were waited for; matrix products, arithmetic and copies ran while one was open for 7% of the time, Pallas kernels for 8%

profile of v2, /device:TPU:0, one launch (start us, length us, event | category | flops | bytes accessed | tf_op | source)
XLA Modules:
  0.0 194.8 jit_solution(4464977218130406088)
XLA Ops:
  0.6 3.1 %copy.15 = bf16[16,8,8,1024]{3,2,0,1:T(8,128)(2,1)} copy(bf16[16,8,8,1024]{3,2,1,0:T(8,128)(2,1)} %bitcast.69) | data formatting | bytes 4194304 | tf_op jit(solution)/shard_map/all_to_all | solution.py:288
  3.8 5.3 %all-to-all-start = ((bf16[128,8,1024]{2,0,1:T(8,128)(2,1)}), bf16[128,8,1024]{2,0,1:T(8,128)(2,1)S(1)}, u32[]{:S(2)}, u32[]{:S(2)}) async-start(bf16[128,8,1024]{2,0,1:T(8,128)(2,1)} %bitcast.68), calls=%async_computation | async-start | bytes 4194304 | tf_op jit(solution)/shard_map/all_to_all | solution.py:288
  9.3 2.1 %collective-permute-start = (bf16[1,144,128]{2,1,0:T(8,128)(2,1)S(1)}, bf16[1,144,128]{2,1,0:T(8,128)(2,1)S(1)}, u32[]{:S(2)}, u32[]{:S(2)}) collective-permute-start(bf16[1,144,128]{2,1,0:T(8,128)(2,1)S(1)} %bitcast.64), channel_id=1, source_target_pairs={{0,4},{4,0},{1,5},{5,1},{2,6},{6,2},{3,7},{7,3},{8,12},{12,8},{9,1... | collective-permute-start | bytes 110600 | tf_op jit(solution)/shard_map/ppermute | solution.py:248
  11.4 0.7 constant_dynamic-slice_fusion.2
  12.1 1.6 collective-permute-start.3
  13.7 1.3 collective-permute-start.4
  15.1 21.0 %collective-permute-done = bf16[1,144,128]{2,1,0:T(8,128)(2,1)S(1)} collective-permute-done((bf16[1,144,128]{2,1,0:T(8,128)(2,1)S(1)}, bf16[1,144,128]{2,1,0:T(8,128)(2,1)S(1)}, u32[]{:S(2)}, u32[]{:S(2)}) %collective-permute-start) | collective-permute-done | bytes 36896 | tf_op jit(solution)/shard_map/ppermute | solution.py:248
  36.2 1.8 constant_dynamic-slice_fusion
  37.9 3.4 %collective-permute-done.8.refs_6_ = bf16[128,1024]{1,0:T(8,128)(2,1)} collective-permute-done((bf16[128,1024]{1,0:T(8,128)(2,1)}, bf16[128,1024]{1,0:T(8,128)(2,1)}, u32[]{:S(2)}, u32[]{:S(2)}) %collective-permute-start.8) | collective-permute-done | bytes 262176 | tf_op jit(solution)/shard_map/ppermute | solution.py:272
  41.3 1.6 collective-permute-start.9
  43.6 1.5 collective-permute-start.2
  45.8 1.4 collective-permute-start.10
  47.1 1.4 collective-permute-start.6
  48.5 0.9 collective-permute-done.9.refs_7_
  49.4 1.4 collective-permute-start.12
  52.1 1.0 broadcast_select_fusion.3
  53.1 1.3 collective-permute-start.5
  54.4 1.3 collective-permute-start.7
  55.7 1.3 collective-permute-start.11
  57.1 1.3 collective-permute-start.13
  58.4 2.5 %multiply_add_fusion = (s32[2,1024]{1,0:T(2,128)S(1)}, s32[2,1024]{1,0:T(2,128)S(1)}, s32[2,1024]{1,0:T(2,128)S(1)}, bf16[8,2,128]{2,1,0:T(2,128)(2,1)S(1)}) fusion(s32[]{:T(128)S(6)} %axis_index.64, s32[]{:T(128)} %bitcast.9, s32[]{:T(128)} %bitcast.8, s32[]{:T(128)} %bitcast.7, s32[]{:T(128)} %bitcast.6, bf16[4,144,128]{2,1,0:T(8,128)(2,1)S(1)} %get-tuple-element.32, ...), kind=kLoop, calls=%fused_computation.49 | loop fusion | flops 124928 | bytes 323604 | tf_op jit(solution)/shard_map/add | solution.py:300
  60.9 5.4 %collective-permute-done.5.refs_3_ = bf16[128,1024]{1,0:T(8,128)(2,1)S(1)} collective-permute-done((bf16[128,1024]{1,0:T(8,128)(2,1)}, bf16[128,1024]{1,0:T(8,128)(2,1)S(1)}, u32[]{:S(2)}, u32[]{:S(2)}) %collective-permute-start.5) | collective-permute-done | bytes 262176 | tf_op jit(solution)/shard_map/ppermute | solution.py:224
  67.0 5.6 %collective-permute-done.7.refs_5_ = bf16[128,1024]{1,0:T(8,128)(2,1)S(1)} collective-permute-done((bf16[128,1024]{1,0:T(8,128)(2,1)}, bf16[128,1024]{1,0:T(8,128)(2,1)S(1)}, u32[]{:S(2)}, u32[]{:S(2)}) %collective-permute-start.7) | collective-permute-done | bytes 262176 | tf_op jit(solution)/shard_map/ppermute | solution.py:225
  73.3 4.9 %collective-permute-done.11.refs_9_ = bf16[128,1024]{1,0:T(8,128)(2,1)S(1)} collective-permute-done((bf16[128,1024]{1,0:T(8,128)(2,1)}, bf16[128,1024]{1,0:T(8,128)(2,1)S(1)}, u32[]{:S(2)}, u32[]{:S(2)}) %collective-permute-start.11) | collective-permute-done | bytes 262176 | tf_op jit(solution)/shard_map/ppermute | solution.py:224
  78.9 3.1 %collective-permute-done.13.refs_11_ = bf16[128,1024]{1,0:T(8,128)(2,1)S(1)} collective-permute-done((bf16[128,1024]{1,0:T(8,128)(2,1)}, bf16[128,1024]{1,0:T(8,128)(2,1)S(1)}, u32[]{:S(2)}, u32[]{:S(2)}) %collective-permute-start.13) | collective-permute-done | bytes 262176 | tf_op jit(solution)/shard_map/ppermute | solution.py:225
  82.7 0.9 copy-done.7
  83.6 0.9 copy-done.9
  84.6 0.9 copy-done.11
  85.5 0.9 copy-done.13
  86.5 5.9 %shard_map.95 = f32[1024,128]{1,0:T(8,128)} custom-call(s32[2,1024]{1,0:T(2,128)S(1)} %multiply_add_fusion.1.ids_ref, bf16[1024,1024]{1,0:T(8,128)(2,1)S(1)} %bitcast.60, bf16[128,1024]{1,0:T(8,128)(2,1)S(1)} %get-tuple-element.30.refs_0_, bf16[128,1024]{1,0:T(8,128)(2,1)S(1)} %collective-permute-done.3.refs_1_, ...), custom_call_target="tpu_custom_call" | custom-call | flops 2147483648 | bytes 6291456 | tf_op jit(solution)/shard_map/pallas_call | solution.py:140
  92.4 3.5 %all-to-all-start.1 = ((f32[8,128,128]{2,1,0:T(8,128)}), f32[8,128,128]{2,1,0:T(8,128)S(1)}, u32[]{:S(2)}, u32[]{:S(2)}) async-start(f32[8,128,128]{2,1,0:T(8,128)} %bitcast.13), calls=%async_computation.1 | async-start | bytes 1048576 | tf_op jit(solution)/shard_map/all_to_all | solution.py:313
  96.0 2.0 %collective-permute-start.23 = (bf16[128,1024]{1,0:T(8,128)(2,1)}, bf16[128,1024]{1,0:T(8,128)(2,1)}, u32[]{:S(2)}, u32[]{:S(2)}) collective-permute-start(bf16[128,1024]{1,0:T(8,128)(2,1)} %collective-permute-done.22.refs_6_), channel_id=1, source_target_pairs={{0,8},{8,0},{16,24},{24,16},{1,9},{9,1},{17,25},{25,17},{2,10},{10... | collective-permute-start | bytes 786440 | tf_op jit(solution)/shard_map/ppermute | solution.py:221
  98.0 1.3 collective-permute-start.18
  99.3 1.7 pad_maximum_fusion.1
  101.0 1.4 collective-permute-start.24
  102.4 2.8 %collective-permute-done.17.refs_1_ = bf16[128,1024]{1,0:T(8,128)(2,1)} collective-permute-done((bf16[128,1024]{1,0:T(8,128)(2,1)S(1)}, bf16[128,1024]{1,0:T(8,128)(2,1)}, u32[]{:S(2)}, u32[]{:S(2)}) %collective-permute-start.17) | collective-permute-done | bytes 262176 | tf_op jit(solution)/shard_map/ppermute | solution.py:221
  105.2 1.4 collective-permute-start.20
  106.5 3.7 %collective-permute-done.23.refs_7_ = bf16[128,1024]{1,0:T(8,128)(2,1)} collective-permute-done((bf16[128,1024]{1,0:T(8,128)(2,1)}, bf16[128,1024]{1,0:T(8,128)(2,1)}, u32[]{:S(2)}, u32[]{:S(2)}) %collective-permute-start.23) | collective-permute-done | bytes 262176 | tf_op jit(solution)/shard_map/ppermute | solution.py:221
  110.2 1.4 collective-permute-start.26
  112.3 1.7 collective-permute-start.14
  114.0 0.9 copy-done.2
  114.9 2.4 %shard_map.98 = (bf16[256,1024]{1,0:T(8,128)(2,1)S(1)}, bf16[256,1024]{1,0:T(8,128)(2,1)S(1)}, bf16[256,1024]{1,0:T(8,128)(2,1)S(1)}, bf16[256,1024]{1,0:T(8,128)(2,1)S(1)}) custom-call(s32[2,1024]{1,0:T(2,128)S(1)} %get-tuple-element.21.ids_ref, bf16[1024,128]{1,0:T(8,128)(2,1)S(1)} %bitcast.62, bf16[1024,1024]{1,0:T(8,128)(2,1)S(1)} %bitcast.61), custom_call_target="tpu_custom_call" | custom-call | flops 2147483648 | bytes 6291456 | tf_op jit(solution)/shard_map/pallas_call | solution.py:89
  117.4 3.3 %collective-permute-start.30 = (bf16[256,1024]{1,0:T(8,128)(2,1)S(1)}, bf16[256,1024]{1,0:T(8,128)(2,1)S(1)}, u32[]{:S(2)}, u32[]{:S(2)}) collective-permute-start(bf16[256,1024]{1,0:T(8,128)(2,1)S(1)} %get-tuple-element.20), channel_id=1, source_target_pairs={{0,8},{24,16},{1,9},{25,17},{2,10},{26,18},{3,11},{27,19},{4,12},{... | collective-permute-start | bytes 1572872 | tf_op jit(solution)/shard_map/ppermute | solution.py:237
  120.8 1.3 collective-permute-start.19
  122.1 1.3 collective-permute-start.21
  123.4 1.3 collective-permute-start.25
  124.7 1.3 collective-permute-start.27
  126.1 5.0 %collective-permute-done.30 = bf16[256,1024]{1,0:T(8,128)(2,1)S(1)} collective-permute-done((bf16[256,1024]{1,0:T(8,128)(2,1)S(1)}, bf16[256,1024]{1,0:T(8,128)(2,1)S(1)}, u32[]{:S(2)}, u32[]{:S(2)}) %collective-permute-start.30) | collective-permute-done | bytes 524320 | tf_op jit(solution)/shard_map/ppermute | solution.py:237
  131.0 1.5 collective-permute-start.16
  132.5 1.0 add_convert_fusion.2
  133.5 2.5 %collective-permute-done.16 = bf16[4,128,128]{2,1,0:T(8,128)(2,1)S(1)} collective-permute-done((bf16[4,128,128]{2,1,0:T(8,128)(2,1)S(1)}, bf16[4,128,128]{2,1,0:T(8,128)(2,1)S(1)}, u32[]{:S(2)}, u32[]{:S(2)}) %collective-permute-start.16) | collective-permute-done | bytes 131104 | tf_op jit(solution)/shard_map/ppermute | solution.py:248
  136.0 5.2 %collective-permute-start.28 = (bf16[256,1024]{1,0:T(8,128)(2,1)S(1)}, bf16[256,1024]{1,0:T(8,128)(2,1)}, u32[]{:S(2)}, u32[]{:S(2)}) collective-permute-start(bf16[256,1024]{1,0:T(8,128)(2,1)S(1)} %get-tuple-element.18), channel_id=1, source_target_pairs={{0,8},{24,16},{1,9},{25,17},{2,10},{26,18},{3,11},{27,19},{4,12},{... | collective-permute-start | bytes 1572872 | tf_op jit(solution)/shard_map/ppermute | solution.py:238
  141.2 1.5 collective-permute-start.31
  143.2 5.2 %collective-permute-done.27.refs_11_ = bf16[128,1024]{1,0:T(8,128)(2,1)S(1)} collective-permute-done((bf16[128,1024]{1,0:T(8,128)(2,1)}, bf16[128,1024]{1,0:T(8,128)(2,1)S(1)}, u32[]{:S(2)}, u32[]{:S(2)}) %collective-permute-start.27) | collective-permute-done | bytes 262176 | tf_op jit(solution)/shard_map/ppermute | solution.py:225
  148.4 6.8 %shard_map.97 = bf16[1024,1024]{1,0:T(8,128)(2,1)} custom-call(s32[2,1024]{1,0:T(2,128)S(1)} %multiply_add_fusion.1.ids_ref, bf16[1024,128]{1,0:T(8,128)(2,1)S(1)} %bitcast.63, bf16[128,1024]{1,0:T(8,128)(2,1)S(1)} %get-tuple-element.28.refs_0_, bf16[128,1024]{1,0:T(8,128)(2,1)} %collective-permute-done.17.refs_1_, ...), custom_call_target="tpu_custom_call" | custom-call | flops 2147483648 | bytes 6291456 | tf_op jit(solution)/shard_map/pallas_call | solution.py:199
  155.3 4.3 %all-to-all-start.2 = ((bf16[8,128,1024]{2,1,0:T(8,128)(2,1)}), bf16[8,128,1024]{2,1,0:T(8,128)(2,1)}, u32[]{:S(2)}, u32[]{:S(2)}) async-start(bf16[8,128,1024]{2,1,0:T(8,128)(2,1)} %bitcast.17), calls=%async_computation.2 | async-start | bytes 4194304 | tf_op jit(solution)/shard_map/all_to_all | solution.py:324
  159.6 1.3 add_convert_fusion.3
  161.6 1.2 add_convert_fusion.1
  162.9 2.5 %collective-permute-start.32 = (bf16[256,1024]{1,0:T(8,128)(2,1)S(1)}, bf16[256,1024]{1,0:T(8,128)(2,1)S(1)}, u32[]{:S(2)}, u32[]{:S(2)}) collective-permute-start(bf16[256,1024]{1,0:T(8,128)(2,1)S(1)} %add_convert_fusion.1), channel_id=1, source_target_pairs={{0,8},{8,0},{16,24},{24,16},{1,9},{9,1},{17,25},{25,17},{2,10},{10... | collective-permute-start | bytes 1572872 | tf_op jit(solution)/shard_map/ppermute | solution.py:241
  165.3 12.2 %collective-permute-done.32 = bf16[256,1024]{1,0:T(8,128)(2,1)S(1)} collective-permute-done((bf16[256,1024]{1,0:T(8,128)(2,1)S(1)}, bf16[256,1024]{1,0:T(8,128)(2,1)S(1)}, u32[]{:S(2)}, u32[]{:S(2)}) %collective-permute-start.32) | collective-permute-done | bytes 524320 | tf_op jit(solution)/shard_map/ppermute | solution.py:241
  177.8 1.7 collective-permute-start.33
  179.5 11.3 %collective-permute-done.33 = bf16[128,1024]{1,0:T(8,128)(2,1)S(1)} collective-permute-done((bf16[128,1024]{1,0:T(8,128)(2,1)S(1)}, bf16[128,1024]{1,0:T(8,128)(2,1)S(1)}, u32[]{:S(2)}, u32[]{:S(2)}) %collective-permute-start.33) | collective-permute-done | bytes 262176 | tf_op jit(solution)/shard_map/ppermute | solution.py:307
  190.8 0.8 pad_maximum_fusion
  191.7 3.2 %copy.13 = bf16[8,16,8,1024]{3,2,0,1:T(8,128)(2,1)} copy(bf16[8,16,8,1024]{3,2,1,0:T(8,128)(2,1)} %bitcast.25) | data formatting | bytes 4194304 | tf_op jit(solution)/shard_map/all_to_all | solution.py:324
  (78 shorter events, 8.5 us)
Async XLA Ops:
  3.8 5.3 %copy-start.3 = (bf16[128,128]{1,0:T(8,128)(2,1)S(1)}, bf16[128,128]{1,0:T(8,128)(2,1)}, u32[]{:S(2)}) copy-start(bf16[128,128]{1,0:T(8,128)(2,1)} %preact_ref.1) | copy-start | bytes 98308
  3.8 5.3 %copy-start.4 = (s32[128,2]{0,1:T(2,128)S(1)}, s32[128,2]{0,1:T(2,128)}, u32[]{:S(2)}) copy-start(s32[128,2]{0,1:T(2,128)} %param.9) | copy-start | bytes 3076
  3.8 5.3 %copy-start.5 = (bf16[128,2]{0,1:T(2,128)(2,1)S(1)}, bf16[128,2]{0,1:T(2,128)(2,1)}, u32[]{:S(2)}) copy-start(bf16[128,2]{0,1:T(2,128)(2,1)} %param.8) | copy-start | bytes 1540
  3.8 7.6 %copy-start.17 = (bf16[2,64,2048]{2,1,0:T(8,128)(2,1)S(1)}, bf16[2,64,2048]{2,1,0:T(8,128)(2,1)}, u32[]{:S(2)}) copy-start(bf16[2,64,2048]{2,1,0:T(8,128)(2,1)} %param.12) | copy-start | bytes 1572868
  3.8 78.9 %all-to-all-start = ((bf16[128,8,1024]{2,0,1:T(8,128)(2,1)}), bf16[128,8,1024]{2,0,1:T(8,128)(2,1)S(1)}, u32[]{:S(2)}, u32[]{:S(2)}) async-start(bf16[128,8,1024]{2,0,1:T(8,128)(2,1)} %bitcast.68), calls=%async_computation | async-start | bytes 4194304 | tf_op jit(solution)/shard_map/all_to_all | solution.py:288
  9.3 26.7 %collective-permute-start = (bf16[1,144,128]{2,1,0:T(8,128)(2,1)S(1)}, bf16[1,144,128]{2,1,0:T(8,128)(2,1)S(1)}, u32[]{:S(2)}, u32[]{:S(2)}) collective-permute-start(bf16[1,144,128]{2,1,0:T(8,128)(2,1)S(1)} %bitcast.64), channel_id=1, source_target_pairs={{0,4},{4,0},{1,5},{5,1},{2,6},{6,2},{3,7},{7,3},{8,12},{12,8},{9,1... | collective-permute-start | bytes 110600 | tf_op jit(solution)/shard_map/ppermute | solution.py:248
  12.1 35.0 %collective-permute-start.3 = (bf16[128,1024]{1,0:T(8,128)(2,1)S(1)}, bf16[128,1024]{1,0:T(8,128)(2,1)S(1)}, u32[]{:S(2)}, u32[]{:S(2)}) collective-permute-start(bf16[128,1024]{1,0:T(8,128)(2,1)S(1)} %get-tuple-element.30.refs_0_), channel_id=1, source_target_pairs={{0,8},{8,0},{16,24},{24,16},{1,9},{9,1},{17,25},{25,17},{2,10},{10... | collective-permute-start | bytes 786440 | tf_op jit(solution)/shard_map/ppermute | solution.py:221
  13.7 39.4 %collective-permute-start.4 = (bf16[128,1024]{1,0:T(8,128)(2,1)S(1)}, bf16[128,1024]{1,0:T(8,128)(2,1)}, u32[]{:S(2)}, u32[]{:S(2)}) collective-permute-start(bf16[128,1024]{1,0:T(8,128)(2,1)S(1)} %get-tuple-element.30.refs_0_), channel_id=1, source_target_pairs={{8,16},{16,8},{9,17},{17,9},{10,18},{18,10},{11,19},{19,11},{12,20... | collective-permute-start | bytes 786440 | tf_op jit(solution)/shard_map/ppermute | solution.py:222
  15.1 26.2 %collective-permute-start.8 = (bf16[128,1024]{1,0:T(8,128)(2,1)}, bf16[128,1024]{1,0:T(8,128)(2,1)}, u32[]{:S(2)}, u32[]{:S(2)}) collective-permute-start(bf16[128,1024]{1,0:T(8,128)(2,1)} %get-tuple-element.29), channel_id=1, source_target_pairs={{0,4},{4,0},{1,5},{5,1},{2,6},{6,2},{3,7},{7,3},{8,12},{12,8},{9,1... | collective-permute-start | bytes 786440 | tf_op jit(solution)/shard_map/ppermute | solution.py:272
  36.1 6.8 %collective-permute-start.1 = (bf16[2,144,128]{2,1,0:T(8,128)(2,1)S(1)}, bf16[2,144,128]{2,1,0:T(8,128)(2,1)S(1)}, u32[]{:S(2)}, u32[]{:S(2)}) collective-permute-start(bf16[2,144,128]{2,1,0:T(8,128)(2,1)S(1)} %pad_maximum_fusion.5), channel_id=1, source_target_pairs={{0,1},{1,0},{2,3},{3,2},{4,5},{5,4},{6,7},{7,6},{8,9},{9,8},{10,11... | collective-permute-start | bytes 221192 | tf_op jit(solution)/shard_map/ppermute | solution.py:248
  41.3 8.1 %collective-permute-start.9 = (bf16[128,1024]{1,0:T(8,128)(2,1)}, bf16[128,1024]{1,0:T(8,128)(2,1)S(1)}, u32[]{:S(2)}, u32[]{:S(2)}) collective-permute-start(bf16[128,1024]{1,0:T(8,128)(2,1)} %collective-permute-done.8.refs_6_), channel_id=1, source_target_pairs={{0,8},{8,0},{16,24},{24,16},{1,9},{9,1},{17,25},{25,17},{2,10},{10... | collective-permute-start | bytes 786440 | tf_op jit(solution)/shard_map/ppermute | solution.py:221
  42.9 8.5 %copy-start.16 = (bf16[2,144,128]{2,1,0:T(8,128)(2,1)}, bf16[2,144,128]{2,1,0:T(8,128)(2,1)S(1)}, u32[]{:S(2)}) copy-start(bf16[2,144,128]{2,1,0:T(8,128)(2,1)S(1)} %get-tuple-element.36) | copy-start | bytes 221188
  43.6 7.8 %collective-permute-start.2 = (bf16[4,144,128]{2,1,0:T(8,128)(2,1)}, bf16[4,144,128]{2,1,0:T(8,128)(2,1)}, u32[]{:S(2)}, u32[]{:S(2)}) collective-permute-start(bf16[4,144,128]{2,1,0:T(8,128)(2,1)} %pad_maximum_fusion.3), channel_id=1, source_target_pairs={{0,2},{2,0},{1,3},{3,1},{4,6},{6,4},{5,7},{7,5},{8,10},{10,8},{9,1... | collective-permute-start | bytes 442376 | tf_op jit(solution)/shard_map/ppermute | solution.py:248
  45.8 10.0 %collective-permute-start.10 = (bf16[128,1024]{1,0:T(8,128)(2,1)}, bf16[128,1024]{1,0:T(8,128)(2,1)}, u32[]{:S(2)}, u32[]{:S(2)}) collective-permute-start(bf16[128,1024]{1,0:T(8,128)(2,1)} %collective-permute-done.8.refs_6_), channel_id=1, source_target_pairs={{8,16},{16,8},{9,17},{17,9},{10,18},{18,10},{11,19},{19,11},{12,20... | collective-permute-start | bytes 786440 | tf_op jit(solution)/shard_map/ppermute | solution.py:222
  47.1 7.3 %collective-permute-start.6 = (bf16[128,1024]{1,0:T(8,128)(2,1)S(1)}, bf16[128,1024]{1,0:T(8,128)(2,1)}, u32[]{:S(2)}, u32[]{:S(2)}) collective-permute-start(bf16[128,1024]{1,0:T(8,128)(2,1)S(1)} %collective-permute-done.3.refs_1_), channel_id=1, source_target_pairs={{8,16},{16,8},{9,17},{17,9},{10,18},{18,10},{11,19},{19,11},{12,20... | collective-permute-start | bytes 786440 | tf_op jit(solution)/shard_map/ppermute | solution.py:223
  49.4 7.7 %collective-permute-start.12 = (bf16[128,1024]{1,0:T(8,128)(2,1)S(1)}, bf16[128,1024]{1,0:T(8,128)(2,1)}, u32[]{:S(2)}, u32[]{:S(2)}) collective-permute-start(bf16[128,1024]{1,0:T(8,128)(2,1)S(1)} %collective-permute-done.9.refs_7_), channel_id=1, source_target_pairs={{8,16},{16,8},{9,17},{17,9},{10,18},{18,10},{11,19},{19,11},{12,20... | collective-permute-start | bytes 786440 | tf_op jit(solution)/shard_map/ppermute | solution.py:223
  51.4 44.6 %collective-permute-start.22 = (bf16[128,1024]{1,0:T(8,128)(2,1)}, bf16[128,1024]{1,0:T(8,128)(2,1)}, u32[]{:S(2)}, u32[]{:S(2)}) collective-permute-start(bf16[128,1024]{1,0:T(8,128)(2,1)} %get-tuple-element.27), channel_id=1, source_target_pairs={{0,4},{4,0},{1,5},{5,1},{2,6},{6,2},{3,7},{7,3},{8,12},{12,8},{9,1... | collective-permute-start | bytes 786440 | tf_op jit(solution)/shard_map/ppermute | solution.py:272
  53.1 25.1 %copy-start.14 = (bf16[4,144,128]{2,1,0:T(8,128)(2,1)}, bf16[4,144,128]{2,1,0:T(8,128)(2,1)S(1)}, u32[]{:S(2)}) copy-start(bf16[4,144,128]{2,1,0:T(8,128)(2,1)S(1)} %get-tuple-element.31) | copy-start | bytes 442372
  53.1 25.1 %copy-start.15 = (bf16[4,144,128]{2,1,0:T(8,128)(2,1)}, bf16[4,144,128]{2,1,0:T(8,128)(2,1)S(1)}, u32[]{:S(2)}) copy-start(bf16[4,144,128]{2,1,0:T(8,128)(2,1)S(1)} %get-tuple-element.32) | copy-start | bytes 442372
  53.1 13.1 %collective-permute-start.5 = (bf16[128,1024]{1,0:T(8,128)(2,1)}, bf16[128,1024]{1,0:T(8,128)(2,1)S(1)}, u32[]{:S(2)}, u32[]{:S(2)}) collective-permute-start(bf16[128,1024]{1,0:T(8,128)(2,1)} %collective-permute-done.4.refs_2_), channel_id=1, source_target_pairs={{8,0},{16,24},{9,1},{17,25},{10,2},{18,26},{11,3},{19,27},{12,4},{... | collective-permute-start | bytes 786440 | tf_op jit(solution)/shard_map/ppermute | solution.py:224
  54.4 18.2 %collective-permute-start.7 = (bf16[128,1024]{1,0:T(8,128)(2,1)}, bf16[128,1024]{1,0:T(8,128)(2,1)S(1)}, u32[]{:S(2)}, u32[]{:S(2)}) collective-permute-start(bf16[128,1024]{1,0:T(8,128)(2,1)} %collective-permute-done.6.refs_4_), channel_id=1, source_target_pairs={{8,0},{16,24},{9,1},{17,25},{10,2},{18,26},{11,3},{19,27},{12,4},{... | collective-permute-start | bytes 786440 | tf_op jit(solution)/shard_map/ppermute | solution.py:225
  55.7 22.5 %collective-permute-start.11 = (bf16[128,1024]{1,0:T(8,128)(2,1)}, bf16[128,1024]{1,0:T(8,128)(2,1)S(1)}, u32[]{:S(2)}, u32[]{:S(2)}) collective-permute-start(bf16[128,1024]{1,0:T(8,128)(2,1)} %collective-permute-done.10.refs_8_), channel_id=1, source_target_pairs={{8,0},{16,24},{9,1},{17,25},{10,2},{18,26},{11,3},{19,27},{12,4},{... | collective-permute-start | bytes 786440 | tf_op jit(solution)/shard_map/ppermute | solution.py:224
  57.1 24.9 %collective-permute-start.13 = (bf16[128,1024]{1,0:T(8,128)(2,1)}, bf16[128,1024]{1,0:T(8,128)(2,1)S(1)}, u32[]{:S(2)}, u32[]{:S(2)}) collective-permute-start(bf16[128,1024]{1,0:T(8,128)(2,1)} %collective-permute-done.12.refs_10_), channel_id=1, source_target_pairs={{8,0},{16,24},{9,1},{17,25},{10,2},{18,26},{11,3},{19,27},{12,4},{... | collective-permute-start | bytes 786440 | tf_op jit(solution)/shard_map/ppermute | solution.py:225
  66.3 0.7 copy-start.6
  72.6 0.7 copy-start.8
  78.2 0.7 copy-start.10
  82.0 0.7 copy-start.12
  82.7 1.0 copy-start.7
  83.6 0.9 copy-start.9
  84.6 0.9 copy-start.11
  85.5 0.9 copy-start.13
  92.4 19.2 %all-to-all-start.1 = ((f32[8,128,128]{2,1,0:T(8,128)}), f32[8,128,128]{2,1,0:T(8,128)S(1)}, u32[]{:S(2)}, u32[]{:S(2)}) async-start(f32[8,128,128]{2,1,0:T(8,128)} %bitcast.13), calls=%async_computation.1 | async-start | bytes 1048576 | tf_op jit(solution)/shard_map/all_to_all | solution.py:313
  95.9 9.3 %collective-permute-start.17 = (bf16[128,1024]{1,0:T(8,128)(2,1)S(1)}, bf16[128,1024]{1,0:T(8,128)(2,1)}, u32[]{:S(2)}, u32[]{:S(2)}) collective-permute-start(bf16[128,1024]{1,0:T(8,128)(2,1)S(1)} %get-tuple-element.28.refs_0_), channel_id=1, source_target_pairs={{0,8},{8,0},{16,24},{24,16},{1,9},{9,1},{17,25},{25,17},{2,10},{10... | collective-permute-start | bytes 786440 | tf_op jit(solution)/shard_map/ppermute | solution.py:221
  96.0 14.3 %collective-permute-start.23 = (bf16[128,1024]{1,0:T(8,128)(2,1)}, bf16[128,1024]{1,0:T(8,128)(2,1)}, u32[]{:S(2)}, u32[]{:S(2)}) collective-permute-start(bf16[128,1024]{1,0:T(8,128)(2,1)} %collective-permute-done.22.refs_6_), channel_id=1, source_target_pairs={{0,8},{8,0},{16,24},{24,16},{1,9},{9,1},{17,25},{25,17},{2,10},{10... | collective-permute-start | bytes 786440 | tf_op jit(solution)/shard_map/ppermute | solution.py:221
  98.0 22.7 %collective-permute-start.18 = (bf16[128,1024]{1,0:T(8,128)(2,1)S(1)}, bf16[128,1024]{1,0:T(8,128)(2,1)}, u32[]{:S(2)}, u32[]{:S(2)}) collective-permute-start(bf16[128,1024]{1,0:T(8,128)(2,1)S(1)} %get-tuple-element.28.refs_0_), channel_id=1, source_target_pairs={{8,16},{16,8},{9,17},{17,9},{10,18},{18,10},{11,19},{19,11},{12,20... | collective-permute-start | bytes 786440 | tf_op jit(solution)/shard_map/ppermute | solution.py:222
  101.0 21.1 %collective-permute-start.24 = (bf16[128,1024]{1,0:T(8,128)(2,1)}, bf16[128,1024]{1,0:T(8,128)(2,1)}, u32[]{:S(2)}, u32[]{:S(2)}) collective-permute-start(bf16[128,1024]{1,0:T(8,128)(2,1)} %collective-permute-done.22.refs_6_), channel_id=1, source_target_pairs={{8,16},{16,8},{9,17},{17,9},{10,18},{18,10},{11,19},{19,11},{12,20... | collective-permute-start | bytes 786440 | tf_op jit(solution)/shard_map/ppermute | solution.py:222
  105.2 15.6 %collective-permute-start.20 = (bf16[128,1024]{1,0:T(8,128)(2,1)}, bf16[128,1024]{1,0:T(8,128)(2,1)}, u32[]{:S(2)}, u32[]{:S(2)}) collective-permute-start(bf16[128,1024]{1,0:T(8,128)(2,1)} %collective-permute-done.17.refs_1_), channel_id=1, source_target_pairs={{8,16},{16,8},{9,17},{17,9},{10,18},{18,10},{11,19},{19,11},{12,20... | collective-permute-start | bytes 786440 | tf_op jit(solution)/shard_map/ppermute | solution.py:223
  110.2 13.2 %collective-permute-start.26 = (bf16[128,1024]{1,0:T(8,128)(2,1)}, bf16[128,1024]{1,0:T(8,128)(2,1)}, u32[]{:S(2)}, u32[]{:S(2)}) collective-permute-start(bf16[128,1024]{1,0:T(8,128)(2,1)} %collective-permute-done.23.refs_7_), channel_id=1, source_target_pairs={{8,16},{16,8},{9,17},{17,9},{10,18},{18,10},{11,19},{19,11},{12,20... | collective-permute-start | bytes 786440 | tf_op jit(solution)/shard_map/ppermute | solution.py:223
  112.3 5.0 %collective-permute-start.14 = (bf16[1,128,128]{2,1,0:T(8,128)(2,1)S(1)}, bf16[1,128,128]{2,1,0:T(8,128)(2,1)S(1)}, u32[]{:S(2)}, u32[]{:S(2)}) collective-permute-start(bf16[1,128,128]{2,1,0:T(8,128)(2,1)S(1)} %bitcast.65), channel_id=1, source_target_pairs={{0,4},{4,0},{1,5},{5,1},{2,6},{6,2},{3,7},{7,3},{8,12},{12,8},{9,1... | collective-permute-start | bytes 98312 | tf_op jit(solution)/shard_map/ppermute | solution.py:248
  114.0 0.9 copy-start.2
  117.4 18.7 %copy-start = (bf16[256,1024]{1,0:T(8,128)(2,1)}, bf16[256,1024]{1,0:T(8,128)(2,1)S(1)}, u32[]{:S(2)}) copy-start(bf16[256,1024]{1,0:T(8,128)(2,1)S(1)} %get-tuple-element.17) | copy-start | bytes 1572868
  117.4 13.7 %collective-permute-start.30 = (bf16[256,1024]{1,0:T(8,128)(2,1)S(1)}, bf16[256,1024]{1,0:T(8,128)(2,1)S(1)}, u32[]{:S(2)}, u32[]{:S(2)}) collective-permute-start(bf16[256,1024]{1,0:T(8,128)(2,1)S(1)} %get-tuple-element.20), channel_id=1, source_target_pairs={{0,8},{24,16},{1,9},{25,17},{2,10},{26,18},{3,11},{27,19},{4,12},{... | collective-permute-start | bytes 1572872 | tf_op jit(solution)/shard_map/ppermute | solution.py:237
  120.7 4.0 %collective-permute-start.15 = (bf16[2,128,128]{2,1,0:T(8,128)(2,1)S(1)}, bf16[2,128,128]{2,1,0:T(8,128)(2,1)S(1)}, u32[]{:S(2)}, u32[]{:S(2)}) collective-permute-start(bf16[2,128,128]{2,1,0:T(8,128)(2,1)S(1)} %pad_maximum_fusion.6), channel_id=1, source_target_pairs={{0,1},{1,0},{2,3},{3,2},{4,5},{5,4},{6,7},{7,6},{8,9},{9,8},{10,11... | collective-permute-start | bytes 196616 | tf_op jit(solution)/shard_map/ppermute | solution.py:248
  120.8 20.4 %collective-permute-start.19 = (bf16[128,1024]{1,0:T(8,128)(2,1)}, bf16[128,1024]{1,0:T(8,128)(2,1)S(1)}, u32[]{:S(2)}, u32[]{:S(2)}) collective-permute-start(bf16[128,1024]{1,0:T(8,128)(2,1)} %collective-permute-done.18.refs_2_), channel_id=1, source_target_pairs={{8,0},{16,24},{9,1},{17,25},{10,2},{18,26},{11,3},{19,27},{12,4},{... | collective-permute-start | bytes 786440 | tf_op jit(solution)/shard_map/ppermute | solution.py:224
  122.1 20.6 %collective-permute-start.21 = (bf16[128,1024]{1,0:T(8,128)(2,1)}, bf16[128,1024]{1,0:T(8,128)(2,1)S(1)}, u32[]{:S(2)}, u32[]{:S(2)}) collective-permute-start(bf16[128,1024]{1,0:T(8,128)(2,1)} %collective-permute-done.20.refs_4_), channel_id=1, source_target_pairs={{8,0},{16,24},{9,1},{17,25},{10,2},{18,26},{11,3},{19,27},{12,4},{... | collective-permute-start | bytes 786440 | tf_op jit(solution)/shard_map/ppermute | solution.py:225
  123.4 19.8 %collective-permute-start.25 = (bf16[128,1024]{1,0:T(8,128)(2,1)}, bf16[128,1024]{1,0:T(8,128)(2,1)S(1)}, u32[]{:S(2)}, u32[]{:S(2)}) collective-permute-start(bf16[128,1024]{1,0:T(8,128)(2,1)} %collective-permute-done.24.refs_8_), channel_id=1, source_target_pairs={{8,0},{16,24},{9,1},{17,25},{10,2},{18,26},{11,3},{19,27},{12,4},{... | collective-permute-start | bytes 786440 | tf_op jit(solution)/shard_map/ppermute | solution.py:224
  124.7 23.7 %collective-permute-start.27 = (bf16[128,1024]{1,0:T(8,128)(2,1)}, bf16[128,1024]{1,0:T(8,128)(2,1)S(1)}, u32[]{:S(2)}, u32[]{:S(2)}) collective-permute-start(bf16[128,1024]{1,0:T(8,128)(2,1)} %collective-permute-done.26.refs_10_), channel_id=1, source_target_pairs={{8,0},{16,24},{9,1},{17,25},{10,2},{18,26},{11,3},{19,27},{12,4},{... | collective-permute-start | bytes 786440 | tf_op jit(solution)/shard_map/ppermute | solution.py:225
  131.0 5.0 %collective-permute-start.16 = (bf16[4,128,128]{2,1,0:T(8,128)(2,1)S(1)}, bf16[4,128,128]{2,1,0:T(8,128)(2,1)S(1)}, u32[]{:S(2)}, u32[]{:S(2)}) collective-permute-start(bf16[4,128,128]{2,1,0:T(8,128)(2,1)S(1)} %pad_maximum_fusion.4), channel_id=1, source_target_pairs={{0,2},{2,0},{1,3},{3,1},{4,6},{6,4},{5,7},{7,5},{8,10},{10,8},{9,1... | collective-permute-start | bytes 393224 | tf_op jit(solution)/shard_map/ppermute | solution.py:248
  136.0 23.6 %collective-permute-start.28 = (bf16[256,1024]{1,0:T(8,128)(2,1)S(1)}, bf16[256,1024]{1,0:T(8,128)(2,1)}, u32[]{:S(2)}, u32[]{:S(2)}) collective-permute-start(bf16[256,1024]{1,0:T(8,128)(2,1)S(1)} %get-tuple-element.18), channel_id=1, source_target_pairs={{0,8},{24,16},{1,9},{25,17},{2,10},{26,18},{3,11},{27,19},{4,12},{... | collective-permute-start | bytes 1572872 | tf_op jit(solution)/shard_map/ppermute | solution.py:238
  141.2 20.4 %collective-permute-start.31 = (bf16[256,1024]{1,0:T(8,128)(2,1)}, bf16[256,1024]{1,0:T(8,128)(2,1)}, u32[]{:S(2)}, u32[]{:S(2)}) collective-permute-start(bf16[256,1024]{1,0:T(8,128)(2,1)} %add_convert_fusion.2), channel_id=1, source_target_pairs={{8,16},{16,8},{9,17},{17,9},{10,18},{18,10},{11,19},{19,11},{12,20... | collective-permute-start | bytes 1572872 | tf_op jit(solution)/shard_map/ppermute | solution.py:239
  155.3 36.4 %all-to-all-start.2 = ((bf16[8,128,1024]{2,1,0:T(8,128)(2,1)}), bf16[8,128,1024]{2,1,0:T(8,128)(2,1)}, u32[]{:S(2)}, u32[]{:S(2)}) async-start(bf16[8,128,1024]{2,1,0:T(8,128)(2,1)} %bitcast.17), calls=%async_computation.2 | async-start | bytes 4194304 | tf_op jit(solution)/shard_map/all_to_all | solution.py:324
  159.6 17.9 %copy-start.1 = (bf16[256,1024]{1,0:T(8,128)(2,1)S(1)}, bf16[256,1024]{1,0:T(8,128)(2,1)}, u32[]{:S(2)}) copy-start(bf16[256,1024]{1,0:T(8,128)(2,1)} %copy-done) | copy-start | bytes 1572868
  160.9 4.4 %collective-permute-start.29 = (bf16[256,1024]{1,0:T(8,128)(2,1)S(1)}, bf16[256,1024]{1,0:T(8,128)(2,1)S(1)}, u32[]{:S(2)}, u32[]{:S(2)}) collective-permute-start(bf16[256,1024]{1,0:T(8,128)(2,1)S(1)} %add_convert_fusion.3), channel_id=1, source_target_pairs={{8,16},{16,8},{9,17},{17,9},{10,18},{18,10},{11,19},{19,11},{12,20... | collective-permute-start | bytes 1572872 | tf_op jit(solution)/shard_map/ppermute | solution.py:240
  162.9 14.6 %collective-permute-start.32 = (bf16[256,1024]{1,0:T(8,128)(2,1)S(1)}, bf16[256,1024]{1,0:T(8,128)(2,1)S(1)}, u32[]{:S(2)}, u32[]{:S(2)}) collective-permute-start(bf16[256,1024]{1,0:T(8,128)(2,1)S(1)} %add_convert_fusion.1), channel_id=1, source_target_pairs={{0,8},{8,0},{16,24},{24,16},{1,9},{9,1},{17,25},{25,17},{2,10},{10... | collective-permute-start | bytes 1572872 | tf_op jit(solution)/shard_map/ppermute | solution.py:241
  177.8 13.0 %collective-permute-start.33 = (bf16[128,1024]{1,0:T(8,128)(2,1)S(1)}, bf16[128,1024]{1,0:T(8,128)(2,1)S(1)}, u32[]{:S(2)}, u32[]{:S(2)}) collective-permute-start(bf16[128,1024]{1,0:T(8,128)(2,1)S(1)} %slice.37), channel_id=1, source_target_pairs={{0,4},{4,0},{1,5},{5,1},{2,6},{6,2},{3,7},{7,3},{8,12},{12,8},{9,1... | collective-permute-start | bytes 786440 | tf_op jit(solution)/shard_map/ppermute | solution.py:307

commit v3 on v1

v3 whole, which is shorter than its diff:
```python
import functools
import jax
import jax.numpy as jnp
from jax import lax
from jax.experimental import pallas as pl
from jax.experimental.pallas import tpu as pltpu
from jax.sharding import Mesh, PartitionSpec as P

root_half = 0.7071067811865476
inv_root_tau = 0.3989422804014327
GROUP = ("inner", "outer", "near")
NEAR = 4
BLOCK = 256
EXTRA = 16
MIB = 1 << 20


def gelu_parts(preact):
    cumulative = 0.5 * (1.0 + lax.erf(preact * root_half))
    density = inv_root_tau * jnp.exp(-0.5 * preact * preact)
    return (preact * cumulative, cumulative + preact * density)


def params():
    return pltpu.CompilerParams(vmem_limit_bytes=40 * MIB)


def cost(rows, inner, columns):
    return pl.CostEstimate(
        flops=2 * rows * inner * columns,
        bytes_accessed=2 * (rows * inner + inner * columns + rows * columns),
        transcendentals=0,
    )


def low_half(shape):
    return lax.broadcasted_iota(jnp.int32, shape, len(shape) - 1) < shape[-1] // 2


def columns_of(pair, wide):
    wanted = lax.broadcasted_iota(jnp.int32, (2, wide), 0)
    return [
        lax.dot_general(
            pair.astype(jnp.bfloat16),
            jnp.where(wanted == k, 1.0, 0.0).astype(jnp.bfloat16),
            (((0,), (0,)), ((), ())),
            preferred_element_type=jnp.float32,
        )
        for k in range(2)
    ]


def prepare_kernel(gates_ref, preact_ref, weighted_ref, activation_ref, scaled_ref):
    rows, wide = preact_ref.shape
    activation, slope = gelu_parts(preact_ref[...].astype(jnp.float32))
    gates = jnp.where(low_half((rows, wide)), *columns_of(gates_ref[...], wide))
    activation_ref[...] = activation
    scaled_ref[...] = gates * slope
    weighted_ref[...] = (gates * activation).astype(jnp.bfloat16)


def weights_kernel(down_ref, up_ref, out_ref):
    rows = out_ref.shape[2]
    out_ref[0, 0] = down_ref[...].reshape(rows, out_ref.shape[3])
    out_ref[0, 1] = up_ref[...].reshape(rows, out_ref.shape[3])


def pack_weights(down, up):
    local_experts, hidden, width = down.shape
    piece = width // NEAR
    spec = pl.BlockSpec((local_experts, hidden, piece), lambda i: (0, 0, i))
    rows = local_experts * hidden
    return pl.pallas_call(
        weights_kernel,
        grid=(NEAR,),
        in_specs=[spec, spec],
        out_specs=pl.BlockSpec((1, 2, rows, piece), lambda i: (i, 0, 0, 0)),
        out_shape=jax.ShapeDtypeStruct((NEAR, 2, rows, piece), jnp.bfloat16),
        compiler_params=params(),
    )(down, up)


def pack_kernel(ids_ref, tokens_ref, out_ref):
    blocks, rows, features = out_ref.shape
    rows -= EXTRA
    ids = ids_ref[...].astype(jnp.bfloat16)
    for block in range(blocks):
        out_ref[block, 0:rows, :] = tokens_ref[:, block * features : (block + 1) * features]
        out_ref[block, rows:, :] = jnp.zeros((EXTRA, features), jnp.bfloat16)
        out_ref[block, rows : rows + 2, 0:rows] = ids


def pack_tokens(ids, tokens, members):
    rows, width = tokens.shape
    features = width // members
    each = members // 4
    return pl.pallas_call(
        pack_kernel,
        grid=(4,),
        in_specs=[
            pl.BlockSpec(ids.shape, lambda i: (0, 0)),
            pl.BlockSpec((rows, each * features), lambda i: (0, i)),
        ],
        out_specs=pl.BlockSpec((each, rows + EXTRA, features), lambda i: (i, 0, 0)),
        out_shape=jax.ShapeDtypeStruct((members, rows + EXTRA, features), jnp.bfloat16),
        compiler_params=params(),
    )(ids, tokens)


def unpack_kernel(parts_ref, out_ref):
    blocks, _, features = parts_ref.shape
    for block in range(blocks):
        out_ref[:, block * features : (block + 1) * features] = parts_ref[block]


def unpack_tokens(parts):
    members, rows, features = parts.shape
    each = members // 4
    return pl.pallas_call(
        unpack_kernel,
        grid=(4,),
        in_specs=[pl.BlockSpec((each, rows, features), lambda i: (i, 0, 0))],
        out_specs=pl.BlockSpec((rows, each * features), lambda i: (0, i)),
        out_shape=jax.ShapeDtypeStruct((rows, members * features), jnp.bfloat16),
        compiler_params=params(),
    )(parts)


def down_kernel(received_ref, weighted_ref, out_ref, turned, numbers, spread):
    sources, rows, wide = weighted_ref.shape
    hidden, each = wide // 2, BLOCK // (wide // 2)

    @pl.when(pl.program_id(0) == 0)
    def _():
        for source in range(sources):
            at = slice(source * rows, (source + 1) * rows)
            turned[:, at] = weighted_ref[source].astype(jnp.float32).T
            numbers[:, at] = received_ref[source, rows : rows + 2, 0:rows].astype(jnp.float32)

    first = pl.program_id(0) * each
    for expert in range(each):
        number = (first + expert).astype(jnp.float32)
        spread[expert * hidden : (expert + 1) * hidden, :] = jnp.where(
            numbers[0:1, :] == number,
            turned[0:hidden, :],
            jnp.where(numbers[1:2, :] == number, turned[hidden:, :], 0.0),
        ).astype(jnp.bfloat16)
    tokens = received_ref[:, 0:rows, :].reshape(sources * rows, received_ref.shape[2])
    out_ref[...] = jnp.dot(
        spread[...], tokens, preferred_element_type=jnp.float32
    ).astype(out_ref.dtype)


def down_partial(received, weighted, rows):
    sources, _, features = received.shape
    total, wide = sources * weighted.shape[1], weighted.shape[2]
    return pl.pallas_call(
        down_kernel,
        grid=(rows // BLOCK,),
        in_specs=[
            pl.BlockSpec(received.shape, lambda i: (0, 0, 0)),
            pl.BlockSpec(weighted.shape, lambda i: (0, 0, 0)),
        ],
        out_specs=pl.BlockSpec((BLOCK, features), lambda i: (i, 0)),
        out_shape=jax.ShapeDtypeStruct((rows, features), jnp.bfloat16),
        scratch_shapes=[
            pltpu.VMEM((wide, total), jnp.float32),
            pltpu.VMEM((2, total), jnp.float32),
            pltpu.VMEM((BLOCK, total), jnp.bfloat16),
        ],
        compiler_params=params(),
        cost_estimate=cost(rows, total, features),
    )(received, weighted)


def lane_numbers(received_ref, rows, wide):
    low = low_half((received_ref.shape[0] * rows, wide))
    found = [
        columns_of(received_ref[source, rows : rows + 2, 0:rows], wide)
        for source in range(received_ref.shape[0])
    ]
    odd = jnp.where(low, 0.0, 1.0)
    return low, *[jnp.concatenate([pair[k] for pair in found]) - odd for k in range(2)]


def project_kernel(received_ref, weight_ref, out_ref):
    sources, rows, wide = out_ref.shape
    low, first, second = lane_numbers(received_ref, rows, wide)
    tokens = received_ref[:, 0:rows, :].reshape(sources * rows, received_ref.shape[2])
    sums = [jnp.zeros((sources * rows, wide), jnp.float32) for _ in range(2)]
    for start in range(0, weight_ref.shape[0], BLOCK):
        product = lax.dot_general(
            tokens,
            weight_ref[start : start + BLOCK, :],
            (((1,), (1,)), ((), ())),
            preferred_element_type=jnp.float32,
        )
        for at in range(0, BLOCK, wide):
            part = product[:, at : at + wide]
            number = (start + at) // wide * 2.0
            sums[0] = jnp.where(first == number, part, sums[0])
            sums[1] = jnp.where(second == number, part, sums[1])
    folded = [value + pltpu.roll(value, wide // 2, 1) for value in sums]
    value = jnp.where(low, folded[0], folded[1]).astype(out_ref.dtype)
    out_ref[...] = value.reshape(out_ref.shape)


def project(received, weight, hidden):
    sources, rows, features = received.shape
    return pl.pallas_call(
        project_kernel,
        grid=(sources // 2,),
        in_specs=[
            pl.BlockSpec((2, rows, features), lambda i: (i, 0, 0)),
            pl.BlockSpec(weight.shape, lambda i: (0, 0)),
        ],
        out_specs=pl.BlockSpec((2, rows - EXTRA, 2 * hidden), lambda i: (i, 0, 0)),
        out_shape=jax.ShapeDtypeStruct((sources, rows - EXTRA, 2 * hidden), jnp.bfloat16),
        compiler_params=params(),
        cost_estimate=cost(sources * rows, features, weight.shape[0]),
    )(received, weight)


def hidden_kernel(parts_ref, activation_ref, scaled_ref, hidden_ref, gate_ref):
    projected = parts_ref[0].astype(jnp.float32)
    for source in range(1, parts_ref.shape[0]):
        projected = projected + parts_ref[source].astype(jnp.float32)
    wide = projected.shape[1]
    half = lax.broadcasted_iota(jnp.int32, (8, wide), 1) // (wide // 2)
    wanted = lax.broadcasted_iota(jnp.int32, (8, wide), 0)
    sums = lax.dot_general(
        jnp.where(wanted == half, 1.0, 0.0),
        activation_ref[...] * projected,
        (((1,), (1,)), ((), ())),
        precision=lax.Precision.HIGHEST,
        preferred_element_type=jnp.float32,
    )
    gate_ref[...] = sums[0:2, :].astype(gate_ref.dtype)
    hidden = (projected * scaled_ref[...]).astype(hidden_ref.dtype)
    for source in range(hidden_ref.shape[0]):
        hidden_ref[source] = hidden


def input_kernel(received_ref, hidden_ref, weight_ref, out_ref, spread):
    sources, rows, wide = hidden_ref.shape
    low, first, second = lane_numbers(received_ref, rows, wide)
    values = hidden_ref[...].reshape(sources * rows, wide).astype(jnp.float32)
    swapped = pltpu.roll(values, wide // 2, 1)
    one = jnp.where(low, values, swapped)
    two = jnp.where(low, swapped, values)
    for start in range(0, weight_ref.shape[0], wide):
        number = start // wide * 2.0
        spread[:, start : start + wide] = jnp.where(
            first == number, one, jnp.where(second == number, two, 0.0)
        ).astype(jnp.bfloat16)
    out_ref[...] = (
        jnp.dot(spread[...], weight_ref[...], preferred_element_type=jnp.float32)
        .astype(out_ref.dtype)
        .reshape(out_ref.shape)
    )


def input_rows(received, hidden_grad, weight):
    sources, rows, wide = hidden_grad.shape
    features = weight.shape[1]
    return pl.pallas_call(
        input_kernel,
        grid=(sources // 2,),
        in_specs=[
            pl.BlockSpec((2, rows + EXTRA, features), lambda i: (i, 0, 0)),
            pl.BlockSpec((2, rows, wide), lambda i: (i, 0, 0)),
            pl.BlockSpec(weight.shape, lambda i: (0, 0)),
        ],
        out_specs=pl.BlockSpec((2, rows, features), lambda i: (i, 0, 0)),
        out_shape=jax.ShapeDtypeStruct((sources, rows, features), jnp.bfloat16),
        scratch_shapes=[pltpu.VMEM((2 * rows, weight.shape[0]), jnp.bfloat16)],
        compiler_params=params(),
        cost_estimate=cost(sources * rows, weight.shape[0], features),
    )(received, hidden_grad, weight)


def exchange(value, axes):
    return lax.all_to_all(value, axes, split_axis=0, concat_axis=0, tiled=True)


def body(token_grads, router_gates, expert_ids, saved_hidden, up_weight, down_weight):
    tok_count = token_grads.shape[0]
    local_experts, hidden, width = up_weight.shape
    members = lax.axis_size(GROUP)
    wide, features = 2 * hidden, width // NEAR
    own_rows = local_experts * hidden
    all_rows = own_rows * NEAR * lax.axis_size("far")

    pieces = exchange(pack_weights(down_weight, up_weight), "near")
    down_full, up_full = [
        lax.all_gather(pieces[:, k].reshape(NEAR * own_rows, features), "far", axis=0, tiled=True)
        for k in range(2)
    ]
    received = exchange(pack_tokens(expert_ids.T, token_grads, members), GROUP)
    weighted, activation, scaled = pl.pallas_call(
        prepare_kernel,
        out_shape=(
            jax.ShapeDtypeStruct((tok_count, wide), jnp.bfloat16),
            jax.ShapeDtypeStruct((tok_count, wide), jnp.float32),
            jax.ShapeDtypeStruct((tok_count, wide), jnp.float32),
        ),
        compiler_params=params(),
    )(router_gates.T, saved_hidden)

    parts = project(received, down_full, hidden)
    weighted = jnp.broadcast_to(weighted, parts.shape)
    back = exchange(jnp.concatenate([parts, weighted], axis=1), GROUP)
    parts, weighted = back[:, :tok_count], back[:, tok_count:]
    hidden_grad, gate_grads = pl.pallas_call(
        hidden_kernel,
        out_shape=(
            jax.ShapeDtypeStruct((members, tok_count, wide), jnp.bfloat16),
            jax.ShapeDtypeStruct((2, tok_count), jnp.bfloat16),
        ),
        compiler_params=params(),
    )(parts, activation, scaled)
    hidden_grad = exchange(hidden_grad, GROUP)
    rows_back = exchange(input_rows(received, hidden_grad, up_full), GROUP)
    input_grads = unpack_tokens(rows_back)

    partial_value = down_partial(received, weighted, all_rows)
    sums = lax.psum_scatter(partial_value, "far", scatter_dimension=0, tiled=True)
    sums = exchange(sums.reshape(NEAR, own_rows, features), "near")
    down_grads = jnp.swapaxes(sums, 0, 1).reshape(down_weight.shape)
    return (input_grads, gate_grads.T, down_grads)


def solution(mesh):
    sizes = [mesh.shape[name] for name in ("expert", "inner", "outer")]
    split = Mesh(
        mesh.devices.reshape(sizes[0] // NEAR, NEAR, *sizes[1:]),
        ("far", "near", "inner", "outer"),
    )
    rows = P(("far", "near", "inner", "outer"), None)
    weights = P(("far", "near"), None, ("inner", "outer"))
    return jax.shard_map(
        body,
        mesh=split,
        in_specs=(rows, rows, rows, rows, weights, weights),
        out_specs=(rows, rows, weights),
        check_vma=False,
    )
```

time: 190 us -> 221 us (1.16)
  waiting for transfers between devices: 15.2 us -> 135 us
  blocking collectives: 118 us -> 19 us
  local copies, waits for them, and re-layouts: 19.2 us -> 9.77 us
  starting transfers between devices: 10.8 us -> 20 us
  Pallas kernels: 11.8 us -> 20.9 us
    all_gather x3 -> x0, blocking collectives: 67.7 us -> none  [the longest x1 34 us: body(): ids = lax.all_gather(expert_ids, GROUP, axis=0, tiled=True)]
    all_gather x2, waiting for transfers between devices: 0.02 us -> 66.9 us  [body(): lax.all_gather(pieces[:, k].reshape(NEAR * own_rows, features), 'far', ax...]
    all_to_all x3 -> x5, waiting for transfers between devices: 15.1 us -> 54.8 us  [exchange(): return lax.all_to_all(value, axes, split_axis=0, concat_axis=0, tiled=True)]
    all_to_all x3 -> x1, blocking collectives: 50.2 us -> 19 us  [exchange(): return lax.all_to_all(value, axes, split_axis=0, concat_axis=0, tiled=True)]
    reduce_scatter x1, waiting for transfers between devices: 0.01 us -> 12.6 us  [body(): lax.psum_scatter(partial_value, 'far', scatter_dimension=0, tiled=True)]
    all_to_all x3 -> x5, starting transfers between devices: 10.7 us -> 19.9 us  [exchange(): return lax.all_to_all(value, axes, split_axis=0, concat_axis=0, tiled=True)]
    pallas_call x4 -> x8, Pallas kernels: 11.8 us -> 20.9 us  [the longest x1 5.94 us: input_rows(): pl.pallas_call(input_kernel, grid=(sources // 2,), in_specs=[pl.BlockSpec...]
    all_to_all x6 -> x0, local copies, waits for them, and re-layouts: 8.55 us -> none  [the longest x2 3.71 us: everywhere(): lax.all_to_all(weight, 'near', split_axis=2, concat_axis=0, tiled=True)]
  transfers between devices with their start and end apart: 6 -> 8, of which waited for: 2 -> 7; matrix products, arithmetic and copies ran while one was open for 5% -> 1% of each run, Pallas kernels for 6% -> 4%
where the time goes in v3:
time: 221 us; the launch traced here: 219 us
  waiting for transfers between devices  135 us (61%)
  Pallas kernels  20.9 us (9%)
  starting transfers between devices  20 us (9%)
  blocking collectives  19 us (9%)
  between operations  13.9 us (6%)
  local copies, waits for them, and re-layouts  9.77 us (4%)
    all_gather x2, waiting for transfers between devices, body(): lax.all_gather(pieces[:, k].reshape(NEAR * own_rows, features), 'far', ax...  66.9 us
    all_to_all x5, waiting for transfers between devices, exchange(): return lax.all_to_all(value, axes, split_axis=0, concat_axis=0, tiled=True)  54.8 us
    all_to_all x5, starting transfers between devices, exchange(): return lax.all_to_all(value, axes, split_axis=0, concat_axis=0, tiled=True)  19.9 us
    all_to_all x1, blocking collectives, exchange(): return lax.all_to_all(value, axes, split_axis=0, concat_axis=0, tiled=True)  19 us
    reduce_scatter x1, waiting for transfers between devices, body(): lax.psum_scatter(partial_value, 'far', scatter_dimension=0, tiled=True)  12.6 us
    unnamed x20, local copies, waits for them, and re-layouts  6.97 us
    pallas_call x1, Pallas kernels, input_rows(): pl.pallas_call(input_kernel, grid=(sources // 2,), in_specs=[pl.BlockSpec...  5.94 us
    pallas_call x1, Pallas kernels, project(): pl.pallas_call(project_kernel, grid=(sources // 2,), in_specs=[pl.BlockSp...  5.27 us
  transfers between devices with their start and end apart: 8, of which 7 were waited for; matrix products, arithmetic and copies ran while one was open for 1% of the time, Pallas kernels for 4%

profile of v3, /device:TPU:0, one launch (start us, length us, event | category | flops | bytes accessed | tf_op | source)
XLA Modules:
  0.0 218.6 jit_solution(1931276865571240967)
XLA Ops:
  7.2 0.0 copy-start
  7.2 0.0 copy-start.3
  7.2 1.2 copy-done.3
  8.4 0.0 copy-start.4
  8.4 1.0 copy-done.4
  9.4 0.0 copy-start.6
  9.4 1.6 shard_map.86
  11.0 5.2 %all-to-all-start.1 = ((bf16[4,2,128,512]{3,2,1,0:T(8,128)(2,1)}), bf16[4,2,128,512]{3,2,1,0:T(8,128)(2,1)S(1)}, u32[]{:S(2)}, u32[]{:S(2)}) async-start(bf16[4,2,128,512]{3,2,1,0:T(8,128)(2,1)} %shard_map.86), calls=%async_computation.1 | async-start | bytes 2097152 | tf_op jit(solution)/shard_map/all_to_all | solution.py:283
  16.3 0.0 copy-done
  16.3 0.0 copy-done.6
  16.3 2.1 shard_map.85
  18.3 11.6 %all-to-all-done.1 = bf16[4,2,128,512]{3,2,1,0:T(8,128)(2,1)S(1)} async-done(((bf16[4,2,128,512]{3,2,1,0:T(8,128)(2,1)}), bf16[4,2,128,512]{3,2,1,0:T(8,128)(2,1)S(1)}, u32[]{:S(2)}, u32[]{:S(2)}) %all-to-all-start.1) | async-done | bytes 1048608 | tf_op jit(solution)/shard_map/all_to_all | solution.py:283
  29.9 3.8 %all-to-all-start = ((bf16[16,144,512]{2,1,0:T(8,128)(2,1)}), bf16[16,144,512]{2,1,0:T(8,128)(2,1)S(1)}, u32[]{:S(2)}, u32[]{:S(2)}) async-start(bf16[16,144,512]{2,1,0:T(8,128)(2,1)} %shard_map.85), calls=%async_computation | async-start | bytes 4718592 | tf_op jit(solution)/shard_map/all_to_all | solution.py:283
  33.7 0.0 copy-start.5
  33.7 0.0 copy-start.7
  33.7 0.0 all-gather.3.cloned.1.call-start
  33.7 1.0 fusion.1
  34.8 0.0 all-gather.3.cloned.1.call-update
  34.8 0.0 reduce-scatter.2.cloned.1.call-start
  34.9 0.0 copy-done.5
  34.9 0.0 copy-done.7
  34.9 0.2 shard_map.88
  35.1 35.6 %all-gather.3.cloned.1.call-done.weight_ref = bf16[1024,512]{1,0:T(8,128)(2,1)} async-done(((bf16[512,512]{1,0:T(8,128)(2,1)}), bf16[1024,512]{1,0:T(8,128)(2,1)}) %all-gather.3.cloned.1.call-update) | async-done | bytes 1048592 | tf_op jit(solution)/shard_map/all_gather | solution.py:296
  70.7 3.1 %all-to-all-done.received_ref = bf16[16,144,512]{2,1,0:T(8,128)(2,1)S(1)} async-done(((bf16[16,144,512]{2,1,0:T(8,128)(2,1)}), bf16[16,144,512]{2,1,0:T(8,128)(2,1)S(1)}, u32[]{:S(2)}, u32[]{:S(2)}) %all-to-all-start) | async-done | bytes 2359328 | tf_op jit(solution)/shard_map/all_to_all | solution.py:283
  73.8 0.0 copy-start.9
  73.8 1.2 copy-done.9
  75.0 5.3 %shard_map.87 = bf16[16,128,128]{2,1,0:T(8,128)(2,1)S(1)} custom-call(bf16[16,144,512]{2,1,0:T(8,128)(2,1)S(1)} %all-to-all-done.received_ref, bf16[1024,512]{1,0:T(8,128)(2,1)S(1)} %copy-done.9), custom_call_target="tpu_custom_call" | custom-call | flops 2415919104 | bytes 8126464 | tf_op jit(solution)/shard_map/pallas_call | solution.py:210
  80.3 0.1 broadcast_in_dim.3
  80.4 0.1 pad_maximum_fusion
  80.5 19.0 %all_to_all.30 = bf16[16,256,128]{2,1,0:T(8,128)(2,1)S(1)} all-to-all(bf16[16,256,128]{2,1,0:T(8,128)(2,1)S(1)} %pad_maximum_fusion), channel_id=1, replica_groups=mesh['far'=2,'near'=4,'inner'=2,'outer'=2] {'inner','outer','near'}, dimensions={0} | all-to-all | bytes 2097152 | tf_op jit(solution)/shard_map/all_to_all | solution.py:283
  99.4 0.1 fusion
  99.5 3.1 %shard_map.92 = bf16[1024,512]{1,0:T(8,128)(2,1)S(1)} custom-call(bf16[16,144,512]{2,1,0:T(8,128)(2,1)S(1)} %all-to-all-done.received_ref, bf16[16,128,128]{2,1,0:T(8,128)(2,1)S(1)} %get-tuple-element.13.weighted_ref), custom_call_target="tpu_custom_call" | custom-call | flops 2147483648 | bytes 7340032 | tf_op jit(solution)/shard_map/pallas_call | solution.py:157
  102.6 0.0 copy-start.2
  102.7 1.0 copy-done.2
  103.6 0.0 reduce-scatter.2.cloned.1.call-update
  103.6 0.9 shard_map.89
  104.6 3.6 %all-to-all-start.3 = ((bf16[16,128,128]{2,1,0:T(8,128)(2,1)}), bf16[16,128,128]{2,1,0:T(8,128)(2,1)S(1)}, u32[]{:S(2)}, u32[]{:S(2)}) async-start(bf16[16,128,128]{2,1,0:T(8,128)(2,1)} %get-tuple-element.11), calls=%async_computation.3 | async-start | bytes 1048576 | tf_op jit(solution)/shard_map/all_to_all | solution.py:283
  108.1 0.0 all-gather.5.cloned.1.call-start
  108.2 0.7 all-gather.5.cloned.1.call-update
  108.9 13.8 %all-to-all-done.3.hidden_ref = bf16[16,128,128]{2,1,0:T(8,128)(2,1)S(1)} async-done(((bf16[16,128,128]{2,1,0:T(8,128)(2,1)}), bf16[16,128,128]{2,1,0:T(8,128)(2,1)S(1)}, u32[]{:S(2)}, u32[]{:S(2)}) %all-to-all-start.3) | async-done | bytes 524320 | tf_op jit(solution)/shard_map/all_to_all | solution.py:283
  122.6 12.6 %reduce-scatter.2.cloned.1.call-done = bf16[512,512]{1,0:T(8,128)(2,1)} async-done(((bf16[1024,512]{1,0:T(8,128)(2,1)}), bf16[512,512]{1,0:T(8,128)(2,1)}) %reduce-scatter.2.cloned.1.call-update) | async-done | bytes 524304 | tf_op jit(solution)/shard_map/reduce_scatter | solution.py:327
  135.2 3.5 %all-to-all-start.5 = ((bf16[4,128,512]{2,1,0:T(8,128)(2,1)}), bf16[4,128,512]{2,1,0:T(8,128)(2,1)S(1)}, u32[]{:S(2)}, u32[]{:S(2)}) async-start(bf16[4,128,512]{2,1,0:T(8,128)(2,1)} %bitcast.12), calls=%async_computation.6 | async-start | bytes 1048576 | tf_op jit(solution)/shard_map/all_to_all | solution.py:283
  138.7 31.2 %all-gather.5.cloned.1.call-done.weight_ref = bf16[1024,512]{1,0:T(8,128)(2,1)} async-done(((bf16[512,512]{1,0:T(8,128)(2,1)}), bf16[1024,512]{1,0:T(8,128)(2,1)}) %all-gather.5.cloned.1.call-update) | async-done | bytes 1048592 | tf_op jit(solution)/shard_map/all_gather | solution.py:296
  169.9 0.0 copy-start.8
  169.9 1.2 copy-done.8
  171.2 5.9 %shard_map.90 = bf16[16,128,512]{2,1,0:T(8,128)(2,1)S(1)} custom-call(bf16[16,144,512]{2,1,0:T(8,128)(2,1)S(1)} %all-to-all-done.received_ref, bf16[16,128,128]{2,1,0:T(8,128)(2,1)S(1)} %all-to-all-done.3.hidden_ref, bf16[1024,512]{1,0:T(8,128)(2,1)S(1)} %copy-done.8), custom_call_target="tpu_custom_call" | custom-call | flops 2147483648 | bytes 7340032 | tf_op jit(solution)/shard_map/pallas_call | solution.py:266
  177.1 0.0 copy-start.1
  177.1 1.3 copy-done.1
  178.4 0.0 all-to-all-done.5
  178.4 3.8 %all-to-all-start.4 = ((bf16[16,128,512]{2,1,0:T(8,128)(2,1)}), bf16[16,128,512]{2,1,0:T(8,128)(2,1)S(1)}, u32[]{:S(2)}, u32[]{:S(2)}) async-start(bf16[16,128,512]{2,1,0:T(8,128)(2,1)} %copy-done.1), calls=%async_computation.4 | async-start | bytes 4194304 | tf_op jit(solution)/shard_map/all_to_all | solution.py:283
  182.3 0.4 copy.9
  182.7 1.2 reshape.13
  183.8 26.4 %all-to-all-done.4.parts_ref = bf16[16,128,512]{2,1,0:T(8,128)(2,1)S(1)} async-done(((bf16[16,128,512]{2,1,0:T(8,128)(2,1)}), bf16[16,128,512]{2,1,0:T(8,128)(2,1)S(1)}, u32[]{:S(2)}, u32[]{:S(2)}) %all-to-all-start.4) | async-done | bytes 2097184 | tf_op jit(solution)/shard_map/all_to_all | solution.py:283
  210.2 1.8 shard_map.91
Async XLA Ops:
  7.2 9.1 %copy-start = (bf16[128,8192]{1,0:T(8,128)(2,1)S(1)}, bf16[128,8192]{1,0:T(8,128)(2,1)}, u32[]{:S(2)}) copy-start(bf16[128,8192]{1,0:T(8,128)(2,1)} %tokens_ref.1) | copy-start | bytes 6291460
  7.2 1.2 copy-start.3
  8.4 1.0 copy-start.4
  9.4 6.9 %copy-start.6 = (s32[128,2]{0,1:T(2,128)S(1)}, s32[128,2]{0,1:T(2,128)}, u32[]{:S(2)}) copy-start(s32[128,2]{0,1:T(2,128)} %param.8) | copy-start | bytes 3076
  11.0 18.9 %all-to-all-start.1 = ((bf16[4,2,128,512]{3,2,1,0:T(8,128)(2,1)}), bf16[4,2,128,512]{3,2,1,0:T(8,128)(2,1)S(1)}, u32[]{:S(2)}, u32[]{:S(2)}) async-start(bf16[4,2,128,512]{3,2,1,0:T(8,128)(2,1)} %shard_map.86), calls=%async_computation.1 | async-start | bytes 2097152 | tf_op jit(solution)/shard_map/all_to_all | solution.py:283
  29.9 43.9 %all-to-all-start = ((bf16[16,144,512]{2,1,0:T(8,128)(2,1)}), bf16[16,144,512]{2,1,0:T(8,128)(2,1)S(1)}, u32[]{:S(2)}, u32[]{:S(2)}) async-start(bf16[16,144,512]{2,1,0:T(8,128)(2,1)} %shard_map.85), calls=%async_computation | async-start | bytes 4718592 | tf_op jit(solution)/shard_map/all_to_all | solution.py:283
  33.7 1.2 copy-start.5
  33.7 1.2 copy-start.7
  33.7 37.0 %all-gather.3.cloned.1.call-start = ((), (), s32[]{:S(2)}) async-start(), calls=%async_computation.7 | async-start | bytes 1572864 | tf_op jit(solution)/shard_map/all_gather | solution.py:296
  34.8 100.4 %reduce-scatter.2.cloned.1.call-start = ((), (), s32[]{:S(2)}) async-start(), calls=%async_computation.9 | async-start | bytes 1572864 | tf_op jit(solution)/shard_map/reduce_scatter | solution.py:327
  73.8 1.2 copy-start.9
  102.6 1.0 copy-start.2
  104.6 18.1 %all-to-all-start.3 = ((bf16[16,128,128]{2,1,0:T(8,128)(2,1)}), bf16[16,128,128]{2,1,0:T(8,128)(2,1)S(1)}, u32[]{:S(2)}, u32[]{:S(2)}) async-start(bf16[16,128,128]{2,1,0:T(8,128)(2,1)} %get-tuple-element.11), calls=%async_computation.3 | async-start | bytes 1048576 | tf_op jit(solution)/shard_map/all_to_all | solution.py:283
  108.1 61.8 %all-gather.5.cloned.1.call-start = ((), (), s32[]{:S(2)}) async-start(), calls=%async_computation.8 | async-start | bytes 1572864 | tf_op jit(solution)/shard_map/all_gather | solution.py:296
  135.2 43.2 %all-to-all-start.5 = ((bf16[4,128,512]{2,1,0:T(8,128)(2,1)}), bf16[4,128,512]{2,1,0:T(8,128)(2,1)S(1)}, u32[]{:S(2)}, u32[]{:S(2)}) async-start(bf16[4,128,512]{2,1,0:T(8,128)(2,1)} %bitcast.12), calls=%async_computation.6 | async-start | bytes 1048576 | tf_op jit(solution)/shard_map/all_to_all | solution.py:283
  169.9 1.2 copy-start.8
  177.1 1.3 copy-start.1
  178.4 31.8 %all-to-all-start.4 = ((bf16[16,128,512]{2,1,0:T(8,128)(2,1)}), bf16[16,128,512]{2,1,0:T(8,128)(2,1)S(1)}, u32[]{:S(2)}, u32[]{:S(2)}) async-start(bf16[16,128,512]{2,1,0:T(8,128)(2,1)} %copy-done.1), calls=%async_computation.4 | async-start | bytes 4194304 | tf_op jit(solution)/shard_map/all_to_all | solution.py:283
Sparse Core Ops, SparseCore 0:
  36.7 34.0 all-gather.2
  103.8 31.4 reduce-scatter.1
  137.4 32.4 all-gather.4

commit v4 on v3

v4 whole, which is shorter than its diff:
```python
import functools
import jax
import jax.numpy as jnp
from jax import lax
from jax.experimental import pallas as pl
from jax.experimental.pallas import tpu as pltpu
from jax.sharding import Mesh, PartitionSpec as P

root_half = 0.7071067811865476
inv_root_tau = 0.3989422804014327
GROUP = ("inner", "outer", "near")
NEAR = 2
BLOCK = 256
TILE = 16
MIB = 1 << 20
CHAIN = ((0, 1, 2, 3), (1, 0, 2, 3), (3, 2, 0, 1), (3, 2, 1, 0))
SIDES = ((0, 1), (1, 0), (2, 3), (3, 2))
MIDDLE = ((1, 2), (2, 1))
OUTWARD = ((1, 0), (2, 3))
INWARD = ((0, 1), (3, 2))
SWAP = ((0, 1), (1, 0))
DOWN, UP, GRADS = 0, 2, 4


def gelu_parts(preact):
    cumulative = 0.5 * (1.0 + lax.erf(preact * root_half))
    density = inv_root_tau * jnp.exp(-0.5 * preact * preact)
    return (preact * cumulative, cumulative + preact * density)


def params():
    return pltpu.CompilerParams(vmem_limit_bytes=40 * MIB)


def cost(rows, inner, columns):
    return pl.CostEstimate(
        flops=2 * rows * inner * columns,
        bytes_accessed=2 * (rows * inner + inner * columns + rows * columns),
        transcendentals=0,
    )


def low_half(shape):
    return lax.broadcasted_iota(jnp.int32, shape, len(shape) - 1) < shape[-1] // 2


def columns_of(pair, wide):
    wanted = lax.broadcasted_iota(jnp.int32, (2, wide), 0)
    return [
        lax.dot_general(
            pair.astype(jnp.bfloat16),
            jnp.where(wanted == k, 1.0, 0.0).astype(jnp.bfloat16),
            (((0,), (0,)), ((), ())),
            preferred_element_type=jnp.float32,
        )
        for k in range(2)
    ]


def pack_kernel(
    local_experts, far_ref, ids_ref, gates_ref, preact_ref, tokens_ref,
    out_ref, activation_ref, scaled_ref, weighted,
):
    blocks, height, features = out_ref.shape
    rows, wide = preact_ref.shape
    far_count = far_ref.shape[0]
    taken = rows * wide // features

    @pl.when(pl.program_id(0) == 0)
    def _():
        activation, slope = gelu_parts(preact_ref[...].astype(jnp.float32))
        gates = jnp.where(low_half((rows, wide)), *columns_of(gates_ref[...], wide))
        activation_ref[...] = activation
        scaled_ref[...] = gates * slope
        weighted[...] = (gates * activation).astype(jnp.bfloat16)

    ids = ids_ref[...]
    local = lax.rem(ids, local_experts)
    line = lax.div(ids, local_experts)
    far, near = lax.div(line, NEAR), lax.rem(line, NEAR)
    far_place = jnp.zeros_like(far)
    for at in range(far_count):
        far_place = jnp.where(far == at, far_ref[at], far_place)
    for block in range(blocks):
        side = lax.rem(near + block, NEAR)
        places = (
            (side * far_count + far_place) * local_experts + local,
            (far * NEAR + side) * local_experts + local,
            (far_place * NEAR + side) * local_experts + local,
        )
        out_ref[block, 0:rows, :] = tokens_ref[:, block * features : (block + 1) * features]
        for at in range(0, features, wide):
            start = at // wide * taken
            out_ref[block, rows : rows + taken, at : at + wide] = weighted[start : start + taken, :]
        last = height - TILE
        out_ref[block, last:, :] = jnp.zeros((TILE, features), jnp.bfloat16)
        for at, place in zip((DOWN, UP, GRADS), places):
            out_ref[block, last + at : last + at + 2, 0:rows] = place.astype(jnp.bfloat16)


def pack_tokens(far_places, ids, gates, preact, tokens, members, local_experts):
    rows, width = tokens.shape
    features = width // members
    each = members // 4
    height = rows + preact.size // features + TILE
    small = jax.ShapeDtypeStruct(preact.shape, jnp.float32)
    whole = [pl.BlockSpec(array.shape, lambda i: (0, 0)) for array in (ids, gates, preact)]
    return pl.pallas_call(
        functools.partial(pack_kernel, local_experts),
        grid=(4,),
        in_specs=[
            pl.BlockSpec(memory_space=pltpu.SMEM),
            *whole,
            pl.BlockSpec((rows, each * features), lambda i: (0, i)),
        ],
        out_specs=(pl.BlockSpec((each, height, features), lambda i: (i, 0, 0)), whole[2], whole[2]),
        out_shape=(
            jax.ShapeDtypeStruct((members, height, features), jnp.bfloat16), small, small,
        ),
        scratch_shapes=[pltpu.VMEM(preact.shape, jnp.bfloat16)],
        compiler_params=params(),
    )(far_places, ids, gates, preact, tokens)


def unpack_kernel(parts_ref, out_ref):
    blocks, _, features = parts_ref.shape
    for block in range(blocks):
        out_ref[:, block * features : (block + 1) * features] = parts_ref[block]


def unpack_tokens(parts):
    members, rows, features = parts.shape
    each = members // 4
    return pl.pallas_call(
        unpack_kernel,
        grid=(4,),
        in_specs=[pl.BlockSpec((each, rows, features), lambda i: (i, 0, 0))],
        out_specs=pl.BlockSpec((rows, each * features), lambda i: (0, i)),
        out_shape=jax.ShapeDtypeStruct((rows, members * features), jnp.bfloat16),
        compiler_params=params(),
    )(parts)


def places_of(received_ref, source, which, rows):
    at = received_ref.shape[1] - TILE + which
    return received_ref[source, at : at + 2, 0:rows]


def token_rows(received_ref, rows):
    sources, _, features = received_ref.shape
    return received_ref[:, 0:rows, :].reshape(sources * rows, features)


def down_kernel(rows, wide, received_ref, *refs):
    out_refs, (turned, numbers, spread) = refs[:-3], refs[-3:]
    sources, _, features = received_ref.shape
    hidden, each = wide // 2, BLOCK // (wide // 2)
    taken = rows * wide // features
    for source in range(sources):
        weighted = jnp.concatenate(
            [
                received_ref[source, rows : rows + taken, at : at + wide].astype(jnp.float32)
                for at in range(0, features, wide)
            ]
        )
        lanes = slice(source * rows, (source + 1) * rows)
        turned[:, lanes] = weighted.T
        numbers[:, lanes] = places_of(received_ref, source, GRADS, rows).astype(jnp.float32)
    number = 0
    for out_ref in out_refs:
        for start in range(0, out_ref.shape[0], BLOCK):
            for expert in range(each):
                spread[expert * hidden : (expert + 1) * hidden, :] = jnp.where(
                    numbers[0:1, :] == number + expert,
                    turned[0:hidden, :],
                    jnp.where(numbers[1:2, :] == number + expert, turned[hidden:, :], 0.0),
                ).astype(jnp.bfloat16)
            number += each
            out_ref[start : start + BLOCK, :] = jnp.dot(
                spread[...], token_rows(received_ref, rows), preferred_element_type=jnp.float32
            ).astype(out_ref.dtype)


def down_partial(received, rows, wide, total_rows, count):
    sources, _, features = received.shape
    total = sources * rows
    return pl.pallas_call(
        functools.partial(down_kernel, rows, wide),
        out_shape=[jax.ShapeDtypeStruct((total_rows // count, features), jnp.bfloat16)] * count,
        scratch_shapes=[
            pltpu.VMEM((wide, total), jnp.float32),
            pltpu.VMEM((2, total), jnp.float32),
            pltpu.VMEM((BLOCK, total), jnp.bfloat16),
        ],
        compiler_params=params(),
        cost_estimate=cost(total_rows, total, features),
    )(received)


def lane_numbers(received_ref, which, rows, wide):
    sources = received_ref.shape[0]
    low = low_half((sources * rows, wide))
    found = [
        columns_of(places_of(received_ref, source, which, rows), wide)
        for source in range(sources)
    ]
    odd = jnp.where(low, 0.0, 1.0)
    return low, *[jnp.concatenate([pair[k] for pair in found]) - odd for k in range(2)]


def join(pieces, piece_refs, full):
    at = start = 0
    for terms in pieces:
        value = piece_refs[at][...]
        for ref in piece_refs[at + 1 : at + terms]:
            value = value + ref[...]
        full[start : start + value.shape[0], :] = value
        at, start = at + terms, start + value.shape[0]


def project_kernel(pieces, received_ref, *refs):
    piece_refs, out_ref, full = refs[:-2], refs[-2], refs[-1]
    pl.when(pl.program_id(0) == 0)(lambda: join(pieces, piece_refs, full))
    sources, rows, wide = out_ref.shape
    low, first, second = lane_numbers(received_ref, DOWN, rows, wide)
    tokens = token_rows(received_ref, rows)
    sums = [jnp.zeros((sources * rows, wide), jnp.float32) for _ in range(2)]
    for start in range(0, full.shape[0], BLOCK):
        product = lax.dot_general(
            tokens,
            full[start : start + BLOCK, :],
            (((1,), (1,)), ((), ())),
            preferred_element_type=jnp.float32,
        )
        for at in range(0, BLOCK, wide):
            part = product[:, at : at + wide]
            number = (start + at) // wide * 2.0
            sums[0] = jnp.where(first == number, part, sums[0])
            sums[1] = jnp.where(second == number, part, sums[1])
    folded = [value + pltpu.roll(value, wide // 2, 1) for value in sums]
    value = jnp.where(low, folded[0], folded[1]).astype(out_ref.dtype)
    out_ref[...] = value.reshape(out_ref.shape)


def project(received, pieces, rows, wide):
    sources, height, features = received.shape
    flat = [term for terms in pieces for term in terms]
    joined = sum(terms[0].shape[0] for terms in pieces)
    return pl.pallas_call(
        functools.partial(project_kernel, [len(terms) for terms in pieces]),
        grid=(sources // 2,),
        in_specs=[
            pl.BlockSpec((2, height, features), lambda i: (i, 0, 0)),
            *[pl.BlockSpec(term.shape, lambda i: (0, 0)) for term in flat],
        ],
        out_specs=pl.BlockSpec((2, rows, wide), lambda i: (i, 0, 0)),
        out_shape=jax.ShapeDtypeStruct((sources, rows, wide), jnp.bfloat16),
        scratch_shapes=[pltpu.VMEM((joined, features), jnp.bfloat16)],
        compiler_params=params(),
        cost_estimate=cost(sources * rows, features, joined),
    )(received, *flat)


def hidden_kernel(parts_ref, activation_ref, scaled_ref, hidden_ref, gate_ref):
    projected = parts_ref[0].astype(jnp.float32)
    for source in range(1, parts_ref.shape[0]):
        projected = projected + parts_ref[source].astype(jnp.float32)
    wide = projected.shape[1]
    half = lax.broadcasted_iota(jnp.int32, (8, wide), 1) // (wide // 2)
    wanted = lax.broadcasted_iota(jnp.int32, (8, wide), 0)
    sums = lax.dot_general(
        jnp.where(wanted == half, 1.0, 0.0),
        activation_ref[...] * projected,
        (((1,), (1,)), ((), ())),
        precision=lax.Precision.HIGHEST,
        preferred_element_type=jnp.float32,
    )
    gate_ref[...] = sums[0:2, :].astype(gate_ref.dtype)
    hidden = (projected * scaled_ref[...]).astype(hidden_ref.dtype)
    for source in range(hidden_ref.shape[0]):
        hidden_ref[source] = hidden


def input_kernel(received_ref, hidden_ref, weight_ref, out_ref, spread):
    sources, rows, wide = hidden_ref.shape
    low, first, second = lane_numbers(received_ref, UP, rows, wide)
    values = hidden_ref[...].reshape(sources * rows, wide).astype(jnp.float32)
    swapped = pltpu.roll(values, wide // 2, 1)
    one = jnp.where(low, values, swapped)
    two = jnp.where(low, swapped, values)
    for start in range(0, weight_ref.shape[0], wide):
        number = start // wide * 2.0
        spread[:, start : start + wide] = jnp.where(
            first == number, one, jnp.where(second == number, two, 0.0)
        ).astype(jnp.bfloat16)
    out_ref[...] = (
        jnp.dot(spread[...], weight_ref[...], preferred_element_type=jnp.float32)
        .astype(out_ref.dtype)
        .reshape(out_ref.shape)
    )


def input_rows(received, hidden_grad, weight):
    sources, rows, wide = hidden_grad.shape
    features = weight.shape[1]
    return pl.pallas_call(
        input_kernel,
        grid=(sources // 2,),
        in_specs=[
            pl.BlockSpec((2, received.shape[1], features), lambda i: (i, 0, 0)),
            pl.BlockSpec((2, rows, wide), lambda i: (i, 0, 0)),
            pl.BlockSpec(weight.shape, lambda i: (0, 0)),
        ],
        out_specs=pl.BlockSpec((2, rows, features), lambda i: (i, 0, 0)),
        out_shape=jax.ShapeDtypeStruct((sources, rows, features), jnp.bfloat16),
        scratch_shapes=[pltpu.VMEM((2 * rows, weight.shape[0]), jnp.bfloat16)],
        compiler_params=params(),
        cost_estimate=cost(sources * rows, weight.shape[0], features),
    )(received, hidden_grad, weight)


def exchange(value, axes):
    return lax.all_to_all(value, axes, split_axis=0, concat_axis=0, tiled=True)


def chain_gather(mine):
    beside = lax.ppermute(mine, "far", SIDES)
    across = lax.ppermute(mine, "far", MIDDLE)
    across_far = lax.ppermute(beside, "far", MIDDLE)
    second = lax.ppermute(across, "far", OUTWARD)
    third = lax.ppermute(across_far, "far", OUTWARD)
    return [(mine,), (beside,), (across, second), (across_far, third)]


def add(*terms):
    return sum(term.astype(jnp.float32) for term in terms).astype(jnp.bfloat16)


def chain_scatter(own, beside, second, third):
    third = add(third, lax.ppermute(third, "far", INWARD))
    second = add(second, lax.ppermute(second, "far", INWARD))
    beside = add(beside, lax.ppermute(third, "far", MIDDLE))
    across = lax.ppermute(second, "far", MIDDLE)
    return add(own, across, lax.ppermute(beside, "far", SIDES))


def body(token_grads, router_gates, expert_ids, saved_hidden, up_weight, down_weight):
    tok_count = token_grads.shape[0]
    local_experts, hidden, width = up_weight.shape
    members, far_count = lax.axis_size(GROUP), lax.axis_size("far")
    wide, features = 2 * hidden, width // NEAR
    own_rows = local_experts * hidden
    near = lax.axis_index("near")
    chained = far_count == len(CHAIN)

    def halves(weight):
        flat = weight.reshape(own_rows, width)
        own = lax.dynamic_slice_in_dim(flat, near * features, features, axis=1)
        other = lax.dynamic_slice_in_dim(flat, (1 - near) * features, features, axis=1)
        return own, lax.ppermute(other, "near", SWAP)

    down_halves, up_halves = halves(down_weight), halves(up_weight)
    if chained:
        down_pieces = [terms for half in down_halves for terms in chain_gather(half)]
        far_places = jnp.asarray(CHAIN, jnp.int32)[lax.axis_index("far")]
    else:
        down_pieces = [(lax.all_gather(half, "far", tiled=True),) for half in down_halves]
        far_places = jnp.arange(far_count, dtype=jnp.int32)
    up_full = lax.all_gather(jnp.concatenate(up_halves), "far", tiled=True)
    packed, activation, scaled = pack_tokens(
        far_places, expert_ids.T, router_gates.T, saved_hidden, token_grads, members, local_experts
    )
    received = exchange(packed, GROUP)

    partial_value = down_partial(
        received, tok_count, wide, own_rows * NEAR * far_count, far_count if chained else 1
    )
    if chained:
        sums = chain_scatter(*partial_value)
    else:
        sums = lax.psum_scatter(partial_value[0], "far", scatter_dimension=0, tiled=True)
    kept, passed = sums[:own_rows], lax.ppermute(sums[own_rows:], "near", SWAP)
    down_grads = jnp.concatenate(
        [jnp.where(near == 0, kept, passed), jnp.where(near == 0, passed, kept)], axis=1
    ).reshape(down_weight.shape)

    parts = exchange(project(received, down_pieces, tok_count, wide), GROUP)
    hidden_grad, gate_grads = pl.pallas_call(
        hidden_kernel,
        out_shape=(
            jax.ShapeDtypeStruct((members, tok_count, wide), jnp.bfloat16),
            jax.ShapeDtypeStruct((2, tok_count), jnp.bfloat16),
        ),
        compiler_params=params(),
    )(parts, activation, scaled)
    hidden_grad = exchange(hidden_grad, GROUP)
    input_grads = unpack_tokens(exchange(input_rows(received, hidden_grad, up_full), GROUP))
    return (input_grads, gate_grads.T, down_grads)


def solution(mesh):
    sizes = [mesh.shape[name] for name in ("expert", "inner", "outer")]
    split = Mesh(
        mesh.devices.reshape(sizes[0] // NEAR, NEAR, *sizes[1:]),
        ("far", "near", "inner", "outer"),
    )
    rows = P(("far", "near", "inner", "outer"), None)
    weights = P(("far", "near"), None, ("inner", "outer"))
    return jax.shard_map(
        body,
        mesh=split,
        in_specs=(rows, rows, rows, rows, weights, weights),
        out_specs=(rows, rows, weights),
        check_vma=False,
    )
```

time: 221 us -> 185 us (0.84)
  waiting for transfers between devices: 135 us -> 72.3 us
  starting transfers between devices: 20 us -> 58.1 us
  blocking collectives: 19 us -> 0 us
  other arithmetic: 0.09 us -> 6.68 us
  local copies, waits for them, and re-layouts: 9.77 us -> 16.1 us
  Pallas kernels: 20.9 us -> 16.8 us
    all_gather x2 -> x1, waiting for transfers between devices: 66.9 us -> 0.01 us  [body(): up_full = lax.all_gather(jnp.concatenate(up_halves), 'far', tiled=True)]
    ppermute x0 -> x18, waiting for transfers between devices: none -> 66.2 us  [the longest x2 31.3 us: halves(): return (own, lax.ppermute(other, 'near', SWAP))]
    all_to_all x5 -> x4, waiting for transfers between devices: 54.8 us -> 6.1 us  [exchange(): return lax.all_to_all(value, axes, split_axis=0, concat_axis=0, tiled=True)]
    ppermute x0 -> x18, starting transfers between devices: none -> 43.4 us  [the longest x1 16.3 us: chain_scatter(): third = add(third, lax.ppermute(third, 'far', INWARD))]
    all_to_all x1 -> x0, blocking collectives: 19 us -> none  [exchange(): return lax.all_to_all(value, axes, split_axis=0, concat_axis=0, tiled=True)]
    reduce_scatter x1 -> x0, waiting for transfers between devices: 12.6 us -> none  [body(): lax.psum_scatter(partial_value, 'far', scatter_dimension=0, tiled=True)]
    unnamed x20 -> x38, local copies, waits for them, and re-layouts: 6.97 us -> 13.2 us
    all_to_all x5 -> x4, starting transfers between devices: 19.9 us -> 14.7 us  [exchange(): return lax.all_to_all(value, axes, split_axis=0, concat_axis=0, tiled=True)]
  transfers between devices with their start and end apart: 8 -> 23, of which waited for: 7 -> 7; matrix products, arithmetic and copies ran while one was open for 1% -> 5% of each run, Pallas kernels for 4% -> 8%
where the time goes in v4:
time: 185 us; the launch traced here: 184 us
  waiting for transfers between devices  72.3 us (39%)
  starting transfers between devices  58.1 us (31%)
  Pallas kernels  16.8 us (9%)
  local copies, waits for them, and re-layouts  16.1 us (9%)
  between operations  14.3 us (8%)
  other arithmetic  6.68 us (4%)
    ppermute x2, waiting for transfers between devices, halves(): return (own, lax.ppermute(other, 'near', SWAP))  31.3 us
    ppermute x1, starting transfers between devices, chain_scatter(): third = add(third, lax.ppermute(third, 'far', INWARD))  16.3 us
    all_to_all x4, starting transfers between devices, exchange(): return lax.all_to_all(value, axes, split_axis=0, concat_axis=0, tiled=True)  14.7 us
    unnamed x38, local copies, waits for them, and re-layouts  13.2 us
    ppermute x1, waiting for transfers between devices, chain_scatter(): return add(own, across, lax.ppermute(beside, 'far', SIDES))  12.2 us
    ppermute x1, waiting for transfers between devices, body(): lax.ppermute(sums[own_rows:], 'near', SWAP)  11.4 us
    ppermute x2, waiting for transfers between devices, chain_gather(): beside = lax.ppermute(mine, 'far', SIDES)  10.5 us
    all_to_all x4, waiting for transfers between devices, exchange(): return lax.all_to_all(value, axes, split_axis=0, concat_axis=0, tiled=True)  6.1 us
  transfers between devices with their start and end apart: 23, of which 7 were waited for; matrix products, arithmetic and copies ran while one was open for 5% of the time, Pallas kernels for 8%

profile of v4, /device:TPU:0, one launch (start us, length us, event | category | flops | bytes accessed | tf_op | source)
XLA Modules:
  0.0 184.4 jit_solution(6862737269452954863)
XLA Ops:
  7.2 1.1 constant_dynamic-slice_fusion.1
  8.2 3.0 %collective-permute-start.11 = (bf16[128,1024]{1,0:T(8,128)(2,1)S(1)}, bf16[128,1024]{1,0:T(8,128)(2,1)S(1)}, u32[]{:S(2)}, u32[]{:S(2)}) collective-permute-start(bf16[128,1024]{1,0:T(8,128)(2,1)S(1)} %get-tuple-element.24), channel_id=1, source_target_pairs={{0,4},{4,0},{1,5},{5,1},{2,6},{6,2},{3,7},{7,3},{8,12},{12,8},{9,1... | collective-permute-start | bytes 786440 | tf_op jit(solution)/shard_map/ppermute | solution.py:360
  11.3 0.7 fusion.far_ref
  12.0 1.6 copy-done.1
  13.6 0.8 copy-done.9
  14.3 0.7 copy-done.10
  15.0 0.7 copy-done.11
  15.6 1.1 shard_map.94
  16.8 1.5 copy-done
  18.3 3.6 %all-to-all-start = ((bf16[8,160,1024]{2,1,0:T(8,128)(2,1)}), bf16[8,160,1024]{2,1,0:T(8,128)(2,1)S(1)}, u32[]{:S(2)}, u32[]{:S(2)}) async-start(bf16[8,160,1024]{2,1,0:T(8,128)(2,1)} %copy-done), calls=%async_computation | async-start | bytes 5242880 | tf_op jit(solution)/shard_map/all_to_all | solution.py:323
  21.9 0.0 all-gather.2.cloned.1.call-start
  22.0 0.8 pad_maximum_fusion
  22.8 0.0 all-gather.2.cloned.1.call-update
  22.8 1.1 constant_dynamic-slice_fusion.2
  23.9 1.9 %collective-permute-start.5 = (bf16[128,1024]{1,0:T(8,128)(2,1)S(1)}, bf16[128,1024]{1,0:T(8,128)(2,1)S(1)}, u32[]{:S(2)}, u32[]{:S(2)}) collective-permute-start(bf16[128,1024]{1,0:T(8,128)(2,1)S(1)} %get-tuple-element.25), channel_id=1, source_target_pairs={{0,4},{4,0},{1,5},{5,1},{2,6},{6,2},{3,7},{7,3},{8,12},{12,8},{9,1... | collective-permute-start | bytes 786440 | tf_op jit(solution)/shard_map/ppermute | solution.py:360
  25.9 1.6 collective-permute-start
  27.4 31.3 %collective-permute-done.5.refs_6_ = bf16[128,1024]{1,0:T(8,128)(2,1)S(1)} collective-permute-done((bf16[128,1024]{1,0:T(8,128)(2,1)S(1)}, bf16[128,1024]{1,0:T(8,128)(2,1)S(1)}, u32[]{:S(2)}, u32[]{:S(2)}) %collective-permute-start.5) | collective-permute-done | bytes 262176 | tf_op jit(solution)/shard_map/ppermute | solution.py:360
  58.8 1.6 collective-permute-start.6
  60.3 1.4 collective-permute-start.1
  61.7 0.0 collective-permute-done.refs_1_
  61.7 1.4 collective-permute-start.3
  63.1 0.7 copy-done.15
  63.7 1.3 collective-permute-start.7
  65.1 0.7 copy-done.13
  65.8 10.5 %collective-permute-done.6.refs_7_ = bf16[128,1024]{1,0:T(8,128)(2,1)S(1)} collective-permute-done((bf16[128,1024]{1,0:T(8,128)(2,1)S(1)}, bf16[128,1024]{1,0:T(8,128)(2,1)S(1)}, u32[]{:S(2)}, u32[]{:S(2)}) %collective-permute-start.6) | collective-permute-done | bytes 262176 | tf_op jit(solution)/shard_map/ppermute | solution.py:327
  76.3 1.3 collective-permute-start.9
  77.7 0.8 copy-done.17
  78.4 1.3 collective-permute-start.2
  79.7 0.0 collective-permute-done.3.refs_4_
  79.7 1.3 collective-permute-start.4
  81.0 0.0 collective-permute-done.7.refs_8_
  81.0 1.3 collective-permute-start.8
  82.3 1.3 collective-permute-start.10
  83.7 3.2 %shard_map.99 = (bf16[256,1024]{1,0:T(8,128)(2,1)S(1)}, bf16[256,1024]{1,0:T(8,128)(2,1)S(1)}, bf16[256,1024]{1,0:T(8,128)(2,1)S(1)}, bf16[256,1024]{1,0:T(8,128)(2,1)}) custom-call(bf16[8,160,1024]{2,1,0:T(8,128)(2,1)S(1)} %all-to-all-done.received_ref), custom_call_target="tpu_custom_call" | custom-call | flops 2147483648 | bytes 6291456 | tf_op jit(solution)/shard_map/pallas_call | solution.py:187
  86.9 0.8 copy-done.3
  87.7 0.8 copy-done.5
  88.5 16.3 %collective-permute-start.14 = (bf16[256,1024]{1,0:T(8,128)(2,1)}, bf16[256,1024]{1,0:T(8,128)(2,1)}, u32[]{:S(2)}, u32[]{:S(2)}) collective-permute-start(bf16[256,1024]{1,0:T(8,128)(2,1)} %get-tuple-element.20), channel_id=1, source_target_pairs={{0,8},{24,16},{1,9},{25,17},{2,10},{26,18},{3,11},{27,19},{4,12},{... | collective-permute-start | bytes 1572872 | tf_op jit(solution)/shard_map/ppermute | solution.py:340
  104.8 0.7 collective-permute-done.10.refs_11_
  105.5 5.6 %shard_map.95 = bf16[8,128,128]{2,1,0:T(8,128)(2,1)S(1)} custom-call(bf16[8,160,1024]{2,1,0:T(8,128)(2,1)S(1)} %all-to-all-done.received_ref, bf16[128,1024]{1,0:T(8,128)(2,1)S(1)} %get-tuple-element.26.refs_0_, bf16[128,1024]{1,0:T(8,128)(2,1)S(1)} %copy-done.16, bf16[128,1024]{1,0:T(8,128)(2,1)} %collective-permute-done.1.refs_2_, ...), custom_call_target="tpu_custom_call" | custom-call | flops 2147483648 | bytes 6291456 | tf_op jit(solution)/shard_map/pallas_call | solution.py:249
  111.1 0.7 copy-done.7
  111.8 3.9 %all-to-all-start.1 = ((bf16[8,128,128]{2,1,0:T(8,128)(2,1)}), bf16[8,128,128]{2,1,0:T(8,128)(2,1)S(1)}, u32[]{:S(2)}, u32[]{:S(2)}) async-start(bf16[8,128,128]{2,1,0:T(8,128)(2,1)} %copy-done.7), calls=%async_computation.1 | async-start | bytes 524288 | tf_op jit(solution)/shard_map/all_to_all | solution.py:323
  115.8 2.2 %collective-permute-start.12 = (bf16[256,1024]{1,0:T(8,128)(2,1)}, bf16[256,1024]{1,0:T(8,128)(2,1)}, u32[]{:S(2)}, u32[]{:S(2)}) collective-permute-start(bf16[256,1024]{1,0:T(8,128)(2,1)} %copy-done.3), channel_id=1, source_target_pairs={{0,8},{24,16},{1,9},{25,17},{2,10},{26,18},{3,11},{27,19},{4,12},{... | collective-permute-start | bytes 1572872 | tf_op jit(solution)/shard_map/ppermute | solution.py:341
  118.0 3.8 %all-to-all-done.1.parts_ref = bf16[8,128,128]{2,1,0:T(8,128)(2,1)S(1)} async-done(((bf16[8,128,128]{2,1,0:T(8,128)(2,1)}), bf16[8,128,128]{2,1,0:T(8,128)(2,1)S(1)}, u32[]{:S(2)}, u32[]{:S(2)}) %all-to-all-start.1) | async-done | bytes 262176 | tf_op jit(solution)/shard_map/all_to_all | solution.py:323
  121.8 0.7 shard_map.96
  122.5 0.7 copy-done.8
  123.2 3.4 %all-to-all-start.2 = ((bf16[8,128,128]{2,1,0:T(8,128)(2,1)}), bf16[8,128,128]{2,1,0:T(8,128)(2,1)S(1)}, u32[]{:S(2)}, u32[]{:S(2)}) async-start(bf16[8,128,128]{2,1,0:T(8,128)(2,1)} %copy-done.8), calls=%async_computation.2 | async-start | bytes 524288 | tf_op jit(solution)/shard_map/all_to_all | solution.py:323
  126.7 2.2 %add_convert_fusion.2 = bf16[256,1024]{1,0:T(8,128)(2,1)} fusion(bf16[256,1024]{1,0:T(8,128)(2,1)} %collective-permute-done.14, bf16[256,1024]{1,0:T(8,128)(2,1)} %get-tuple-element.20), kind=kLoop, calls=%fused_computation.2 | loop fusion | flops 1048576 | bytes 1572864 | tf_op jit(solution)/shard_map/convert_element_type | solution.py:336
  128.9 1.5 collective-permute-start.15
  130.3 2.3 %all-to-all-done.2.hidden_ref = bf16[8,128,128]{2,1,0:T(8,128)(2,1)S(1)} async-done(((bf16[8,128,128]{2,1,0:T(8,128)(2,1)}), bf16[8,128,128]{2,1,0:T(8,128)(2,1)S(1)}, u32[]{:S(2)}, u32[]{:S(2)}) %all-to-all-start.2) | async-done | bytes 262176 | tf_op jit(solution)/shard_map/all_to_all | solution.py:323
  132.6 1.6 copy-done.12
  134.2 4.3 %shard_map.97 = bf16[8,128,1024]{2,1,0:T(8,128)(2,1)S(1)} custom-call(bf16[8,160,1024]{2,1,0:T(8,128)(2,1)S(1)} %all-to-all-done.received_ref, bf16[8,128,128]{2,1,0:T(8,128)(2,1)S(1)} %all-to-all-done.2.hidden_ref, bf16[1024,1024]{1,0:T(8,128)(2,1)S(1)} %copy-done.12), custom_call_target="tpu_custom_call" | custom-call | flops 2147483648 | bytes 6291456 | tf_op jit(solution)/shard_map/pallas_call | solution.py:306
  138.5 0.0 copy-start.2
  138.6 1.3 copy-done.2
  139.9 3.7 %all-to-all-start.3 = ((bf16[8,128,1024]{2,1,0:T(8,128)(2,1)}), bf16[8,128,1024]{2,1,0:T(8,128)(2,1)S(1)}, u32[]{:S(2)}, u32[]{:S(2)}) async-start(bf16[8,128,1024]{2,1,0:T(8,128)(2,1)} %copy-done.2), calls=%async_computation.3 | async-start | bytes 4194304 | tf_op jit(solution)/shard_map/all_to_all | solution.py:323
  143.6 1.3 add_convert_fusion.3
  144.9 0.7 collective-permute-start.13
  145.6 1.2 add_convert_fusion.1
  146.9 2.3 %collective-permute-start.16 = (bf16[256,1024]{1,0:T(8,128)(2,1)S(1)}, bf16[256,1024]{1,0:T(8,128)(2,1)S(1)}, u32[]{:S(2)}, u32[]{:S(2)}) collective-permute-start(bf16[256,1024]{1,0:T(8,128)(2,1)S(1)} %add_convert_fusion.1), channel_id=1, source_target_pairs={{0,8},{8,0},{16,24},{24,16},{1,9},{9,1},{17,25},{25,17},{2,10},{10... | collective-permute-start | bytes 1572872 | tf_op jit(solution)/shard_map/ppermute | solution.py:344
  149.2 12.2 %collective-permute-done.16 = bf16[256,1024]{1,0:T(8,128)(2,1)S(1)} collective-permute-done((bf16[256,1024]{1,0:T(8,128)(2,1)S(1)}, bf16[256,1024]{1,0:T(8,128)(2,1)S(1)}, u32[]{:S(2)}, u32[]{:S(2)}) %collective-permute-start.16) | collective-permute-done | bytes 524320 | tf_op jit(solution)/shard_map/ppermute | solution.py:344
  161.4 0.3 add_convert_fusion
  161.7 1.7 collective-permute-start.17
  163.4 11.4 %collective-permute-done.17 = bf16[128,1024]{1,0:T(8,128)(2,1)S(1)} collective-permute-done((bf16[128,1024]{1,0:T(8,128)(2,1)S(1)}, bf16[128,1024]{1,0:T(8,128)(2,1)S(1)}, u32[]{:S(2)}, u32[]{:S(2)}) %collective-permute-start.17) | collective-permute-done | bytes 262176 | tf_op jit(solution)/shard_map/ppermute | solution.py:382
  174.9 0.8 pad_maximum_fusion.1
  175.7 1.8 shard_map.98
  (38 shorter events, 0.1 us)
Async XLA Ops:
  8.2 13.7 %collective-permute-start.11 = (bf16[128,1024]{1,0:T(8,128)(2,1)S(1)}, bf16[128,1024]{1,0:T(8,128)(2,1)S(1)}, u32[]{:S(2)}, u32[]{:S(2)}) collective-permute-start(bf16[128,1024]{1,0:T(8,128)(2,1)S(1)} %get-tuple-element.24), channel_id=1, source_target_pairs={{0,4},{4,0},{1,5},{5,1},{2,6},{6,2},{3,7},{7,3},{8,12},{12,8},{9,1... | collective-permute-start | bytes 786440 | tf_op jit(solution)/shard_map/ppermute | solution.py:360
  12.0 1.6 copy-start.1
  13.6 0.8 copy-start.9
  14.3 0.7 copy-start.10
  15.0 0.7 copy-start.11
  16.8 1.5 copy-start
  18.3 65.3 %all-to-all-start = ((bf16[8,160,1024]{2,1,0:T(8,128)(2,1)}), bf16[8,160,1024]{2,1,0:T(8,128)(2,1)S(1)}, u32[]{:S(2)}, u32[]{:S(2)}) async-start(bf16[8,160,1024]{2,1,0:T(8,128)(2,1)} %copy-done), calls=%async_computation | async-start | bytes 5242880 | tf_op jit(solution)/shard_map/all_to_all | solution.py:323
  21.9 110.7 %all-gather.2.cloned.1.call-start = ((), (), s32[]{:S(2)}) async-start(), calls=%async_computation.4 | async-start | bytes 2621440 | tf_op jit(solution)/shard_map/all_gather | solution.py:369
  23.9 34.8 %collective-permute-start.5 = (bf16[128,1024]{1,0:T(8,128)(2,1)S(1)}, bf16[128,1024]{1,0:T(8,128)(2,1)S(1)}, u32[]{:S(2)}, u32[]{:S(2)}) collective-permute-start(bf16[128,1024]{1,0:T(8,128)(2,1)S(1)} %get-tuple-element.25), channel_id=1, source_target_pairs={{0,4},{4,0},{1,5},{5,1},{2,6},{6,2},{3,7},{7,3},{8,12},{12,8},{9,1... | collective-permute-start | bytes 786440 | tf_op jit(solution)/shard_map/ppermute | solution.py:360
  25.9 35.8 %collective-permute-start = (bf16[128,1024]{1,0:T(8,128)(2,1)S(1)}, bf16[128,1024]{1,0:T(8,128)(2,1)S(1)}, u32[]{:S(2)}, u32[]{:S(2)}) collective-permute-start(bf16[128,1024]{1,0:T(8,128)(2,1)S(1)} %get-tuple-element.26.refs_0_), channel_id=1, source_target_pairs={{0,8},{8,0},{16,24},{24,16},{1,9},{9,1},{17,25},{25,17},{2,10},{10... | collective-permute-start | bytes 786440 | tf_op jit(solution)/shard_map/ppermute | solution.py:327
  58.8 17.5 %collective-permute-start.6 = (bf16[128,1024]{1,0:T(8,128)(2,1)S(1)}, bf16[128,1024]{1,0:T(8,128)(2,1)S(1)}, u32[]{:S(2)}, u32[]{:S(2)}) collective-permute-start(bf16[128,1024]{1,0:T(8,128)(2,1)S(1)} %collective-permute-done.5.refs_6_), channel_id=1, source_target_pairs={{0,8},{8,0},{16,24},{24,16},{1,9},{9,1},{17,25},{25,17},{2,10},{10... | collective-permute-start | bytes 786440 | tf_op jit(solution)/shard_map/ppermute | solution.py:327
  60.3 18.1 %collective-permute-start.1 = (bf16[128,1024]{1,0:T(8,128)(2,1)S(1)}, bf16[128,1024]{1,0:T(8,128)(2,1)}, u32[]{:S(2)}, u32[]{:S(2)}) collective-permute-start(bf16[128,1024]{1,0:T(8,128)(2,1)S(1)} %get-tuple-element.26.refs_0_), channel_id=1, source_target_pairs={{8,16},{16,8},{9,17},{17,9},{10,18},{18,10},{11,19},{19,11},{12,20... | collective-permute-start | bytes 786440 | tf_op jit(solution)/shard_map/ppermute | solution.py:328
  61.7 18.0 %collective-permute-start.3 = (bf16[128,1024]{1,0:T(8,128)(2,1)S(1)}, bf16[128,1024]{1,0:T(8,128)(2,1)}, u32[]{:S(2)}, u32[]{:S(2)}) collective-permute-start(bf16[128,1024]{1,0:T(8,128)(2,1)S(1)} %collective-permute-done.refs_1_), channel_id=1, source_target_pairs={{8,16},{16,8},{9,17},{17,9},{10,18},{18,10},{11,19},{19,11},{12,20... | collective-permute-start | bytes 786440 | tf_op jit(solution)/shard_map/ppermute | solution.py:329
  63.1 0.7 copy-start.15
  63.7 17.3 %collective-permute-start.7 = (bf16[128,1024]{1,0:T(8,128)(2,1)S(1)}, bf16[128,1024]{1,0:T(8,128)(2,1)}, u32[]{:S(2)}, u32[]{:S(2)}) collective-permute-start(bf16[128,1024]{1,0:T(8,128)(2,1)S(1)} %collective-permute-done.5.refs_6_), channel_id=1, source_target_pairs={{8,16},{16,8},{9,17},{17,9},{10,18},{18,10},{11,19},{19,11},{12,20... | collective-permute-start | bytes 786440 | tf_op jit(solution)/shard_map/ppermute | solution.py:328
  65.1 0.7 copy-start.13
  76.3 6.0 %collective-permute-start.9 = (bf16[128,1024]{1,0:T(8,128)(2,1)S(1)}, bf16[128,1024]{1,0:T(8,128)(2,1)}, u32[]{:S(2)}, u32[]{:S(2)}) collective-permute-start(bf16[128,1024]{1,0:T(8,128)(2,1)S(1)} %collective-permute-done.6.refs_7_), channel_id=1, source_target_pairs={{8,16},{16,8},{9,17},{17,9},{10,18},{18,10},{11,19},{19,11},{12,20... | collective-permute-start | bytes 786440 | tf_op jit(solution)/shard_map/ppermute | solution.py:329
  77.7 0.8 copy-start.17
  78.4 26.4 %collective-permute-start.2 = (bf16[128,1024]{1,0:T(8,128)(2,1)}, bf16[128,1024]{1,0:T(8,128)(2,1)}, u32[]{:S(2)}, u32[]{:S(2)}) collective-permute-start(bf16[128,1024]{1,0:T(8,128)(2,1)} %collective-permute-done.1.refs_2_), channel_id=1, source_target_pairs={{8,0},{16,24},{9,1},{17,25},{10,2},{18,26},{11,3},{19,27},{12,4},{... | collective-permute-start | bytes 786440 | tf_op jit(solution)/shard_map/ppermute | solution.py:330
  79.7 25.1 %collective-permute-start.4 = (bf16[128,1024]{1,0:T(8,128)(2,1)}, bf16[128,1024]{1,0:T(8,128)(2,1)}, u32[]{:S(2)}, u32[]{:S(2)}) collective-permute-start(bf16[128,1024]{1,0:T(8,128)(2,1)} %collective-permute-done.3.refs_4_), channel_id=1, source_target_pairs={{8,0},{16,24},{9,1},{17,25},{10,2},{18,26},{11,3},{19,27},{12,4},{... | collective-permute-start | bytes 786440 | tf_op jit(solution)/shard_map/ppermute | solution.py:331
  81.0 23.8 %collective-permute-start.8 = (bf16[128,1024]{1,0:T(8,128)(2,1)}, bf16[128,1024]{1,0:T(8,128)(2,1)}, u32[]{:S(2)}, u32[]{:S(2)}) collective-permute-start(bf16[128,1024]{1,0:T(8,128)(2,1)} %collective-permute-done.7.refs_8_), channel_id=1, source_target_pairs={{8,0},{16,24},{9,1},{17,25},{10,2},{18,26},{11,3},{19,27},{12,4},{... | collective-permute-start | bytes 786440 | tf_op jit(solution)/shard_map/ppermute | solution.py:330
  82.3 23.2 %collective-permute-start.10 = (bf16[128,1024]{1,0:T(8,128)(2,1)}, bf16[128,1024]{1,0:T(8,128)(2,1)}, u32[]{:S(2)}, u32[]{:S(2)}) collective-permute-start(bf16[128,1024]{1,0:T(8,128)(2,1)} %collective-permute-done.9.refs_10_), channel_id=1, source_target_pairs={{8,0},{16,24},{9,1},{17,25},{10,2},{18,26},{11,3},{19,27},{12,4},{... | collective-permute-start | bytes 786440 | tf_op jit(solution)/shard_map/ppermute | solution.py:331
  83.6 21.8 %copy-start.14 = (bf16[128,1024]{1,0:T(8,128)(2,1)S(1)}, bf16[128,1024]{1,0:T(8,128)(2,1)}, u32[]{:S(2)}) copy-start(bf16[128,1024]{1,0:T(8,128)(2,1)} %copy-done.13) | copy-start | bytes 786436
  83.7 21.8 %copy-start.16 = (bf16[128,1024]{1,0:T(8,128)(2,1)S(1)}, bf16[128,1024]{1,0:T(8,128)(2,1)}, u32[]{:S(2)}) copy-start(bf16[128,1024]{1,0:T(8,128)(2,1)} %copy-done.15) | copy-start | bytes 786436
  83.7 21.8 %copy-start.18 = (bf16[128,1024]{1,0:T(8,128)(2,1)S(1)}, bf16[128,1024]{1,0:T(8,128)(2,1)}, u32[]{:S(2)}) copy-start(bf16[128,1024]{1,0:T(8,128)(2,1)} %copy-done.17) | copy-start | bytes 786436
  86.9 0.8 copy-start.3
  87.7 0.8 copy-start.5
  88.5 38.2 %collective-permute-start.14 = (bf16[256,1024]{1,0:T(8,128)(2,1)}, bf16[256,1024]{1,0:T(8,128)(2,1)}, u32[]{:S(2)}, u32[]{:S(2)}) collective-permute-start(bf16[256,1024]{1,0:T(8,128)(2,1)} %get-tuple-element.20), channel_id=1, source_target_pairs={{0,8},{24,16},{1,9},{25,17},{2,10},{26,18},{3,11},{27,19},{4,12},{... | collective-permute-start | bytes 1572872 | tf_op jit(solution)/shard_map/ppermute | solution.py:340
  111.1 0.7 copy-start.7
  111.8 10.0 %all-to-all-start.1 = ((bf16[8,128,128]{2,1,0:T(8,128)(2,1)}), bf16[8,128,128]{2,1,0:T(8,128)(2,1)S(1)}, u32[]{:S(2)}, u32[]{:S(2)}) async-start(bf16[8,128,128]{2,1,0:T(8,128)(2,1)} %copy-done.7), calls=%async_computation.1 | async-start | bytes 524288 | tf_op jit(solution)/shard_map/all_to_all | solution.py:323
  115.8 27.9 %collective-permute-start.12 = (bf16[256,1024]{1,0:T(8,128)(2,1)}, bf16[256,1024]{1,0:T(8,128)(2,1)}, u32[]{:S(2)}, u32[]{:S(2)}) collective-permute-start(bf16[256,1024]{1,0:T(8,128)(2,1)} %copy-done.3), channel_id=1, source_target_pairs={{0,8},{24,16},{1,9},{25,17},{2,10},{26,18},{3,11},{27,19},{4,12},{... | collective-permute-start | bytes 1572872 | tf_op jit(solution)/shard_map/ppermute | solution.py:341
  122.5 0.7 copy-start.8
  123.2 9.4 %all-to-all-start.2 = ((bf16[8,128,128]{2,1,0:T(8,128)(2,1)}), bf16[8,128,128]{2,1,0:T(8,128)(2,1)S(1)}, u32[]{:S(2)}, u32[]{:S(2)}) async-start(bf16[8,128,128]{2,1,0:T(8,128)(2,1)} %copy-done.8), calls=%async_computation.2 | async-start | bytes 524288 | tf_op jit(solution)/shard_map/all_to_all | solution.py:323
  128.9 16.8 %collective-permute-start.15 = (bf16[256,1024]{1,0:T(8,128)(2,1)}, bf16[256,1024]{1,0:T(8,128)(2,1)}, u32[]{:S(2)}, u32[]{:S(2)}) collective-permute-start(bf16[256,1024]{1,0:T(8,128)(2,1)} %add_convert_fusion.2), channel_id=1, source_target_pairs={{8,16},{16,8},{9,17},{17,9},{10,18},{18,10},{11,19},{19,11},{12,20... | collective-permute-start | bytes 1572872 | tf_op jit(solution)/shard_map/ppermute | solution.py:342
  132.6 1.6 copy-start.12
  138.5 1.3 copy-start.2
  139.9 3.8 %copy-start.4 = (bf16[256,1024]{1,0:T(8,128)(2,1)S(1)}, bf16[256,1024]{1,0:T(8,128)(2,1)}, u32[]{:S(2)}) copy-start(bf16[256,1024]{1,0:T(8,128)(2,1)} %copy-done.3) | copy-start | bytes 1572868
  139.9 35.8 %all-to-all-start.3 = ((bf16[8,128,1024]{2,1,0:T(8,128)(2,1)}), bf16[8,128,1024]{2,1,0:T(8,128)(2,1)S(1)}, u32[]{:S(2)}, u32[]{:S(2)}) async-start(bf16[8,128,1024]{2,1,0:T(8,128)(2,1)} %copy-done.2), calls=%async_computation.3 | async-start | bytes 4194304 | tf_op jit(solution)/shard_map/all_to_all | solution.py:323
  143.6 17.8 %copy-start.6 = (bf16[256,1024]{1,0:T(8,128)(2,1)S(1)}, bf16[256,1024]{1,0:T(8,128)(2,1)}, u32[]{:S(2)}) copy-start(bf16[256,1024]{1,0:T(8,128)(2,1)} %copy-done.5) | copy-start | bytes 1572868
  144.9 4.2 %collective-permute-start.13 = (bf16[256,1024]{1,0:T(8,128)(2,1)S(1)}, bf16[256,1024]{1,0:T(8,128)(2,1)S(1)}, u32[]{:S(2)}, u32[]{:S(2)}) collective-permute-start(bf16[256,1024]{1,0:T(8,128)(2,1)S(1)} %add_convert_fusion.3), channel_id=1, source_target_pairs={{8,16},{16,8},{9,17},{17,9},{10,18},{18,10},{11,19},{19,11},{12,20... | collective-permute-start | bytes 1572872 | tf_op jit(solution)/shard_map/ppermute | solution.py:343
  146.9 14.5 %collective-permute-start.16 = (bf16[256,1024]{1,0:T(8,128)(2,1)S(1)}, bf16[256,1024]{1,0:T(8,128)(2,1)S(1)}, u32[]{:S(2)}, u32[]{:S(2)}) collective-permute-start(bf16[256,1024]{1,0:T(8,128)(2,1)S(1)} %add_convert_fusion.1), channel_id=1, source_target_pairs={{0,8},{8,0},{16,24},{24,16},{1,9},{9,1},{17,25},{25,17},{2,10},{10... | collective-permute-start | bytes 1572872 | tf_op jit(solution)/shard_map/ppermute | solution.py:344
  161.7 13.1 %collective-permute-start.17 = (bf16[128,1024]{1,0:T(8,128)(2,1)S(1)}, bf16[128,1024]{1,0:T(8,128)(2,1)S(1)}, u32[]{:S(2)}, u32[]{:S(2)}) collective-permute-start(bf16[128,1024]{1,0:T(8,128)(2,1)S(1)} %slice.9), channel_id=1, source_target_pairs={{0,4},{4,0},{1,5},{5,1},{2,6},{6,2},{3,7},{7,3},{8,12},{12,8},{9,1... | collective-permute-start | bytes 786440 | tf_op jit(solution)/shard_map/ppermute | solution.py:382
Sparse Core Ops, SparseCore 0:
  24.9 50.2 all-gather.1

commit v5 on v4

--- a/solution.py
+++ b/solution.py
@@ -17,9 +17,8 @@
 SIDES = ((0, 1), (1, 0), (2, 3), (3, 2))
 MIDDLE = ((1, 2), (2, 1))
 OUTWARD = ((1, 0), (2, 3))
-INWARD = ((0, 1), (3, 2))
 SWAP = ((0, 1), (1, 0))
-DOWN, UP, GRADS = 0, 2, 4
+DOWN, UP = 0, 2
 
 
 def gelu_parts(preact):
@@ -58,9 +57,9 @@
 
 
 def pack_kernel(
-    local_experts, far_ref, ids_ref, gates_ref, preact_ref, tokens_ref,
-    out_ref, activation_ref, scaled_ref, weighted,
+    local_experts, far_ref, ids_ref, gates_ref, preact_ref, tokens_ref, *refs
 ):
+    out_ref, activation_ref, scaled_ref, weighted = refs[-4:]
     blocks, height, features = out_ref.shape
     rows, wide = preact_ref.shape
     far_count = far_ref.shape[0]
@@ -84,9 +83,8 @@
     for block in range(blocks):
         side = lax.rem(near + block, NEAR)
         places = (
-            (side * far_count + far_place) * local_experts + local,
+            (far_place * NEAR + side) * local_experts + local,
             (far * NEAR + side) * local_experts + local,
-            (far_place * NEAR + side) * local_experts + local,
         )
         out_ref[block, 0:rows, :] = tokens_ref[:, block * features : (block + 1) * features]
         for at in range(0, features, wide):
@@ -94,11 +92,11 @@
             out_ref[block, rows : rows + taken, at : at + wide] = weighted[start : start + taken, :]
         last = height - TILE
         out_ref[block, last:, :] = jnp.zeros((TILE, features), jnp.bfloat16)
-        for at, place in zip((DOWN, UP, GRADS), places):
+        for at, place in zip((DOWN, UP), places):
             out_ref[block, last + at : last + at + 2, 0:rows] = place.astype(jnp.bfloat16)
 
 
-def pack_tokens(far_places, ids, gates, preact, tokens, members, local_experts):
+def pack_tokens(far_places, ids, gates, preact, tokens, members, local_experts, before):
     rows, width = tokens.shape
     features = width // members
     each = members // 4
@@ -112,6 +110,7 @@
             pl.BlockSpec(memory_space=pltpu.SMEM),
             *whole,
             pl.BlockSpec((rows, each * features), lambda i: (0, i)),
+            *[pl.BlockSpec(memory_space=pl.ANY) for _ in before],
         ],
         out_specs=(pl.BlockSpec((each, height, features), lambda i: (i, 0, 0)), whole[2], whole[2]),
         out_shape=(
@@ -119,7 +118,7 @@
         ),
         scratch_shapes=[pltpu.VMEM(preact.shape, jnp.bfloat16)],
         compiler_params=params(),
-    )(far_places, ids, gates, preact, tokens)
+    )(far_places, ids, gates, preact, tokens, *before)
 
 
 def unpack_kernel(parts_ref, out_ref):
@@ -152,7 +151,7 @@
 
 
 def down_kernel(rows, wide, received_ref, *refs):
-    out_refs, (turned, numbers, spread) = refs[:-3], refs[-3:]
+    out_ref, turned, numbers, spread = refs[-4:]
     sources, _, features = received_ref.shape
     hidden, each = wide // 2, BLOCK // (wide // 2)
     taken = rows * wide // features
@@ -165,28 +164,30 @@
         )
         lanes = slice(source * rows, (source + 1) * rows)
         turned[:, lanes] = weighted.T
-        numbers[:, lanes] = places_of(received_ref, source, GRADS, rows).astype(jnp.float32)
-    number = 0
-    for out_ref in out_refs:
-        for start in range(0, out_ref.shape[0], BLOCK):
-            for expert in range(each):
-                spread[expert * hidden : (expert + 1) * hidden, :] = jnp.where(
-                    numbers[0:1, :] == number + expert,
-                    turned[0:hidden, :],
-                    jnp.where(numbers[1:2, :] == number + expert, turned[hidden:, :], 0.0),
-                ).astype(jnp.bfloat16)
-            number += each
-            out_ref[start : start + BLOCK, :] = jnp.dot(
-                spread[...], token_rows(received_ref, rows), preferred_element_type=jnp.float32
-            ).astype(out_ref.dtype)
-
-
-def down_partial(received, rows, wide, total_rows, count):
+        numbers[:, lanes] = places_of(received_ref, source, UP, rows).astype(jnp.float32)
+    for start in range(0, out_ref.shape[0], BLOCK):
+        for expert in range(each):
+            number = start // hidden + expert
+            spread[expert * hidden : (expert + 1) * hidden, :] = jnp.where(
+                numbers[0:1, :] == number,
+                turned[0:hidden, :],
+                jnp.where(numbers[1:2, :] == number, turned[hidden:, :], 0.0),
+            ).astype(jnp.bfloat16)
+        out_ref[start : start + BLOCK, :] = jnp.dot(
+            spread[...], token_rows(received_ref, rows), preferred_element_type=jnp.float32
+        ).astype(out_ref.dtype)
+
+
+def down_partial(received, rows, wide, total_rows, before):
     sources, _, features = received.shape
     total = sources * rows
     return pl.pallas_call(
         functools.partial(down_kernel, rows, wide),
-        out_shape=[jax.ShapeDtypeStruct((total_rows // count, features), jnp.bfloat16)] * count,
+        in_specs=[
+            pl.BlockSpec(memory_space=pltpu.VMEM),
+            *[pl.BlockSpec(memory_space=pl.ANY) for _ in before],
+        ],
+        out_shape=jax.ShapeDtypeStruct((total_rows, features), jnp.bfloat16),
         scratch_shapes=[
             pltpu.VMEM((wide, total), jnp.float32),
             pltpu.VMEM((2, total), jnp.float32),
@@ -194,7 +195,7 @@
         ],
         compiler_params=params(),
         cost_estimate=cost(total_rows, total, features),
-    )(received)
+    )(received, *before)
 
 
 def lane_numbers(received_ref, which, rows, wide):
@@ -332,18 +333,6 @@
     return [(mine,), (beside,), (across, second), (across_far, third)]
 
 
-def add(*terms):
-    return sum(term.astype(jnp.float32) for term in terms).astype(jnp.bfloat16)
-
-
-def chain_scatter(own, beside, second, third):
-    third = add(third, lax.ppermute(third, "far", INWARD))
-    second = add(second, lax.ppermute(second, "far", INWARD))
-    beside = add(beside, lax.ppermute(third, "far", MIDDLE))
-    across = lax.ppermute(second, "far", MIDDLE)
-    return add(own, across, lax.ppermute(beside, "far", SIDES))
-
-
 def body(token_grads, router_gates, expert_ids, saved_hidden, up_weight, down_weight):
     tok_count = token_grads.shape[0]
     local_experts, hidden, width = up_weight.shape
@@ -357,34 +346,24 @@
         flat = weight.reshape(own_rows, width)
         own = lax.dynamic_slice_in_dim(flat, near * features, features, axis=1)
         other = lax.dynamic_slice_in_dim(flat, (1 - near) * features, features, axis=1)
-        return own, lax.ppermute(other, "near", SWAP)
-
-    down_halves, up_halves = halves(down_weight), halves(up_weight)
-    if chained:
-        down_pieces = [terms for half in down_halves for terms in chain_gather(half)]
+        return jnp.concatenate([own, lax.ppermute(other, "near", SWAP)])
+
+    down_own, up_own = halves(down_weight), halves(up_weight)
+    if far_count == len(CHAIN):
+        down_pieces = chain_gather(down_own)
         far_places = jnp.asarray(CHAIN, jnp.int32)[lax.axis_index("far")]
     else:
-        down_pieces = [(lax.all_gather(half, "far", tiled=True),) for half in down_halves]
+        down_pieces = [(lax.all_gather(down_own, "far", tiled=True),)]
         far_places = jnp.arange(far_count, dtype=jnp.int32)
-    up_full = lax.all_gather(jnp.concatenate(up_halves), "far", tiled=True)
+    up_full = lax.all_gather(up_own, "far", tiled=True)
     packed, activation, scaled = pack_tokens(
-        far_places, expert_ids.T, router_gates.T, saved_hidden, token_grads, members, local_experts
+        far_places, expert_ids.T, router_gates.T, saved_hidden, token_grads, members,
+        local_experts, (down_own, up_own),
     )
     received = exchange(packed, GROUP)
 
-    partial_value = down_partial(
-        received, tok_count, wide, own_rows * NEAR * far_count, far_count if chained else 1
-    )
-    if chained:
-        sums = chain_scatter(*partial_value)
-    else:
-        sums = lax.psum_scatter(partial_value[0], "far", scatter_dimension=0, tiled=True)
-    kept, passed = sums[:own_rows], lax.ppermute(sums[own_rows:], "near", SWAP)
-    down_grads = jnp.concatenate(
-        [jnp.where(near == 0, kept, passed), jnp.where(near == 0, passed, kept)], axis=1
-    ).reshape(down_weight.shape)
-
-    parts = exchange(project(received, down_pieces, tok_count, wide), GROUP)
+    projected = project(received, down_pieces, tok_count, wide)
+    parts = exchange(projected, GROUP)
     hidden_grad, gate_grads = pl.pallas_call(
         hidden_kernel,
         out_shape=(
@@ -395,6 +374,15 @@
     )(parts, activation, scaled)
     hidden_grad = exchange(hidden_grad, GROUP)
     input_grads = unpack_tokens(exchange(input_rows(received, hidden_grad, up_full), GROUP))
+
+    partial_value = down_partial(
+        received, tok_count, wide, up_full.shape[0], (up_full, projected)
+    )
+    sums = lax.psum_scatter(partial_value, "far", scatter_dimension=0, tiled=True)
+    kept, passed = sums[:own_rows], lax.ppermute(sums[own_rows:], "near", SWAP)
+    down_grads = jnp.concatenate(
+        [jnp.where(near == 0, kept, passed), jnp.where(near == 0, passed, kept)], axis=1
+    ).reshape(down_weight.shape)
     return (input_grads, gate_grads.T, down_grads)
 
 

time: 185 us -> 187 us (1.011)
  starting transfers between devices: 58.1 us -> 19.2 us
  waiting for transfers between devices: 72.3 us -> 96.8 us
  blocking collectives: 0 us -> 18.3 us
  local copies, waits for them, and re-layouts: 16.1 us -> 20.8 us
  other arithmetic: 6.68 us -> 2.68 us
  Pallas kernels: 16.8 us -> 14.4 us
    ppermute x7 -> x2, waiting for transfers between devices: 43.6 us -> 11.6 us  [halves(): return jnp.concatenate([own, lax.ppermute(other, 'near', SWAP)])]
    ppermute x2 -> x1, waiting for transfers between devices: 10.5 us -> 36.2 us  [chain_gather(): beside = lax.ppermute(mine, 'far', SIDES)]
    ppermute x7 -> x2, starting transfers between devices: 27.9 us -> 4.77 us  [halves(): return jnp.concatenate([own, lax.ppermute(other, 'near', SWAP)])]
    all_to_all x0 -> x2, blocking collectives: none -> 18.3 us  [exchange(): return lax.all_to_all(value, axes, split_axis=0, concat_axis=0, tiled=True)]
    reduce_scatter x0 -> x1, waiting for transfers between devices: none -> 14.8 us  [body(): lax.psum_scatter(partial_value, 'far', scatter_dimension=0, tiled=True)]
    ppermute x2 -> x1, waiting for transfers between devices: 0.01 us -> 12 us  [chain_gather(): second = lax.ppermute(across, 'far', OUTWARD)]
    ppermute x2 -> x1, waiting for transfers between devices: 0.7 us -> 10.1 us  [chain_gather(): third = lax.ppermute(across_far, 'far', OUTWARD)]
    ppermute x1, waiting for transfers between devices: 11.4 us -> 3.68 us  [body(): lax.ppermute(sums[own_rows:], 'near', SWAP)]
  transfers between devices with their start and end apart: 23 -> 12, of which waited for: 7 -> 8; matrix products, arithmetic and copies ran while one was open for 5% -> 2% of each run, Pallas kernels for 8% -> 6%
where the time goes in v5:
time: 187 us; the launch traced here: 186 us
  waiting for transfers between devices  96.8 us (52%)
  local copies, waits for them, and re-layouts  20.8 us (11%)
  starting transfers between devices  19.2 us (10%)
  blocking collectives  18.3 us (10%)
  Pallas kernels  14.4 us (8%)
  between operations  14.3 us (8%)
  other arithmetic  2.68 us (1%)
    ppermute x1, waiting for transfers between devices, chain_gather(): beside = lax.ppermute(mine, 'far', SIDES)  36.2 us
    all_to_all x2, blocking collectives, exchange(): return lax.all_to_all(value, axes, split_axis=0, concat_axis=0, tiled=True)  18.3 us
    unnamed x46, local copies, waits for them, and re-layouts  17.3 us
    reduce_scatter x1, waiting for transfers between devices, body(): lax.psum_scatter(partial_value, 'far', scatter_dimension=0, tiled=True)  14.8 us
    ppermute x1, waiting for transfers between devices, chain_gather(): second = lax.ppermute(across, 'far', OUTWARD)  12 us
    ppermute x2, waiting for transfers between devices, halves(): return jnp.concatenate([own, lax.ppermute(other, 'near', SWAP)])  11.6 us
    ppermute x1, waiting for transfers between devices, chain_gather(): third = lax.ppermute(across_far, 'far', OUTWARD)  10.1 us
    all_to_all x2, waiting for transfers between devices, exchange(): return lax.all_to_all(value, axes, split_axis=0, concat_axis=0, tiled=True)  8.35 us
  transfers between devices with their start and end apart: 12, of which 8 were waited for; matrix products, arithmetic and copies ran while one was open for 2% of the time, Pallas kernels for 6%

profile of v5, /device:TPU:0, one launch (start us, length us, event | category | flops | bytes accessed | tf_op | source)
XLA Modules:
  0.0 186.5 jit_solution(8493947138364906511)
XLA Ops:
  7.2 0.0 copy-start.20
  7.2 0.0 all-gather.2.cloned.1.call-start
  7.2 1.1 constant_dynamic-slice_fusion.1
  8.3 0.0 copy-start.2
  8.4 0.0 copy-start.5
  8.4 0.0 copy-start.6
  8.4 0.0 copy-start.7
  8.4 3.0 %collective-permute-start.1 = (bf16[128,1024]{1,0:T(8,128)(2,1)S(1)}, bf16[128,1024]{1,0:T(8,128)(2,1)S(1)}, u32[]{:S(2)}, u32[]{:S(2)}) collective-permute-start(bf16[128,1024]{1,0:T(8,128)(2,1)S(1)} %get-tuple-element.16), channel_id=1, source_target_pairs={{0,4},{4,0},{1,5},{5,1},{2,6},{6,2},{3,7},{7,3},{8,12},{12,8},{9,1... | collective-permute-start | bytes 786440 | tf_op jit(solution)/shard_map/ppermute | solution.py:349
  11.4 6.3 %collective-permute-done.1 = bf16[128,1024]{1,0:T(8,128)(2,1)S(1)} collective-permute-done((bf16[128,1024]{1,0:T(8,128)(2,1)S(1)}, bf16[128,1024]{1,0:T(8,128)(2,1)S(1)}, u32[]{:S(2)}, u32[]{:S(2)}) %collective-permute-start.1) | collective-permute-done | bytes 262176 | tf_op jit(solution)/shard_map/ppermute | solution.py:349
  17.7 0.8 pad_maximum_fusion.1.refs_1_
  18.6 0.0 all-gather.2.cloned.1.call-update
  18.6 0.8 constant_dynamic-slice_fusion.3
  19.3 1.7 collective-permute-start
  21.1 0.7 fusion.far_ref
  21.8 5.3 %collective-permute-done = bf16[128,1024]{1,0:T(8,128)(2,1)S(1)} collective-permute-done((bf16[128,1024]{1,0:T(8,128)(2,1)}, bf16[128,1024]{1,0:T(8,128)(2,1)S(1)}, u32[]{:S(2)}, u32[]{:S(2)}) %collective-permute-start) | collective-permute-done | bytes 262176 | tf_op jit(solution)/shard_map/ppermute | solution.py:349
  27.1 0.7 copy-done.22
  27.8 1.0 pad_maximum_fusion.refs_0_
  28.8 1.2 shard_map.94
  30.0 1.5 copy-done.1
  31.4 3.6 %all-to-all-start = ((bf16[8,160,1024]{2,1,0:T(8,128)(2,1)}), bf16[8,160,1024]{2,1,0:T(8,128)(2,1)S(1)}, u32[]{:S(2)}, u32[]{:S(2)}) async-start(bf16[8,160,1024]{2,1,0:T(8,128)(2,1)} %copy-done.1), calls=%async_computation | async-start | bytes 5242880 | tf_op jit(solution)/shard_map/all_to_all | solution.py:324
  35.1 0.0 reduce-scatter.2.cloned.1.call-start
  35.1 1.6 collective-permute-start.2
  36.8 0.7 collective-permute-start.3
  37.4 36.2 %collective-permute-done.2.refs_1_ = bf16[256,1024]{1,0:T(8,128)(2,1)S(1)} collective-permute-done((bf16[256,1024]{1,0:T(8,128)(2,1)S(1)}, bf16[256,1024]{1,0:T(8,128)(2,1)S(1)}, u32[]{:S(2)}, u32[]{:S(2)}) %collective-permute-start.2) | collective-permute-done | bytes 524320 | tf_op jit(solution)/shard_map/ppermute | solution.py:328
  73.6 0.7 collective-permute-start.5
  74.3 0.0 copy-start.10
  74.3 0.8 copy-done.10
  75.1 0.0 collective-permute-done.3.refs_2_
  75.1 1.3 collective-permute-start.4
  76.4 0.8 copy-done.12
  77.3 0.0 collective-permute-done.5.refs_4_
  77.3 1.3 collective-permute-start.6
  78.6 0.8 copy-done.14
  79.4 12.0 %collective-permute-done.4.refs_3_ = bf16[256,1024]{1,0:T(8,128)(2,1)S(1)} collective-permute-done((bf16[256,1024]{1,0:T(8,128)(2,1)S(1)}, bf16[256,1024]{1,0:T(8,128)(2,1)S(1)}, u32[]{:S(2)}, u32[]{:S(2)}) %collective-permute-start.4) | collective-permute-done | bytes 524320 | tf_op jit(solution)/shard_map/ppermute | solution.py:331
  91.4 0.8 copy-done.16
  92.2 10.1 %collective-permute-done.6.refs_5_ = bf16[256,1024]{1,0:T(8,128)(2,1)S(1)} collective-permute-done((bf16[256,1024]{1,0:T(8,128)(2,1)S(1)}, bf16[256,1024]{1,0:T(8,128)(2,1)S(1)}, u32[]{:S(2)}, u32[]{:S(2)}) %collective-permute-start.6) | collective-permute-done | bytes 524320 | tf_op jit(solution)/shard_map/ppermute | solution.py:332
  102.2 0.8 copy-done.18
  103.0 0.0 all-to-all-done.received_ref
  103.0 1.0 copy-done.11
  104.1 1.0 copy-done.13
  105.1 1.0 copy-done.15
  106.2 1.0 copy-done.17
  107.2 1.0 copy-done.19
  108.3 4.0 %shard_map.95.refs_1_ = bf16[8,128,128]{2,1,0:T(8,128)(2,1)S(1)} custom-call(bf16[8,160,1024]{2,1,0:T(8,128)(2,1)S(1)} %all-to-all-done.received_ref, bf16[256,1024]{1,0:T(8,128)(2,1)S(1)} %pad_maximum_fusion.refs_0_, bf16[256,1024]{1,0:T(8,128)(2,1)S(1)} %copy-done.11, bf16[256,1024]{1,0:T(8,128)(2,1)S(1)} %copy-done.13, bf16[256,1024]{1,0:T(8,128)(2,1)S(1)} %copy-done.17, ...), custom_call_target="tpu_custom_call" | custom-call | flops 2147483648 | bytes 6291456 | tf_op jit(solution)/shard_map/pallas_call | solution.py:250
  112.2 0.0 all-gather.2.cloned.1.call-done.weight_ref.refs_0_
  112.3 1.6 copy-done.8
  113.9 2.4 %shard_map.99 = bf16[1024,1024]{1,0:T(8,128)(2,1)S(1)} custom-call(bf16[8,160,1024]{2,1,0:T(8,128)(2,1)S(1)} %all-to-all-done.received_ref, bf16[1024,1024]{1,0:T(8,128)(2,1)S(1)} %copy-done.8, bf16[8,128,128]{2,1,0:T(8,128)(2,1)S(1)} %shard_map.95.refs_1_), custom_call_target="tpu_custom_call" | custom-call | flops 2147483648 | bytes 6291456 | tf_op jit(solution)/shard_map/pallas_call | solution.py:184
  116.3 1.4 copy-done.3
  117.6 0.0 reduce-scatter.2.cloned.1.call-update
  117.7 9.7 %all_to_all.20.parts_ref = bf16[8,128,128]{2,1,0:T(8,128)(2,1)S(1)} all-to-all(bf16[8,128,128]{2,1,0:T(8,128)(2,1)S(1)} %shard_map.95.refs_1_), channel_id=1, replica_groups=mesh['far'=4,'near'=2,'inner'=2,'outer'=2] {'inner','outer','near'}, dimensions={0} | all-to-all | bytes 524288 | tf_op jit(solution)/shard_map/all_to_all | solution.py:324
  127.4 0.7 shard_map.96
  128.1 8.6 %all_to_all.21.hidden_ref = bf16[8,128,128]{2,1,0:T(8,128)(2,1)S(1)} all-to-all(bf16[8,128,128]{2,1,0:T(8,128)(2,1)S(1)} %get-tuple-element.11), channel_id=1, replica_groups=mesh['far'=4,'near'=2,'inner'=2,'outer'=2] {'inner','outer','near'}, dimensions={0} | all-to-all | bytes 524288 | tf_op jit(solution)/shard_map/all_to_all | solution.py:324
  136.7 1.6 copy-done.9
  138.3 4.3 %shard_map.97 = bf16[8,128,1024]{2,1,0:T(8,128)(2,1)S(1)} custom-call(bf16[8,160,1024]{2,1,0:T(8,128)(2,1)S(1)} %all-to-all-done.received_ref, bf16[8,128,128]{2,1,0:T(8,128)(2,1)S(1)} %all_to_all.21.hidden_ref, bf16[1024,1024]{1,0:T(8,128)(2,1)S(1)} %copy-done.9), custom_call_target="tpu_custom_call" | custom-call | flops 2147483648 | bytes 6291456 | tf_op jit(solution)/shard_map/pallas_call | solution.py:307
  142.6 0.0 copy-start.4
  142.6 1.3 copy-done.4
  143.9 3.6 %all-to-all-start.3 = ((bf16[8,128,1024]{2,1,0:T(8,128)(2,1)}), bf16[8,128,1024]{2,1,0:T(8,128)(2,1)S(1)}, u32[]{:S(2)}, u32[]{:S(2)}) async-start(bf16[8,128,1024]{2,1,0:T(8,128)(2,1)} %copy-done.4), calls=%async_computation.3 | async-start | bytes 4194304 | tf_op jit(solution)/shard_map/all_to_all | solution.py:324
  147.5 14.8 %reduce-scatter.2.cloned.1.call-done = bf16[256,1024]{1,0:T(8,128)(2,1)} async-done(((bf16[1024,1024]{1,0:T(8,128)(2,1)}), bf16[256,1024]{1,0:T(8,128)(2,1)}) %reduce-scatter.2.cloned.1.call-update) | async-done | bytes 524304 | tf_op jit(solution)/shard_map/reduce_scatter | solution.py:381
  162.4 1.0 slice.9
  163.4 1.5 collective-permute-start.7
  164.9 8.3 %all-to-all-done.3.parts_ref = bf16[8,128,1024]{2,1,0:T(8,128)(2,1)S(1)} async-done(((bf16[8,128,1024]{2,1,0:T(8,128)(2,1)}), bf16[8,128,1024]{2,1,0:T(8,128)(2,1)S(1)}, u32[]{:S(2)}, u32[]{:S(2)}) %all-to-all-start.3) | async-done | bytes 2097184 | tf_op jit(solution)/shard_map/all_to_all | solution.py:324
  173.3 1.8 shard_map.98
  175.1 3.7 %collective-permute-done.7 = bf16[128,1024]{1,0:T(8,128)(2,1)S(1)} collective-permute-done((bf16[128,1024]{1,0:T(8,128)(2,1)S(1)}, bf16[128,1024]{1,0:T(8,128)(2,1)S(1)}, u32[]{:S(2)}, u32[]{:S(2)}) %collective-permute-start.7) | collective-permute-done | bytes 262176 | tf_op jit(solution)/shard_map/ppermute | solution.py:382
  178.8 0.8 pad_maximum_fusion.2
  (24 shorter events, 0.1 us)
Async XLA Ops:
  7.2 11.4 %copy-start.20 = (bf16[2,64,2048]{2,1,0:T(8,128)(2,1)S(1)}, bf16[2,64,2048]{2,1,0:T(8,128)(2,1)}, u32[]{:S(2)}) copy-start(bf16[2,64,2048]{2,1,0:T(8,128)(2,1)} %param.12) | copy-start | bytes 1572868
  7.2 105.1 %all-gather.2.cloned.1.call-start = ((), (), s32[]{:S(2)}) async-start(), calls=%async_computation.5 | async-start | bytes 2621440 | tf_op jit(solution)/shard_map/all_gather | solution.py:358
  8.3 20.4 %copy-start.2 = (bf16[128,8192]{1,0:T(8,128)(2,1)S(1)}, bf16[128,8192]{1,0:T(8,128)(2,1)}, u32[]{:S(2)}) copy-start(bf16[128,8192]{1,0:T(8,128)(2,1)} %tokens_ref.1) | copy-start | bytes 6291460
  8.4 20.4 %copy-start.5 = (bf16[128,128]{1,0:T(8,128)(2,1)S(1)}, bf16[128,128]{1,0:T(8,128)(2,1)}, u32[]{:S(2)}) copy-start(bf16[128,128]{1,0:T(8,128)(2,1)} %preact_ref.1) | copy-start | bytes 98308
  8.4 20.4 %copy-start.6 = (s32[128,2]{0,1:T(2,128)S(1)}, s32[128,2]{0,1:T(2,128)}, u32[]{:S(2)}) copy-start(s32[128,2]{0,1:T(2,128)} %param.9) | copy-start | bytes 3076
  8.4 20.4 %copy-start.7 = (bf16[128,2]{0,1:T(2,128)(2,1)S(1)}, bf16[128,2]{0,1:T(2,128)(2,1)}, u32[]{:S(2)}) copy-start(bf16[128,2]{0,1:T(2,128)(2,1)} %param.8) | copy-start | bytes 1540
  8.4 9.3 %collective-permute-start.1 = (bf16[128,1024]{1,0:T(8,128)(2,1)S(1)}, bf16[128,1024]{1,0:T(8,128)(2,1)S(1)}, u32[]{:S(2)}, u32[]{:S(2)}) collective-permute-start(bf16[128,1024]{1,0:T(8,128)(2,1)S(1)} %get-tuple-element.16), channel_id=1, source_target_pairs={{0,4},{4,0},{1,5},{5,1},{2,6},{6,2},{3,7},{7,3},{8,12},{12,8},{9,1... | collective-permute-start | bytes 786440 | tf_op jit(solution)/shard_map/ppermute | solution.py:349
  18.6 10.2 %copy-start = (bf16[256,1024]{1,0:T(8,128)(2,1)S(1)}, bf16[256,1024]{1,0:T(8,128)(2,1)}, u32[]{:S(2)}) copy-start(bf16[256,1024]{1,0:T(8,128)(2,1)} %pad_maximum_fusion.1.refs_1_) | copy-start | bytes 1572868
  19.3 7.7 %collective-permute-start = (bf16[128,1024]{1,0:T(8,128)(2,1)}, bf16[128,1024]{1,0:T(8,128)(2,1)S(1)}, u32[]{:S(2)}, u32[]{:S(2)}) collective-permute-start(bf16[128,1024]{1,0:T(8,128)(2,1)} %get-tuple-element.18), channel_id=1, source_target_pairs={{0,4},{4,0},{1,5},{5,1},{2,6},{6,2},{3,7},{7,3},{8,12},{12,8},{9,1... | collective-permute-start | bytes 786440 | tf_op jit(solution)/shard_map/ppermute | solution.py:349
  27.1 0.7 copy-start.22
  30.0 1.5 copy-start.1
  31.4 71.6 %all-to-all-start = ((bf16[8,160,1024]{2,1,0:T(8,128)(2,1)}), bf16[8,160,1024]{2,1,0:T(8,128)(2,1)S(1)}, u32[]{:S(2)}, u32[]{:S(2)}) async-start(bf16[8,160,1024]{2,1,0:T(8,128)(2,1)} %copy-done.1), calls=%async_computation | async-start | bytes 5242880 | tf_op jit(solution)/shard_map/all_to_all | solution.py:324
  35.1 127.3 %reduce-scatter.2.cloned.1.call-start = ((), (), s32[]{:S(2)}) async-start(), calls=%async_computation.6 | async-start | bytes 2621440 | tf_op jit(solution)/shard_map/reduce_scatter | solution.py:381
  35.1 38.5 %collective-permute-start.2 = (bf16[256,1024]{1,0:T(8,128)(2,1)S(1)}, bf16[256,1024]{1,0:T(8,128)(2,1)S(1)}, u32[]{:S(2)}, u32[]{:S(2)}) collective-permute-start(bf16[256,1024]{1,0:T(8,128)(2,1)S(1)} %pad_maximum_fusion.refs_0_), channel_id=1, source_target_pairs={{0,8},{8,0},{16,24},{24,16},{1,9},{9,1},{17,25},{25,17},{2,10},{10... | collective-permute-start | bytes 1572872 | tf_op jit(solution)/shard_map/ppermute | solution.py:328
  36.8 38.4 %collective-permute-start.3 = (bf16[256,1024]{1,0:T(8,128)(2,1)S(1)}, bf16[256,1024]{1,0:T(8,128)(2,1)S(1)}, u32[]{:S(2)}, u32[]{:S(2)}) collective-permute-start(bf16[256,1024]{1,0:T(8,128)(2,1)S(1)} %pad_maximum_fusion.refs_0_), channel_id=1, source_target_pairs={{8,16},{16,8},{9,17},{17,9},{10,18},{18,10},{11,19},{19,11},{12,20... | collective-permute-start | bytes 1572872 | tf_op jit(solution)/shard_map/ppermute | solution.py:329
  73.6 3.6 %collective-permute-start.5 = (bf16[256,1024]{1,0:T(8,128)(2,1)S(1)}, bf16[256,1024]{1,0:T(8,128)(2,1)S(1)}, u32[]{:S(2)}, u32[]{:S(2)}) collective-permute-start(bf16[256,1024]{1,0:T(8,128)(2,1)S(1)} %collective-permute-done.2.refs_1_), channel_id=1, source_target_pairs={{8,16},{16,8},{9,17},{17,9},{10,18},{18,10},{11,19},{19,11},{12,20... | collective-permute-start | bytes 1572872 | tf_op jit(solution)/shard_map/ppermute | solution.py:330
  74.3 0.8 copy-start.10
  75.1 16.3 %collective-permute-start.4 = (bf16[256,1024]{1,0:T(8,128)(2,1)S(1)}, bf16[256,1024]{1,0:T(8,128)(2,1)S(1)}, u32[]{:S(2)}, u32[]{:S(2)}) collective-permute-start(bf16[256,1024]{1,0:T(8,128)(2,1)S(1)} %collective-permute-done.3.refs_2_), channel_id=1, source_target_pairs={{8,0},{16,24},{9,1},{17,25},{10,2},{18,26},{11,3},{19,27},{12,4},{... | collective-permute-start | bytes 1572872 | tf_op jit(solution)/shard_map/ppermute | solution.py:331
  76.4 0.8 copy-start.12
  77.3 25.0 %collective-permute-start.6 = (bf16[256,1024]{1,0:T(8,128)(2,1)S(1)}, bf16[256,1024]{1,0:T(8,128)(2,1)S(1)}, u32[]{:S(2)}, u32[]{:S(2)}) collective-permute-start(bf16[256,1024]{1,0:T(8,128)(2,1)S(1)} %collective-permute-done.5.refs_4_), channel_id=1, source_target_pairs={{8,0},{16,24},{9,1},{17,25},{10,2},{18,26},{11,3},{19,27},{12,4},{... | collective-permute-start | bytes 1572872 | tf_op jit(solution)/shard_map/ppermute | solution.py:332
  78.5 0.8 copy-start.14
  91.4 0.8 copy-start.16
  102.2 0.8 copy-start.18
  103.0 1.0 copy-start.11
  104.1 1.0 copy-start.13
  105.1 1.0 copy-start.15
  106.2 1.0 copy-start.17
  107.2 1.0 copy-start.19
  112.3 1.6 copy-start.8
  116.3 1.4 copy-start.3
  136.7 1.6 copy-start.9
  142.6 1.3 copy-start.4
  143.9 29.3 %all-to-all-start.3 = ((bf16[8,128,1024]{2,1,0:T(8,128)(2,1)}), bf16[8,128,1024]{2,1,0:T(8,128)(2,1)S(1)}, u32[]{:S(2)}, u32[]{:S(2)}) async-start(bf16[8,128,1024]{2,1,0:T(8,128)(2,1)} %copy-done.4), calls=%async_computation.3 | async-start | bytes 4194304 | tf_op jit(solution)/shard_map/all_to_all | solution.py:324
  163.4 15.4 %collective-permute-start.7 = (bf16[128,1024]{1,0:T(8,128)(2,1)S(1)}, bf16[128,1024]{1,0:T(8,128)(2,1)S(1)}, u32[]{:S(2)}, u32[]{:S(2)}) collective-permute-start(bf16[128,1024]{1,0:T(8,128)(2,1)S(1)} %slice.9), channel_id=1, source_target_pairs={{0,4},{4,0},{1,5},{5,1},{2,6},{6,2},{3,7},{7,3},{8,12},{12,8},{9,1... | collective-permute-start | bytes 786440 | tf_op jit(solution)/shard_map/ppermute | solution.py:382
  164.9 13.9 %copy-start.21 = (bf16[256,1024]{1,0:T(8,128)(2,1)S(1)}, bf16[256,1024]{1,0:T(8,128)(2,1)}, u32[]{:S(2)}) copy-start(bf16[256,1024]{1,0:T(8,128)(2,1)} %reduce-scatter.2.cloned.1.call-done) | copy-start | bytes 1572868
Sparse Core Ops, SparseCore 0:
  18.7 58.4 all-gather.1
  117.8 44.5 reduce-scatter.1

commit v6 on v4

--- a/solution.py
+++ b/solution.py
@@ -19,7 +19,7 @@
 OUTWARD = ((1, 0), (2, 3))
 INWARD = ((0, 1), (3, 2))
 SWAP = ((0, 1), (1, 0))
-DOWN, UP, GRADS = 0, 2, 4
+DOWN, UP = 0, 2
 
 
 def gelu_parts(preact):
@@ -28,8 +28,8 @@
     return (preact * cumulative, cumulative + preact * density)
 
 
-def params():
-    return pltpu.CompilerParams(vmem_limit_bytes=40 * MIB)
+def params(grant=40):
+    return pltpu.CompilerParams(vmem_limit_bytes=grant * MIB)
 
 
 def cost(rows, inner, columns):
@@ -57,10 +57,28 @@
     ]
 
 
+def stack_kernel(own_ref, other_ref, *refs):
+    rows = own_ref.shape[0]
+    refs[-1][0:rows, :] = own_ref[...]
+    refs[-1][rows:, :] = other_ref[...]
+
+
+def stack(own, other, before):
+    return pl.pallas_call(
+        stack_kernel,
+        in_specs=[
+            *[pl.BlockSpec(memory_space=pltpu.VMEM)] * 2,
+            *[pl.BlockSpec(memory_space=pl.ANY) for _ in before],
+        ],
+        out_shape=jax.ShapeDtypeStruct((2 * own.shape[0], own.shape[1]), own.dtype),
+        compiler_params=params(),
+    )(own, other, *before)
+
+
 def pack_kernel(
-    local_experts, far_ref, ids_ref, gates_ref, preact_ref, tokens_ref,
-    out_ref, activation_ref, scaled_ref, weighted,
+    local_experts, far_ref, ids_ref, gates_ref, preact_ref, tokens_ref, *refs
 ):
+    out_ref, activation_ref, scaled_ref, weighted = refs[-4:]
     blocks, height, features = out_ref.shape
     rows, wide = preact_ref.shape
     far_count = far_ref.shape[0]
@@ -84,8 +102,7 @@
     for block in range(blocks):
         side = lax.rem(near + block, NEAR)
         places = (
-            (side * far_count + far_place) * local_experts + local,
-            (far * NEAR + side) * local_experts + local,
+            (side * far_count + far) * local_experts + local,
             (far_place * NEAR + side) * local_experts + local,
         )
         out_ref[block, 0:rows, :] = tokens_ref[:, block * features : (block + 1) * features]
@@ -94,11 +111,11 @@
             out_ref[block, rows : rows + taken, at : at + wide] = weighted[start : start + taken, :]
         last = height - TILE
         out_ref[block, last:, :] = jnp.zeros((TILE, features), jnp.bfloat16)
-        for at, place in zip((DOWN, UP, GRADS), places):
+        for at, place in zip((DOWN, UP), places):
             out_ref[block, last + at : last + at + 2, 0:rows] = place.astype(jnp.bfloat16)
 
 
-def pack_tokens(far_places, ids, gates, preact, tokens, members, local_experts):
+def pack_tokens(far_places, ids, gates, preact, tokens, members, local_experts, before):
     rows, width = tokens.shape
     features = width // members
     each = members // 4
@@ -112,6 +129,7 @@
             pl.BlockSpec(memory_space=pltpu.SMEM),
             *whole,
             pl.BlockSpec((rows, each * features), lambda i: (0, i)),
+            *[pl.BlockSpec(memory_space=pl.ANY) for _ in before],
         ],
         out_specs=(pl.BlockSpec((each, height, features), lambda i: (i, 0, 0)), whole[2], whole[2]),
         out_shape=(
@@ -119,7 +137,7 @@
         ),
         scratch_shapes=[pltpu.VMEM(preact.shape, jnp.bfloat16)],
         compiler_params=params(),
-    )(far_places, ids, gates, preact, tokens)
+    )(far_places, ids, gates, preact, tokens, *before)
 
 
 def unpack_kernel(parts_ref, out_ref):
@@ -151,8 +169,8 @@
     return received_ref[:, 0:rows, :].reshape(sources * rows, features)
 
 
-def down_kernel(rows, wide, received_ref, *refs):
-    out_refs, (turned, numbers, spread) = refs[:-3], refs[-3:]
+def down_kernel(rows, wide, count, received_ref, *refs):
+    out_refs, (turned, numbers, spread) = refs[-3 - count : -3], refs[-3:]
     sources, _, features = received_ref.shape
     hidden, each = wide // 2, BLOCK // (wide // 2)
     taken = rows * wide // features
@@ -165,7 +183,7 @@
         )
         lanes = slice(source * rows, (source + 1) * rows)
         turned[:, lanes] = weighted.T
-        numbers[:, lanes] = places_of(received_ref, source, GRADS, rows).astype(jnp.float32)
+        numbers[:, lanes] = places_of(received_ref, source, UP, rows).astype(jnp.float32)
     number = 0
     for out_ref in out_refs:
         for start in range(0, out_ref.shape[0], BLOCK):
@@ -181,11 +199,15 @@
             ).astype(out_ref.dtype)
 
 
-def down_partial(received, rows, wide, total_rows, count):
+def down_partial(received, rows, wide, total_rows, count, before):
     sources, _, features = received.shape
     total = sources * rows
     return pl.pallas_call(
-        functools.partial(down_kernel, rows, wide),
+        functools.partial(down_kernel, rows, wide, count),
+        in_specs=[
+            pl.BlockSpec(memory_space=pltpu.VMEM),
+            *[pl.BlockSpec(memory_space=pl.ANY) for _ in before],
+        ],
         out_shape=[jax.ShapeDtypeStruct((total_rows // count, features), jnp.bfloat16)] * count,
         scratch_shapes=[
             pltpu.VMEM((wide, total), jnp.float32),
@@ -194,7 +216,7 @@
         ],
         compiler_params=params(),
         cost_estimate=cost(total_rows, total, features),
-    )(received)
+    )(received, *before)
 
 
 def lane_numbers(received_ref, which, rows, wide):
@@ -218,47 +240,46 @@
         at, start = at + terms, start + value.shape[0]
 
 
-def project_kernel(pieces, received_ref, *refs):
-    piece_refs, out_ref, full = refs[:-2], refs[-2], refs[-1]
-    pl.when(pl.program_id(0) == 0)(lambda: join(pieces, piece_refs, full))
+def project_kernel(received_ref, *refs):
+    weight_refs, out_ref = refs[:-1], refs[-1]
     sources, rows, wide = out_ref.shape
     low, first, second = lane_numbers(received_ref, DOWN, rows, wide)
     tokens = token_rows(received_ref, rows)
     sums = [jnp.zeros((sources * rows, wide), jnp.float32) for _ in range(2)]
-    for start in range(0, full.shape[0], BLOCK):
+    number = 0.0
+    for weight_ref, start in [
+        (ref, at) for ref in weight_refs for at in range(0, ref.shape[0], BLOCK)
+    ]:
         product = lax.dot_general(
             tokens,
-            full[start : start + BLOCK, :],
+            weight_ref[start : start + BLOCK, :],
             (((1,), (1,)), ((), ())),
             preferred_element_type=jnp.float32,
         )
         for at in range(0, BLOCK, wide):
             part = product[:, at : at + wide]
-            number = (start + at) // wide * 2.0
             sums[0] = jnp.where(first == number, part, sums[0])
             sums[1] = jnp.where(second == number, part, sums[1])
+            number += 2.0
     folded = [value + pltpu.roll(value, wide // 2, 1) for value in sums]
     value = jnp.where(low, folded[0], folded[1]).astype(out_ref.dtype)
     out_ref[...] = value.reshape(out_ref.shape)
 
 
-def project(received, pieces, rows, wide):
+def project(received, weights, rows, wide):
     sources, height, features = received.shape
-    flat = [term for terms in pieces for term in terms]
-    joined = sum(terms[0].shape[0] for terms in pieces)
-    return pl.pallas_call(
-        functools.partial(project_kernel, [len(terms) for terms in pieces]),
+    return pl.pallas_call(
+        project_kernel,
         grid=(sources // 2,),
         in_specs=[
             pl.BlockSpec((2, height, features), lambda i: (i, 0, 0)),
-            *[pl.BlockSpec(term.shape, lambda i: (0, 0)) for term in flat],
+            *[pl.BlockSpec(weight.shape, lambda i: (0, 0)) for weight in weights],
         ],
         out_specs=pl.BlockSpec((2, rows, wide), lambda i: (i, 0, 0)),
         out_shape=jax.ShapeDtypeStruct((sources, rows, wide), jnp.bfloat16),
-        scratch_shapes=[pltpu.VMEM((joined, features), jnp.bfloat16)],
-        compiler_params=params(),
-        cost_estimate=cost(sources * rows, features, joined),
-    )(received, *flat)
+        compiler_params=params(),
+        cost_estimate=cost(sources * rows, features, sum(w.shape[0] for w in weights)),
+    )(received, *weights)
 
 
 def hidden_kernel(parts_ref, activation_ref, scaled_ref, hidden_ref, gate_ref):
@@ -281,42 +302,48 @@
         hidden_ref[source] = hidden
 
 
-def input_kernel(received_ref, hidden_ref, weight_ref, out_ref, spread):
+def input_kernel(pieces, received_ref, hidden_ref, *refs):
+    piece_refs, out_ref, full, spread = refs[:-3], refs[-3], refs[-2], refs[-1]
+    pl.when(pl.program_id(0) == 0)(lambda: join(pieces, piece_refs, full))
     sources, rows, wide = hidden_ref.shape
     low, first, second = lane_numbers(received_ref, UP, rows, wide)
     values = hidden_ref[...].reshape(sources * rows, wide).astype(jnp.float32)
     swapped = pltpu.roll(values, wide // 2, 1)
     one = jnp.where(low, values, swapped)
     two = jnp.where(low, swapped, values)
-    for start in range(0, weight_ref.shape[0], wide):
+    for start in range(0, full.shape[0], wide):
         number = start // wide * 2.0
         spread[:, start : start + wide] = jnp.where(
             first == number, one, jnp.where(second == number, two, 0.0)
         ).astype(jnp.bfloat16)
     out_ref[...] = (
-        jnp.dot(spread[...], weight_ref[...], preferred_element_type=jnp.float32)
+        jnp.dot(spread[...], full[...], preferred_element_type=jnp.float32)
         .astype(out_ref.dtype)
         .reshape(out_ref.shape)
     )
 
 
-def input_rows(received, hidden_grad, weight):
+def input_rows(received, hidden_grad, pieces):
     sources, rows, wide = hidden_grad.shape
-    features = weight.shape[1]
-    return pl.pallas_call(
-        input_kernel,
+    flat = [term for terms in pieces for term in terms]
+    joined, features = sum(terms[0].shape[0] for terms in pieces), flat[0].shape[1]
+    return pl.pallas_call(
+        functools.partial(input_kernel, [len(terms) for terms in pieces]),
         grid=(sources // 2,),
         in_specs=[
             pl.BlockSpec((2, received.shape[1], features), lambda i: (i, 0, 0)),
             pl.BlockSpec((2, rows, wide), lambda i: (i, 0, 0)),
-            pl.BlockSpec(weight.shape, lambda i: (0, 0)),
+            *[pl.BlockSpec(term.shape, lambda i: (0, 0)) for term in flat],
         ],
         out_specs=pl.BlockSpec((2, rows, features), lambda i: (i, 0, 0)),
         out_shape=jax.ShapeDtypeStruct((sources, rows, features), jnp.bfloat16),
-        scratch_shapes=[pltpu.VMEM((2 * rows, weight.shape[0]), jnp.bfloat16)],
-        compiler_params=params(),
-        cost_estimate=cost(sources * rows, weight.shape[0], features),
-    )(received, hidden_grad, weight)
+        scratch_shapes=[
+            pltpu.VMEM((joined, features), jnp.bfloat16),
+            pltpu.VMEM((2 * rows, joined), jnp.bfloat16),
+        ],
+        compiler_params=params(),
+        cost_estimate=cost(sources * rows, joined, features),
+    )(received, hidden_grad, *flat)
 
 
 def exchange(value, axes):
@@ -353,6 +380,8 @@
     near = lax.axis_index("near")
     chained = far_count == len(CHAIN)
 
+    chained = far_count == len(CHAIN)
+
     def halves(weight):
         flat = weight.reshape(own_rows, width)
         own = lax.dynamic_slice_in_dim(flat, near * features, features, axis=1)
@@ -360,20 +389,36 @@
         return own, lax.ppermute(other, "near", SWAP)
 
     down_halves, up_halves = halves(down_weight), halves(up_weight)
+    down_full = [lax.all_gather(half, "far", tiled=True) for half in down_halves]
+    up_own = stack(*up_halves, down_full)
     if chained:
-        down_pieces = [terms for half in down_halves for terms in chain_gather(half)]
+        up_pieces = chain_gather(up_own)
         far_places = jnp.asarray(CHAIN, jnp.int32)[lax.axis_index("far")]
     else:
-        down_pieces = [(lax.all_gather(half, "far", tiled=True),) for half in down_halves]
+        up_pieces = [(lax.all_gather(up_own, "far", tiled=True),)]
         far_places = jnp.arange(far_count, dtype=jnp.int32)
-    up_full = lax.all_gather(jnp.concatenate(up_halves), "far", tiled=True)
     packed, activation, scaled = pack_tokens(
-        far_places, expert_ids.T, router_gates.T, saved_hidden, token_grads, members, local_experts
+        far_places, expert_ids.T, router_gates.T, saved_hidden, token_grads, members,
+        local_experts, (down_halves[1], up_halves[1]),
     )
     received = exchange(packed, GROUP)
 
+    projected = project(received, down_full, tok_count, wide)
+    parts = exchange(projected, GROUP)
+    hidden_grad, gate_grads = pl.pallas_call(
+        hidden_kernel,
+        out_shape=(
+            jax.ShapeDtypeStruct((members, tok_count, wide), jnp.bfloat16),
+            jax.ShapeDtypeStruct((2, tok_count), jnp.bfloat16),
+        ),
+        compiler_params=params(),
+    )(parts, activation, scaled)
+    hidden_grad = exchange(hidden_grad, GROUP)
+    input_grads = unpack_tokens(exchange(input_rows(received, hidden_grad, up_pieces), GROUP))
+
     partial_value = down_partial(
-        received, tok_count, wide, own_rows * NEAR * far_count, far_count if chained else 1
+        received, tok_count, wide, own_rows * NEAR * far_count, far_count if chained else 1,
+        (projected,),
     )
     if chained:
         sums = chain_scatter(*partial_value)
@@ -383,18 +428,6 @@
     down_grads = jnp.concatenate(
         [jnp.where(near == 0, kept, passed), jnp.where(near == 0, passed, kept)], axis=1
     ).reshape(down_weight.shape)
-
-    parts = exchange(project(received, down_pieces, tok_count, wide), GROUP)
-    hidden_grad, gate_grads = pl.pallas_call(
-        hidden_kernel,
-        out_shape=(
-            jax.ShapeDtypeStruct((members, tok_count, wide), jnp.bfloat16),
-            jax.ShapeDtypeStruct((2, tok_count), jnp.bfloat16),
-        ),
-        compiler_params=params(),
-    )(parts, activation, scaled)
-    hidden_grad = exchange(hidden_grad, GROUP)
-    input_grads = unpack_tokens(exchange(input_rows(received, hidden_grad, up_full), GROUP))
     return (input_grads, gate_grads.T, down_grads)
 
 

time: 185 us -> 191 us (1.032)
  waiting for transfers between devices: 72.3 us -> 92.6 us
  starting transfers between devices: 58.1 us -> 44 us
    all_gather x1 -> x2, waiting for transfers between devices: 0.01 us -> 38.3 us  [body(): lax.all_gather(half, 'far', tiled=True)]
    ppermute x2, waiting for transfers between devices: 31.3 us -> 9.45 us  [halves(): return (own, lax.ppermute(other, 'near', SWAP))]
    ppermute x1, starting transfers between devices: 16.3 us -> 5.77 us  [chain_scatter(): third = add(third, lax.ppermute(third, 'far', INWARD))]
    ppermute x2 -> x1, waiting for transfers between devices: 0.7 us -> 6.6 us  [chain_gather(): third = lax.ppermute(across_far, 'far', OUTWARD)]
    ppermute x1, starting transfers between devices: 2.22 us -> 6.89 us  [chain_scatter(): second = add(second, lax.ppermute(second, 'far', INWARD))]
    all_to_all x4, waiting for transfers between devices: 6.1 us -> 2.39 us  [exchange(): return lax.all_to_all(value, axes, split_axis=0, concat_axis=0, tiled=True)]
    dynamic_slice x1 -> x2, local copies, waits for them, and re-layouts: 1.07 us -> 3.68 us  [halves(): own = lax.dynamic_slice_in_dim(flat, near * features, features, axis=1)]
    ppermute x2, starting transfers between devices: 4.97 us -> 3.06 us  [halves(): return (own, lax.ppermute(other, 'near', SWAP))]
  transfers between devices with their start and end apart: 23 -> 19, of which waited for: 7 -> 9; matrix products, arithmetic and copies ran while one was open for 5% -> 4% of each run, Pallas kernels for 8% -> 8%
where the time goes in v6:
time: 191 us; the launch traced here: 190 us
  waiting for transfers between devices  92.6 us (48%)
  starting transfers between devices  44 us (23%)
  Pallas kernels  17 us (9%)
  local copies, waits for them, and re-layouts  16.2 us (8%)
  between operations  14.3 us (7%)
  other arithmetic  5.85 us (3%)
    all_gather x2, waiting for transfers between devices, body(): lax.all_gather(half, 'far', tiled=True)  38.3 us
    all_to_all x4, starting transfers between devices, exchange(): return lax.all_to_all(value, axes, split_axis=0, concat_axis=0, tiled=True)  15.7 us
    ppermute x1, waiting for transfers between devices, chain_scatter(): return add(own, across, lax.ppermute(beside, 'far', SIDES))  12.8 us
    unnamed x42, local copies, waits for them, and re-layouts  11.8 us
    ppermute x1, waiting for transfers between devices, body(): lax.ppermute(sums[own_rows:], 'near', SWAP)  11.6 us
    ppermute x1, waiting for transfers between devices, chain_gather(): beside = lax.ppermute(mine, 'far', SIDES)  10.7 us
    ppermute x2, waiting for transfers between devices, halves(): return (own, lax.ppermute(other, 'near', SWAP))  9.45 us
    ppermute x1, starting transfers between devices, chain_scatter(): second = add(second, lax.ppermute(second, 'far', INWARD))  6.89 us
  transfers between devices with their start and end apart: 19, of which 9 were waited for; matrix products, arithmetic and copies ran while one was open for 4% of the time, Pallas kernels for 8%

profile of v6, /device:TPU:0, one launch (start us, length us, event | category | flops | bytes accessed | tf_op | source)
XLA Modules:
  0.0 189.9 jit_solution(7786761764599473646)
XLA Ops:
  7.2 0.0 all-gather.3.cloned.1.call-start
  7.3 1.9 %constant_dynamic-slice_fusion.1 = (bf16[128,1024]{1,0:T(8,128)(2,1)}, bf16[128,1024]{1,0:T(8,128)(2,1)S(1)}) fusion(bf16[128,2048]{1,0:T(8,128)(2,1)} %bitcast.10, s32[]{:T(128)S(6)} %select_n.25, s32[]{:T(128)S(6)} %select_n.24), kind=kLoop, calls=%fused_computation.8 | loop fusion | bytes 1048584 | tf_op jit(solution)/shard_map/dynamic_slice | solution.py:387
  9.2 0.0 all-gather.3.cloned.1.call-update
  9.2 3.0 %collective-permute-start = (bf16[128,1024]{1,0:T(8,128)(2,1)S(1)}, bf16[128,1024]{1,0:T(8,128)(2,1)S(1)}, u32[]{:S(2)}, u32[]{:S(2)}) collective-permute-start(bf16[128,1024]{1,0:T(8,128)(2,1)S(1)} %get-tuple-element.26), channel_id=1, source_target_pairs={{0,4},{4,0},{1,5},{5,1},{2,6},{6,2},{3,7},{7,3},{8,12},{12,8},{9,1... | collective-permute-start | bytes 786440 | tf_op jit(solution)/shard_map/ppermute | solution.py:389
  12.2 1.8 constant_dynamic-slice_fusion
  14.0 0.0 collective-permute-start.1
  14.0 0.7 fusion.far_ref
  14.7 4.7 %collective-permute-done.refs_0_ = bf16[128,1024]{1,0:T(8,128)(2,1)S(1)} collective-permute-done((bf16[128,1024]{1,0:T(8,128)(2,1)S(1)}, bf16[128,1024]{1,0:T(8,128)(2,1)S(1)}, u32[]{:S(2)}, u32[]{:S(2)}) %collective-permute-start) | collective-permute-done | bytes 262176 | tf_op jit(solution)/shard_map/ppermute | solution.py:389
  19.4 4.8 %collective-permute-done.1.refs_1_.other_ref = bf16[128,1024]{1,0:T(8,128)(2,1)S(1)} collective-permute-done((bf16[128,1024]{1,0:T(8,128)(2,1)}, bf16[128,1024]{1,0:T(8,128)(2,1)S(1)}, u32[]{:S(2)}, u32[]{:S(2)}) %collective-permute-start.1) | collective-permute-done | bytes 262176 | tf_op jit(solution)/shard_map/ppermute | solution.py:389
  24.2 1.2 shard_map.94
  25.4 1.5 copy-done.1
  26.8 3.9 %all-to-all-start = ((bf16[8,160,1024]{2,1,0:T(8,128)(2,1)}), bf16[8,160,1024]{2,1,0:T(8,128)(2,1)S(1)}, u32[]{:S(2)}, u32[]{:S(2)}) async-start(bf16[8,160,1024]{2,1,0:T(8,128)(2,1)} %copy-done.1), calls=%async_computation | async-start | bytes 5242880 | tf_op jit(solution)/shard_map/all_to_all | solution.py:350
  30.8 0.0 all-gather.5.cloned.1.call-start
  30.8 0.7 all-gather.5.cloned.1.call-update
  31.5 9.3 %all-gather.3.cloned.1.call-done.refs_0_ = bf16[512,1024]{1,0:T(8,128)(2,1)} async-done(((bf16[128,1024]{1,0:T(8,128)(2,1)}), bf16[512,1024]{1,0:T(8,128)(2,1)}) %all-gather.3.cloned.1.call-update) | async-done | bytes 1048592 | tf_op jit(solution)/shard_map/all_gather | solution.py:392
  40.8 29.0 %all-gather.5.cloned.1.call-done.refs_1_ = bf16[512,1024]{1,0:T(8,128)(2,1)} async-done(((bf16[128,1024]{1,0:T(8,128)(2,1)}), bf16[512,1024]{1,0:T(8,128)(2,1)}) %all-gather.5.cloned.1.call-update) | async-done | bytes 1048592 | tf_op jit(solution)/shard_map/all_gather | solution.py:392
  69.9 1.2 copy-done.3
  71.1 1.2 copy-done.5
  72.3 0.9 copy-done.8
  73.3 1.5 collective-permute-start.2
  74.8 1.5 collective-permute-start.3
  76.3 10.7 %collective-permute-done.2.refs_1_ = bf16[256,1024]{1,0:T(8,128)(2,1)} collective-permute-done((bf16[256,1024]{1,0:T(8,128)(2,1)S(1)}, bf16[256,1024]{1,0:T(8,128)(2,1)}, u32[]{:S(2)}, u32[]{:S(2)}) %collective-permute-start.2) | collective-permute-done | bytes 524320 | tf_op jit(solution)/shard_map/ppermute | solution.py:354
  87.0 1.4 collective-permute-start.5
  88.5 0.0 all-to-all-done.received_ref
  88.5 1.2 copy-done.4
  89.7 1.2 copy-done.6
  90.9 3.8 %shard_map.95.refs_0_ = bf16[8,128,128]{2,1,0:T(8,128)(2,1)S(1)} custom-call(bf16[8,160,1024]{2,1,0:T(8,128)(2,1)S(1)} %all-to-all-done.received_ref, bf16[512,1024]{1,0:T(8,128)(2,1)S(1)} %copy-done.4, bf16[512,1024]{1,0:T(8,128)(2,1)S(1)} %copy-done.6), custom_call_target="tpu_custom_call" | custom-call | flops 2147483648 | bytes 6291456 | tf_op jit(solution)/shard_map/pallas_call | solution.py:271
  94.7 0.0 copy-start.16
  94.7 3.2 %shard_map.100 = (bf16[256,1024]{1,0:T(8,128)(2,1)S(1)}, bf16[256,1024]{1,0:T(8,128)(2,1)S(1)}, bf16[256,1024]{1,0:T(8,128)(2,1)S(1)}, bf16[256,1024]{1,0:T(8,128)(2,1)}) custom-call(bf16[8,160,1024]{2,1,0:T(8,128)(2,1)S(1)} %all-to-all-done.received_ref, bf16[8,128,128]{2,1,0:T(8,128)(2,1)S(1)} %shard_map.95.refs_0_), custom_call_target="tpu_custom_call" | custom-call | flops 2147483648 | bytes 6291456 | tf_op jit(solution)/shard_map/pallas_call | solution.py:205
  97.9 0.8 copy-done.10
  98.7 0.8 copy-done.12
  99.5 0.8 copy-done.14
  100.3 5.8 %collective-permute-start.9 = (bf16[256,1024]{1,0:T(8,128)(2,1)}, bf16[256,1024]{1,0:T(8,128)(2,1)}, u32[]{:S(2)}, u32[]{:S(2)}) collective-permute-start(bf16[256,1024]{1,0:T(8,128)(2,1)} %get-tuple-element.20), channel_id=1, source_target_pairs={{0,8},{24,16},{1,9},{25,17},{2,10},{26,18},{3,11},{27,19},{4,12},{... | collective-permute-start | bytes 1572872 | tf_op jit(solution)/shard_map/ppermute | solution.py:367
  106.1 3.7 %all-to-all-start.1 = ((bf16[8,128,128]{2,1,0:T(8,128)(2,1)}), bf16[8,128,128]{2,1,0:T(8,128)(2,1)S(1)}, u32[]{:S(2)}, u32[]{:S(2)}) async-start(bf16[8,128,128]{2,1,0:T(8,128)(2,1)} %copy-done.16), calls=%async_computation.1 | async-start | bytes 524288 | tf_op jit(solution)/shard_map/all_to_all | solution.py:350
  109.7 0.0 collective-permute-done.3.refs_2_
  109.7 1.3 collective-permute-start.4
  111.0 0.0 collective-permute-done.5.refs_4_
  111.1 1.3 collective-permute-start.6
  112.4 6.9 %collective-permute-start.7 = (bf16[256,1024]{1,0:T(8,128)(2,1)}, bf16[256,1024]{1,0:T(8,128)(2,1)}, u32[]{:S(2)}, u32[]{:S(2)}) collective-permute-start(bf16[256,1024]{1,0:T(8,128)(2,1)} %copy-done.12), channel_id=1, source_target_pairs={{0,8},{24,16},{1,9},{25,17},{2,10},{26,18},{3,11},{27,19},{4,12},{... | collective-permute-start | bytes 1572872 | tf_op jit(solution)/shard_map/ppermute | solution.py:368
  119.2 0.0 all-to-all-done.1.parts_ref
  119.3 0.7 shard_map.96
  120.0 0.7 copy-done.17
  120.7 4.2 %all-to-all-start.2 = ((bf16[8,128,128]{2,1,0:T(8,128)(2,1)}), bf16[8,128,128]{2,1,0:T(8,128)(2,1)S(1)}, u32[]{:S(2)}, u32[]{:S(2)}) async-start(bf16[8,128,128]{2,1,0:T(8,128)(2,1)} %copy-done.17), calls=%async_computation.2 | async-start | bytes 524288 | tf_op jit(solution)/shard_map/all_to_all | solution.py:350
  124.9 0.0 collective-permute-done.9
  124.9 2.2 %add_convert_fusion.2 = bf16[256,1024]{1,0:T(8,128)(2,1)} fusion(bf16[256,1024]{1,0:T(8,128)(2,1)} %collective-permute-done.9, bf16[256,1024]{1,0:T(8,128)(2,1)} %get-tuple-element.20), kind=kLoop, calls=%fused_computation.2 | loop fusion | flops 1048576 | bytes 1572864 | tf_op jit(solution)/shard_map/convert_element_type | solution.py:363
  127.1 1.4 collective-permute-start.10
  128.5 2.4 %all-to-all-done.2.hidden_ref = bf16[8,128,128]{2,1,0:T(8,128)(2,1)S(1)} async-done(((bf16[8,128,128]{2,1,0:T(8,128)(2,1)}), bf16[8,128,128]{2,1,0:T(8,128)(2,1)S(1)}, u32[]{:S(2)}, u32[]{:S(2)}) %all-to-all-start.2) | async-done | bytes 262176 | tf_op jit(solution)/shard_map/all_to_all | solution.py:350
  130.9 6.6 %collective-permute-done.6.refs_5_ = bf16[256,1024]{1,0:T(8,128)(2,1)} collective-permute-done((bf16[256,1024]{1,0:T(8,128)(2,1)}, bf16[256,1024]{1,0:T(8,128)(2,1)}, u32[]{:S(2)}, u32[]{:S(2)}) %collective-permute-start.6) | collective-permute-done | bytes 524320 | tf_op jit(solution)/shard_map/ppermute | solution.py:358
  137.5 6.2 %shard_map.98 = bf16[8,128,1024]{2,1,0:T(8,128)(2,1)S(1)} custom-call(bf16[8,160,1024]{2,1,0:T(8,128)(2,1)S(1)} %all-to-all-done.received_ref, bf16[8,128,128]{2,1,0:T(8,128)(2,1)S(1)} %all-to-all-done.2.hidden_ref, bf16[256,1024]{1,0:T(8,128)(2,1)S(1)} %shard_map.97.refs_0_, bf16[256,1024]{1,0:T(8,128)(2,1)} %collective-permute-done.2.refs_1_, ...), custom_call_target="tpu_custom_call" | custom-call | flops 2147483648 | bytes 6291456 | tf_op jit(solution)/shard_map/pallas_call | solution.py:330
  143.7 0.0 copy-start
  143.7 1.3 copy-done
  145.1 4.0 %all-to-all-start.3 = ((bf16[8,128,1024]{2,1,0:T(8,128)(2,1)}), bf16[8,128,1024]{2,1,0:T(8,128)(2,1)S(1)}, u32[]{:S(2)}, u32[]{:S(2)}) async-start(bf16[8,128,1024]{2,1,0:T(8,128)(2,1)} %copy-done), calls=%async_computation.3 | async-start | bytes 4194304 | tf_op jit(solution)/shard_map/all_to_all | solution.py:350
  149.0 0.0 collective-permute-done.7
  149.0 1.3 add_convert_fusion.3
  150.3 0.7 collective-permute-start.8
  151.1 1.2 add_convert_fusion.1
  152.3 1.6 collective-permute-start.11
  153.9 12.8 %collective-permute-done.11 = bf16[256,1024]{1,0:T(8,128)(2,1)S(1)} collective-permute-done((bf16[256,1024]{1,0:T(8,128)(2,1)S(1)}, bf16[256,1024]{1,0:T(8,128)(2,1)S(1)}, u32[]{:S(2)}, u32[]{:S(2)}) %collective-permute-start.11) | collective-permute-done | bytes 524320 | tf_op jit(solution)/shard_map/ppermute | solution.py:371
  166.7 0.3 add_convert_fusion
  167.0 1.7 collective-permute-start.12
  168.7 11.6 %collective-permute-done.12 = bf16[128,1024]{1,0:T(8,128)(2,1)S(1)} collective-permute-done((bf16[128,1024]{1,0:T(8,128)(2,1)S(1)}, bf16[128,1024]{1,0:T(8,128)(2,1)S(1)}, u32[]{:S(2)}, u32[]{:S(2)}) %collective-permute-start.12) | collective-permute-done | bytes 262176 | tf_op jit(solution)/shard_map/ppermute | solution.py:427
  180.4 0.8 pad_maximum_fusion
  181.2 0.0 all-to-all-done.3.parts_ref
  181.2 1.8 shard_map.99
  (35 shorter events, 0.2 us)
Async XLA Ops:
  7.2 17.0 %copy-start.19 = (s32[128,2]{0,1:T(2,128)S(1)}, s32[128,2]{0,1:T(2,128)}, u32[]{:S(2)}) copy-start(s32[128,2]{0,1:T(2,128)} %param.9) | copy-start | bytes 3076
  7.2 17.0 %copy-start.20 = (bf16[128,2]{0,1:T(2,128)(2,1)S(1)}, bf16[128,2]{0,1:T(2,128)(2,1)}, u32[]{:S(2)}) copy-start(bf16[128,2]{0,1:T(2,128)(2,1)} %param.8) | copy-start | bytes 1540
  7.2 17.0 %copy-start.18 = (bf16[128,128]{1,0:T(8,128)(2,1)S(1)}, bf16[128,128]{1,0:T(8,128)(2,1)}, u32[]{:S(2)}) copy-start(bf16[128,128]{1,0:T(8,128)(2,1)} %preact_ref.1) | copy-start | bytes 98308
  7.2 17.0 %copy-start.2 = (bf16[128,8192]{1,0:T(8,128)(2,1)S(1)}, bf16[128,8192]{1,0:T(8,128)(2,1)}, u32[]{:S(2)}) copy-start(bf16[128,8192]{1,0:T(8,128)(2,1)} %tokens_ref.1) | copy-start | bytes 6291460
  7.2 33.6 %all-gather.3.cloned.1.call-start = ((), (), s32[]{:S(2)}) async-start(), calls=%async_computation.4 | async-start | bytes 1310720 | tf_op jit(solution)/shard_map/all_gather | solution.py:392
  9.2 10.2 %collective-permute-start = (bf16[128,1024]{1,0:T(8,128)(2,1)S(1)}, bf16[128,1024]{1,0:T(8,128)(2,1)S(1)}, u32[]{:S(2)}, u32[]{:S(2)}) collective-permute-start(bf16[128,1024]{1,0:T(8,128)(2,1)S(1)} %get-tuple-element.26), channel_id=1, source_target_pairs={{0,4},{4,0},{1,5},{5,1},{2,6},{6,2},{3,7},{7,3},{8,12},{12,8},{9,1... | collective-permute-start | bytes 786440 | tf_op jit(solution)/shard_map/ppermute | solution.py:389
  14.0 10.2 %collective-permute-start.1 = (bf16[128,1024]{1,0:T(8,128)(2,1)}, bf16[128,1024]{1,0:T(8,128)(2,1)S(1)}, u32[]{:S(2)}, u32[]{:S(2)}) collective-permute-start(bf16[128,1024]{1,0:T(8,128)(2,1)} %get-tuple-element.24), channel_id=1, source_target_pairs={{0,4},{4,0},{1,5},{5,1},{2,6},{6,2},{3,7},{7,3},{8,12},{12,8},{9,1... | collective-permute-start | bytes 786440 | tf_op jit(solution)/shard_map/ppermute | solution.py:389
  19.4 7.5 %copy-start.9 = (bf16[128,1024]{1,0:T(8,128)(2,1)}, bf16[128,1024]{1,0:T(8,128)(2,1)S(1)}, u32[]{:S(2)}) copy-start(bf16[128,1024]{1,0:T(8,128)(2,1)S(1)} %collective-permute-done.refs_0_) | copy-start | bytes 786436
  24.2 2.7 %copy-start.7 = (bf16[128,1024]{1,0:T(8,128)(2,1)}, bf16[128,1024]{1,0:T(8,128)(2,1)S(1)}, u32[]{:S(2)}) copy-start(bf16[128,1024]{1,0:T(8,128)(2,1)S(1)} %collective-permute-done.1.refs_1_.other_ref) | copy-start | bytes 786436
  25.3 1.5 copy-start.1
  26.8 61.6 %all-to-all-start = ((bf16[8,160,1024]{2,1,0:T(8,128)(2,1)}), bf16[8,160,1024]{2,1,0:T(8,128)(2,1)S(1)}, u32[]{:S(2)}, u32[]{:S(2)}) async-start(bf16[8,160,1024]{2,1,0:T(8,128)(2,1)} %copy-done.1), calls=%async_computation | async-start | bytes 5242880 | tf_op jit(solution)/shard_map/all_to_all | solution.py:350
  30.8 39.1 %all-gather.5.cloned.1.call-start = ((), (), s32[]{:S(2)}) async-start(), calls=%async_computation.5 | async-start | bytes 1310720 | tf_op jit(solution)/shard_map/all_gather | solution.py:392
  69.9 1.2 copy-start.3
  71.1 1.2 copy-start.5
  72.3 0.9 copy-start.8
  73.3 13.7 %collective-permute-start.2 = (bf16[256,1024]{1,0:T(8,128)(2,1)S(1)}, bf16[256,1024]{1,0:T(8,128)(2,1)}, u32[]{:S(2)}, u32[]{:S(2)}) collective-permute-start(bf16[256,1024]{1,0:T(8,128)(2,1)S(1)} %shard_map.97.refs_0_), channel_id=1, source_target_pairs={{0,8},{8,0},{16,24},{24,16},{1,9},{9,1},{17,25},{25,17},{2,10},{10... | collective-permute-start | bytes 1572872 | tf_op jit(solution)/shard_map/ppermute | solution.py:354
  74.8 34.9 %collective-permute-start.3 = (bf16[256,1024]{1,0:T(8,128)(2,1)S(1)}, bf16[256,1024]{1,0:T(8,128)(2,1)}, u32[]{:S(2)}, u32[]{:S(2)}) collective-permute-start(bf16[256,1024]{1,0:T(8,128)(2,1)S(1)} %shard_map.97.refs_0_), channel_id=1, source_target_pairs={{8,16},{16,8},{9,17},{17,9},{10,18},{18,10},{11,19},{19,11},{12,20... | collective-permute-start | bytes 1572872 | tf_op jit(solution)/shard_map/ppermute | solution.py:355
  87.0 24.0 %collective-permute-start.5 = (bf16[256,1024]{1,0:T(8,128)(2,1)}, bf16[256,1024]{1,0:T(8,128)(2,1)}, u32[]{:S(2)}, u32[]{:S(2)}) collective-permute-start(bf16[256,1024]{1,0:T(8,128)(2,1)} %collective-permute-done.2.refs_1_), channel_id=1, source_target_pairs={{8,16},{16,8},{9,17},{17,9},{10,18},{18,10},{11,19},{19,11},{12,20... | collective-permute-start | bytes 1572872 | tf_op jit(solution)/shard_map/ppermute | solution.py:356
  88.5 1.2 copy-start.4
  89.7 1.2 copy-start.6
  94.7 3.2 %copy-start.16 = (bf16[8,128,128]{2,1,0:T(8,128)(2,1)}, bf16[8,128,128]{2,1,0:T(8,128)(2,1)S(1)}, u32[]{:S(2)}) copy-start(bf16[8,128,128]{2,1,0:T(8,128)(2,1)S(1)} %shard_map.95.refs_0_) | copy-start | bytes 786436
  97.9 0.8 copy-start.10
  98.7 0.8 copy-start.12
  99.5 0.8 copy-start.14
  100.3 24.6 %collective-permute-start.9 = (bf16[256,1024]{1,0:T(8,128)(2,1)}, bf16[256,1024]{1,0:T(8,128)(2,1)}, u32[]{:S(2)}, u32[]{:S(2)}) collective-permute-start(bf16[256,1024]{1,0:T(8,128)(2,1)} %get-tuple-element.20), channel_id=1, source_target_pairs={{0,8},{24,16},{1,9},{25,17},{2,10},{26,18},{3,11},{27,19},{4,12},{... | collective-permute-start | bytes 1572872 | tf_op jit(solution)/shard_map/ppermute | solution.py:367
  106.1 13.2 %all-to-all-start.1 = ((bf16[8,128,128]{2,1,0:T(8,128)(2,1)}), bf16[8,128,128]{2,1,0:T(8,128)(2,1)S(1)}, u32[]{:S(2)}, u32[]{:S(2)}) async-start(bf16[8,128,128]{2,1,0:T(8,128)(2,1)} %copy-done.16), calls=%async_computation.1 | async-start | bytes 524288 | tf_op jit(solution)/shard_map/all_to_all | solution.py:350
  109.7 18.8 %collective-permute-start.4 = (bf16[256,1024]{1,0:T(8,128)(2,1)}, bf16[256,1024]{1,0:T(8,128)(2,1)}, u32[]{:S(2)}, u32[]{:S(2)}) collective-permute-start(bf16[256,1024]{1,0:T(8,128)(2,1)} %collective-permute-done.3.refs_2_), channel_id=1, source_target_pairs={{8,0},{16,24},{9,1},{17,25},{10,2},{18,26},{11,3},{19,27},{12,4},{... | collective-permute-start | bytes 1572872 | tf_op jit(solution)/shard_map/ppermute | solution.py:357
  111.1 26.5 %collective-permute-start.6 = (bf16[256,1024]{1,0:T(8,128)(2,1)}, bf16[256,1024]{1,0:T(8,128)(2,1)}, u32[]{:S(2)}, u32[]{:S(2)}) collective-permute-start(bf16[256,1024]{1,0:T(8,128)(2,1)} %collective-permute-done.5.refs_4_), channel_id=1, source_target_pairs={{8,0},{16,24},{9,1},{17,25},{10,2},{18,26},{11,3},{19,27},{12,4},{... | collective-permute-start | bytes 1572872 | tf_op jit(solution)/shard_map/ppermute | solution.py:358
  112.4 36.7 %collective-permute-start.7 = (bf16[256,1024]{1,0:T(8,128)(2,1)}, bf16[256,1024]{1,0:T(8,128)(2,1)}, u32[]{:S(2)}, u32[]{:S(2)}) collective-permute-start(bf16[256,1024]{1,0:T(8,128)(2,1)} %copy-done.12), channel_id=1, source_target_pairs={{0,8},{24,16},{1,9},{25,17},{2,10},{26,18},{3,11},{27,19},{4,12},{... | collective-permute-start | bytes 1572872 | tf_op jit(solution)/shard_map/ppermute | solution.py:368
  120.0 0.7 copy-start.17
  120.7 10.2 %all-to-all-start.2 = ((bf16[8,128,128]{2,1,0:T(8,128)(2,1)}), bf16[8,128,128]{2,1,0:T(8,128)(2,1)S(1)}, u32[]{:S(2)}, u32[]{:S(2)}) async-start(bf16[8,128,128]{2,1,0:T(8,128)(2,1)} %copy-done.17), calls=%async_computation.2 | async-start | bytes 524288 | tf_op jit(solution)/shard_map/all_to_all | solution.py:350
  127.1 24.0 %collective-permute-start.10 = (bf16[256,1024]{1,0:T(8,128)(2,1)}, bf16[256,1024]{1,0:T(8,128)(2,1)}, u32[]{:S(2)}, u32[]{:S(2)}) collective-permute-start(bf16[256,1024]{1,0:T(8,128)(2,1)} %add_convert_fusion.2), channel_id=1, source_target_pairs={{8,16},{16,8},{9,17},{17,9},{10,18},{18,10},{11,19},{19,11},{12,20... | collective-permute-start | bytes 1572872 | tf_op jit(solution)/shard_map/ppermute | solution.py:369
  143.7 1.3 copy-start
  145.1 4.0 %copy-start.13 = (bf16[256,1024]{1,0:T(8,128)(2,1)S(1)}, bf16[256,1024]{1,0:T(8,128)(2,1)}, u32[]{:S(2)}) copy-start(bf16[256,1024]{1,0:T(8,128)(2,1)} %copy-done.12) | copy-start | bytes 1572868
  145.1 6.0 %copy-start.11 = (bf16[256,1024]{1,0:T(8,128)(2,1)S(1)}, bf16[256,1024]{1,0:T(8,128)(2,1)}, u32[]{:S(2)}) copy-start(bf16[256,1024]{1,0:T(8,128)(2,1)} %copy-done.10) | copy-start | bytes 1572868
  145.1 36.2 %all-to-all-start.3 = ((bf16[8,128,1024]{2,1,0:T(8,128)(2,1)}), bf16[8,128,1024]{2,1,0:T(8,128)(2,1)S(1)}, u32[]{:S(2)}, u32[]{:S(2)}) async-start(bf16[8,128,1024]{2,1,0:T(8,128)(2,1)} %copy-done), calls=%async_computation.3 | async-start | bytes 4194304 | tf_op jit(solution)/shard_map/all_to_all | solution.py:350
  149.0 17.7 %copy-start.15 = (bf16[256,1024]{1,0:T(8,128)(2,1)S(1)}, bf16[256,1024]{1,0:T(8,128)(2,1)}, u32[]{:S(2)}) copy-start(bf16[256,1024]{1,0:T(8,128)(2,1)} %copy-done.14) | copy-start | bytes 1572868
  150.3 3.6 %collective-permute-start.8 = (bf16[256,1024]{1,0:T(8,128)(2,1)S(1)}, bf16[256,1024]{1,0:T(8,128)(2,1)S(1)}, u32[]{:S(2)}, u32[]{:S(2)}) collective-permute-start(bf16[256,1024]{1,0:T(8,128)(2,1)S(1)} %add_convert_fusion.3), channel_id=1, source_target_pairs={{8,16},{16,8},{9,17},{17,9},{10,18},{18,10},{11,19},{19,11},{12,20... | collective-permute-start | bytes 1572872 | tf_op jit(solution)/shard_map/ppermute | solution.py:370
  152.3 14.4 %collective-permute-start.11 = (bf16[256,1024]{1,0:T(8,128)(2,1)S(1)}, bf16[256,1024]{1,0:T(8,128)(2,1)S(1)}, u32[]{:S(2)}, u32[]{:S(2)}) collective-permute-start(bf16[256,1024]{1,0:T(8,128)(2,1)S(1)} %add_convert_fusion.1), channel_id=1, source_target_pairs={{0,8},{8,0},{16,24},{24,16},{1,9},{9,1},{17,25},{25,17},{2,10},{10... | collective-permute-start | bytes 1572872 | tf_op jit(solution)/shard_map/ppermute | solution.py:371
  167.0 13.3 %collective-permute-start.12 = (bf16[128,1024]{1,0:T(8,128)(2,1)S(1)}, bf16[128,1024]{1,0:T(8,128)(2,1)S(1)}, u32[]{:S(2)}, u32[]{:S(2)}) collective-permute-start(bf16[128,1024]{1,0:T(8,128)(2,1)S(1)} %slice.9), channel_id=1, source_target_pairs={{0,4},{4,0},{1,5},{5,1},{2,6},{6,2},{3,7},{7,3},{8,12},{12,8},{9,1... | collective-permute-start | bytes 786440 | tf_op jit(solution)/shard_map/ppermute | solution.py:427
Sparse Core Ops, SparseCore 0:
  10.2 30.6 all-gather.2
  42.4 27.4 all-gather.4

commit v7 on v6

--- a/solution.py
+++ b/solution.py
@@ -19,7 +19,6 @@
 OUTWARD = ((1, 0), (2, 3))
 INWARD = ((0, 1), (3, 2))
 SWAP = ((0, 1), (1, 0))
-DOWN, UP = 0, 2
 
 
 def gelu_parts(preact):
@@ -28,7 +27,7 @@
     return (preact * cumulative, cumulative + preact * density)
 
 
-def params(grant=40):
+def params(grant=20):
     return pltpu.CompilerParams(vmem_limit_bytes=grant * MIB)
 
 
@@ -75,6 +74,39 @@
     )(own, other, *before)
 
 
+def pass_on(value, before):
+    anywhere = pl.BlockSpec(memory_space=pl.ANY)
+    return pl.pallas_call(
+        lambda *refs: None,
+        in_specs=[anywhere] * (1 + len(before)),
+        out_specs=anywhere,
+        out_shape=jax.ShapeDtypeStruct(value.shape, value.dtype),
+        input_output_aliases={0: 0},
+        compiler_params=params(),
+    )(value, *before)
+
+
+def add_kernel(count, *refs):
+    terms, out_refs = refs[: 2 * count], refs[-count:]
+    for at in range(count):
+        left, right = terms[2 * at][...], terms[2 * at + 1][...]
+        total = left.astype(jnp.float32) + right.astype(jnp.float32)
+        out_refs[at][...] = total.astype(out_refs[at].dtype)
+
+
+def add_pairs(pairs, before):
+    flat = [term for pair in pairs for term in pair]
+    return pl.pallas_call(
+        functools.partial(add_kernel, len(pairs)),
+        in_specs=[
+            *[pl.BlockSpec(memory_space=pltpu.VMEM) for _ in flat],
+            *[pl.BlockSpec(memory_space=pl.ANY) for _ in before],
+        ],
+        out_shape=[jax.ShapeDtypeStruct(pair[0].shape, pair[0].dtype) for pair in pairs],
+        compiler_params=params(),
+    )(*flat, *before)
+
+
 def pack_kernel(
     local_experts, far_ref, ids_ref, gates_ref, preact_ref, tokens_ref, *refs
 ):
@@ -101,18 +133,14 @@
         far_place = jnp.where(far == at, far_ref[at], far_place)
     for block in range(blocks):
         side = lax.rem(near + block, NEAR)
-        places = (
-            (side * far_count + far) * local_experts + local,
-            (far_place * NEAR + side) * local_experts + local,
-        )
+        place = (far_place * NEAR + side) * local_experts + local
         out_ref[block, 0:rows, :] = tokens_ref[:, block * features : (block + 1) * features]
         for at in range(0, features, wide):
             start = at // wide * taken
             out_ref[block, rows : rows + taken, at : at + wide] = weighted[start : start + taken, :]
         last = height - TILE
         out_ref[block, last:, :] = jnp.zeros((TILE, features), jnp.bfloat16)
-        for at, place in zip((DOWN, UP), places):
-            out_ref[block, last + at : last + at + 2, 0:rows] = place.astype(jnp.bfloat16)
+        out_ref[block, last : last + 2, 0:rows] = place.astype(jnp.bfloat16)
 
 
 def pack_tokens(far_places, ids, gates, preact, tokens, members, local_experts, before):
@@ -159,8 +187,8 @@
     )(parts)
 
 
-def places_of(received_ref, source, which, rows):
-    at = received_ref.shape[1] - TILE + which
+def places_of(received_ref, source, rows):
+    at = received_ref.shape[1] - TILE
     return received_ref[source, at : at + 2, 0:rows]
 
 
@@ -183,7 +211,7 @@
         )
         lanes = slice(source * rows, (source + 1) * rows)
         turned[:, lanes] = weighted.T
-        numbers[:, lanes] = places_of(received_ref, source, UP, rows).astype(jnp.float32)
+        numbers[:, lanes] = places_of(received_ref, source, rows).astype(jnp.float32)
     number = 0
     for out_ref in out_refs:
         for start in range(0, out_ref.shape[0], BLOCK):
@@ -219,11 +247,11 @@
     )(received, *before)
 
 
-def lane_numbers(received_ref, which, rows, wide):
+def lane_numbers(received_ref, rows, wide):
     sources = received_ref.shape[0]
     low = low_half((sources * rows, wide))
     found = [
-        columns_of(places_of(received_ref, source, which, rows), wide)
+        columns_of(places_of(received_ref, source, rows), wide)
         for source in range(sources)
     ]
     odd = jnp.where(low, 0.0, 1.0)
@@ -240,19 +268,18 @@
         at, start = at + terms, start + value.shape[0]
 
 
-def project_kernel(received_ref, *refs):
-    weight_refs, out_ref = refs[:-1], refs[-1]
+def project_kernel(pieces, received_ref, *refs):
+    piece_refs, out_ref, full = refs[:-2], refs[-2], refs[-1]
+    pl.when(pl.program_id(0) == 0)(lambda: join(pieces, piece_refs, full))
     sources, rows, wide = out_ref.shape
-    low, first, second = lane_numbers(received_ref, DOWN, rows, wide)
+    low, first, second = lane_numbers(received_ref, rows, wide)
     tokens = token_rows(received_ref, rows)
     sums = [jnp.zeros((sources * rows, wide), jnp.float32) for _ in range(2)]
     number = 0.0
-    for weight_ref, start in [
-        (ref, at) for ref in weight_refs for at in range(0, ref.shape[0], BLOCK)
-    ]:
+    for start in range(0, full.shape[0], BLOCK):
         product = lax.dot_general(
             tokens,
-            weight_ref[start : start + BLOCK, :],
+            full[start : start + BLOCK, :],
             (((1,), (1,)), ((), ())),
             preferred_element_type=jnp.float32,
         )
@@ -266,20 +293,23 @@
     out_ref[...] = value.reshape(out_ref.shape)
 
 
-def project(received, weights, rows, wide):
+def project(received, pieces, rows, wide):
     sources, height, features = received.shape
-    return pl.pallas_call(
-        project_kernel,
+    flat = [term for terms in pieces for term in terms]
+    joined = sum(terms[0].shape[0] for terms in pieces)
+    return pl.pallas_call(
+        functools.partial(project_kernel, [len(terms) for terms in pieces]),
         grid=(sources // 2,),
         in_specs=[
             pl.BlockSpec((2, height, features), lambda i: (i, 0, 0)),
-            *[pl.BlockSpec(weight.shape, lambda i: (0, 0)) for weight in weights],
+            *[pl.BlockSpec(term.shape, lambda i: (0, 0)) for term in flat],
         ],
         out_specs=pl.BlockSpec((2, rows, wide), lambda i: (i, 0, 0)),
         out_shape=jax.ShapeDtypeStruct((sources, rows, wide), jnp.bfloat16),
-        compiler_params=params(),
-        cost_estimate=cost(sources * rows, features, sum(w.shape[0] for w in weights)),
-    )(received, *weights)
+        scratch_shapes=[pltpu.VMEM((joined, features), jnp.bfloat16)],
+        compiler_params=params(),
+        cost_estimate=cost(sources * rows, features, joined),
+    )(received, *flat)
 
 
 def hidden_kernel(parts_ref, activation_ref, scaled_ref, hidden_ref, gate_ref):
@@ -306,7 +336,7 @@
     piece_refs, out_ref, full, spread = refs[:-3], refs[-3], refs[-2], refs[-1]
     pl.when(pl.program_id(0) == 0)(lambda: join(pieces, piece_refs, full))
     sources, rows, wide = hidden_ref.shape
-    low, first, second = lane_numbers(received_ref, UP, rows, wide)
+    low, first, second = lane_numbers(received_ref, rows, wide)
     values = hidden_ref[...].reshape(sources * rows, wide).astype(jnp.float32)
     swapped = pltpu.roll(values, wide // 2, 1)
     one = jnp.where(low, values, swapped)
@@ -353,7 +383,10 @@
 def chain_gather(mine):
     beside = lax.ppermute(mine, "far", SIDES)
     across = lax.ppermute(mine, "far", MIDDLE)
-    across_far = lax.ppermute(beside, "far", MIDDLE)
+    return beside, across, lax.ppermute(beside, "far", MIDDLE)
+
+
+def chain_finish(mine, beside, across, across_far):
     second = lax.ppermute(across, "far", OUTWARD)
     third = lax.ppermute(across_far, "far", OUTWARD)
     return [(mine,), (beside,), (across, second), (across_far, third)]
@@ -363,11 +396,13 @@
     return sum(term.astype(jnp.float32) for term in terms).astype(jnp.bfloat16)
 
 
-def chain_scatter(own, beside, second, third):
-    third = add(third, lax.ppermute(third, "far", INWARD))
-    second = add(second, lax.ppermute(second, "far", INWARD))
-    beside = add(beside, lax.ppermute(third, "far", MIDDLE))
+def chain_scatter(blocks, before_second, before_third):
+    own, beside, second, third = blocks
+    second, third = add_pairs(
+        [(block, lax.ppermute(block, "far", INWARD)) for block in (second, third)], before_second
+    )
     across = lax.ppermute(second, "far", MIDDLE)
+    (beside,) = add_pairs([(beside, lax.ppermute(third, "far", MIDDLE))], before_third)
     return add(own, across, lax.ppermute(beside, "far", SIDES))
 
 
@@ -389,21 +424,33 @@
         return own, lax.ppermute(other, "near", SWAP)
 
     down_halves, up_halves = halves(down_weight), halves(up_weight)
-    down_full = [lax.all_gather(half, "far", tiled=True) for half in down_halves]
-    up_own = stack(*up_halves, down_full)
+    down_own = stack(*down_halves, ())
     if chained:
-        up_pieces = chain_gather(up_own)
         far_places = jnp.asarray(CHAIN, jnp.int32)[lax.axis_index("far")]
+        reached = chain_gather(down_own)
+        down_pieces = chain_finish(down_own, *reached)
+        up_own = stack(*up_halves, reached[2:])
+        up_reached = chain_gather(up_own)
     else:
-        up_pieces = [(lax.all_gather(up_own, "far", tiled=True),)]
         far_places = jnp.arange(far_count, dtype=jnp.int32)
+        down_pieces = [(lax.all_gather(down_own, "far", tiled=True),)]
+        up_own = stack(*up_halves, ())
     packed, activation, scaled = pack_tokens(
         far_places, expert_ids.T, router_gates.T, saved_hidden, token_grads, members,
         local_experts, (down_halves[1], up_halves[1]),
     )
     received = exchange(packed, GROUP)
 
-    projected = project(received, down_full, tok_count, wide)
+    projected = project(received, down_pieces, tok_count, wide)
+    if chained:
+        beside, across, across_far = up_reached
+        up_pieces = chain_finish(up_own, beside, across, pass_on(across_far, (projected,)))
+    else:
+        up_pieces = [(lax.all_gather(up_own, "far", tiled=True),)]
+    partial_value = down_partial(
+        received, tok_count, wide, own_rows * NEAR * far_count, far_count if chained else 1,
+        (projected,),
+    )
     parts = exchange(projected, GROUP)
     hidden_grad, gate_grads = pl.pallas_call(
         hidden_kernel,
@@ -413,15 +460,10 @@
         ),
         compiler_params=params(),
     )(parts, activation, scaled)
-    hidden_grad = exchange(hidden_grad, GROUP)
-    input_grads = unpack_tokens(exchange(input_rows(received, hidden_grad, up_pieces), GROUP))
-
-    partial_value = down_partial(
-        received, tok_count, wide, own_rows * NEAR * far_count, far_count if chained else 1,
-        (projected,),
-    )
+    rows_back = input_rows(received, exchange(hidden_grad, GROUP), up_pieces)
+    input_grads = unpack_tokens(exchange(rows_back, GROUP))
     if chained:
-        sums = chain_scatter(*partial_value)
+        sums = chain_scatter(partial_value, (hidden_grad,), (rows_back,))
     else:
         sums = lax.psum_scatter(partial_value[0], "far", scatter_dimension=0, tiled=True)
     kept, passed = sums[:own_rows], lax.ppermute(sums[own_rows:], "near", SWAP)

time: 191 us -> 182 us (0.953)
  waiting for transfers between devices: 92.6 us -> 73.1 us
  between operations: 14.3 us -> 0.95 us
  starting transfers between devices: 44 us -> 54.7 us
  blocking collectives: 0 us -> 8.82 us
  other arithmetic: 5.85 us -> 1.14 us
  Pallas kernels: 17 us -> 21.6 us
  local copies, waits for them, and re-layouts: 16.2 us -> 19.7 us
    all_gather x2 -> x0, waiting for transfers between devices: 38.3 us -> none  [body(): lax.all_gather(half, 'far', tiled=True)]
    ppermute x6 -> x9, waiting for transfers between devices: 6.61 us -> 23.7 us  [the longest x2 11.6 us: chain_finish(): second = lax.ppermute(across, 'far', OUTWARD)]
    ppermute x1 -> x2, starting transfers between devices: 1.51 us -> 17.8 us  [chain_gather(): beside = lax.ppermute(mine, 'far', SIDES)]
    all_to_all x0 -> x1, blocking collectives: none -> 8.82 us  [exchange(): return lax.all_to_all(value, axes, split_axis=0, concat_axis=0, tiled=True)]
    ppermute x1 -> x2, waiting for transfers between devices: 10.7 us -> 17.7 us  [chain_gather(): beside = lax.ppermute(mine, 'far', SIDES)]
    ppermute x6 -> x9, starting transfers between devices: 18.1 us -> 13.1 us  [the longest x2 4.33 us: chain_scatter(): lax.ppermute(block, 'far', INWARD)]
    convert_element_type x4 -> x1, other arithmetic: 4.98 us -> 0.27 us  [add(): sum((term.astype(jnp.float32) for term in terms)).astype(jnp.bfloat16)]
    all_to_all x4 -> x3, starting transfers between devices: 15.7 us -> 11.1 us  [exchange(): return lax.all_to_all(value, axes, split_axis=0, concat_axis=0, tiled=True)]
  transfers between devices with their start and end apart: 19 -> 21, of which waited for: 9 -> 10; matrix products, arithmetic and copies ran while one was open for 4% -> 2% of each run, Pallas kernels for 8% -> 10%
where the time goes in v7:
time: 182 us; the launch traced here: 180 us
  waiting for transfers between devices  73.1 us (40%)
  starting transfers between devices  54.7 us (30%)
  Pallas kernels  21.6 us (12%)
  local copies, waits for them, and re-layouts  19.7 us (11%)
  blocking collectives  8.82 us (5%)
    ppermute x2, starting transfers between devices, chain_gather(): beside = lax.ppermute(mine, 'far', SIDES)  17.8 us
    ppermute x2, waiting for transfers between devices, chain_gather(): beside = lax.ppermute(mine, 'far', SIDES)  17.7 us
    unnamed x54, local copies, waits for them, and re-layouts  15.3 us
    ppermute x1, waiting for transfers between devices, chain_scatter(): return add(own, across, lax.ppermute(beside, 'far', SIDES))  12.3 us
    ppermute x2, waiting for transfers between devices, chain_finish(): second = lax.ppermute(across, 'far', OUTWARD)  11.6 us
    all_to_all x3, starting transfers between devices, exchange(): return lax.all_to_all(value, axes, split_axis=0, concat_axis=0, tiled=True)  11.1 us
    ppermute x2, waiting for transfers between devices, chain_finish(): third = lax.ppermute(across_far, 'far', OUTWARD)  9.96 us
    ppermute x1, waiting for transfers between devices, body(): lax.ppermute(sums[own_rows:], 'near', SWAP)  9.76 us
  transfers between devices with their start and end apart: 21, of which 10 were waited for; matrix products, arithmetic and copies ran while one was open for 2% of the time, Pallas kernels for 10%

profile of v7, /device:TPU:0, one launch (start us, length us, event | category | flops | bytes accessed | tf_op | source)
XLA Modules:
  0.0 180.0 jit_solution(3540221327125230708)
XLA Ops:
  0.7 1.9 %constant_dynamic-slice_fusion.1 = (bf16[128,1024]{1,0:T(8,128)(2,1)S(1)}, bf16[128,1024]{1,0:T(8,128)(2,1)}) fusion(bf16[128,2048]{1,0:T(8,128)(2,1)} %bitcast.10, s32[]{:T(128)S(6)} %select_n.25, s32[]{:T(128)S(6)} %select_n.24), kind=kLoop, calls=%fused_computation.5 | loop fusion | bytes 1048584 | tf_op jit(solution)/shard_map/dynamic_slice | solution.py:422
  2.6 3.0 %collective-permute-start = (bf16[128,1024]{1,0:T(8,128)(2,1)}, bf16[128,1024]{1,0:T(8,128)(2,1)S(1)}, u32[]{:S(2)}, u32[]{:S(2)}) collective-permute-start(bf16[128,1024]{1,0:T(8,128)(2,1)} %get-tuple-element.30), channel_id=1, source_target_pairs={{0,4},{4,0},{1,5},{5,1},{2,6},{6,2},{3,7},{7,3},{8,12},{12,8},{9,1... | collective-permute-start | bytes 786440 | tf_op jit(solution)/shard_map/ppermute | solution.py:424
  5.6 1.8 constant_dynamic-slice_fusion
  7.3 0.0 collective-permute-start.1
  7.3 0.7 fusion.far_ref
  8.0 4.9 %collective-permute-done.refs_0_.other_ref = bf16[128,1024]{1,0:T(8,128)(2,1)S(1)} collective-permute-done((bf16[128,1024]{1,0:T(8,128)(2,1)}, bf16[128,1024]{1,0:T(8,128)(2,1)S(1)}, u32[]{:S(2)}, u32[]{:S(2)}) %collective-permute-start) | collective-permute-done | bytes 262176 | tf_op jit(solution)/shard_map/ppermute | solution.py:424
  12.9 4.8 %collective-permute-done.1.refs_1_.other_ref = bf16[128,1024]{1,0:T(8,128)(2,1)S(1)} collective-permute-done((bf16[128,1024]{1,0:T(8,128)(2,1)}, bf16[128,1024]{1,0:T(8,128)(2,1)S(1)}, u32[]{:S(2)}, u32[]{:S(2)}) %collective-permute-start.1) | collective-permute-done | bytes 262176 | tf_op jit(solution)/shard_map/ppermute | solution.py:424
  17.7 1.2 shard_map.94
  18.9 1.5 copy-done
  20.4 3.9 %all-to-all-start = ((bf16[8,160,1024]{2,1,0:T(8,128)(2,1)}), bf16[8,160,1024]{2,1,0:T(8,128)(2,1)S(1)}, u32[]{:S(2)}, u32[]{:S(2)}) async-start(bf16[8,160,1024]{2,1,0:T(8,128)(2,1)} %copy-done), calls=%async_computation | async-start | bytes 5242880 | tf_op jit(solution)/shard_map/all_to_all | solution.py:380
  24.4 0.0 copy-start.10
  24.4 1.6 collective-permute-start.2
  26.0 12.8 %collective-permute-done.2.refs_1_ = bf16[256,1024]{1,0:T(8,128)(2,1)S(1)} collective-permute-done((bf16[256,1024]{1,0:T(8,128)(2,1)S(1)}, bf16[256,1024]{1,0:T(8,128)(2,1)S(1)}, u32[]{:S(2)}, u32[]{:S(2)}) %collective-permute-start.2) | collective-permute-done | bytes 524320 | tf_op jit(solution)/shard_map/ppermute | solution.py:384
  38.8 0.7 collective-permute-start.5
  39.5 0.0 copy-start.17
  39.5 0.8 copy-done.17
  40.3 0.7 collective-permute-start.3
  40.9 0.0 collective-permute-done.5.refs_4_.refs_0_
  41.0 1.1 copy-done.5
  42.1 16.1 %collective-permute-start.7 = (bf16[256,1024]{1,0:T(8,128)(2,1)S(1)}, bf16[256,1024]{1,0:T(8,128)(2,1)}, u32[]{:S(2)}, u32[]{:S(2)}) collective-permute-start(bf16[256,1024]{1,0:T(8,128)(2,1)S(1)} %shard_map.98.refs_0_), channel_id=1, source_target_pairs={{0,8},{8,0},{16,24},{24,16},{1,9},{9,1},{17,25},{25,17},{2,10},{10... | collective-permute-start | bytes 1572872 | tf_op jit(solution)/shard_map/ppermute | solution.py:384
  58.3 1.3 collective-permute-start.4
  59.6 0.8 copy-done.21
  60.4 1.3 collective-permute-start.6
  61.6 1.5 collective-permute-start.8
  63.1 4.9 %collective-permute-done.7.refs_1_ = bf16[256,1024]{1,0:T(8,128)(2,1)} collective-permute-done((bf16[256,1024]{1,0:T(8,128)(2,1)S(1)}, bf16[256,1024]{1,0:T(8,128)(2,1)}, u32[]{:S(2)}, u32[]{:S(2)}) %collective-permute-start.7) | collective-permute-done | bytes 524320 | tf_op jit(solution)/shard_map/ppermute | solution.py:384
  68.0 1.5 collective-permute-start.10
  69.5 11.6 %collective-permute-done.4.refs_3_ = bf16[256,1024]{1,0:T(8,128)(2,1)S(1)} collective-permute-done((bf16[256,1024]{1,0:T(8,128)(2,1)S(1)}, bf16[256,1024]{1,0:T(8,128)(2,1)S(1)}, u32[]{:S(2)}, u32[]{:S(2)}) %collective-permute-start.4) | collective-permute-done | bytes 524320 | tf_op jit(solution)/shard_map/ppermute | solution.py:390
  81.1 0.8 copy-done.23
  81.9 8.6 %collective-permute-done.6.refs_5_ = bf16[256,1024]{1,0:T(8,128)(2,1)S(1)} collective-permute-done((bf16[256,1024]{1,0:T(8,128)(2,1)S(1)}, bf16[256,1024]{1,0:T(8,128)(2,1)S(1)}, u32[]{:S(2)}, u32[]{:S(2)}) %collective-permute-start.6) | collective-permute-done | bytes 524320 | tf_op jit(solution)/shard_map/ppermute | solution.py:391
  90.5 0.8 copy-done.25
  91.4 1.0 copy-done.9
  92.4 1.0 copy-done.11
  93.4 1.0 copy-done.18
  94.5 1.0 copy-done.22
  95.5 1.0 copy-done.24
  96.6 1.0 copy-done.26
  97.6 4.0 %shard_map.96.refs_1_.refs_0_ = bf16[8,128,128]{2,1,0:T(8,128)(2,1)S(1)} custom-call(bf16[8,160,1024]{2,1,0:T(8,128)(2,1)S(1)} %all-to-all-done.received_ref, bf16[256,1024]{1,0:T(8,128)(2,1)S(1)} %copy-done.11, bf16[256,1024]{1,0:T(8,128)(2,1)S(1)} %copy-done.18, bf16[256,1024]{1,0:T(8,128)(2,1)S(1)} %copy-done.22, bf16[256,1024]{1,0:T(8,128)(2,1)S(1)} %copy-done.24, ...), custom_call_target="tpu_custom_call" | custom-call | flops 2147483648 | bytes 6291456 | tf_op jit(solution)/shard_map/pallas_call | solution.py:300
  101.6 3.2 %shard_map.102 = (bf16[256,1024]{1,0:T(8,128)(2,1)S(1)}, bf16[256,1024]{1,0:T(8,128)(2,1)S(1)}, bf16[256,1024]{1,0:T(8,128)(2,1)}, bf16[256,1024]{1,0:T(8,128)(2,1)}) custom-call(bf16[8,160,1024]{2,1,0:T(8,128)(2,1)S(1)} %all-to-all-done.received_ref, bf16[8,128,128]{2,1,0:T(8,128)(2,1)S(1)} %shard_map.96.refs_1_.refs_0_), custom_call_target="tpu_custom_call" | custom-call | flops 2147483648 | bytes 6291456 | tf_op jit(solution)/shard_map/pallas_call | solution.py:233
  104.8 0.8 copy-done.12
  105.6 2.2 %collective-permute-start.12 = (bf16[256,1024]{1,0:T(8,128)(2,1)}, bf16[256,1024]{1,0:T(8,128)(2,1)}, u32[]{:S(2)}, u32[]{:S(2)}) collective-permute-start(bf16[256,1024]{1,0:T(8,128)(2,1)} %get-tuple-element.20.refs_0_), channel_id=1, source_target_pairs={{0,8},{24,16},{1,9},{25,17},{2,10},{26,18},{3,11},{27,19},{4,12},{... | collective-permute-start | bytes 1572872 | tf_op jit(solution)/shard_map/ppermute | solution.py:402
  107.8 2.1 %collective-permute-start.13 = (bf16[256,1024]{1,0:T(8,128)(2,1)}, bf16[256,1024]{1,0:T(8,128)(2,1)}, u32[]{:S(2)}, u32[]{:S(2)}) collective-permute-start(bf16[256,1024]{1,0:T(8,128)(2,1)} %get-tuple-element.21.refs_2_), channel_id=1, source_target_pairs={{0,8},{24,16},{1,9},{25,17},{2,10},{26,18},{3,11},{27,19},{4,12},{... | collective-permute-start | bytes 1572872 | tf_op jit(solution)/shard_map/ppermute | solution.py:402
  109.9 1.3 collective-permute-start.9
  111.2 1.3 collective-permute-start.11
  112.5 8.8 %all_to_all.20.parts_ref = bf16[8,128,128]{2,1,0:T(8,128)(2,1)S(1)} all-to-all(bf16[8,128,128]{2,1,0:T(8,128)(2,1)S(1)} %shard_map.96.refs_1_.refs_0_), channel_id=1, replica_groups=mesh['far'=4,'near'=2,'inner'=2,'outer'=2] {'inner','outer','near'}, dimensions={0} | all-to-all | bytes 524288 | tf_op jit(solution)/shard_map/all_to_all | solution.py:380
  121.4 0.7 shard_map.97
  122.1 0.7 copy-done.2
  122.8 3.4 %all-to-all-start.2 = ((bf16[8,128,128]{2,1,0:T(8,128)(2,1)}), bf16[8,128,128]{2,1,0:T(8,128)(2,1)S(1)}, u32[]{:S(2)}, u32[]{:S(2)}) async-start(bf16[8,128,128]{2,1,0:T(8,128)(2,1)} %copy-done.2), calls=%async_computation.2 | async-start | bytes 524288 | tf_op jit(solution)/shard_map/all_to_all | solution.py:380
  126.2 2.1 %collective-permute-done.13.refs_3_ = bf16[256,1024]{1,0:T(8,128)(2,1)} collective-permute-done((bf16[256,1024]{1,0:T(8,128)(2,1)}, bf16[256,1024]{1,0:T(8,128)(2,1)}, u32[]{:S(2)}, u32[]{:S(2)}) %collective-permute-start.13) | collective-permute-done | bytes 524320 | tf_op jit(solution)/shard_map/ppermute | solution.py:402
  128.3 0.9 copy-done.3
  129.3 2.4 %shard_map.103 = (bf16[256,1024]{1,0:T(8,128)(2,1)S(1)}, bf16[256,1024]{1,0:T(8,128)(2,1)}) custom-call(bf16[256,1024]{1,0:T(8,128)(2,1)} %get-tuple-element.20.refs_0_, bf16[256,1024]{1,0:T(8,128)(2,1)} %collective-permute-done.12.refs_1_, bf16[256,1024]{1,0:T(8,128)(2,1)} %get-tuple-element.21.refs_2_, bf16[256,1024]{1,0:T(8,128)(2,1)} %collective-permute-done.13.refs_3_, ...), custom_call_target="tpu_custom_call" | custom-call | tf_op jit(solution)/shard_map/pallas_call | solution.py:99
  131.7 0.8 copy-done.19
  132.5 1.5 collective-permute-start.15
  134.0 1.4 collective-permute-done.11.refs_5_
  135.3 7.0 %shard_map.100.refs_2_ = bf16[8,128,1024]{2,1,0:T(8,128)(2,1)} custom-call(bf16[8,160,1024]{2,1,0:T(8,128)(2,1)S(1)} %all-to-all-done.received_ref, bf16[8,128,128]{2,1,0:T(8,128)(2,1)S(1)} %all-to-all-done.2.hidden_ref, bf16[256,1024]{1,0:T(8,128)(2,1)S(1)} %shard_map.98.refs_0_, bf16[256,1024]{1,0:T(8,128)(2,1)} %collective-permute-done.7.refs_1_, ...), custom_call_target="tpu_custom_call" | custom-call | flops 2147483648 | bytes 6291456 | tf_op jit(solution)/shard_map/pallas_call | solution.py:360
  142.3 3.7 %all-to-all-start.3 = ((bf16[8,128,1024]{2,1,0:T(8,128)(2,1)}), bf16[8,128,1024]{2,1,0:T(8,128)(2,1)S(1)}, u32[]{:S(2)}, u32[]{:S(2)}) async-start(bf16[8,128,1024]{2,1,0:T(8,128)(2,1)} %shard_map.100.refs_2_), calls=%async_computation.3 | async-start | bytes 4194304 | tf_op jit(solution)/shard_map/all_to_all | solution.py:380
  146.1 0.8 collective-permute-start.14
  147.0 1.2 shard_map.104
  148.1 5.1 %collective-permute-start.16 = (bf16[256,1024]{1,0:T(8,128)(2,1)S(1)}, bf16[256,1024]{1,0:T(8,128)(2,1)S(1)}, u32[]{:S(2)}, u32[]{:S(2)}) collective-permute-start(bf16[256,1024]{1,0:T(8,128)(2,1)S(1)} %shard_map.104), channel_id=1, source_target_pairs={{0,8},{8,0},{16,24},{24,16},{1,9},{9,1},{17,25},{25,17},{2,10},{10... | collective-permute-start | bytes 1572872 | tf_op jit(solution)/shard_map/ppermute | solution.py:406
  153.2 12.3 %collective-permute-done.16 = bf16[256,1024]{1,0:T(8,128)(2,1)S(1)} collective-permute-done((bf16[256,1024]{1,0:T(8,128)(2,1)S(1)}, bf16[256,1024]{1,0:T(8,128)(2,1)S(1)}, u32[]{:S(2)}, u32[]{:S(2)}) %collective-permute-start.16) | collective-permute-done | bytes 524320 | tf_op jit(solution)/shard_map/ppermute | solution.py:406
  165.5 0.3 add_convert_fusion
  165.8 1.7 collective-permute-start.17
  167.5 9.8 %collective-permute-done.17 = bf16[128,1024]{1,0:T(8,128)(2,1)S(1)} collective-permute-done((bf16[128,1024]{1,0:T(8,128)(2,1)S(1)}, bf16[128,1024]{1,0:T(8,128)(2,1)S(1)}, u32[]{:S(2)}, u32[]{:S(2)}) %collective-permute-start.17) | collective-permute-done | bytes 262176 | tf_op jit(solution)/shard_map/ppermute | solution.py:469
  177.3 0.8 pad_maximum_fusion
  178.2 1.8 %shard_map.101 = bf16[128,8192]{1,0:T(8,128)(2,1)} custom-call(bf16[8,128,1024]{2,1,0:T(8,128)(2,1)S(1)} %all-to-all-done.3.parts_ref), custom_call_target="tpu_custom_call" | custom-call | tf_op jit(solution)/shard_map/pallas_call | solution.py:180
  (51 shorter events, 0.2 us)
Async XLA Ops:
  0.6 17.1 %copy-start.15 = (s32[128,2]{0,1:T(2,128)S(1)}, s32[128,2]{0,1:T(2,128)}, u32[]{:S(2)}) copy-start(s32[128,2]{0,1:T(2,128)} %param.9) | copy-start | bytes 3076
  0.6 17.1 %copy-start.16 = (bf16[128,2]{0,1:T(2,128)(2,1)S(1)}, bf16[128,2]{0,1:T(2,128)(2,1)}, u32[]{:S(2)}) copy-start(bf16[128,2]{0,1:T(2,128)(2,1)} %param.8) | copy-start | bytes 1540
  0.7 17.1 %copy-start.14 = (bf16[128,128]{1,0:T(8,128)(2,1)S(1)}, bf16[128,128]{1,0:T(8,128)(2,1)}, u32[]{:S(2)}) copy-start(bf16[128,128]{1,0:T(8,128)(2,1)} %preact_ref.1) | copy-start | bytes 98308
  0.7 17.1 %copy-start.1 = (bf16[128,8192]{1,0:T(8,128)(2,1)S(1)}, bf16[128,8192]{1,0:T(8,128)(2,1)}, u32[]{:S(2)}) copy-start(bf16[128,8192]{1,0:T(8,128)(2,1)} %tokens_ref.1) | copy-start | bytes 6291460
  2.6 10.3 %collective-permute-start = (bf16[128,1024]{1,0:T(8,128)(2,1)}, bf16[128,1024]{1,0:T(8,128)(2,1)S(1)}, u32[]{:S(2)}, u32[]{:S(2)}) collective-permute-start(bf16[128,1024]{1,0:T(8,128)(2,1)} %get-tuple-element.30), channel_id=1, source_target_pairs={{0,4},{4,0},{1,5},{5,1},{2,6},{6,2},{3,7},{7,3},{8,12},{12,8},{9,1... | collective-permute-start | bytes 786440 | tf_op jit(solution)/shard_map/ppermute | solution.py:424
  7.3 10.4 %collective-permute-start.1 = (bf16[128,1024]{1,0:T(8,128)(2,1)}, bf16[128,1024]{1,0:T(8,128)(2,1)S(1)}, u32[]{:S(2)}, u32[]{:S(2)}) collective-permute-start(bf16[128,1024]{1,0:T(8,128)(2,1)} %get-tuple-element.28), channel_id=1, source_target_pairs={{0,4},{4,0},{1,5},{5,1},{2,6},{6,2},{3,7},{7,3},{8,12},{12,8},{9,1... | collective-permute-start | bytes 786440 | tf_op jit(solution)/shard_map/ppermute | solution.py:424
  17.7 2.7 %copy-start.4 = (bf16[128,1024]{1,0:T(8,128)(2,1)}, bf16[128,1024]{1,0:T(8,128)(2,1)S(1)}, u32[]{:S(2)}) copy-start(bf16[128,1024]{1,0:T(8,128)(2,1)S(1)} %collective-permute-done.1.refs_1_.other_ref) | copy-start | bytes 786436
  18.9 1.5 copy-start
  20.4 71.0 %all-to-all-start = ((bf16[8,160,1024]{2,1,0:T(8,128)(2,1)}), bf16[8,160,1024]{2,1,0:T(8,128)(2,1)S(1)}, u32[]{:S(2)}, u32[]{:S(2)}) async-start(bf16[8,160,1024]{2,1,0:T(8,128)(2,1)} %copy-done), calls=%async_computation | async-start | bytes 5242880 | tf_op jit(solution)/shard_map/all_to_all | solution.py:380
  24.4 56.8 %copy-start.10 = (bf16[256,1024]{1,0:T(8,128)(2,1)}, bf16[256,1024]{1,0:T(8,128)(2,1)S(1)}, u32[]{:S(2)}) copy-start(bf16[256,1024]{1,0:T(8,128)(2,1)S(1)} %shard_map.95.refs_0_) | copy-start | bytes 1572868
  24.4 14.4 %collective-permute-start.2 = (bf16[256,1024]{1,0:T(8,128)(2,1)S(1)}, bf16[256,1024]{1,0:T(8,128)(2,1)S(1)}, u32[]{:S(2)}, u32[]{:S(2)}) collective-permute-start(bf16[256,1024]{1,0:T(8,128)(2,1)S(1)} %shard_map.95.refs_0_), channel_id=1, source_target_pairs={{0,8},{8,0},{16,24},{24,16},{1,9},{9,1},{17,25},{25,17},{2,10},{10... | collective-permute-start | bytes 1572872 | tf_op jit(solution)/shard_map/ppermute | solution.py:384
  38.8 2.2 %collective-permute-start.5 = (bf16[256,1024]{1,0:T(8,128)(2,1)S(1)}, bf16[256,1024]{1,0:T(8,128)(2,1)S(1)}, u32[]{:S(2)}, u32[]{:S(2)}) collective-permute-start(bf16[256,1024]{1,0:T(8,128)(2,1)S(1)} %collective-permute-done.2.refs_1_), channel_id=1, source_target_pairs={{8,16},{16,8},{9,17},{17,9},{10,18},{18,10},{11,19},{19,11},{12,20... | collective-permute-start | bytes 1572872 | tf_op jit(solution)/shard_map/ppermute | solution.py:386
  39.5 0.8 copy-start.17
  40.3 18.0 %collective-permute-start.3 = (bf16[256,1024]{1,0:T(8,128)(2,1)S(1)}, bf16[256,1024]{1,0:T(8,128)(2,1)S(1)}, u32[]{:S(2)}, u32[]{:S(2)}) collective-permute-start(bf16[256,1024]{1,0:T(8,128)(2,1)S(1)} %shard_map.95.refs_0_), channel_id=1, source_target_pairs={{8,16},{16,8},{9,17},{17,9},{10,18},{18,10},{11,19},{19,11},{12,20... | collective-permute-start | bytes 1572872 | tf_op jit(solution)/shard_map/ppermute | solution.py:385
  41.0 40.2 %copy-start.8 = (bf16[256,1024]{1,0:T(8,128)(2,1)}, bf16[256,1024]{1,0:T(8,128)(2,1)S(1)}, u32[]{:S(2)}) copy-start(bf16[256,1024]{1,0:T(8,128)(2,1)S(1)} %collective-permute-done.5.refs_4_.refs_0_) | copy-start | bytes 1572868
  41.0 1.1 copy-start.5
  42.1 25.9 %collective-permute-start.7 = (bf16[256,1024]{1,0:T(8,128)(2,1)S(1)}, bf16[256,1024]{1,0:T(8,128)(2,1)}, u32[]{:S(2)}, u32[]{:S(2)}) collective-permute-start(bf16[256,1024]{1,0:T(8,128)(2,1)S(1)} %shard_map.98.refs_0_), channel_id=1, source_target_pairs={{0,8},{8,0},{16,24},{24,16},{1,9},{9,1},{17,25},{25,17},{2,10},{10... | collective-permute-start | bytes 1572872 | tf_op jit(solution)/shard_map/ppermute | solution.py:384
  58.3 22.8 %collective-permute-start.4 = (bf16[256,1024]{1,0:T(8,128)(2,1)S(1)}, bf16[256,1024]{1,0:T(8,128)(2,1)S(1)}, u32[]{:S(2)}, u32[]{:S(2)}) collective-permute-start(bf16[256,1024]{1,0:T(8,128)(2,1)S(1)} %collective-permute-done.3.refs_2_), channel_id=1, source_target_pairs={{8,0},{16,24},{9,1},{17,25},{10,2},{18,26},{11,3},{19,27},{12,4},{... | collective-permute-start | bytes 1572872 | tf_op jit(solution)/shard_map/ppermute | solution.py:390
  59.6 0.8 copy-start.21
  60.4 30.2 %collective-permute-start.6 = (bf16[256,1024]{1,0:T(8,128)(2,1)S(1)}, bf16[256,1024]{1,0:T(8,128)(2,1)S(1)}, u32[]{:S(2)}, u32[]{:S(2)}) collective-permute-start(bf16[256,1024]{1,0:T(8,128)(2,1)S(1)} %collective-permute-done.5.refs_4_.refs_0_), channel_id=1, source_target_pairs={{8,0},{16,24},{9,1},{17,25},{10,2},{18,26},{11,3},{19,27},{12,4},{... | collective-permute-start | bytes 1572872 | tf_op jit(solution)/shard_map/ppermute | solution.py:391
  61.6 48.3 %collective-permute-start.8 = (bf16[256,1024]{1,0:T(8,128)(2,1)S(1)}, bf16[256,1024]{1,0:T(8,128)(2,1)}, u32[]{:S(2)}, u32[]{:S(2)}) collective-permute-start(bf16[256,1024]{1,0:T(8,128)(2,1)S(1)} %shard_map.98.refs_0_), channel_id=1, source_target_pairs={{8,16},{16,8},{9,17},{17,9},{10,18},{18,10},{11,19},{19,11},{12,20... | collective-permute-start | bytes 1572872 | tf_op jit(solution)/shard_map/ppermute | solution.py:385
  68.0 43.2 %collective-permute-start.10 = (bf16[256,1024]{1,0:T(8,128)(2,1)}, bf16[256,1024]{1,0:T(8,128)(2,1)}, u32[]{:S(2)}, u32[]{:S(2)}) collective-permute-start(bf16[256,1024]{1,0:T(8,128)(2,1)} %collective-permute-done.7.refs_1_), channel_id=1, source_target_pairs={{8,16},{16,8},{9,17},{17,9},{10,18},{18,10},{11,19},{19,11},{12,20... | collective-permute-start | bytes 1572872 | tf_op jit(solution)/shard_map/ppermute | solution.py:386
  81.1 0.8 copy-start.23
  90.5 0.8 copy-start.25
  91.4 1.0 copy-start.9
  92.4 1.0 copy-start.11
  93.4 1.0 copy-start.18
  94.5 1.0 copy-start.22
  95.5 1.0 copy-start.24
  96.6 1.0 copy-start.26
  104.8 0.8 copy-start.12
  105.6 5.6 %copy-start.6 = (bf16[256,1024]{1,0:T(8,128)(2,1)}, bf16[256,1024]{1,0:T(8,128)(2,1)S(1)}, u32[]{:S(2)}) copy-start(bf16[256,1024]{1,0:T(8,128)(2,1)S(1)} %get-tuple-element.23.refs_0_) | copy-start | bytes 1572868
  105.6 20.6 %collective-permute-start.12 = (bf16[256,1024]{1,0:T(8,128)(2,1)}, bf16[256,1024]{1,0:T(8,128)(2,1)}, u32[]{:S(2)}, u32[]{:S(2)}) collective-permute-start(bf16[256,1024]{1,0:T(8,128)(2,1)} %get-tuple-element.20.refs_0_), channel_id=1, source_target_pairs={{0,8},{24,16},{1,9},{25,17},{2,10},{26,18},{3,11},{27,19},{4,12},{... | collective-permute-start | bytes 1572872 | tf_op jit(solution)/shard_map/ppermute | solution.py:402
  107.8 20.5 %collective-permute-start.13 = (bf16[256,1024]{1,0:T(8,128)(2,1)}, bf16[256,1024]{1,0:T(8,128)(2,1)}, u32[]{:S(2)}, u32[]{:S(2)}) collective-permute-start(bf16[256,1024]{1,0:T(8,128)(2,1)} %get-tuple-element.21.refs_2_), channel_id=1, source_target_pairs={{0,8},{24,16},{1,9},{25,17},{2,10},{26,18},{3,11},{27,19},{4,12},{... | collective-permute-start | bytes 1572872 | tf_op jit(solution)/shard_map/ppermute | solution.py:402
  109.9 24.1 %collective-permute-start.9 = (bf16[256,1024]{1,0:T(8,128)(2,1)}, bf16[256,1024]{1,0:T(8,128)(2,1)}, u32[]{:S(2)}, u32[]{:S(2)}) collective-permute-start(bf16[256,1024]{1,0:T(8,128)(2,1)} %collective-permute-done.8.refs_2_), channel_id=1, source_target_pairs={{8,0},{16,24},{9,1},{17,25},{10,2},{18,26},{11,3},{19,27},{12,4},{... | collective-permute-start | bytes 1572872 | tf_op jit(solution)/shard_map/ppermute | solution.py:390
  111.2 24.1 %collective-permute-start.11 = (bf16[256,1024]{1,0:T(8,128)(2,1)}, bf16[256,1024]{1,0:T(8,128)(2,1)}, u32[]{:S(2)}, u32[]{:S(2)}) collective-permute-start(bf16[256,1024]{1,0:T(8,128)(2,1)} %shard_map.99.refs_4_), channel_id=1, source_target_pairs={{8,0},{16,24},{9,1},{17,25},{10,2},{18,26},{11,3},{19,27},{12,4},{... | collective-permute-start | bytes 1572872 | tf_op jit(solution)/shard_map/ppermute | solution.py:391
  122.1 0.7 copy-start.2
  122.8 11.2 %all-to-all-start.2 = ((bf16[8,128,128]{2,1,0:T(8,128)(2,1)}), bf16[8,128,128]{2,1,0:T(8,128)(2,1)S(1)}, u32[]{:S(2)}, u32[]{:S(2)}) async-start(bf16[8,128,128]{2,1,0:T(8,128)(2,1)} %copy-done.2), calls=%async_computation.2 | async-start | bytes 524288 | tf_op jit(solution)/shard_map/all_to_all | solution.py:380
  128.3 0.9 copy-start.3
  131.7 0.8 copy-start.19
  132.5 14.4 %collective-permute-start.15 = (bf16[256,1024]{1,0:T(8,128)(2,1)}, bf16[256,1024]{1,0:T(8,128)(2,1)}, u32[]{:S(2)}, u32[]{:S(2)}) collective-permute-start(bf16[256,1024]{1,0:T(8,128)(2,1)} %get-tuple-element.24), channel_id=1, source_target_pairs={{8,16},{16,8},{9,17},{17,9},{10,18},{18,10},{11,19},{19,11},{12,20... | collective-permute-start | bytes 1572872 | tf_op jit(solution)/shard_map/ppermute | solution.py:405
  142.3 3.8 %copy-start.20 = (bf16[256,1024]{1,0:T(8,128)(2,1)S(1)}, bf16[256,1024]{1,0:T(8,128)(2,1)}, u32[]{:S(2)}) copy-start(bf16[256,1024]{1,0:T(8,128)(2,1)} %copy-done.19) | copy-start | bytes 1572868
  142.3 4.6 %copy-start.7 = (bf16[256,1024]{1,0:T(8,128)(2,1)S(1)}, bf16[256,1024]{1,0:T(8,128)(2,1)}, u32[]{:S(2)}) copy-start(bf16[256,1024]{1,0:T(8,128)(2,1)} %copy-done.6) | copy-start | bytes 1572868
  142.3 35.8 %all-to-all-start.3 = ((bf16[8,128,1024]{2,1,0:T(8,128)(2,1)}), bf16[8,128,1024]{2,1,0:T(8,128)(2,1)S(1)}, u32[]{:S(2)}, u32[]{:S(2)}) async-start(bf16[8,128,1024]{2,1,0:T(8,128)(2,1)} %shard_map.100.refs_2_), calls=%async_computation.3 | async-start | bytes 4194304 | tf_op jit(solution)/shard_map/all_to_all | solution.py:380
  146.1 19.4 %copy-start.13 = (bf16[256,1024]{1,0:T(8,128)(2,1)S(1)}, bf16[256,1024]{1,0:T(8,128)(2,1)}, u32[]{:S(2)}) copy-start(bf16[256,1024]{1,0:T(8,128)(2,1)} %copy-done.12) | copy-start | bytes 1572868
  146.1 7.1 %collective-permute-start.14 = (bf16[256,1024]{1,0:T(8,128)(2,1)S(1)}, bf16[256,1024]{1,0:T(8,128)(2,1)S(1)}, u32[]{:S(2)}, u32[]{:S(2)}) collective-permute-start(bf16[256,1024]{1,0:T(8,128)(2,1)S(1)} %copy-done.20), channel_id=1, source_target_pairs={{8,16},{16,8},{9,17},{17,9},{10,18},{18,10},{11,19},{19,11},{12,20... | collective-permute-start | bytes 1572872 | tf_op jit(solution)/shard_map/ppermute | solution.py:404
  148.1 17.4 %collective-permute-start.16 = (bf16[256,1024]{1,0:T(8,128)(2,1)S(1)}, bf16[256,1024]{1,0:T(8,128)(2,1)S(1)}, u32[]{:S(2)}, u32[]{:S(2)}) collective-permute-start(bf16[256,1024]{1,0:T(8,128)(2,1)S(1)} %shard_map.104), channel_id=1, source_target_pairs={{0,8},{8,0},{16,24},{24,16},{1,9},{9,1},{17,25},{25,17},{2,10},{10... | collective-permute-start | bytes 1572872 | tf_op jit(solution)/shard_map/ppermute | solution.py:406
  165.8 11.5 %collective-permute-start.17 = (bf16[128,1024]{1,0:T(8,128)(2,1)S(1)}, bf16[128,1024]{1,0:T(8,128)(2,1)S(1)}, u32[]{:S(2)}, u32[]{:S(2)}) collective-permute-start(bf16[128,1024]{1,0:T(8,128)(2,1)S(1)} %slice.9), channel_id=1, source_target_pairs={{0,4},{4,0},{1,5},{5,1},{2,6},{6,2},{3,7},{7,3},{8,12},{12,8},{9,1... | collective-permute-start | bytes 786440 | tf_op jit(solution)/shard_map/ppermute | solution.py:469

commit v8 on v7

--- a/solution.py
+++ b/solution.py
@@ -9,15 +9,11 @@
 root_half = 0.7071067811865476
 inv_root_tau = 0.3989422804014327
 GROUP = ("inner", "outer", "near")
-NEAR = 2
+FAR = ("high", "low")
+PAIR = 2
 BLOCK = 256
 TILE = 16
 MIB = 1 << 20
-CHAIN = ((0, 1, 2, 3), (1, 0, 2, 3), (3, 2, 0, 1), (3, 2, 1, 0))
-SIDES = ((0, 1), (1, 0), (2, 3), (3, 2))
-MIDDLE = ((1, 2), (2, 1))
-OUTWARD = ((1, 0), (2, 3))
-INWARD = ((0, 1), (3, 2))
 SWAP = ((0, 1), (1, 0))
 
 
@@ -74,18 +70,6 @@
     )(own, other, *before)
 
 
-def pass_on(value, before):
-    anywhere = pl.BlockSpec(memory_space=pl.ANY)
-    return pl.pallas_call(
-        lambda *refs: None,
-        in_specs=[anywhere] * (1 + len(before)),
-        out_specs=anywhere,
-        out_shape=jax.ShapeDtypeStruct(value.shape, value.dtype),
-        input_output_aliases={0: 0},
-        compiler_params=params(),
-    )(value, *before)
-
-
 def add_kernel(count, *refs):
     terms, out_refs = refs[: 2 * count], refs[-count:]
     for at in range(count):
@@ -127,13 +111,14 @@
     ids = ids_ref[...]
     local = lax.rem(ids, local_experts)
     line = lax.div(ids, local_experts)
-    far, near = lax.div(line, NEAR), lax.rem(line, NEAR)
+    near = lax.rem(lax.div(line, PAIR), PAIR)
+    far = lax.div(line, PAIR * PAIR) * PAIR + lax.rem(line, PAIR)
     far_place = jnp.zeros_like(far)
     for at in range(far_count):
         far_place = jnp.where(far == at, far_ref[at], far_place)
     for block in range(blocks):
-        side = lax.rem(near + block, NEAR)
-        place = (far_place * NEAR + side) * local_experts + local
+        side = lax.rem(near + block, PAIR)
+        place = (far_place * PAIR + side) * local_experts + local
         out_ref[block, 0:rows, :] = tokens_ref[:, block * features : (block + 1) * features]
         for at in range(0, features, wide):
             start = at // wide * taken
@@ -258,28 +243,24 @@
     return low, *[jnp.concatenate([pair[k] for pair in found]) - odd for k in range(2)]
 
 
-def join(pieces, piece_refs, full):
-    at = start = 0
-    for terms in pieces:
-        value = piece_refs[at][...]
-        for ref in piece_refs[at + 1 : at + terms]:
-            value = value + ref[...]
-        full[start : start + value.shape[0], :] = value
-        at, start = at + terms, start + value.shape[0]
-
-
-def project_kernel(pieces, received_ref, *refs):
-    piece_refs, out_ref, full = refs[:-2], refs[-2], refs[-1]
-    pl.when(pl.program_id(0) == 0)(lambda: join(pieces, piece_refs, full))
+def join(piece_refs, full):
+    start = 0
+    for ref in piece_refs:
+        full[start : start + ref.shape[0], :] = ref[...]
+        start += ref.shape[0]
+
+
+def project_kernel(received_ref, *refs):
+    piece_refs, out_ref = refs[:-1], refs[-1]
     sources, rows, wide = out_ref.shape
     low, first, second = lane_numbers(received_ref, rows, wide)
     tokens = token_rows(received_ref, rows)
     sums = [jnp.zeros((sources * rows, wide), jnp.float32) for _ in range(2)]
     number = 0.0
-    for start in range(0, full.shape[0], BLOCK):
+    for ref, start in [(ref, at) for ref in piece_refs for at in range(0, ref.shape[0], BLOCK)]:
         product = lax.dot_general(
             tokens,
-            full[start : start + BLOCK, :],
+            ref[start : start + BLOCK, :],
             (((1,), (1,)), ((), ())),
             preferred_element_type=jnp.float32,
         )
@@ -295,21 +276,18 @@
 
 def project(received, pieces, rows, wide):
     sources, height, features = received.shape
-    flat = [term for terms in pieces for term in terms]
-    joined = sum(terms[0].shape[0] for terms in pieces)
-    return pl.pallas_call(
-        functools.partial(project_kernel, [len(terms) for terms in pieces]),
+    return pl.pallas_call(
+        project_kernel,
         grid=(sources // 2,),
         in_specs=[
             pl.BlockSpec((2, height, features), lambda i: (i, 0, 0)),
-            *[pl.BlockSpec(term.shape, lambda i: (0, 0)) for term in flat],
+            *[pl.BlockSpec(piece.shape, lambda i: (0, 0)) for piece in pieces],
         ],
         out_specs=pl.BlockSpec((2, rows, wide), lambda i: (i, 0, 0)),
         out_shape=jax.ShapeDtypeStruct((sources, rows, wide), jnp.bfloat16),
-        scratch_shapes=[pltpu.VMEM((joined, features), jnp.bfloat16)],
-        compiler_params=params(),
-        cost_estimate=cost(sources * rows, features, joined),
-    )(received, *flat)
+        compiler_params=params(),
+        cost_estimate=cost(sources * rows, features, sum(p.shape[0] for p in pieces)),
+    )(received, *pieces)
 
 
 def hidden_kernel(parts_ref, activation_ref, scaled_ref, hidden_ref, gate_ref):
@@ -332,9 +310,9 @@
         hidden_ref[source] = hidden
 
 
-def input_kernel(pieces, received_ref, hidden_ref, *refs):
+def input_kernel(received_ref, hidden_ref, *refs):
     piece_refs, out_ref, full, spread = refs[:-3], refs[-3], refs[-2], refs[-1]
-    pl.when(pl.program_id(0) == 0)(lambda: join(pieces, piece_refs, full))
+    pl.when(pl.program_id(0) == 0)(lambda: join(piece_refs, full))
     sources, rows, wide = hidden_ref.shape
     low, first, second = lane_numbers(received_ref, rows, wide)
     values = hidden_ref[...].reshape(sources * rows, wide).astype(jnp.float32)
@@ -355,15 +333,14 @@
 
 def input_rows(received, hidden_grad, pieces):
     sources, rows, wide = hidden_grad.shape
-    flat = [term for terms in pieces for term in terms]
-    joined, features = sum(terms[0].shape[0] for terms in pieces), flat[0].shape[1]
-    return pl.pallas_call(
-        functools.partial(input_kernel, [len(terms) for terms in pieces]),
+    joined, features = sum(piece.shape[0] for piece in pieces), pieces[0].shape[1]
+    return pl.pallas_call(
+        input_kernel,
         grid=(sources // 2,),
         in_specs=[
             pl.BlockSpec((2, received.shape[1], features), lambda i: (i, 0, 0)),
             pl.BlockSpec((2, rows, wide), lambda i: (i, 0, 0)),
-            *[pl.BlockSpec(term.shape, lambda i: (0, 0)) for term in flat],
+            *[pl.BlockSpec(piece.shape, lambda i: (0, 0)) for piece in pieces],
         ],
         out_specs=pl.BlockSpec((2, rows, features), lambda i: (i, 0, 0)),
         out_shape=jax.ShapeDtypeStruct((sources, rows, features), jnp.bfloat16),
@@ -373,68 +350,51 @@
         ],
         compiler_params=params(),
         cost_estimate=cost(sources * rows, joined, features),
-    )(received, hidden_grad, *flat)
+    )(received, hidden_grad, *pieces)
 
 
 def exchange(value, axes):
     return lax.all_to_all(value, axes, split_axis=0, concat_axis=0, tiled=True)
 
 
-def chain_gather(mine):
-    beside = lax.ppermute(mine, "far", SIDES)
-    across = lax.ppermute(mine, "far", MIDDLE)
-    return beside, across, lax.ppermute(beside, "far", MIDDLE)
-
-
-def chain_finish(mine, beside, across, across_far):
-    second = lax.ppermute(across, "far", OUTWARD)
-    third = lax.ppermute(across_far, "far", OUTWARD)
-    return [(mine,), (beside,), (across, second), (across_far, third)]
+def swap(value, axis):
+    return lax.ppermute(value, axis, SWAP)
 
 
 def add(*terms):
     return sum(term.astype(jnp.float32) for term in terms).astype(jnp.bfloat16)
-
-
-def chain_scatter(blocks, before_second, before_third):
-    own, beside, second, third = blocks
-    second, third = add_pairs(
-        [(block, lax.ppermute(block, "far", INWARD)) for block in (second, third)], before_second
-    )
-    across = lax.ppermute(second, "far", MIDDLE)
-    (beside,) = add_pairs([(beside, lax.ppermute(third, "far", MIDDLE))], before_third)
-    return add(own, across, lax.ppermute(beside, "far", SIDES))
 
 
 def body(token_grads, router_gates, expert_ids, saved_hidden, up_weight, down_weight):
     tok_count = token_grads.shape[0]
     local_experts, hidden, width = up_weight.shape
-    members, far_count = lax.axis_size(GROUP), lax.axis_size("far")
-    wide, features = 2 * hidden, width // NEAR
+    members, far_count = lax.axis_size(GROUP), lax.axis_size(FAR)
+    wide, features = 2 * hidden, width // PAIR
     own_rows = local_experts * hidden
     near = lax.axis_index("near")
-    chained = far_count == len(CHAIN)
-
-    chained = far_count == len(CHAIN)
+    paired = lax.axis_size("high") == PAIR
 
     def halves(weight):
         flat = weight.reshape(own_rows, width)
         own = lax.dynamic_slice_in_dim(flat, near * features, features, axis=1)
         other = lax.dynamic_slice_in_dim(flat, (1 - near) * features, features, axis=1)
-        return own, lax.ppermute(other, "near", SWAP)
+        return own, swap(other, "near")
 
     down_halves, up_halves = halves(down_weight), halves(up_weight)
     down_own = stack(*down_halves, ())
-    if chained:
-        far_places = jnp.asarray(CHAIN, jnp.int32)[lax.axis_index("far")]
-        reached = chain_gather(down_own)
-        down_pieces = chain_finish(down_own, *reached)
-        up_own = stack(*up_halves, reached[2:])
-        up_reached = chain_gather(up_own)
+    far_places = jnp.arange(far_count, dtype=jnp.int32)
+    if paired:
+        high_place = far_places // PAIR ^ lax.axis_index("high")
+        far_places = (far_places % PAIR ^ lax.axis_index("low")) * PAIR + high_place
+        beside = swap(down_own, "high")
+        down_pieces = [down_own, beside, swap(down_own, "low"), swap(beside, "low")]
+        up_own = stack(*up_halves, (beside,))
+        up_beside = swap(up_own, "high")
+        up_low = swap(stack(*up_halves, down_pieces[2:]), "low")
+        up_pieces = [up_own, up_beside, up_low, swap(up_beside, "low")]
     else:
-        far_places = jnp.arange(far_count, dtype=jnp.int32)
-        down_pieces = [(lax.all_gather(down_own, "far", tiled=True),)]
-        up_own = stack(*up_halves, ())
+        down_pieces = [lax.all_gather(down_own, FAR, tiled=True)]
+        up_pieces = [lax.all_gather(stack(*up_halves, ()), FAR, tiled=True)]
     packed, activation, scaled = pack_tokens(
         far_places, expert_ids.T, router_gates.T, saved_hidden, token_grads, members,
         local_experts, (down_halves[1], up_halves[1]),
@@ -442,13 +402,8 @@
     received = exchange(packed, GROUP)
 
     projected = project(received, down_pieces, tok_count, wide)
-    if chained:
-        beside, across, across_far = up_reached
-        up_pieces = chain_finish(up_own, beside, across, pass_on(across_far, (projected,)))
-    else:
-        up_pieces = [(lax.all_gather(up_own, "far", tiled=True),)]
     partial_value = down_partial(
-        received, tok_count, wide, own_rows * NEAR * far_count, far_count if chained else 1,
+        received, tok_count, wide, own_rows * PAIR * far_count, far_count if paired else 1,
         (projected,),
     )
     parts = exchange(projected, GROUP)
@@ -462,11 +417,14 @@
     )(parts, activation, scaled)
     rows_back = input_rows(received, exchange(hidden_grad, GROUP), up_pieces)
     input_grads = unpack_tokens(exchange(rows_back, GROUP))
-    if chained:
-        sums = chain_scatter(partial_value, (hidden_grad,), (rows_back,))
+
+    if paired:
+        own, beside, low, low_beside = partial_value
+        (beside,) = add_pairs([(beside, swap(low_beside, "low"))], (hidden_grad,))
+        sums = add(own, swap(low, "low"), swap(beside, "high"))
     else:
-        sums = lax.psum_scatter(partial_value[0], "far", scatter_dimension=0, tiled=True)
-    kept, passed = sums[:own_rows], lax.ppermute(sums[own_rows:], "near", SWAP)
+        sums = lax.psum_scatter(partial_value[0], FAR, scatter_dimension=0, tiled=True)
+    kept, passed = sums[:own_rows], swap(sums[own_rows:], "near")
     down_grads = jnp.concatenate(
         [jnp.where(near == 0, kept, passed), jnp.where(near == 0, passed, kept)], axis=1
     ).reshape(down_weight.shape)
@@ -475,12 +433,13 @@
 
 def solution(mesh):
     sizes = [mesh.shape[name] for name in ("expert", "inner", "outer")]
+    expert = ("high", "near", "low")
     split = Mesh(
-        mesh.devices.reshape(sizes[0] // NEAR, NEAR, *sizes[1:]),
-        ("far", "near", "inner", "outer"),
-    )
-    rows = P(("far", "near", "inner", "outer"), None)
-    weights = P(("far", "near"), None, ("inner", "outer"))
+        mesh.devices.reshape(sizes[0] // PAIR**2, PAIR, PAIR, *sizes[1:]),
+        (*expert, "inner", "outer"),
+    )
+    rows = P((*expert, "inner", "outer"), None)
+    weights = P(expert, None, ("inner", "outer"))
     return jax.shard_map(
         body,
         mesh=split,

time: 182 us -> 189 us (1.038)
  waiting for transfers between devices: 73.1 us -> 117 us
  starting transfers between devices: 54.7 us -> 34.5 us
  blocking collectives: 8.82 us -> 0 us
  Pallas kernels: 21.6 us -> 17.7 us
  local copies, waits for them, and re-layouts: 19.7 us -> 17.1 us
    ppermute x18 -> x12, waiting for transfers between devices: 73.1 us -> 115 us  [swap(): return lax.ppermute(value, axis, SWAP)]
    ppermute x18 -> x12, starting transfers between devices: 43.6 us -> 16.5 us  [swap(): return lax.ppermute(value, axis, SWAP)]
    all_to_all x1 -> x0, blocking collectives: 8.82 us -> none  [exchange(): return lax.all_to_all(value, axes, split_axis=0, concat_axis=0, tiled=True)]
    all_to_all x3 -> x4, starting transfers between devices: 11.1 us -> 18 us  [exchange(): return lax.all_to_all(value, axes, split_axis=0, concat_axis=0, tiled=True)]
    pallas_call x2 -> x1, Pallas kernels: 3.59 us -> 0.12 us  [add_pairs(): pl.pallas_call(functools.partial(add_kernel, len(pairs)), in_specs=[*[pl....]
    unnamed x54 -> x44, local copies, waits for them, and re-layouts: 15.3 us -> 14.1 us
    pallas_call x3 -> x2, Pallas kernels: 11 us -> 9.78 us  [the longest x1 6.01 us: input_rows(): pl.pallas_call(input_kernel, grid=(sources // 2,), in_specs=[pl.BlockSpec...]
  transfers between devices with their start and end apart: 21 -> 16, of which waited for: 10 -> 11; matrix products, arithmetic and copies ran while one was open for 2% -> 2% of each run, Pallas kernels for 10% -> 5%
where the time goes in v8:
time: 189 us; the launch traced here: 188 us
  waiting for transfers between devices  117 us (62%)
  starting transfers between devices  34.5 us (18%)
  Pallas kernels  17.7 us (9%)
  local copies, waits for them, and re-layouts  17.1 us (9%)
    ppermute x12, waiting for transfers between devices, swap(): return lax.ppermute(value, axis, SWAP)  115 us
    all_to_all x4, starting transfers between devices, exchange(): return lax.all_to_all(value, axes, split_axis=0, concat_axis=0, tiled=True)  18 us
    ppermute x12, starting transfers between devices, swap(): return lax.ppermute(value, axis, SWAP)  16.5 us
    unnamed x44, local copies, waits for them, and re-layouts  14.1 us
    pallas_call x1, Pallas kernels, input_rows(): pl.pallas_call(input_kernel, grid=(sources // 2,), in_specs=[pl.BlockSpec...  6.01 us
  transfers between devices with their start and end apart: 16, of which 11 were waited for; matrix products, arithmetic and copies ran while one was open for 2% of the time, Pallas kernels for 5%

profile of v8, /device:TPU:0, one launch (start us, length us, event | category | flops | bytes accessed | tf_op | source)
XLA Modules:
  0.0 188.2 jit_solution(13862626377803325548)
XLA Ops:
  0.6 0.0 copy-start.20
  0.6 0.0 copy-start.21
  0.7 0.0 copy-start.19
  0.7 1.2 constant_dynamic-slice_fusion.1
  1.9 3.1 %collective-permute-start = (bf16[128,1024]{1,0:T(8,128)(2,1)S(1)}, bf16[128,1024]{1,0:T(8,128)(2,1)S(1)}, u32[]{:S(2)}, u32[]{:S(2)}) collective-permute-start(bf16[128,1024]{1,0:T(8,128)(2,1)S(1)} %get-tuple-element.26), channel_id=1, source_target_pairs={{0,8},{8,0},{1,9},{9,1},{2,10},{10,2},{3,11},{11,3},{4,12},{12,4},... | collective-permute-start | bytes 786440 | tf_op jit(solution)/shard_map/ppermute | solution.py:361
  5.0 1.8 constant_dynamic-slice_fusion
  6.8 0.0 collective-permute-start.1
  6.8 5.3 %collective-permute-done.refs_0_.other_ref = bf16[128,1024]{1,0:T(8,128)(2,1)S(1)} collective-permute-done((bf16[128,1024]{1,0:T(8,128)(2,1)S(1)}, bf16[128,1024]{1,0:T(8,128)(2,1)S(1)}, u32[]{:S(2)}, u32[]{:S(2)}) %collective-permute-start) | collective-permute-done | bytes 262176 | tf_op jit(solution)/shard_map/ppermute | solution.py:361
  12.1 4.8 %collective-permute-done.1.refs_1_.other_ref = bf16[128,1024]{1,0:T(8,128)(2,1)S(1)} collective-permute-done((bf16[128,1024]{1,0:T(8,128)(2,1)}, bf16[128,1024]{1,0:T(8,128)(2,1)S(1)}, u32[]{:S(2)}, u32[]{:S(2)}) %collective-permute-start.1) | collective-permute-done | bytes 262176 | tf_op jit(solution)/shard_map/ppermute | solution.py:361
  16.9 1.2 shard_map.85
  18.1 1.5 copy-done.2
  19.6 3.9 %all-to-all-start = ((bf16[8,160,1024]{2,1,0:T(8,128)(2,1)}), bf16[8,160,1024]{2,1,0:T(8,128)(2,1)S(1)}, u32[]{:S(2)}, u32[]{:S(2)}) async-start(bf16[8,160,1024]{2,1,0:T(8,128)(2,1)} %copy-done.2), calls=%async_computation | async-start | bytes 5242880 | tf_op jit(solution)/shard_map/all_to_all | solution.py:357
  23.5 0.9 copy-done.6
  24.5 0.0 copy-start.9
  24.5 2.7 %collective-permute-start.2 = (bf16[256,1024]{1,0:T(8,128)(2,1)S(1)}, bf16[256,1024]{1,0:T(8,128)(2,1)S(1)}, u32[]{:S(2)}, u32[]{:S(2)}) collective-permute-start(bf16[256,1024]{1,0:T(8,128)(2,1)S(1)} %shard_map.86.refs_0_), channel_id=1, source_target_pairs={{0,16},{16,0},{1,17},{17,1},{2,18},{18,2},{3,19},{19,3},{4,20},{20... | collective-permute-start | bytes 1572872 | tf_op jit(solution)/shard_map/ppermute | solution.py:361
  27.2 1.5 collective-permute-start.3
  28.7 35.3 %collective-permute-done.2.refs_1_.refs_0_ = bf16[256,1024]{1,0:T(8,128)(2,1)S(1)} collective-permute-done((bf16[256,1024]{1,0:T(8,128)(2,1)S(1)}, bf16[256,1024]{1,0:T(8,128)(2,1)S(1)}, u32[]{:S(2)}, u32[]{:S(2)}) %collective-permute-start.2) | collective-permute-done | bytes 524320 | tf_op jit(solution)/shard_map/ppermute | solution.py:361
  64.0 1.5 collective-permute-start.4
  65.5 0.8 shard_map.89.refs_0_
  66.3 3.4 %collective-permute-start.5 = (bf16[256,1024]{1,0:T(8,128)(2,1)}, bf16[256,1024]{1,0:T(8,128)(2,1)}, u32[]{:S(2)}, u32[]{:S(2)}) collective-permute-start(bf16[256,1024]{1,0:T(8,128)(2,1)} %shard_map.89.refs_0_), channel_id=1, source_target_pairs={{0,16},{16,0},{1,17},{17,1},{2,18},{18,2},{3,19},{19,3},{4,20},{20... | collective-permute-start | bytes 1572872 | tf_op jit(solution)/shard_map/ppermute | solution.py:361
  69.7 0.0 collective-permute-done.3.refs_2_.refs_0_
  69.7 0.8 copy-done.11
  70.5 7.2 %collective-permute-done.4.refs_3_.refs_1_ = bf16[256,1024]{1,0:T(8,128)(2,1)S(1)} collective-permute-done((bf16[256,1024]{1,0:T(8,128)(2,1)S(1)}, bf16[256,1024]{1,0:T(8,128)(2,1)S(1)}, u32[]{:S(2)}, u32[]{:S(2)}) %collective-permute-start.4) | collective-permute-done | bytes 524320 | tf_op jit(solution)/shard_map/ppermute | solution.py:361
  77.7 0.8 copy-done.14
  78.5 0.0 all-to-all-done.received_ref
  78.5 1.0 copy-done.8
  79.6 1.0 copy-done.10
  80.6 1.0 copy-done.12
  81.7 1.0 copy-done.15
  82.7 3.8 %shard_map.87.refs_0_ = bf16[8,128,128]{2,1,0:T(8,128)(2,1)S(1)} custom-call(bf16[8,160,1024]{2,1,0:T(8,128)(2,1)S(1)} %all-to-all-done.received_ref, bf16[256,1024]{1,0:T(8,128)(2,1)S(1)} %copy-done.10, bf16[256,1024]{1,0:T(8,128)(2,1)S(1)} %copy-done.8, bf16[256,1024]{1,0:T(8,128)(2,1)S(1)} %copy-done.12, bf16[256,1024]{1,0:T(8,128)(2,1)S(1)} %copy-done.15), custom_call_target="tpu_custom_call" | custom-call | flops 2147483648 | bytes 6291456 | tf_op jit(solution)/shard_map/pallas_call | solution.py:279
  86.5 0.7 copy-done.17
  87.2 6.6 %all-to-all-start.1 = ((bf16[8,128,128]{2,1,0:T(8,128)(2,1)}), bf16[8,128,128]{2,1,0:T(8,128)(2,1)S(1)}, u32[]{:S(2)}, u32[]{:S(2)}) async-start(bf16[8,128,128]{2,1,0:T(8,128)(2,1)} %copy-done.17), calls=%async_computation.1 | async-start | bytes 524288 | tf_op jit(solution)/shard_map/all_to_all | solution.py:357
  93.9 1.0 copy-done.13
  94.9 1.0 copy-done.16
  95.9 0.8 shard_map.90
  96.8 1.5 collective-permute-start.6
  98.3 0.0 collective-permute-done.5.refs_1_
  98.3 0.5 collective-permute-start.7
  98.8 1.5 all-to-all-done.1.parts_ref
  100.3 0.8 shard_map.88
  101.1 3.4 %all-to-all-start.2 = ((bf16[8,128,128]{2,1,0:T(8,128)(2,1)}), bf16[8,128,128]{2,1,0:T(8,128)(2,1)S(1)}, u32[]{:S(2)}, u32[]{:S(2)}) async-start(bf16[8,128,128]{2,1,0:T(8,128)(2,1)} %get-tuple-element.15.refs_2_), calls=%async_computation.2 | async-start | bytes 524288 | tf_op jit(solution)/shard_map/all_to_all | solution.py:357
  104.5 7.3 %collective-permute-done.6.refs_2_ = bf16[256,1024]{1,0:T(8,128)(2,1)} collective-permute-done((bf16[256,1024]{1,0:T(8,128)(2,1)}, bf16[256,1024]{1,0:T(8,128)(2,1)}, u32[]{:S(2)}, u32[]{:S(2)}) %collective-permute-start.6) | collective-permute-done | bytes 524320 | tf_op jit(solution)/shard_map/ppermute | solution.py:361
  111.8 10.9 %collective-permute-done.7.refs_3_ = bf16[256,1024]{1,0:T(8,128)(2,1)} collective-permute-done((bf16[256,1024]{1,0:T(8,128)(2,1)}, bf16[256,1024]{1,0:T(8,128)(2,1)}, u32[]{:S(2)}, u32[]{:S(2)}) %collective-permute-start.7) | collective-permute-done | bytes 524320 | tf_op jit(solution)/shard_map/ppermute | solution.py:361
  122.6 0.0 all-to-all-done.2.hidden_ref
  122.6 0.0 copy-done
  122.7 6.0 %shard_map.91 = bf16[8,128,1024]{2,1,0:T(8,128)(2,1)S(1)} custom-call(bf16[8,160,1024]{2,1,0:T(8,128)(2,1)S(1)} %all-to-all-done.received_ref, bf16[8,128,128]{2,1,0:T(8,128)(2,1)S(1)} %all-to-all-done.2.hidden_ref, bf16[256,1024]{1,0:T(8,128)(2,1)} %shard_map.89.refs_0_, bf16[256,1024]{1,0:T(8,128)(2,1)} %collective-permute-done.5.refs_1_, ...), custom_call_target="tpu_custom_call" | custom-call | flops 2147483648 | bytes 6291456 | tf_op jit(solution)/shard_map/pallas_call | solution.py:337
  128.7 0.0 copy-start.4
  128.7 1.3 copy-done.4
  130.0 4.0 %all-to-all-start.3 = ((bf16[8,128,1024]{2,1,0:T(8,128)(2,1)}), bf16[8,128,1024]{2,1,0:T(8,128)(2,1)S(1)}, u32[]{:S(2)}, u32[]{:S(2)}) async-start(bf16[8,128,1024]{2,1,0:T(8,128)(2,1)} %copy-done.4), calls=%async_computation.3 | async-start | bytes 4194304 | tf_op jit(solution)/shard_map/all_to_all | solution.py:357
  134.0 1.7 copy-done.1
  135.7 2.4 %shard_map.93 = (bf16[256,1024]{1,0:T(8,128)(2,1)S(1)}, bf16[256,1024]{1,0:T(8,128)(2,1)S(1)}, bf16[256,1024]{1,0:T(8,128)(2,1)S(1)}, bf16[256,1024]{1,0:T(8,128)(2,1)S(1)}) custom-call(bf16[8,160,1024]{2,1,0:T(8,128)(2,1)S(1)} %copy-done.1, bf16[8,128,128]{2,1,0:T(8,128)(2,1)S(1)} %copy-done.18), custom_call_target="tpu_custom_call" | custom-call | flops 2147483648 | bytes 6291456 | tf_op jit(solution)/shard_map/pallas_call | solution.py:218
  138.1 1.6 collective-permute-start.9
  139.7 0.5 collective-permute-start.8
  140.2 12.7 %collective-permute-done.9.refs_1_ = bf16[256,1024]{1,0:T(8,128)(2,1)S(1)} collective-permute-done((bf16[256,1024]{1,0:T(8,128)(2,1)S(1)}, bf16[256,1024]{1,0:T(8,128)(2,1)S(1)}, u32[]{:S(2)}, u32[]{:S(2)}) %collective-permute-start.9) | collective-permute-done | bytes 524320 | tf_op jit(solution)/shard_map/ppermute | solution.py:361
  152.9 0.1 shard_map.94
  153.0 0.2 collective-permute-start.10
  153.2 10.6 %collective-permute-done.8 = bf16[256,1024]{1,0:T(8,128)(2,1)S(1)} collective-permute-done((bf16[256,1024]{1,0:T(8,128)(2,1)S(1)}, bf16[256,1024]{1,0:T(8,128)(2,1)S(1)}, u32[]{:S(2)}, u32[]{:S(2)}) %collective-permute-start.8) | collective-permute-done | bytes 524320 | tf_op jit(solution)/shard_map/ppermute | solution.py:361
  163.8 14.7 %collective-permute-done.10 = bf16[256,1024]{1,0:T(8,128)(2,1)S(1)} collective-permute-done((bf16[256,1024]{1,0:T(8,128)(2,1)S(1)}, bf16[256,1024]{1,0:T(8,128)(2,1)S(1)}, u32[]{:S(2)}, u32[]{:S(2)}) %collective-permute-start.10) | collective-permute-done | bytes 524320 | tf_op jit(solution)/shard_map/ppermute | solution.py:361
  178.4 0.3 add_convert_fusion
  178.8 0.1 collective-permute-start.11
  178.8 6.7 %collective-permute-done.11 = bf16[128,1024]{1,0:T(8,128)(2,1)S(1)} collective-permute-done((bf16[128,1024]{1,0:T(8,128)(2,1)S(1)}, bf16[128,1024]{1,0:T(8,128)(2,1)S(1)}, u32[]{:S(2)}, u32[]{:S(2)}) %collective-permute-start.11) | collective-permute-done | bytes 262176 | tf_op jit(solution)/shard_map/ppermute | solution.py:361
  185.5 0.8 pad_maximum_fusion
  186.4 0.0 all-to-all-done.3.parts_ref
  186.4 1.8 shard_map.92
  (29 shorter events, 0.1 us)
Async XLA Ops:
  0.6 16.3 %copy-start.20 = (s32[128,2]{0,1:T(2,128)S(1)}, s32[128,2]{0,1:T(2,128)}, u32[]{:S(2)}) copy-start(s32[128,2]{0,1:T(2,128)} %param.8) | copy-start | bytes 3076
  0.6 16.3 %copy-start.21 = (bf16[128,2]{0,1:T(2,128)(2,1)S(1)}, bf16[128,2]{0,1:T(2,128)(2,1)}, u32[]{:S(2)}) copy-start(bf16[128,2]{0,1:T(2,128)(2,1)} %param.7) | copy-start | bytes 1540
  0.7 16.3 %copy-start.19 = (bf16[128,128]{1,0:T(8,128)(2,1)S(1)}, bf16[128,128]{1,0:T(8,128)(2,1)}, u32[]{:S(2)}) copy-start(bf16[128,128]{1,0:T(8,128)(2,1)} %preact_ref.1) | copy-start | bytes 98308
  0.7 16.3 %copy-start.3 = (bf16[128,8192]{1,0:T(8,128)(2,1)S(1)}, bf16[128,8192]{1,0:T(8,128)(2,1)}, u32[]{:S(2)}) copy-start(bf16[128,8192]{1,0:T(8,128)(2,1)} %tokens_ref.1) | copy-start | bytes 6291460
  1.9 10.2 %collective-permute-start = (bf16[128,1024]{1,0:T(8,128)(2,1)S(1)}, bf16[128,1024]{1,0:T(8,128)(2,1)S(1)}, u32[]{:S(2)}, u32[]{:S(2)}) collective-permute-start(bf16[128,1024]{1,0:T(8,128)(2,1)S(1)} %get-tuple-element.26), channel_id=1, source_target_pairs={{0,8},{8,0},{1,9},{9,1},{2,10},{10,2},{3,11},{11,3},{4,12},{12,4},... | collective-permute-start | bytes 786440 | tf_op jit(solution)/shard_map/ppermute | solution.py:361
  6.8 10.2 %collective-permute-start.1 = (bf16[128,1024]{1,0:T(8,128)(2,1)}, bf16[128,1024]{1,0:T(8,128)(2,1)S(1)}, u32[]{:S(2)}, u32[]{:S(2)}) collective-permute-start(bf16[128,1024]{1,0:T(8,128)(2,1)} %get-tuple-element.24), channel_id=1, source_target_pairs={{0,8},{8,0},{1,9},{9,1},{2,10},{10,2},{3,11},{11,3},{4,12},{12,4},... | collective-permute-start | bytes 786440 | tf_op jit(solution)/shard_map/ppermute | solution.py:361
  12.1 7.5 %copy-start.5 = (bf16[128,1024]{1,0:T(8,128)(2,1)}, bf16[128,1024]{1,0:T(8,128)(2,1)S(1)}, u32[]{:S(2)}) copy-start(bf16[128,1024]{1,0:T(8,128)(2,1)S(1)} %collective-permute-done.refs_0_.other_ref) | copy-start | bytes 786436
  18.1 1.5 copy-start.2
  19.6 58.9 %all-to-all-start = ((bf16[8,160,1024]{2,1,0:T(8,128)(2,1)}), bf16[8,160,1024]{2,1,0:T(8,128)(2,1)S(1)}, u32[]{:S(2)}, u32[]{:S(2)}) async-start(bf16[8,160,1024]{2,1,0:T(8,128)(2,1)} %copy-done.2), calls=%async_computation | async-start | bytes 5242880 | tf_op jit(solution)/shard_map/all_to_all | solution.py:357
  23.5 0.9 copy-start.6
  24.5 45.2 %copy-start.9 = (bf16[256,1024]{1,0:T(8,128)(2,1)}, bf16[256,1024]{1,0:T(8,128)(2,1)S(1)}, u32[]{:S(2)}) copy-start(bf16[256,1024]{1,0:T(8,128)(2,1)S(1)} %shard_map.86.refs_0_) | copy-start | bytes 1572868
  24.5 39.4 %collective-permute-start.2 = (bf16[256,1024]{1,0:T(8,128)(2,1)S(1)}, bf16[256,1024]{1,0:T(8,128)(2,1)S(1)}, u32[]{:S(2)}, u32[]{:S(2)}) collective-permute-start(bf16[256,1024]{1,0:T(8,128)(2,1)S(1)} %shard_map.86.refs_0_), channel_id=1, source_target_pairs={{0,16},{16,0},{1,17},{17,1},{2,18},{18,2},{3,19},{19,3},{4,20},{20... | collective-permute-start | bytes 1572872 | tf_op jit(solution)/shard_map/ppermute | solution.py:361
  27.2 42.5 %collective-permute-start.3 = (bf16[256,1024]{1,0:T(8,128)(2,1)S(1)}, bf16[256,1024]{1,0:T(8,128)(2,1)S(1)}, u32[]{:S(2)}, u32[]{:S(2)}) collective-permute-start(bf16[256,1024]{1,0:T(8,128)(2,1)S(1)} %shard_map.86.refs_0_), channel_id=1, source_target_pairs={{0,4},{4,0},{1,5},{5,1},{2,6},{6,2},{3,7},{7,3},{8,12},{12,8},{9,1... | collective-permute-start | bytes 1572872 | tf_op jit(solution)/shard_map/ppermute | solution.py:361
  64.0 5.7 %copy-start.7 = (bf16[256,1024]{1,0:T(8,128)(2,1)}, bf16[256,1024]{1,0:T(8,128)(2,1)S(1)}, u32[]{:S(2)}) copy-start(bf16[256,1024]{1,0:T(8,128)(2,1)S(1)} %collective-permute-done.2.refs_1_.refs_0_) | copy-start | bytes 1572868
  64.0 13.8 %collective-permute-start.4 = (bf16[256,1024]{1,0:T(8,128)(2,1)S(1)}, bf16[256,1024]{1,0:T(8,128)(2,1)S(1)}, u32[]{:S(2)}, u32[]{:S(2)}) collective-permute-start(bf16[256,1024]{1,0:T(8,128)(2,1)S(1)} %collective-permute-done.2.refs_1_.refs_0_), channel_id=1, source_target_pairs={{0,4},{4,0},{1,5},{5,1},{2,6},{6,2},{3,7},{7,3},{8,12},{12,8},{9,1... | collective-permute-start | bytes 1572872 | tf_op jit(solution)/shard_map/ppermute | solution.py:361
  66.3 32.0 %collective-permute-start.5 = (bf16[256,1024]{1,0:T(8,128)(2,1)}, bf16[256,1024]{1,0:T(8,128)(2,1)}, u32[]{:S(2)}, u32[]{:S(2)}) collective-permute-start(bf16[256,1024]{1,0:T(8,128)(2,1)} %shard_map.89.refs_0_), channel_id=1, source_target_pairs={{0,16},{16,0},{1,17},{17,1},{2,18},{18,2},{3,19},{19,3},{4,20},{20... | collective-permute-start | bytes 1572872 | tf_op jit(solution)/shard_map/ppermute | solution.py:361
  69.7 0.8 copy-start.11
  77.7 0.8 copy-start.14
  78.5 1.0 copy-start.8
  79.6 1.0 copy-start.10
  80.6 1.0 copy-start.12
  81.7 1.0 copy-start.15
  82.7 39.9 %copy-start = (bf16[8,160,1024]{2,1,0:T(8,128)(2,1)}, bf16[8,160,1024]{2,1,0:T(8,128)(2,1)S(1)}, u32[]{:S(2)}) copy-start(bf16[8,160,1024]{2,1,0:T(8,128)(2,1)S(1)} %all-to-all-done.received_ref) | copy-start | bytes 7864324
  86.5 0.7 copy-start.17
  87.2 13.1 %all-to-all-start.1 = ((bf16[8,128,128]{2,1,0:T(8,128)(2,1)}), bf16[8,128,128]{2,1,0:T(8,128)(2,1)S(1)}, u32[]{:S(2)}, u32[]{:S(2)}) async-start(bf16[8,128,128]{2,1,0:T(8,128)(2,1)} %copy-done.17), calls=%async_computation.1 | async-start | bytes 524288 | tf_op jit(solution)/shard_map/all_to_all | solution.py:357
  93.8 1.0 copy-start.13
  94.9 1.0 copy-start.16
  96.8 15.0 %collective-permute-start.6 = (bf16[256,1024]{1,0:T(8,128)(2,1)}, bf16[256,1024]{1,0:T(8,128)(2,1)}, u32[]{:S(2)}, u32[]{:S(2)}) collective-permute-start(bf16[256,1024]{1,0:T(8,128)(2,1)} %shard_map.90), channel_id=1, source_target_pairs={{0,4},{4,0},{1,5},{5,1},{2,6},{6,2},{3,7},{7,3},{8,12},{12,8},{9,1... | collective-permute-start | bytes 1572872 | tf_op jit(solution)/shard_map/ppermute | solution.py:361
  98.3 24.4 %collective-permute-start.7 = (bf16[256,1024]{1,0:T(8,128)(2,1)}, bf16[256,1024]{1,0:T(8,128)(2,1)}, u32[]{:S(2)}, u32[]{:S(2)}) collective-permute-start(bf16[256,1024]{1,0:T(8,128)(2,1)} %collective-permute-done.5.refs_1_), channel_id=1, source_target_pairs={{0,4},{4,0},{1,5},{5,1},{2,6},{6,2},{3,7},{7,3},{8,12},{12,8},{9,1... | collective-permute-start | bytes 1572872 | tf_op jit(solution)/shard_map/ppermute | solution.py:361
  101.1 21.6 %all-to-all-start.2 = ((bf16[8,128,128]{2,1,0:T(8,128)(2,1)}), bf16[8,128,128]{2,1,0:T(8,128)(2,1)S(1)}, u32[]{:S(2)}, u32[]{:S(2)}) async-start(bf16[8,128,128]{2,1,0:T(8,128)(2,1)} %get-tuple-element.15.refs_2_), calls=%async_computation.2 | async-start | bytes 524288 | tf_op jit(solution)/shard_map/all_to_all | solution.py:357
  128.7 1.3 copy-start.4
  130.0 4.0 %copy-start.18 = (bf16[8,128,128]{2,1,0:T(8,128)(2,1)S(1)}, bf16[8,128,128]{2,1,0:T(8,128)(2,1)}, u32[]{:S(2)}) copy-start(bf16[8,128,128]{2,1,0:T(8,128)(2,1)} %copy-done.17) | copy-start | bytes 786436
  130.0 56.4 %all-to-all-start.3 = ((bf16[8,128,1024]{2,1,0:T(8,128)(2,1)}), bf16[8,128,1024]{2,1,0:T(8,128)(2,1)S(1)}, u32[]{:S(2)}, u32[]{:S(2)}) async-start(bf16[8,128,1024]{2,1,0:T(8,128)(2,1)} %copy-done.4), calls=%async_computation.3 | async-start | bytes 4194304 | tf_op jit(solution)/shard_map/all_to_all | solution.py:357
  134.0 1.7 copy-start.1
  138.1 14.8 %collective-permute-start.9 = (bf16[256,1024]{1,0:T(8,128)(2,1)S(1)}, bf16[256,1024]{1,0:T(8,128)(2,1)S(1)}, u32[]{:S(2)}, u32[]{:S(2)}) collective-permute-start(bf16[256,1024]{1,0:T(8,128)(2,1)S(1)} %get-tuple-element.20), channel_id=1, source_target_pairs={{0,4},{4,0},{1,5},{5,1},{2,6},{6,2},{3,7},{7,3},{8,12},{12,8},{9,1... | collective-permute-start | bytes 1572872 | tf_op jit(solution)/shard_map/ppermute | solution.py:361
  139.7 24.1 %collective-permute-start.8 = (bf16[256,1024]{1,0:T(8,128)(2,1)S(1)}, bf16[256,1024]{1,0:T(8,128)(2,1)S(1)}, u32[]{:S(2)}, u32[]{:S(2)}) collective-permute-start(bf16[256,1024]{1,0:T(8,128)(2,1)S(1)} %get-tuple-element.18), channel_id=1, source_target_pairs={{0,4},{4,0},{1,5},{5,1},{2,6},{6,2},{3,7},{7,3},{8,12},{12,8},{9,1... | collective-permute-start | bytes 1572872 | tf_op jit(solution)/shard_map/ppermute | solution.py:361
  153.0 25.4 %collective-permute-start.10 = (bf16[256,1024]{1,0:T(8,128)(2,1)S(1)}, bf16[256,1024]{1,0:T(8,128)(2,1)S(1)}, u32[]{:S(2)}, u32[]{:S(2)}) collective-permute-start(bf16[256,1024]{1,0:T(8,128)(2,1)S(1)} %shard_map.94), channel_id=1, source_target_pairs={{0,16},{16,0},{1,17},{17,1},{2,18},{18,2},{3,19},{19,3},{4,20},{20... | collective-permute-start | bytes 1572872 | tf_op jit(solution)/shard_map/ppermute | solution.py:361
  178.8 6.8 %collective-permute-start.11 = (bf16[128,1024]{1,0:T(8,128)(2,1)S(1)}, bf16[128,1024]{1,0:T(8,128)(2,1)S(1)}, u32[]{:S(2)}, u32[]{:S(2)}) collective-permute-start(bf16[128,1024]{1,0:T(8,128)(2,1)S(1)} %slice.9), channel_id=1, source_target_pairs={{0,8},{8,0},{1,9},{9,1},{2,10},{10,2},{3,11},{11,3},{4,12},{12,4},... | collective-permute-start | bytes 786440 | tf_op jit(solution)/shard_map/ppermute | solution.py:361

commit v9 on v8

--- a/solution.py
+++ b/solution.py
@@ -290,7 +290,8 @@
     )(received, *pieces)
 
 
-def hidden_kernel(parts_ref, activation_ref, scaled_ref, hidden_ref, gate_ref):
+def hidden_kernel(parts_ref, activation_ref, scaled_ref, *refs):
+    hidden_ref, gate_ref = refs[-2:]
     projected = parts_ref[0].astype(jnp.float32)
     for source in range(1, parts_ref.shape[0]):
         projected = projected + parts_ref[source].astype(jnp.float32)
@@ -310,8 +311,8 @@
         hidden_ref[source] = hidden
 
 
-def input_kernel(received_ref, hidden_ref, *refs):
-    piece_refs, out_ref, full, spread = refs[:-3], refs[-3], refs[-2], refs[-1]
+def input_kernel(count, received_ref, hidden_ref, *refs):
+    piece_refs, (out_ref, full, spread) = refs[:count], refs[-3:]
     pl.when(pl.program_id(0) == 0)(lambda: join(piece_refs, full))
     sources, rows, wide = hidden_ref.shape
     low, first, second = lane_numbers(received_ref, rows, wide)
@@ -331,16 +332,17 @@
     )
 
 
-def input_rows(received, hidden_grad, pieces):
+def input_rows(received, hidden_grad, pieces, before):
     sources, rows, wide = hidden_grad.shape
     joined, features = sum(piece.shape[0] for piece in pieces), pieces[0].shape[1]
     return pl.pallas_call(
-        input_kernel,
+        functools.partial(input_kernel, len(pieces)),
         grid=(sources // 2,),
         in_specs=[
             pl.BlockSpec((2, received.shape[1], features), lambda i: (i, 0, 0)),
             pl.BlockSpec((2, rows, wide), lambda i: (i, 0, 0)),
             *[pl.BlockSpec(piece.shape, lambda i: (0, 0)) for piece in pieces],
+            *[pl.BlockSpec(memory_space=pl.ANY) for _ in before],
         ],
         out_specs=pl.BlockSpec((2, rows, features), lambda i: (i, 0, 0)),
         out_shape=jax.ShapeDtypeStruct((sources, rows, features), jnp.bfloat16),
@@ -350,7 +352,7 @@
         ],
         compiler_params=params(),
         cost_estimate=cost(sources * rows, joined, features),
-    )(received, hidden_grad, *pieces)
+    )(received, hidden_grad, *pieces, *before)
 
 
 def exchange(value, axes):
@@ -382,12 +384,14 @@
 
     down_halves, up_halves = halves(down_weight), halves(up_weight)
     down_own = stack(*down_halves, ())
+    first = [down_halves[1], up_halves[1]]
     far_places = jnp.arange(far_count, dtype=jnp.int32)
     if paired:
         high_place = far_places // PAIR ^ lax.axis_index("high")
         far_places = (far_places % PAIR ^ lax.axis_index("low")) * PAIR + high_place
         beside = swap(down_own, "high")
         down_pieces = [down_own, beside, swap(down_own, "low"), swap(beside, "low")]
+        first += [down_pieces[2]]
         up_own = stack(*up_halves, (beside,))
         up_beside = swap(up_own, "high")
         up_low = swap(stack(*up_halves, down_pieces[2:]), "low")
@@ -397,7 +401,7 @@
         up_pieces = [lax.all_gather(stack(*up_halves, ()), FAR, tiled=True)]
     packed, activation, scaled = pack_tokens(
         far_places, expert_ids.T, router_gates.T, saved_hidden, token_grads, members,
-        local_experts, (down_halves[1], up_halves[1]),
+        local_experts, first,
     )
     received = exchange(packed, GROUP)
 
@@ -409,21 +413,26 @@
     parts = exchange(projected, GROUP)
     hidden_grad, gate_grads = pl.pallas_call(
         hidden_kernel,
+        in_specs=[
+            *[pl.BlockSpec(memory_space=pltpu.VMEM) for _ in range(3)],
+            *[pl.BlockSpec(memory_space=pl.ANY) for _ in partial_value],
+        ],
         out_shape=(
             jax.ShapeDtypeStruct((members, tok_count, wide), jnp.bfloat16),
             jax.ShapeDtypeStruct((2, tok_count), jnp.bfloat16),
         ),
         compiler_params=params(),
-    )(parts, activation, scaled)
-    rows_back = input_rows(received, exchange(hidden_grad, GROUP), up_pieces)
-    input_grads = unpack_tokens(exchange(rows_back, GROUP))
-
+    )(parts, activation, scaled, *partial_value)
     if paired:
         own, beside, low, low_beside = partial_value
-        (beside,) = add_pairs([(beside, swap(low_beside, "low"))], (hidden_grad,))
-        sums = add(own, swap(low, "low"), swap(beside, "high"))
+        before = add_pairs([(beside, swap(low_beside, "low"))], ())
+        sums = add(own, swap(low, "low"), swap(before[0], "high"))
     else:
+        before = ()
         sums = lax.psum_scatter(partial_value[0], FAR, scatter_dimension=0, tiled=True)
+    rows_back = input_rows(received, exchange(hidden_grad, GROUP), up_pieces, before)
+    input_grads = unpack_tokens(exchange(rows_back, GROUP))
+
     kept, passed = sums[:own_rows], swap(sums[own_rows:], "near")
     down_grads = jnp.concatenate(
         [jnp.where(near == 0, kept, passed), jnp.where(near == 0, passed, kept)], axis=1

time: 189 us -> 208 us (1.10)
  waiting for transfers between devices: 117 us -> 124 us
  starting transfers between devices: 34.5 us -> 39.5 us
  Pallas kernels: 17.7 us -> 21.4 us
  local copies, waits for them, and re-layouts: 17.1 us -> 19.8 us
    ppermute x12, waiting for transfers between devices: 115 us -> 124 us  [swap(): return lax.ppermute(value, axis, SWAP)]
    ppermute x12, starting transfers between devices: 16.5 us -> 21.1 us  [swap(): return lax.ppermute(value, axis, SWAP)]
    unnamed x44 -> x50, local copies, waits for them, and re-layouts: 14.1 us -> 16.8 us
  transfers between devices with their start and end apart: 16 -> 16, of which waited for: 11 -> 11; matrix products, arithmetic and copies ran while one was open for 2% -> 1% of each run, Pallas kernels for 5% -> 6%
where the time goes in v9:
time: 208 us; the launch traced here: 206 us
  waiting for transfers between devices  124 us (60%)
  starting transfers between devices  39.5 us (19%)
  Pallas kernels  21.4 us (10%)
  local copies, waits for them, and re-layouts  19.8 us (10%)
    ppermute x12, waiting for transfers between devices, swap(): return lax.ppermute(value, axis, SWAP)  124 us
    ppermute x12, starting transfers between devices, swap(): return lax.ppermute(value, axis, SWAP)  21.1 us
    all_to_all x4, starting transfers between devices, exchange(): return lax.all_to_all(value, axes, split_axis=0, concat_axis=0, tiled=True)  18.3 us
    unnamed x50, local copies, waits for them, and re-layouts  16.8 us
    pallas_call x1, Pallas kernels, input_rows(): pl.pallas_call(functools.partial(input_kernel, len(pieces)), grid=(source...  5.99 us
    pallas_call x1, Pallas kernels, project(): pl.pallas_call(project_kernel, grid=(sources // 2,), in_specs=[pl.BlockSp...  4.83 us
  transfers between devices with their start and end apart: 16, of which 11 were waited for; matrix products, arithmetic and copies ran while one was open for 1% of the time, Pallas kernels for 6%

profile of v9, /device:TPU:0, one launch (start us, length us, event | category | flops | bytes accessed | tf_op | source)
XLA Modules:
  0.0 206.5 jit_solution(14874812254562858037)
XLA Ops:
  0.7 1.2 constant_dynamic-slice_fusion.1
  1.9 3.1 %collective-permute-start = (bf16[128,1024]{1,0:T(8,128)(2,1)S(1)}, bf16[128,1024]{1,0:T(8,128)(2,1)S(1)}, u32[]{:S(2)}, u32[]{:S(2)}) collective-permute-start(bf16[128,1024]{1,0:T(8,128)(2,1)S(1)} %get-tuple-element.26), channel_id=1, source_target_pairs={{0,8},{8,0},{1,9},{9,1},{2,10},{10,2},{3,11},{11,3},{4,12},{12,4},... | collective-permute-start | bytes 786440 | tf_op jit(solution)/shard_map/ppermute | solution.py:363
  5.0 6.3 %collective-permute-done.other_ref.refs_0_ = bf16[128,1024]{1,0:T(8,128)(2,1)S(1)} collective-permute-done((bf16[128,1024]{1,0:T(8,128)(2,1)S(1)}, bf16[128,1024]{1,0:T(8,128)(2,1)S(1)}, u32[]{:S(2)}, u32[]{:S(2)}) %collective-permute-start) | collective-permute-done | bytes 262176 | tf_op jit(solution)/shard_map/ppermute | solution.py:363
  11.3 0.8 shard_map.85.refs_0_
  12.1 1.7 collective-permute-start.2
  13.8 1.8 constant_dynamic-slice_fusion
  15.6 1.6 collective-permute-start.1
  17.1 5.5 %collective-permute-done.1.refs_1_.other_ref = bf16[128,1024]{1,0:T(8,128)(2,1)S(1)} collective-permute-done((bf16[128,1024]{1,0:T(8,128)(2,1)}, bf16[128,1024]{1,0:T(8,128)(2,1)S(1)}, u32[]{:S(2)}, u32[]{:S(2)}) %collective-permute-start.1) | collective-permute-done | bytes 262176 | tf_op jit(solution)/shard_map/ppermute | solution.py:363
  22.7 2.8 %collective-permute-done.2.refs_2_.refs_0_ = bf16[256,1024]{1,0:T(8,128)(2,1)S(1)} collective-permute-done((bf16[256,1024]{1,0:T(8,128)(2,1)}, bf16[256,1024]{1,0:T(8,128)(2,1)S(1)}, u32[]{:S(2)}, u32[]{:S(2)}) %collective-permute-start.2) | collective-permute-done | bytes 524320 | tf_op jit(solution)/shard_map/ppermute | solution.py:363
  25.4 0.0 copy-start.22
  25.5 0.8 copy-done.22
  26.3 1.1 shard_map.86
  27.4 1.5 copy-done
  28.9 3.6 %all-to-all-start = ((bf16[8,160,1024]{2,1,0:T(8,128)(2,1)}), bf16[8,160,1024]{2,1,0:T(8,128)(2,1)S(1)}, u32[]{:S(2)}, u32[]{:S(2)}) async-start(bf16[8,160,1024]{2,1,0:T(8,128)(2,1)} %copy-done), calls=%async_computation | async-start | bytes 5242880 | tf_op jit(solution)/shard_map/all_to_all | solution.py:359
  32.5 2.6 %collective-permute-start.3 = (bf16[256,1024]{1,0:T(8,128)(2,1)}, bf16[256,1024]{1,0:T(8,128)(2,1)S(1)}, u32[]{:S(2)}, u32[]{:S(2)}) collective-permute-start(bf16[256,1024]{1,0:T(8,128)(2,1)} %shard_map.85.refs_0_), channel_id=1, source_target_pairs={{0,16},{16,0},{1,17},{17,1},{2,18},{18,2},{3,19},{19,3},{4,20},{20... | collective-permute-start | bytes 1572872 | tf_op jit(solution)/shard_map/ppermute | solution.py:363
  35.1 37.9 %collective-permute-done.3.refs_1_.refs_0_ = bf16[256,1024]{1,0:T(8,128)(2,1)S(1)} collective-permute-done((bf16[256,1024]{1,0:T(8,128)(2,1)}, bf16[256,1024]{1,0:T(8,128)(2,1)S(1)}, u32[]{:S(2)}, u32[]{:S(2)}) %collective-permute-start.3) | collective-permute-done | bytes 524320 | tf_op jit(solution)/shard_map/ppermute | solution.py:363
  73.1 1.5 collective-permute-start.4
  74.6 0.8 shard_map.90.refs_0_
  75.4 3.3 %collective-permute-start.5 = (bf16[256,1024]{1,0:T(8,128)(2,1)}, bf16[256,1024]{1,0:T(8,128)(2,1)}, u32[]{:S(2)}, u32[]{:S(2)}) collective-permute-start(bf16[256,1024]{1,0:T(8,128)(2,1)} %shard_map.90.refs_0_), channel_id=1, source_target_pairs={{0,16},{16,0},{1,17},{17,1},{2,18},{18,2},{3,19},{19,3},{4,20},{20... | collective-permute-start | bytes 1572872 | tf_op jit(solution)/shard_map/ppermute | solution.py:363
  78.7 8.1 %collective-permute-done.4.refs_3_.refs_1_ = bf16[256,1024]{1,0:T(8,128)(2,1)S(1)} collective-permute-done((bf16[256,1024]{1,0:T(8,128)(2,1)S(1)}, bf16[256,1024]{1,0:T(8,128)(2,1)S(1)}, u32[]{:S(2)}, u32[]{:S(2)}) %collective-permute-start.4) | collective-permute-done | bytes 524320 | tf_op jit(solution)/shard_map/ppermute | solution.py:363
  86.8 0.8 copy-done.16
  87.6 1.0 copy-done.7
  88.7 1.0 copy-done.15
  89.7 1.0 copy-done.17
  90.8 4.8 %shard_map.87.refs_0_ = bf16[8,128,128]{2,1,0:T(8,128)(2,1)S(1)} custom-call(bf16[8,160,1024]{2,1,0:T(8,128)(2,1)S(1)} %all-to-all-done.received_ref, bf16[256,1024]{1,0:T(8,128)(2,1)} %shard_map.85.refs_0_, bf16[256,1024]{1,0:T(8,128)(2,1)S(1)} %copy-done.15, bf16[256,1024]{1,0:T(8,128)(2,1)S(1)} %copy-done.7, bf16[256,1024]{1,0:T(8,128)(2,1)S(1)} %copy-done.17), custom_call_target="tpu_custom_call" | custom-call | flops 2147483648 | bytes 6291456 | tf_op jit(solution)/shard_map/pallas_call | solution.py:279
  95.6 0.7 copy-done.19
  96.3 6.5 %all-to-all-start.1 = ((bf16[8,128,128]{2,1,0:T(8,128)(2,1)}), bf16[8,128,128]{2,1,0:T(8,128)(2,1)S(1)}, u32[]{:S(2)}, u32[]{:S(2)}) async-start(bf16[8,128,128]{2,1,0:T(8,128)(2,1)} %copy-done.19), calls=%async_computation.1 | async-start | bytes 524288 | tf_op jit(solution)/shard_map/all_to_all | solution.py:359
  102.8 1.0 copy-done.8
  103.9 1.0 copy-done.18
  104.9 0.8 shard_map.91
  105.7 0.2 copy-done.20
  105.9 3.2 %shard_map.88 = (bf16[256,1024]{1,0:T(8,128)(2,1)S(1)}, bf16[256,1024]{1,0:T(8,128)(2,1)S(1)}, bf16[256,1024]{1,0:T(8,128)(2,1)S(1)}, bf16[256,1024]{1,0:T(8,128)(2,1)}) custom-call(bf16[8,160,1024]{2,1,0:T(8,128)(2,1)S(1)} %all-to-all-done.received_ref, bf16[8,128,128]{2,1,0:T(8,128)(2,1)S(1)} %copy-done.20), custom_call_target="tpu_custom_call" | custom-call | flops 2147483648 | bytes 6291456 | tf_op jit(solution)/shard_map/pallas_call | solution.py:218
  109.1 0.8 copy-done.3
  110.0 0.8 copy-done.9
  110.8 1.5 collective-permute-start.8
  112.3 0.5 collective-permute-start.6
  112.8 1.5 collective-permute-start.7
  114.3 0.0 all-to-all-done.1.parts_ref
  114.3 1.0 copy-done.4
  115.4 1.0 copy-done.10
  116.4 0.7 shard_map.89
  117.1 0.7 copy-done.21
  117.8 4.2 %all-to-all-start.2 = ((bf16[8,128,128]{2,1,0:T(8,128)(2,1)}), bf16[8,128,128]{2,1,0:T(8,128)(2,1)S(1)}, u32[]{:S(2)}, u32[]{:S(2)}) async-start(bf16[8,128,128]{2,1,0:T(8,128)(2,1)} %copy-done.21), calls=%async_computation.2 | async-start | bytes 524288 | tf_op jit(solution)/shard_map/all_to_all | solution.py:359
  122.1 3.7 %collective-permute-done.8.refs_1_ = bf16[256,1024]{1,0:T(8,128)(2,1)} collective-permute-done((bf16[256,1024]{1,0:T(8,128)(2,1)}, bf16[256,1024]{1,0:T(8,128)(2,1)}, u32[]{:S(2)}, u32[]{:S(2)}) %collective-permute-start.8) | collective-permute-done | bytes 524320 | tf_op jit(solution)/shard_map/ppermute | solution.py:363
  125.8 1.2 shard_map.92.refs_4_
  127.0 0.0 copy-start.12
  127.0 0.8 copy-done.12
  127.8 9.3 %collective-permute-done.6.refs_2_ = bf16[256,1024]{1,0:T(8,128)(2,1)} collective-permute-done((bf16[256,1024]{1,0:T(8,128)(2,1)}, bf16[256,1024]{1,0:T(8,128)(2,1)}, u32[]{:S(2)}, u32[]{:S(2)}) %collective-permute-start.6) | collective-permute-done | bytes 524320 | tf_op jit(solution)/shard_map/ppermute | solution.py:363
  137.0 10.8 %collective-permute-done.7.refs_3_ = bf16[256,1024]{1,0:T(8,128)(2,1)} collective-permute-done((bf16[256,1024]{1,0:T(8,128)(2,1)}, bf16[256,1024]{1,0:T(8,128)(2,1)}, u32[]{:S(2)}, u32[]{:S(2)}) %collective-permute-start.7) | collective-permute-done | bytes 524320 | tf_op jit(solution)/shard_map/ppermute | solution.py:363
  147.9 0.0 all-to-all-done.2.hidden_ref
  147.9 1.0 copy-done.13
  148.9 6.0 %shard_map.93 = bf16[8,128,1024]{2,1,0:T(8,128)(2,1)S(1)} custom-call(bf16[8,160,1024]{2,1,0:T(8,128)(2,1)S(1)} %all-to-all-done.received_ref, bf16[8,128,128]{2,1,0:T(8,128)(2,1)S(1)} %all-to-all-done.2.hidden_ref, bf16[256,1024]{1,0:T(8,128)(2,1)} %shard_map.90.refs_0_, bf16[256,1024]{1,0:T(8,128)(2,1)} %collective-permute-done.5.refs_1_, ...), custom_call_target="tpu_custom_call" | custom-call | flops 2147483648 | bytes 6291456 | tf_op jit(solution)/shard_map/pallas_call | solution.py:338
  154.9 0.0 copy-start.2
  154.9 1.3 copy-done.2
  156.2 4.0 %all-to-all-start.3 = ((bf16[8,128,1024]{2,1,0:T(8,128)(2,1)}), bf16[8,128,1024]{2,1,0:T(8,128)(2,1)S(1)}, u32[]{:S(2)}, u32[]{:S(2)}) async-start(bf16[8,128,1024]{2,1,0:T(8,128)(2,1)} %copy-done.2), calls=%async_computation.3 | async-start | bytes 4194304 | tf_op jit(solution)/shard_map/all_to_all | solution.py:359
  160.2 1.6 collective-permute-start.9
  161.8 0.1 collective-permute-start.10
  161.9 12.7 %collective-permute-done.9 = bf16[256,1024]{1,0:T(8,128)(2,1)S(1)} collective-permute-done((bf16[256,1024]{1,0:T(8,128)(2,1)S(1)}, bf16[256,1024]{1,0:T(8,128)(2,1)S(1)}, u32[]{:S(2)}, u32[]{:S(2)}) %collective-permute-start.9) | collective-permute-done | bytes 524320 | tf_op jit(solution)/shard_map/ppermute | solution.py:363
  174.6 20.6 %collective-permute-done.10 = bf16[256,1024]{1,0:T(8,128)(2,1)S(1)} collective-permute-done((bf16[256,1024]{1,0:T(8,128)(2,1)}, bf16[256,1024]{1,0:T(8,128)(2,1)S(1)}, u32[]{:S(2)}, u32[]{:S(2)}) %collective-permute-start.10) | collective-permute-done | bytes 524320 | tf_op jit(solution)/shard_map/ppermute | solution.py:363
  195.1 0.3 add_convert_fusion
  195.4 2.2 %collective-permute-start.11 = (bf16[128,1024]{1,0:T(8,128)(2,1)S(1)}, bf16[128,1024]{1,0:T(8,128)(2,1)S(1)}, u32[]{:S(2)}, u32[]{:S(2)}) collective-permute-start(bf16[128,1024]{1,0:T(8,128)(2,1)S(1)} %slice.9), channel_id=1, source_target_pairs={{0,8},{8,0},{1,9},{9,1},{2,10},{10,2},{3,11},{11,3},{4,12},{12,4},... | collective-permute-start | bytes 786440 | tf_op jit(solution)/shard_map/ppermute | solution.py:363
  197.7 6.1 %collective-permute-done.11 = bf16[128,1024]{1,0:T(8,128)(2,1)S(1)} collective-permute-done((bf16[128,1024]{1,0:T(8,128)(2,1)S(1)}, bf16[128,1024]{1,0:T(8,128)(2,1)S(1)}, u32[]{:S(2)}, u32[]{:S(2)}) %collective-permute-start.11) | collective-permute-done | bytes 262176 | tf_op jit(solution)/shard_map/ppermute | solution.py:363
  203.8 0.8 pad_maximum_fusion
  204.6 1.8 shard_map.94
  (35 shorter events, 0.1 us)
Async XLA Ops:
  0.6 24.8 %copy-start.23 = (s32[128,2]{0,1:T(2,128)S(1)}, s32[128,2]{0,1:T(2,128)}, u32[]{:S(2)}) copy-start(s32[128,2]{0,1:T(2,128)} %param.8) | copy-start | bytes 3076
  0.6 24.8 %copy-start.24 = (bf16[128,2]{0,1:T(2,128)(2,1)S(1)}, bf16[128,2]{0,1:T(2,128)(2,1)}, u32[]{:S(2)}) copy-start(bf16[128,2]{0,1:T(2,128)(2,1)} %param.7) | copy-start | bytes 1540
  0.7 24.8 %copy-start.1 = (bf16[128,8192]{1,0:T(8,128)(2,1)S(1)}, bf16[128,8192]{1,0:T(8,128)(2,1)}, u32[]{:S(2)}) copy-start(bf16[128,8192]{1,0:T(8,128)(2,1)} %tokens_ref.1) | copy-start | bytes 6291460
  1.9 9.4 %collective-permute-start = (bf16[128,1024]{1,0:T(8,128)(2,1)S(1)}, bf16[128,1024]{1,0:T(8,128)(2,1)S(1)}, u32[]{:S(2)}, u32[]{:S(2)}) collective-permute-start(bf16[128,1024]{1,0:T(8,128)(2,1)S(1)} %get-tuple-element.26), channel_id=1, source_target_pairs={{0,8},{8,0},{1,9},{9,1},{2,10},{10,2},{3,11},{11,3},{4,12},{12,4},... | collective-permute-start | bytes 786440 | tf_op jit(solution)/shard_map/ppermute | solution.py:363
  12.1 13.3 %collective-permute-start.2 = (bf16[256,1024]{1,0:T(8,128)(2,1)}, bf16[256,1024]{1,0:T(8,128)(2,1)S(1)}, u32[]{:S(2)}, u32[]{:S(2)}) collective-permute-start(bf16[256,1024]{1,0:T(8,128)(2,1)} %shard_map.85.refs_0_), channel_id=1, source_target_pairs={{0,4},{4,0},{1,5},{5,1},{2,6},{6,2},{3,7},{7,3},{8,12},{12,8},{9,1... | collective-permute-start | bytes 1572872 | tf_op jit(solution)/shard_map/ppermute | solution.py:363
  15.6 7.1 %collective-permute-start.1 = (bf16[128,1024]{1,0:T(8,128)(2,1)}, bf16[128,1024]{1,0:T(8,128)(2,1)S(1)}, u32[]{:S(2)}, u32[]{:S(2)}) collective-permute-start(bf16[128,1024]{1,0:T(8,128)(2,1)} %get-tuple-element.24), channel_id=1, source_target_pairs={{0,8},{8,0},{1,9},{9,1},{2,10},{10,2},{3,11},{11,3},{4,12},{12,4},... | collective-permute-start | bytes 786440 | tf_op jit(solution)/shard_map/ppermute | solution.py:363
  25.4 3.5 %copy-start.6 = (bf16[256,1024]{1,0:T(8,128)(2,1)}, bf16[256,1024]{1,0:T(8,128)(2,1)S(1)}, u32[]{:S(2)}) copy-start(bf16[256,1024]{1,0:T(8,128)(2,1)S(1)} %collective-permute-done.2.refs_2_.refs_0_) | copy-start | bytes 1572868
  25.4 0.8 copy-start.22
  27.4 1.5 copy-start
  28.9 58.7 %all-to-all-start = ((bf16[8,160,1024]{2,1,0:T(8,128)(2,1)}), bf16[8,160,1024]{2,1,0:T(8,128)(2,1)S(1)}, u32[]{:S(2)}, u32[]{:S(2)}) async-start(bf16[8,160,1024]{2,1,0:T(8,128)(2,1)} %copy-done), calls=%async_computation | async-start | bytes 5242880 | tf_op jit(solution)/shard_map/all_to_all | solution.py:359
  32.5 40.5 %collective-permute-start.3 = (bf16[256,1024]{1,0:T(8,128)(2,1)}, bf16[256,1024]{1,0:T(8,128)(2,1)S(1)}, u32[]{:S(2)}, u32[]{:S(2)}) collective-permute-start(bf16[256,1024]{1,0:T(8,128)(2,1)} %shard_map.85.refs_0_), channel_id=1, source_target_pairs={{0,16},{16,0},{1,17},{17,1},{2,18},{18,2},{3,19},{19,3},{4,20},{20... | collective-permute-start | bytes 1572872 | tf_op jit(solution)/shard_map/ppermute | solution.py:363
  73.1 5.6 %copy-start.14 = (bf16[256,1024]{1,0:T(8,128)(2,1)}, bf16[256,1024]{1,0:T(8,128)(2,1)S(1)}, u32[]{:S(2)}) copy-start(bf16[256,1024]{1,0:T(8,128)(2,1)S(1)} %collective-permute-done.3.refs_1_.refs_0_) | copy-start | bytes 1572868
  73.1 13.8 %collective-permute-start.4 = (bf16[256,1024]{1,0:T(8,128)(2,1)S(1)}, bf16[256,1024]{1,0:T(8,128)(2,1)S(1)}, u32[]{:S(2)}, u32[]{:S(2)}) collective-permute-start(bf16[256,1024]{1,0:T(8,128)(2,1)S(1)} %collective-permute-done.3.refs_1_.refs_0_), channel_id=1, source_target_pairs={{0,4},{4,0},{1,5},{5,1},{2,6},{6,2},{3,7},{7,3},{8,12},{12,8},{9,1... | collective-permute-start | bytes 1572872 | tf_op jit(solution)/shard_map/ppermute | solution.py:363
  75.4 37.4 %collective-permute-start.5 = (bf16[256,1024]{1,0:T(8,128)(2,1)}, bf16[256,1024]{1,0:T(8,128)(2,1)}, u32[]{:S(2)}, u32[]{:S(2)}) collective-permute-start(bf16[256,1024]{1,0:T(8,128)(2,1)} %shard_map.90.refs_0_), channel_id=1, source_target_pairs={{0,16},{16,0},{1,17},{17,1},{2,18},{18,2},{3,19},{19,3},{4,20},{20... | collective-permute-start | bytes 1572872 | tf_op jit(solution)/shard_map/ppermute | solution.py:363
  86.8 0.8 copy-start.16
  87.6 1.0 copy-start.7
  88.7 1.0 copy-start.15
  89.7 1.0 copy-start.17
  95.6 0.7 copy-start.19
  96.3 18.0 %all-to-all-start.1 = ((bf16[8,128,128]{2,1,0:T(8,128)(2,1)}), bf16[8,128,128]{2,1,0:T(8,128)(2,1)S(1)}, u32[]{:S(2)}, u32[]{:S(2)}) async-start(bf16[8,128,128]{2,1,0:T(8,128)(2,1)} %copy-done.19), calls=%async_computation.1 | async-start | bytes 524288 | tf_op jit(solution)/shard_map/all_to_all | solution.py:359
  102.8 1.0 copy-start.8
  103.9 1.0 copy-start.18
  104.9 1.0 copy-start.20
  109.1 0.8 copy-start.3
  110.0 0.8 copy-start.9
  110.8 15.0 %collective-permute-start.8 = (bf16[256,1024]{1,0:T(8,128)(2,1)}, bf16[256,1024]{1,0:T(8,128)(2,1)}, u32[]{:S(2)}, u32[]{:S(2)}) collective-permute-start(bf16[256,1024]{1,0:T(8,128)(2,1)} %get-tuple-element.18.refs_3_), channel_id=1, source_target_pairs={{0,4},{4,0},{1,5},{5,1},{2,6},{6,2},{3,7},{7,3},{8,12},{12,8},{9,1... | collective-permute-start | bytes 1572872 | tf_op jit(solution)/shard_map/ppermute | solution.py:363
  112.3 24.7 %collective-permute-start.6 = (bf16[256,1024]{1,0:T(8,128)(2,1)}, bf16[256,1024]{1,0:T(8,128)(2,1)}, u32[]{:S(2)}, u32[]{:S(2)}) collective-permute-start(bf16[256,1024]{1,0:T(8,128)(2,1)} %shard_map.91), channel_id=1, source_target_pairs={{0,4},{4,0},{1,5},{5,1},{2,6},{6,2},{3,7},{7,3},{8,12},{12,8},{9,1... | collective-permute-start | bytes 1572872 | tf_op jit(solution)/shard_map/ppermute | solution.py:363
  112.8 35.1 %collective-permute-start.7 = (bf16[256,1024]{1,0:T(8,128)(2,1)}, bf16[256,1024]{1,0:T(8,128)(2,1)}, u32[]{:S(2)}, u32[]{:S(2)}) collective-permute-start(bf16[256,1024]{1,0:T(8,128)(2,1)} %collective-permute-done.5.refs_1_), channel_id=1, source_target_pairs={{0,4},{4,0},{1,5},{5,1},{2,6},{6,2},{3,7},{7,3},{8,12},{12,8},{9,1... | collective-permute-start | bytes 1572872 | tf_op jit(solution)/shard_map/ppermute | solution.py:363
  114.3 1.0 copy-start.4
  115.4 1.0 copy-start.10
  117.1 0.7 copy-start.21
  117.8 30.0 %all-to-all-start.2 = ((bf16[8,128,128]{2,1,0:T(8,128)(2,1)}), bf16[8,128,128]{2,1,0:T(8,128)(2,1)S(1)}, u32[]{:S(2)}, u32[]{:S(2)}) async-start(bf16[8,128,128]{2,1,0:T(8,128)(2,1)} %copy-done.21), calls=%async_computation.2 | async-start | bytes 524288 | tf_op jit(solution)/shard_map/all_to_all | solution.py:359
  127.0 0.8 copy-start.12
  147.9 1.0 copy-start.13
  154.9 1.3 copy-start.2
  156.2 4.0 %copy-start.11 = (bf16[256,1024]{1,0:T(8,128)(2,1)S(1)}, bf16[256,1024]{1,0:T(8,128)(2,1)}, u32[]{:S(2)}) copy-start(bf16[256,1024]{1,0:T(8,128)(2,1)} %copy-done.9) | copy-start | bytes 1572868
  156.2 38.9 %copy-start.5 = (bf16[256,1024]{1,0:T(8,128)(2,1)S(1)}, bf16[256,1024]{1,0:T(8,128)(2,1)}, u32[]{:S(2)}) copy-start(bf16[256,1024]{1,0:T(8,128)(2,1)} %copy-done.3) | copy-start | bytes 1572868
  156.2 48.4 %all-to-all-start.3 = ((bf16[8,128,1024]{2,1,0:T(8,128)(2,1)}), bf16[8,128,1024]{2,1,0:T(8,128)(2,1)S(1)}, u32[]{:S(2)}, u32[]{:S(2)}) async-start(bf16[8,128,1024]{2,1,0:T(8,128)(2,1)} %copy-done.2), calls=%async_computation.3 | async-start | bytes 4194304 | tf_op jit(solution)/shard_map/all_to_all | solution.py:359
  160.2 14.3 %collective-permute-start.9 = (bf16[256,1024]{1,0:T(8,128)(2,1)S(1)}, bf16[256,1024]{1,0:T(8,128)(2,1)S(1)}, u32[]{:S(2)}, u32[]{:S(2)}) collective-permute-start(bf16[256,1024]{1,0:T(8,128)(2,1)S(1)} %copy-done.11), channel_id=1, source_target_pairs={{0,4},{4,0},{1,5},{5,1},{2,6},{6,2},{3,7},{7,3},{8,12},{12,8},{9,1... | collective-permute-start | bytes 1572872 | tf_op jit(solution)/shard_map/ppermute | solution.py:363
  161.8 33.3 %collective-permute-start.10 = (bf16[256,1024]{1,0:T(8,128)(2,1)}, bf16[256,1024]{1,0:T(8,128)(2,1)S(1)}, u32[]{:S(2)}, u32[]{:S(2)}) collective-permute-start(bf16[256,1024]{1,0:T(8,128)(2,1)} %copy-done.12), channel_id=1, source_target_pairs={{0,16},{16,0},{1,17},{17,1},{2,18},{18,2},{3,19},{19,3},{4,20},{20... | collective-permute-start | bytes 1572872 | tf_op jit(solution)/shard_map/ppermute | solution.py:363
  195.4 8.3 %collective-permute-start.11 = (bf16[128,1024]{1,0:T(8,128)(2,1)S(1)}, bf16[128,1024]{1,0:T(8,128)(2,1)S(1)}, u32[]{:S(2)}, u32[]{:S(2)}) collective-permute-start(bf16[128,1024]{1,0:T(8,128)(2,1)S(1)} %slice.9), channel_id=1, source_target_pairs={{0,8},{8,0},{1,9},{9,1},{2,10},{10,2},{3,11},{11,3},{4,12},{12,4},... | collective-permute-start | bytes 786440 | tf_op jit(solution)/shard_map/ppermute | solution.py:363

commit v10 on v9

--- a/solution.py
+++ b/solution.py
@@ -111,8 +111,7 @@
     ids = ids_ref[...]
     local = lax.rem(ids, local_experts)
     line = lax.div(ids, local_experts)
-    near = lax.rem(lax.div(line, PAIR), PAIR)
-    far = lax.div(line, PAIR * PAIR) * PAIR + lax.rem(line, PAIR)
+    far, near = lax.div(line, PAIR), lax.rem(line, PAIR)
     far_place = jnp.zeros_like(far)
     for at in range(far_count):
         far_place = jnp.where(far == at, far_ref[at], far_place)
@@ -251,16 +250,17 @@
 
 
 def project_kernel(received_ref, *refs):
-    piece_refs, out_ref = refs[:-1], refs[-1]
+    piece_refs, (out_ref, full) = refs[:-2], refs[-2:]
+    pl.when(pl.program_id(0) == 0)(lambda: join(piece_refs, full))
     sources, rows, wide = out_ref.shape
     low, first, second = lane_numbers(received_ref, rows, wide)
     tokens = token_rows(received_ref, rows)
     sums = [jnp.zeros((sources * rows, wide), jnp.float32) for _ in range(2)]
     number = 0.0
-    for ref, start in [(ref, at) for ref in piece_refs for at in range(0, ref.shape[0], BLOCK)]:
+    for start in range(0, full.shape[0], BLOCK):
         product = lax.dot_general(
             tokens,
-            ref[start : start + BLOCK, :],
+            full[start : start + BLOCK, :],
             (((1,), (1,)), ((), ())),
             preferred_element_type=jnp.float32,
         )
@@ -276,6 +276,7 @@
 
 def project(received, pieces, rows, wide):
     sources, height, features = received.shape
+    joined = sum(piece.shape[0] for piece in pieces)
     return pl.pallas_call(
         project_kernel,
         grid=(sources // 2,),
@@ -285,13 +286,13 @@
         ],
         out_specs=pl.BlockSpec((2, rows, wide), lambda i: (i, 0, 0)),
         out_shape=jax.ShapeDtypeStruct((sources, rows, wide), jnp.bfloat16),
-        compiler_params=params(),
-        cost_estimate=cost(sources * rows, features, sum(p.shape[0] for p in pieces)),
+        scratch_shapes=[pltpu.VMEM((joined, features), jnp.bfloat16)],
+        compiler_params=params(),
+        cost_estimate=cost(sources * rows, features, joined),
     )(received, *pieces)
 
 
-def hidden_kernel(parts_ref, activation_ref, scaled_ref, *refs):
-    hidden_ref, gate_ref = refs[-2:]
+def hidden_kernel(parts_ref, activation_ref, scaled_ref, hidden_ref, gate_ref):
     projected = parts_ref[0].astype(jnp.float32)
     for source in range(1, parts_ref.shape[0]):
         projected = projected + parts_ref[source].astype(jnp.float32)
@@ -383,21 +384,22 @@
         return own, swap(other, "near")
 
     down_halves, up_halves = halves(down_weight), halves(up_weight)
-    down_own = stack(*down_halves, ())
     first = [down_halves[1], up_halves[1]]
     far_places = jnp.arange(far_count, dtype=jnp.int32)
     if paired:
         high_place = far_places // PAIR ^ lax.axis_index("high")
         far_places = (far_places % PAIR ^ lax.axis_index("low")) * PAIR + high_place
-        beside = swap(down_own, "high")
-        down_pieces = [down_own, beside, swap(down_own, "low"), swap(beside, "low")]
-        first += [down_pieces[2]]
-        up_own = stack(*up_halves, (beside,))
+        beside = [swap(half, "high") for half in down_halves]
+        low = [swap(half, "low") for half in down_halves]
+        low_beside = [swap(half, "low") for half in beside]
+        down_pieces = [*down_halves, *beside, *low, *low_beside]
+        first += beside[:1]
+        up_own = stack(*up_halves, beside[1:])
         up_beside = swap(up_own, "high")
-        up_low = swap(stack(*up_halves, down_pieces[2:]), "low")
+        up_low = swap(stack(*up_halves, low_beside), "low")
         up_pieces = [up_own, up_beside, up_low, swap(up_beside, "low")]
     else:
-        down_pieces = [lax.all_gather(down_own, FAR, tiled=True)]
+        down_pieces = [lax.all_gather(stack(*down_halves, ()), FAR, tiled=True)]
         up_pieces = [lax.all_gather(stack(*up_halves, ()), FAR, tiled=True)]
     packed, activation, scaled = pack_tokens(
         far_places, expert_ids.T, router_gates.T, saved_hidden, token_grads, members,
@@ -413,16 +415,12 @@
     parts = exchange(projected, GROUP)
     hidden_grad, gate_grads = pl.pallas_call(
         hidden_kernel,
-        in_specs=[
-            *[pl.BlockSpec(memory_space=pltpu.VMEM) for _ in range(3)],
-            *[pl.BlockSpec(memory_space=pl.ANY) for _ in partial_value],
-        ],
         out_shape=(
             jax.ShapeDtypeStruct((members, tok_count, wide), jnp.bfloat16),
             jax.ShapeDtypeStruct((2, tok_count), jnp.bfloat16),
         ),
         compiler_params=params(),
-    )(parts, activation, scaled, *partial_value)
+    )(parts, activation, scaled)
     if paired:
         own, beside, low, low_beside = partial_value
         before = add_pairs([(beside, swap(low_beside, "low"))], ())
@@ -442,7 +440,7 @@
 
 def solution(mesh):
     sizes = [mesh.shape[name] for name in ("expert", "inner", "outer")]
-    expert = ("high", "near", "low")
+    expert = ("high", "low", "near")
     split = Mesh(
         mesh.devices.reshape(sizes[0] // PAIR**2, PAIR, PAIR, *sizes[1:]),
         (*expert, "inner", "outer"),

time: 208 us -> 175 us (0.84)
  waiting for transfers between devices: 124 us -> 91.2 us
  blocking collectives: 0 us -> 9.63 us
  starting transfers between devices: 39.5 us -> 30.2 us
    ppermute x12 -> x15, waiting for transfers between devices: 124 us -> 91.2 us  [swap(): return lax.ppermute(value, axis, SWAP)]
    all_to_all x0 -> x1, blocking collectives: none -> 9.63 us  [exchange(): return lax.all_to_all(value, axes, split_axis=0, concat_axis=0, tiled=True)]
    all_to_all x4 -> x3, starting transfers between devices: 18.3 us -> 11.1 us  [exchange(): return lax.all_to_all(value, axes, split_axis=0, concat_axis=0, tiled=True)]
    ppermute x12 -> x15, starting transfers between devices: 21.1 us -> 19.2 us  [swap(): return lax.ppermute(value, axis, SWAP)]
    unnamed x50 -> x58, local copies, waits for them, and re-layouts: 16.8 us -> 17.5 us
  transfers between devices with their start and end apart: 16 -> 18, of which waited for: 11 -> 11; matrix products, arithmetic and copies ran while one was open for 1% -> 2% of each run, Pallas kernels for 6% -> 6%
where the time goes in v10:
time: 175 us; the launch traced here: 174 us
  waiting for transfers between devices  91.2 us (52%)
  starting transfers between devices  30.2 us (17%)
  local copies, waits for them, and re-layouts  21.2 us (12%)
  Pallas kernels  19.8 us (11%)
  blocking collectives  9.63 us (6%)
    ppermute x15, waiting for transfers between devices, swap(): return lax.ppermute(value, axis, SWAP)  91.2 us
    ppermute x15, starting transfers between devices, swap(): return lax.ppermute(value, axis, SWAP)  19.2 us
    unnamed x58, local copies, waits for them, and re-layouts  17.5 us
    all_to_all x3, starting transfers between devices, exchange(): return lax.all_to_all(value, axes, split_axis=0, concat_axis=0, tiled=True)  11.1 us
    all_to_all x1, blocking collectives, exchange(): return lax.all_to_all(value, axes, split_axis=0, concat_axis=0, tiled=True)  9.63 us
    pallas_call x1, Pallas kernels, input_rows(): pl.pallas_call(functools.partial(input_kernel, len(pieces)), grid=(source...  5.99 us
    pallas_call x1, Pallas kernels, project(): pl.pallas_call(project_kernel, grid=(sources // 2,), in_specs=[pl.BlockSp...  3.95 us
    dynamic_slice x2, local copies, waits for them, and re-layouts, halves(): own = lax.dynamic_slice_in_dim(flat, near * features, features, axis=1)  3.67 us
  transfers between devices with their start and end apart: 18, of which 11 were waited for; matrix products, arithmetic and copies ran while one was open for 2% of the time, Pallas kernels for 6%

profile of v10, /device:TPU:0, one launch (start us, length us, event | category | flops | bytes accessed | tf_op | source)
XLA Modules:
  0.0 174.1 jit_solution(10538601575215361309)
XLA Ops:
  0.7 1.9 %constant_dynamic-slice_fusion.1 = (bf16[128,1024]{1,0:T(8,128)(2,1)S(1)}, bf16[128,1024]{1,0:T(8,128)(2,1)}) fusion(bf16[128,2048]{1,0:T(8,128)(2,1)} %bitcast.8, s32[]{:T(128)S(6)} %select_n.35, s32[]{:T(128)S(6)} %select_n.34), kind=kLoop, calls=%fused_computation.7 | loop fusion | bytes 1048584 | tf_op jit(solution)/shard_map/dynamic_slice | solution.py:382
  2.6 4.0 %collective-permute-start.2 = (bf16[128,1024]{1,0:T(8,128)(2,1)S(1)}, bf16[128,1024]{1,0:T(8,128)(2,1)S(1)}, u32[]{:S(2)}, u32[]{:S(2)}) collective-permute-start(bf16[128,1024]{1,0:T(8,128)(2,1)S(1)} %get-tuple-element.25.refs_0_), channel_id=1, source_target_pairs={{0,16},{16,0},{1,17},{17,1},{2,18},{18,2},{3,19},{19,3},{4,20},{20... | collective-permute-start | bytes 786440 | tf_op jit(solution)/shard_map/ppermute | solution.py:364
  6.6 1.5 collective-permute-start
  8.1 1.8 %constant_dynamic-slice_fusion = (bf16[128,1024]{1,0:T(8,128)(2,1)S(1)}, bf16[128,1024]{1,0:T(8,128)(2,1)}) fusion(bf16[128,2048]{1,0:T(8,128)(2,1)} %bitcast.9, s32[]{:T(128)S(6)} %select_n.35, s32[]{:T(128)S(6)} %select_n.34), kind=kLoop, calls=%fused_computation.6 | loop fusion | bytes 1048584 | tf_op jit(solution)/shard_map/dynamic_slice | solution.py:382
  9.9 0.5 collective-permute-start.1
  10.4 8.1 %collective-permute-done.2.refs_2_ = bf16[128,1024]{1,0:T(8,128)(2,1)S(1)} collective-permute-done((bf16[128,1024]{1,0:T(8,128)(2,1)S(1)}, bf16[128,1024]{1,0:T(8,128)(2,1)S(1)}, u32[]{:S(2)}, u32[]{:S(2)}) %collective-permute-start.2) | collective-permute-done | bytes 262176 | tf_op jit(solution)/shard_map/ppermute | solution.py:364
  18.6 1.7 collective-permute-done.1.refs_1_.other_ref
  20.3 0.9 copy-done.8
  21.2 0.9 copy-done.11
  22.2 0.8 copy-done.21
  22.9 1.1 shard_map.85
  24.1 1.5 copy-done
  25.5 3.7 %all-to-all-start = ((bf16[8,160,1024]{2,1,0:T(8,128)(2,1)}), bf16[8,160,1024]{2,1,0:T(8,128)(2,1)S(1)}, u32[]{:S(2)}, u32[]{:S(2)}) async-start(bf16[8,160,1024]{2,1,0:T(8,128)(2,1)} %copy-done), calls=%async_computation | async-start | bytes 5242880 | tf_op jit(solution)/shard_map/all_to_all | solution.py:360
  29.3 0.3 collective-permute-start.3
  29.6 2.9 %collective-permute-start.4 = (bf16[128,1024]{1,0:T(8,128)(2,1)S(1)}, bf16[128,1024]{1,0:T(8,128)(2,1)S(1)}, u32[]{:S(2)}, u32[]{:S(2)}) collective-permute-start(bf16[128,1024]{1,0:T(8,128)(2,1)S(1)} %get-tuple-element.25.refs_0_), channel_id=1, source_target_pairs={{0,8},{8,0},{1,9},{9,1},{2,10},{10,2},{3,11},{11,3},{4,12},{12,4},... | collective-permute-start | bytes 786440 | tf_op jit(solution)/shard_map/ppermute | solution.py:364
  32.5 0.0 collective-permute-start.6
  32.5 2.0 %collective-permute-start.5 = (bf16[128,1024]{1,0:T(8,128)(2,1)}, bf16[128,1024]{1,0:T(8,128)(2,1)S(1)}, u32[]{:S(2)}, u32[]{:S(2)}) collective-permute-start(bf16[128,1024]{1,0:T(8,128)(2,1)} %copy-done.10), channel_id=1, source_target_pairs={{0,8},{8,0},{1,9},{9,1},{2,10},{10,2},{3,11},{11,3},{4,12},{12,4},... | collective-permute-start | bytes 786440 | tf_op jit(solution)/shard_map/ppermute | solution.py:364
  34.5 10.3 %collective-permute-done.3.refs_3_.refs_0_ = bf16[128,1024]{1,0:T(8,128)(2,1)S(1)} collective-permute-done((bf16[128,1024]{1,0:T(8,128)(2,1)}, bf16[128,1024]{1,0:T(8,128)(2,1)S(1)}, u32[]{:S(2)}, u32[]{:S(2)}) %collective-permute-start.3) | collective-permute-done | bytes 262176 | tf_op jit(solution)/shard_map/ppermute | solution.py:364
  44.8 0.0 collective-permute-start.7
  44.8 0.9 shard_map.88.refs_0_
  45.7 1.8 %collective-permute-start.8 = (bf16[256,1024]{1,0:T(8,128)(2,1)}, bf16[256,1024]{1,0:T(8,128)(2,1)}, u32[]{:S(2)}, u32[]{:S(2)}) collective-permute-start(bf16[256,1024]{1,0:T(8,128)(2,1)} %shard_map.88.refs_0_), channel_id=1, source_target_pairs={{0,16},{16,0},{1,17},{17,1},{2,18},{18,2},{3,19},{19,3},{4,20},{20... | collective-permute-start | bytes 1572872 | tf_op jit(solution)/shard_map/ppermute | solution.py:364
  47.5 0.7 copy-done.25
  48.2 13.5 %collective-permute-done.6.refs_6_.refs_0_ = bf16[128,1024]{1,0:T(8,128)(2,1)S(1)} collective-permute-done((bf16[128,1024]{1,0:T(8,128)(2,1)}, bf16[128,1024]{1,0:T(8,128)(2,1)S(1)}, u32[]{:S(2)}, u32[]{:S(2)}) %collective-permute-start.6) | collective-permute-done | bytes 262176 | tf_op jit(solution)/shard_map/ppermute | solution.py:364
  61.6 0.7 copy-done.15
  62.3 4.9 %collective-permute-done.5.refs_5_ = bf16[128,1024]{1,0:T(8,128)(2,1)S(1)} collective-permute-done((bf16[128,1024]{1,0:T(8,128)(2,1)}, bf16[128,1024]{1,0:T(8,128)(2,1)S(1)}, u32[]{:S(2)}, u32[]{:S(2)}) %collective-permute-start.5) | collective-permute-done | bytes 262176 | tf_op jit(solution)/shard_map/ppermute | solution.py:364
  67.2 0.7 copy-done.27
  67.9 4.9 %collective-permute-done.7.refs_7_.refs_1_ = bf16[128,1024]{1,0:T(8,128)(2,1)S(1)} collective-permute-done((bf16[128,1024]{1,0:T(8,128)(2,1)S(1)}, bf16[128,1024]{1,0:T(8,128)(2,1)S(1)}, u32[]{:S(2)}, u32[]{:S(2)}) %collective-permute-start.7) | collective-permute-done | bytes 262176 | tf_op jit(solution)/shard_map/ppermute | solution.py:364
  72.8 0.7 copy-done.18
  73.5 0.0 all-to-all-done.received_ref
  73.5 0.9 copy-done.9
  74.5 0.9 copy-done.12
  75.4 0.9 copy-done.14
  76.4 0.9 copy-done.16
  77.3 0.9 copy-done.19
  78.3 0.9 copy-done.26
  79.2 0.9 copy-done.28
  80.2 4.0 %shard_map.86.refs_0_ = bf16[8,128,128]{2,1,0:T(8,128)(2,1)S(1)} custom-call(bf16[8,160,1024]{2,1,0:T(8,128)(2,1)S(1)} %all-to-all-done.received_ref, bf16[128,1024]{1,0:T(8,128)(2,1)S(1)} %get-tuple-element.25.refs_0_, bf16[128,1024]{1,0:T(8,128)(2,1)S(1)} %copy-done.12, bf16[128,1024]{1,0:T(8,128)(2,1)S(1)} %copy-done.9, bf16[128,1024]{1,0:T(8,128)(2,1)S(1)} %copy-done.14, ...), custom_call_target="tpu_custom_call" | custom-call | flops 2147483648 | bytes 6291456 | tf_op jit(solution)/shard_map/pallas_call | solution.py:280
  84.1 3.2 %shard_map.90 = (bf16[256,1024]{1,0:T(8,128)(2,1)S(1)}, bf16[256,1024]{1,0:T(8,128)(2,1)S(1)}, bf16[256,1024]{1,0:T(8,128)(2,1)S(1)}, bf16[256,1024]{1,0:T(8,128)(2,1)}) custom-call(bf16[8,160,1024]{2,1,0:T(8,128)(2,1)S(1)} %all-to-all-done.received_ref, bf16[8,128,128]{2,1,0:T(8,128)(2,1)S(1)} %shard_map.86.refs_0_), custom_call_target="tpu_custom_call" | custom-call | flops 2147483648 | bytes 6291456 | tf_op jit(solution)/shard_map/pallas_call | solution.py:217
  87.4 0.8 copy-done.3
  88.2 0.8 copy-done.5
  89.0 0.9 shard_map.89
  89.9 2.0 %collective-permute-start.9 = (bf16[256,1024]{1,0:T(8,128)(2,1)}, bf16[256,1024]{1,0:T(8,128)(2,1)}, u32[]{:S(2)}, u32[]{:S(2)}) collective-permute-start(bf16[256,1024]{1,0:T(8,128)(2,1)} %shard_map.89), channel_id=1, source_target_pairs={{0,8},{8,0},{1,9},{9,1},{2,10},{10,2},{3,11},{11,3},{4,12},{12,4},... | collective-permute-start | bytes 1572872 | tf_op jit(solution)/shard_map/ppermute | solution.py:364
  91.8 0.0 collective-permute-done.8.refs_1_
  91.8 0.1 collective-permute-start.10
  91.9 9.6 %all_to_all.20.parts_ref = bf16[8,128,128]{2,1,0:T(8,128)(2,1)S(1)} all-to-all(bf16[8,128,128]{2,1,0:T(8,128)(2,1)S(1)} %shard_map.86.refs_0_), channel_id=1, replica_groups=mesh['high'=2,'low'=2,'near'=2,'inner'=2,'outer'=2] {'inner','outer','ne..., dimensions={0} | all-to-all | bytes 524288 | tf_op jit(solution)/shard_map/all_to_all | solution.py:360
  101.5 0.8 shard_map.87
  102.3 3.4 %all-to-all-start.2 = ((bf16[8,128,128]{2,1,0:T(8,128)(2,1)}), bf16[8,128,128]{2,1,0:T(8,128)(2,1)S(1)}, u32[]{:S(2)}, u32[]{:S(2)}) async-start(bf16[8,128,128]{2,1,0:T(8,128)(2,1)} %get-tuple-element.15), calls=%async_computation.2 | async-start | bytes 524288 | tf_op jit(solution)/shard_map/all_to_all | solution.py:360
  105.7 1.0 copy-done.4
  106.7 1.2 shard_map.91.refs_4_
  107.9 7.4 %collective-permute-done.9.refs_2_ = bf16[256,1024]{1,0:T(8,128)(2,1)} collective-permute-done((bf16[256,1024]{1,0:T(8,128)(2,1)}, bf16[256,1024]{1,0:T(8,128)(2,1)}, u32[]{:S(2)}, u32[]{:S(2)}) %collective-permute-start.9) | collective-permute-done | bytes 524320 | tf_op jit(solution)/shard_map/ppermute | solution.py:364
  115.3 10.3 %collective-permute-done.10.refs_3_ = bf16[256,1024]{1,0:T(8,128)(2,1)} collective-permute-done((bf16[256,1024]{1,0:T(8,128)(2,1)}, bf16[256,1024]{1,0:T(8,128)(2,1)}, u32[]{:S(2)}, u32[]{:S(2)}) %collective-permute-start.10) | collective-permute-done | bytes 524320 | tf_op jit(solution)/shard_map/ppermute | solution.py:364
  125.6 6.0 %shard_map.92 = bf16[8,128,1024]{2,1,0:T(8,128)(2,1)S(1)} custom-call(bf16[8,160,1024]{2,1,0:T(8,128)(2,1)S(1)} %all-to-all-done.received_ref, bf16[8,128,128]{2,1,0:T(8,128)(2,1)S(1)} %all-to-all-done.2.hidden_ref, bf16[256,1024]{1,0:T(8,128)(2,1)} %shard_map.88.refs_0_, bf16[256,1024]{1,0:T(8,128)(2,1)} %collective-permute-done.8.refs_1_, ...), custom_call_target="tpu_custom_call" | custom-call | flops 2147483648 | bytes 6291456 | tf_op jit(solution)/shard_map/pallas_call | solution.py:339
  131.6 0.0 copy-start.2
  131.6 1.3 copy-done.2
  132.9 3.9 %all-to-all-start.3 = ((bf16[8,128,1024]{2,1,0:T(8,128)(2,1)}), bf16[8,128,1024]{2,1,0:T(8,128)(2,1)S(1)}, u32[]{:S(2)}, u32[]{:S(2)}) async-start(bf16[8,128,1024]{2,1,0:T(8,128)(2,1)} %copy-done.2), calls=%async_computation.3 | async-start | bytes 4194304 | tf_op jit(solution)/shard_map/all_to_all | solution.py:360
  136.9 0.3 collective-permute-start.12
  137.2 2.1 %collective-permute-start.13 = (bf16[256,1024]{1,0:T(8,128)(2,1)S(1)}, bf16[256,1024]{1,0:T(8,128)(2,1)S(1)}, u32[]{:S(2)}, u32[]{:S(2)}) collective-permute-start(bf16[256,1024]{1,0:T(8,128)(2,1)S(1)} %shard_map.91.refs_4_), channel_id=1, source_target_pairs={{0,16},{16,0},{1,17},{17,1},{2,18},{18,2},{3,19},{19,3},{4,20},{20... | collective-permute-start | bytes 1572872 | tf_op jit(solution)/shard_map/ppermute | solution.py:364
  139.2 22.7 %collective-permute-done.12 = bf16[256,1024]{1,0:T(8,128)(2,1)S(1)} collective-permute-done((bf16[256,1024]{1,0:T(8,128)(2,1)}, bf16[256,1024]{1,0:T(8,128)(2,1)S(1)}, u32[]{:S(2)}, u32[]{:S(2)}) %collective-permute-start.12) | collective-permute-done | bytes 524320 | tf_op jit(solution)/shard_map/ppermute | solution.py:364
  161.9 1.5 collective-permute-done.13
  163.4 0.3 add_convert_fusion
  163.7 1.7 collective-permute-start.14
  165.4 6.0 %collective-permute-done.14 = bf16[128,1024]{1,0:T(8,128)(2,1)S(1)} collective-permute-done((bf16[128,1024]{1,0:T(8,128)(2,1)S(1)}, bf16[128,1024]{1,0:T(8,128)(2,1)S(1)}, u32[]{:S(2)}, u32[]{:S(2)}) %collective-permute-start.14) | collective-permute-done | bytes 262176 | tf_op jit(solution)/shard_map/ppermute | solution.py:364
  171.4 0.8 pad_maximum_fusion
  172.3 1.8 %shard_map.93 = bf16[128,8192]{1,0:T(8,128)(2,1)} custom-call(bf16[8,128,1024]{2,1,0:T(8,128)(2,1)S(1)} %all-to-all-done.3.parts_ref), custom_call_target="tpu_custom_call" | custom-call | tf_op jit(solution)/shard_map/pallas_call | solution.py:164
  (47 shorter events, 0.1 us)
Async XLA Ops:
  0.6 19.6 %copy-start.22 = (s32[128,2]{0,1:T(2,128)S(1)}, s32[128,2]{0,1:T(2,128)}, u32[]{:S(2)}) copy-start(s32[128,2]{0,1:T(2,128)} %param.8) | copy-start | bytes 3076
  0.6 19.6 %copy-start.23 = (bf16[128,2]{0,1:T(2,128)(2,1)S(1)}, bf16[128,2]{0,1:T(2,128)(2,1)}, u32[]{:S(2)}) copy-start(bf16[128,2]{0,1:T(2,128)(2,1)} %param.7) | copy-start | bytes 1540
  0.7 19.6 %copy-start.1 = (bf16[128,8192]{1,0:T(8,128)(2,1)S(1)}, bf16[128,8192]{1,0:T(8,128)(2,1)}, u32[]{:S(2)}) copy-start(bf16[128,8192]{1,0:T(8,128)(2,1)} %tokens_ref.1) | copy-start | bytes 6291460
  2.6 16.0 %collective-permute-start.2 = (bf16[128,1024]{1,0:T(8,128)(2,1)S(1)}, bf16[128,1024]{1,0:T(8,128)(2,1)S(1)}, u32[]{:S(2)}, u32[]{:S(2)}) collective-permute-start(bf16[128,1024]{1,0:T(8,128)(2,1)S(1)} %get-tuple-element.25.refs_0_), channel_id=1, source_target_pairs={{0,16},{16,0},{1,17},{17,1},{2,18},{18,2},{3,19},{19,3},{4,20},{20... | collective-permute-start | bytes 786440 | tf_op jit(solution)/shard_map/ppermute | solution.py:364
  6.6 11.9 %collective-permute-start = (bf16[128,1024]{1,0:T(8,128)(2,1)}, bf16[128,1024]{1,0:T(8,128)(2,1)S(1)}, u32[]{:S(2)}, u32[]{:S(2)}) collective-permute-start(bf16[128,1024]{1,0:T(8,128)(2,1)} %get-tuple-element.26), channel_id=1, source_target_pairs={{0,4},{4,0},{1,5},{5,1},{2,6},{6,2},{3,7},{7,3},{8,12},{12,8},{9,1... | collective-permute-start | bytes 786440 | tf_op jit(solution)/shard_map/ppermute | solution.py:364
  9.9 10.3 %collective-permute-start.1 = (bf16[128,1024]{1,0:T(8,128)(2,1)}, bf16[128,1024]{1,0:T(8,128)(2,1)S(1)}, u32[]{:S(2)}, u32[]{:S(2)}) collective-permute-start(bf16[128,1024]{1,0:T(8,128)(2,1)} %get-tuple-element.24), channel_id=1, source_target_pairs={{0,4},{4,0},{1,5},{5,1},{2,6},{6,2},{3,7},{7,3},{8,12},{12,8},{9,1... | collective-permute-start | bytes 786440 | tf_op jit(solution)/shard_map/ppermute | solution.py:364
  18.5 1.7 copy-start.7
  18.6 1.7 copy-start.10
  20.2 1.0 copy-start.8
  21.2 0.9 copy-start.11
  22.2 0.8 copy-start.21
  24.1 1.5 copy-start
  25.5 48.0 %all-to-all-start = ((bf16[8,160,1024]{2,1,0:T(8,128)(2,1)}), bf16[8,160,1024]{2,1,0:T(8,128)(2,1)S(1)}, u32[]{:S(2)}, u32[]{:S(2)}) async-start(bf16[8,160,1024]{2,1,0:T(8,128)(2,1)} %copy-done), calls=%async_computation | async-start | bytes 5242880 | tf_op jit(solution)/shard_map/all_to_all | solution.py:360
  29.3 15.5 %collective-permute-start.3 = (bf16[128,1024]{1,0:T(8,128)(2,1)}, bf16[128,1024]{1,0:T(8,128)(2,1)S(1)}, u32[]{:S(2)}, u32[]{:S(2)}) collective-permute-start(bf16[128,1024]{1,0:T(8,128)(2,1)} %copy-done.10), channel_id=1, source_target_pairs={{0,16},{16,0},{1,17},{17,1},{2,18},{18,2},{3,19},{19,3},{4,20},{20... | collective-permute-start | bytes 786440 | tf_op jit(solution)/shard_map/ppermute | solution.py:364
  29.6 17.8 %collective-permute-start.4 = (bf16[128,1024]{1,0:T(8,128)(2,1)S(1)}, bf16[128,1024]{1,0:T(8,128)(2,1)S(1)}, u32[]{:S(2)}, u32[]{:S(2)}) collective-permute-start(bf16[128,1024]{1,0:T(8,128)(2,1)S(1)} %get-tuple-element.25.refs_0_), channel_id=1, source_target_pairs={{0,8},{8,0},{1,9},{9,1},{2,10},{10,2},{3,11},{11,3},{4,12},{12,4},... | collective-permute-start | bytes 786440 | tf_op jit(solution)/shard_map/ppermute | solution.py:364
  32.5 29.1 %collective-permute-start.6 = (bf16[128,1024]{1,0:T(8,128)(2,1)}, bf16[128,1024]{1,0:T(8,128)(2,1)S(1)}, u32[]{:S(2)}, u32[]{:S(2)}) collective-permute-start(bf16[128,1024]{1,0:T(8,128)(2,1)} %copy-done.7), channel_id=1, source_target_pairs={{0,8},{8,0},{1,9},{9,1},{2,10},{10,2},{3,11},{11,3},{4,12},{12,4},... | collective-permute-start | bytes 786440 | tf_op jit(solution)/shard_map/ppermute | solution.py:364
  32.5 34.7 %collective-permute-start.5 = (bf16[128,1024]{1,0:T(8,128)(2,1)}, bf16[128,1024]{1,0:T(8,128)(2,1)S(1)}, u32[]{:S(2)}, u32[]{:S(2)}) collective-permute-start(bf16[128,1024]{1,0:T(8,128)(2,1)} %copy-done.10), channel_id=1, source_target_pairs={{0,8},{8,0},{1,9},{9,1},{2,10},{10,2},{3,11},{11,3},{4,12},{12,4},... | collective-permute-start | bytes 786440 | tf_op jit(solution)/shard_map/ppermute | solution.py:364
  44.8 22.4 %copy-start.13 = (bf16[128,1024]{1,0:T(8,128)(2,1)}, bf16[128,1024]{1,0:T(8,128)(2,1)S(1)}, u32[]{:S(2)}) copy-start(bf16[128,1024]{1,0:T(8,128)(2,1)S(1)} %collective-permute-done.3.refs_3_.refs_0_) | copy-start | bytes 786436
  44.8 28.0 %collective-permute-start.7 = (bf16[128,1024]{1,0:T(8,128)(2,1)S(1)}, bf16[128,1024]{1,0:T(8,128)(2,1)S(1)}, u32[]{:S(2)}, u32[]{:S(2)}) collective-permute-start(bf16[128,1024]{1,0:T(8,128)(2,1)S(1)} %collective-permute-done.3.refs_3_.refs_0_), channel_id=1, source_target_pairs={{0,8},{8,0},{1,9},{9,1},{2,10},{10,2},{3,11},{11,3},{4,12},{12,4},... | collective-permute-start | bytes 786440 | tf_op jit(solution)/shard_map/ppermute | solution.py:364
  45.7 46.1 %collective-permute-start.8 = (bf16[256,1024]{1,0:T(8,128)(2,1)}, bf16[256,1024]{1,0:T(8,128)(2,1)}, u32[]{:S(2)}, u32[]{:S(2)}) collective-permute-start(bf16[256,1024]{1,0:T(8,128)(2,1)} %shard_map.88.refs_0_), channel_id=1, source_target_pairs={{0,16},{16,0},{1,17},{17,1},{2,18},{18,2},{3,19},{19,3},{4,20},{20... | collective-permute-start | bytes 1572872 | tf_op jit(solution)/shard_map/ppermute | solution.py:364
  47.5 0.7 copy-start.25
  61.6 0.7 copy-start.15
  67.2 0.7 copy-start.27
  72.8 0.7 copy-start.18
  73.5 1.0 copy-start.9
  74.5 0.9 copy-start.12
  75.4 0.9 copy-start.14
  76.4 0.9 copy-start.16
  77.3 0.9 copy-start.19
  78.3 0.9 copy-start.26
  79.2 0.9 copy-start.28
  84.1 4.8 %copy-start.17 = (bf16[128,1024]{1,0:T(8,128)(2,1)S(1)}, bf16[128,1024]{1,0:T(8,128)(2,1)}, u32[]{:S(2)}) copy-start(bf16[128,1024]{1,0:T(8,128)(2,1)} %copy-done.15) | copy-start | bytes 786436
  84.1 4.8 %copy-start.20 = (bf16[128,1024]{1,0:T(8,128)(2,1)S(1)}, bf16[128,1024]{1,0:T(8,128)(2,1)}, u32[]{:S(2)}) copy-start(bf16[128,1024]{1,0:T(8,128)(2,1)} %copy-done.18) | copy-start | bytes 786436
  87.4 0.8 copy-start.3
  88.2 0.8 copy-start.5
  88.9 13.3 %copy-start.24 = (bf16[256,1024]{1,0:T(8,128)(2,1)}, bf16[256,1024]{1,0:T(8,128)(2,1)S(1)}, u32[]{:S(2)}) copy-start(bf16[256,1024]{1,0:T(8,128)(2,1)S(1)} %get-tuple-element.20) | copy-start | bytes 1572868
  88.9 16.7 %collective-permute-start.11 = (bf16[256,1024]{1,0:T(8,128)(2,1)}, bf16[256,1024]{1,0:T(8,128)(2,1)}, u32[]{:S(2)}, u32[]{:S(2)}) collective-permute-start(bf16[256,1024]{1,0:T(8,128)(2,1)} %get-tuple-element.17), channel_id=1, source_target_pairs={{0,8},{8,0},{1,9},{9,1},{2,10},{10,2},{3,11},{11,3},{4,12},{12,4},... | collective-permute-start | bytes 1572872 | tf_op jit(solution)/shard_map/ppermute | solution.py:364
  89.9 25.4 %collective-permute-start.9 = (bf16[256,1024]{1,0:T(8,128)(2,1)}, bf16[256,1024]{1,0:T(8,128)(2,1)}, u32[]{:S(2)}, u32[]{:S(2)}) collective-permute-start(bf16[256,1024]{1,0:T(8,128)(2,1)} %shard_map.89), channel_id=1, source_target_pairs={{0,8},{8,0},{1,9},{9,1},{2,10},{10,2},{3,11},{11,3},{4,12},{12,4},... | collective-permute-start | bytes 1572872 | tf_op jit(solution)/shard_map/ppermute | solution.py:364
  91.8 33.8 %collective-permute-start.10 = (bf16[256,1024]{1,0:T(8,128)(2,1)}, bf16[256,1024]{1,0:T(8,128)(2,1)}, u32[]{:S(2)}, u32[]{:S(2)}) collective-permute-start(bf16[256,1024]{1,0:T(8,128)(2,1)} %collective-permute-done.8.refs_1_), channel_id=1, source_target_pairs={{0,8},{8,0},{1,9},{9,1},{2,10},{10,2},{3,11},{11,3},{4,12},{12,4},... | collective-permute-start | bytes 1572872 | tf_op jit(solution)/shard_map/ppermute | solution.py:364
  102.3 23.4 %all-to-all-start.2 = ((bf16[8,128,128]{2,1,0:T(8,128)(2,1)}), bf16[8,128,128]{2,1,0:T(8,128)(2,1)S(1)}, u32[]{:S(2)}, u32[]{:S(2)}) async-start(bf16[8,128,128]{2,1,0:T(8,128)(2,1)} %get-tuple-element.15), calls=%async_computation.2 | async-start | bytes 524288 | tf_op jit(solution)/shard_map/all_to_all | solution.py:360
  105.7 1.0 copy-start.4
  131.6 1.3 copy-start.2
  132.9 30.5 %copy-start.6 = (bf16[256,1024]{1,0:T(8,128)(2,1)S(1)}, bf16[256,1024]{1,0:T(8,128)(2,1)}, u32[]{:S(2)}) copy-start(bf16[256,1024]{1,0:T(8,128)(2,1)} %copy-done.5) | copy-start | bytes 1572868
  132.9 39.3 %all-to-all-start.3 = ((bf16[8,128,1024]{2,1,0:T(8,128)(2,1)}), bf16[8,128,1024]{2,1,0:T(8,128)(2,1)S(1)}, u32[]{:S(2)}, u32[]{:S(2)}) async-start(bf16[8,128,1024]{2,1,0:T(8,128)(2,1)} %copy-done.2), calls=%async_computation.3 | async-start | bytes 4194304 | tf_op jit(solution)/shard_map/all_to_all | solution.py:360
  136.9 25.0 %collective-permute-start.12 = (bf16[256,1024]{1,0:T(8,128)(2,1)}, bf16[256,1024]{1,0:T(8,128)(2,1)S(1)}, u32[]{:S(2)}, u32[]{:S(2)}) collective-permute-start(bf16[256,1024]{1,0:T(8,128)(2,1)} %copy-done.24), channel_id=1, source_target_pairs={{0,8},{8,0},{1,9},{9,1},{2,10},{10,2},{3,11},{11,3},{4,12},{12,4},... | collective-permute-start | bytes 1572872 | tf_op jit(solution)/shard_map/ppermute | solution.py:364
  137.2 26.2 %collective-permute-start.13 = (bf16[256,1024]{1,0:T(8,128)(2,1)S(1)}, bf16[256,1024]{1,0:T(8,128)(2,1)S(1)}, u32[]{:S(2)}, u32[]{:S(2)}) collective-permute-start(bf16[256,1024]{1,0:T(8,128)(2,1)S(1)} %shard_map.91.refs_4_), channel_id=1, source_target_pairs={{0,16},{16,0},{1,17},{17,1},{2,18},{18,2},{3,19},{19,3},{4,20},{20... | collective-permute-start | bytes 1572872 | tf_op jit(solution)/shard_map/ppermute | solution.py:364
  163.7 7.7 %collective-permute-start.14 = (bf16[128,1024]{1,0:T(8,128)(2,1)S(1)}, bf16[128,1024]{1,0:T(8,128)(2,1)S(1)}, u32[]{:S(2)}, u32[]{:S(2)}) collective-permute-start(bf16[128,1024]{1,0:T(8,128)(2,1)S(1)} %slice.9), channel_id=1, source_target_pairs={{0,4},{4,0},{1,5},{5,1},{2,6},{6,2},{3,7},{7,3},{8,12},{12,8},{9,1... | collective-permute-start | bytes 786440 | tf_op jit(solution)/shard_map/ppermute | solution.py:364

commit v11 on v10

--- a/solution.py
+++ b/solution.py
@@ -52,6 +52,10 @@
     ]
 
 
+def in_hbm(*arrays):
+    return [pltpu.with_memory_space_constraint(array, pltpu.HBM) for array in arrays]
+
+
 def stack_kernel(own_ref, other_ref, *refs):
     rows = own_ref.shape[0]
     refs[-1][0:rows, :] = own_ref[...]
@@ -67,7 +71,7 @@
         ],
         out_shape=jax.ShapeDtypeStruct((2 * own.shape[0], own.shape[1]), own.dtype),
         compiler_params=params(),
-    )(own, other, *before)
+    )(own, other, *in_hbm(*before))
 
 
 def add_kernel(count, *refs):
@@ -88,7 +92,7 @@
         ],
         out_shape=[jax.ShapeDtypeStruct(pair[0].shape, pair[0].dtype) for pair in pairs],
         compiler_params=params(),
-    )(*flat, *before)
+    )(*flat, *in_hbm(*before))
 
 
 def pack_kernel(
@@ -145,11 +149,11 @@
         ],
         out_specs=(pl.BlockSpec((each, height, features), lambda i: (i, 0, 0)), whole[2], whole[2]),
         out_shape=(
-            jax.ShapeDtypeStruct((members, height, features), jnp.bfloat16), small, small,
+            pltpu.HBM((members, height, features), jnp.bfloat16), small, small,
         ),
         scratch_shapes=[pltpu.VMEM(preact.shape, jnp.bfloat16)],
         compiler_params=params(),
-    )(far_places, ids, gates, preact, tokens, *before)
+    )(far_places, ids, gates, preact, tokens, *in_hbm(*before))
 
 
 def unpack_kernel(parts_ref, out_ref):
@@ -228,7 +232,7 @@
         ],
         compiler_params=params(),
         cost_estimate=cost(total_rows, total, features),
-    )(received, *before)
+    )(received, *in_hbm(*before))
 
 
 def lane_numbers(received_ref, rows, wide):
@@ -249,8 +253,8 @@
         start += ref.shape[0]
 
 
-def project_kernel(received_ref, *refs):
-    piece_refs, (out_ref, full) = refs[:-2], refs[-2:]
+def project_kernel(count, received_ref, *refs):
+    piece_refs, (out_ref, full) = refs[:count], refs[-2:]
     pl.when(pl.program_id(0) == 0)(lambda: join(piece_refs, full))
     sources, rows, wide = out_ref.shape
     low, first, second = lane_numbers(received_ref, rows, wide)
@@ -274,22 +278,23 @@
     out_ref[...] = value.reshape(out_ref.shape)
 
 
-def project(received, pieces, rows, wide):
+def project(received, pieces, rows, wide, before):
     sources, height, features = received.shape
     joined = sum(piece.shape[0] for piece in pieces)
     return pl.pallas_call(
-        project_kernel,
+        functools.partial(project_kernel, len(pieces)),
         grid=(sources // 2,),
         in_specs=[
             pl.BlockSpec((2, height, features), lambda i: (i, 0, 0)),
             *[pl.BlockSpec(piece.shape, lambda i: (0, 0)) for piece in pieces],
+            *[pl.BlockSpec(memory_space=pl.ANY) for _ in before],
         ],
         out_specs=pl.BlockSpec((2, rows, wide), lambda i: (i, 0, 0)),
         out_shape=jax.ShapeDtypeStruct((sources, rows, wide), jnp.bfloat16),
         scratch_shapes=[pltpu.VMEM((joined, features), jnp.bfloat16)],
         compiler_params=params(),
         cost_estimate=cost(sources * rows, features, joined),
-    )(received, *pieces)
+    )(received, *in_hbm(*pieces, *before))
 
 
 def hidden_kernel(parts_ref, activation_ref, scaled_ref, hidden_ref, gate_ref):
@@ -353,7 +358,7 @@
         ],
         compiler_params=params(),
         cost_estimate=cost(sources * rows, joined, features),
-    )(received, hidden_grad, *pieces, *before)
+    )(received, hidden_grad, *in_hbm(*pieces, *before))
 
 
 def exchange(value, axes):
@@ -393,10 +398,10 @@
         low = [swap(half, "low") for half in down_halves]
         low_beside = [swap(half, "low") for half in beside]
         down_pieces = [*down_halves, *beside, *low, *low_beside]
-        first += beside[:1]
+        first += [beside[0], *low]
         up_own = stack(*up_halves, beside[1:])
         up_beside = swap(up_own, "high")
-        up_low = swap(stack(*up_halves, low_beside), "low")
+        up_low = swap(up_own, "low")
         up_pieces = [up_own, up_beside, up_low, swap(up_beside, "low")]
     else:
         down_pieces = [lax.all_gather(stack(*down_halves, ()), FAR, tiled=True)]
@@ -407,11 +412,10 @@
     )
     received = exchange(packed, GROUP)
 
-    projected = project(received, down_pieces, tok_count, wide)
     partial_value = down_partial(
-        received, tok_count, wide, own_rows * PAIR * far_count, far_count if paired else 1,
-        (projected,),
-    )
+        received, tok_count, wide, own_rows * PAIR * far_count, far_count if paired else 1, ()
+    )
+    projected = project(received, down_pieces, tok_count, wide, partial_value[:1])
     parts = exchange(projected, GROUP)
     hidden_grad, gate_grads = pl.pallas_call(
         hidden_kernel,

time: 175 us -> 159 us (0.909)
  local copies, waits for them, and re-layouts: 21.2 us -> 8.01 us
  waiting for transfers between devices: 91.2 us -> 84.6 us
  starting transfers between devices: 30.2 us -> 32.7 us
  Pallas kernels: 19.8 us -> 22.1 us
    unnamed x58 -> x36, local copies, waits for them, and re-layouts: 17.5 us -> 5 us
    ppermute x15, waiting for transfers between devices: 91.2 us -> 84.6 us  [swap(): return lax.ppermute(value, axis, SWAP)]
    ppermute x15, starting transfers between devices: 19.2 us -> 21.7 us  [swap(): return lax.ppermute(value, axis, SWAP)]
  transfers between devices with their start and end apart: 18 -> 18, of which waited for: 11 -> 9; matrix products, arithmetic and copies ran while one was open for 2% -> 2% of each run, Pallas kernels for 6% -> 7%
where the time goes in v11:
time: 159 us
  waiting for transfers between devices  84.6 us (53%)
  starting transfers between devices  32.7 us (21%)
  Pallas kernels  22.1 us (14%)
  blocking collectives  9.48 us (6%)
  local copies, waits for them, and re-layouts  8.01 us (5%)
    ppermute x15, waiting for transfers between devices, swap(): return lax.ppermute(value, axis, SWAP)  84.6 us
    ppermute x15, starting transfers between devices, swap(): return lax.ppermute(value, axis, SWAP)  21.7 us
    all_to_all x3, starting transfers between devices, exchange(): return lax.all_to_all(value, axes, split_axis=0, concat_axis=0, tiled=True)  10.9 us
    all_to_all x1, blocking collectives, exchange(): return lax.all_to_all(value, axes, split_axis=0, concat_axis=0, tiled=True)  9.48 us
    pallas_call x1, Pallas kernels, input_rows(): pl.pallas_call(functools.partial(input_kernel, len(pieces)), grid=(source...  6.01 us
    pallas_call x1, Pallas kernels, project(): pl.pallas_call(functools.partial(project_kernel, len(pieces)), grid=(sour...  5.5 us
    unnamed x36, local copies, waits for them, and re-layouts  5 us
    pallas_call x1, Pallas kernels, down_partial(): pl.pallas_call(functools.partial(down_kernel, rows, wide, count), in_spec...  3.2 us
  transfers between devices with their start and end apart: 18, of which 9 were waited for; matrix products, arithmetic and copies ran while one was open for 2% of the time, Pallas kernels for 7%

profile of v11, /device:TPU:0, one launch (start us, length us, event | category | flops | bytes accessed | tf_op | source)
XLA Modules:
  0.0 158.9 jit_solution(13144008865193002065)
XLA Ops:
  0.6 0.0 copy-start.10
  0.6 0.0 copy-start.11
  0.7 0.0 copy-start
  0.7 0.0 copy-start.9
  0.7 1.2 constant_dynamic-slice_fusion.1
  1.9 0.0 copy-start.13
  1.9 3.0 %collective-permute-start = (bf16[128,1024]{1,0:T(8,128)(2,1)S(1)}, bf16[128,1024]{1,0:T(8,128)(2,1)S(1)}, u32[]{:S(2)}, u32[]{:S(2)}) collective-permute-start(bf16[128,1024]{1,0:T(8,128)(2,1)S(1)} %get-tuple-element.26), channel_id=1, source_target_pairs={{0,4},{4,0},{1,5},{5,1},{2,6},{6,2},{3,7},{7,3},{8,12},{12,8},{9,1... | collective-permute-start | bytes 786440 | tf_op jit(solution)/shard_map/ppermute | solution.py:369
  4.9 2.6 %collective-permute-start.2 = (bf16[128,1024]{1,0:T(8,128)(2,1)S(1)}, bf16[128,1024]{1,0:T(8,128)(2,1)}, u32[]{:S(2)}, u32[]{:S(2)}) collective-permute-start(bf16[128,1024]{1,0:T(8,128)(2,1)S(1)} %get-tuple-element.25.refs_0_), channel_id=1, source_target_pairs={{0,16},{16,0},{1,17},{17,1},{2,18},{18,2},{3,19},{19,3},{4,20},{20... | collective-permute-start | bytes 786440 | tf_op jit(solution)/shard_map/ppermute | solution.py:369
  7.5 1.6 collective-permute-start.3
  9.1 1.8 %constant_dynamic-slice_fusion = (bf16[128,1024]{1,0:T(8,128)(2,1)S(1)}, bf16[128,1024]{1,0:T(8,128)(2,1)}) fusion(bf16[128,2048]{1,0:T(8,128)(2,1)} %bitcast.9, s32[]{:T(128)S(6)} %select_n.35, s32[]{:T(128)S(6)} %select_n.34), kind=kLoop, calls=%fused_computation.6 | loop fusion | bytes 1048584 | tf_op jit(solution)/shard_map/dynamic_slice | solution.py:387
  10.9 0.5 collective-permute-start.1
  11.4 0.0 collective-permute-done.refs_0_.refs_1_
  11.4 1.7 %collective-permute-start.4 = (bf16[128,1024]{1,0:T(8,128)(2,1)S(1)}, bf16[128,1024]{1,0:T(8,128)(2,1)}, u32[]{:S(2)}, u32[]{:S(2)}) collective-permute-start(bf16[128,1024]{1,0:T(8,128)(2,1)S(1)} %collective-permute-done.refs_0_.refs_1_), channel_id=1, source_target_pairs={{0,8},{8,0},{1,9},{9,1},{2,10},{10,2},{3,11},{11,3},{4,12},{12,4},... | collective-permute-start | bytes 786440 | tf_op jit(solution)/shard_map/ppermute | solution.py:369
  13.1 6.4 %collective-permute-done.2.refs_2_ = bf16[128,1024]{1,0:T(8,128)(2,1)} collective-permute-done((bf16[128,1024]{1,0:T(8,128)(2,1)S(1)}, bf16[128,1024]{1,0:T(8,128)(2,1)}, u32[]{:S(2)}, u32[]{:S(2)}) %collective-permute-start.2) | collective-permute-done | bytes 262176 | tf_op jit(solution)/shard_map/ppermute | solution.py:369
  19.4 2.0 %collective-permute-done.3.refs_3_.refs_4_ = bf16[128,1024]{1,0:T(8,128)(2,1)} collective-permute-done((bf16[128,1024]{1,0:T(8,128)(2,1)S(1)}, bf16[128,1024]{1,0:T(8,128)(2,1)}, u32[]{:S(2)}, u32[]{:S(2)}) %collective-permute-start.3) | collective-permute-done | bytes 262176 | tf_op jit(solution)/shard_map/ppermute | solution.py:369
  21.4 0.0 collective-permute-done.1.refs_1_.other_ref
  21.4 3.9 %collective-permute-done.4.refs_4_.refs_5_ = bf16[128,1024]{1,0:T(8,128)(2,1)} collective-permute-done((bf16[128,1024]{1,0:T(8,128)(2,1)S(1)}, bf16[128,1024]{1,0:T(8,128)(2,1)}, u32[]{:S(2)}, u32[]{:S(2)}) %collective-permute-start.4) | collective-permute-done | bytes 262176 | tf_op jit(solution)/shard_map/ppermute | solution.py:369
  25.2 0.0 copy-done.13
  25.3 2.9 %shard_map.85 = (bf16[8,160,1024]{2,1,0:T(8,128)(2,1)}, f32[128,128]{1,0:T(8,128)S(1)}, f32[128,128]{1,0:T(8,128)S(1)}) custom-call(s32[4]{0:T(128)S(1)} %fusion.2.far_ref, s32[2,128]{1,0:T(2,128)S(1)} %bitcast.6, bf16[2,128]{1,0:T(2,128)(2,1)S(1)} %bitcast.7, bf16[128,128]{1,0:T(8,128)(2,1)S(1)} %copy-done.9, bf16[128,8192]{1,0:T(8,128)(2,1)S(1)} %copy-done, ...), custom_call_target="tpu_custom_call" | custom-call | tf_op jit(solution)/shard_map/pallas_call | solution.py:141
  28.2 3.8 %all-to-all-start = ((bf16[8,160,1024]{2,1,0:T(8,128)(2,1)}), bf16[8,160,1024]{2,1,0:T(8,128)(2,1)S(1)}, u32[]{:S(2)}, u32[]{:S(2)}) async-start(bf16[8,160,1024]{2,1,0:T(8,128)(2,1)} %get-tuple-element.12), calls=%async_computation | async-start | bytes 5242880 | tf_op jit(solution)/shard_map/all_to_all | solution.py:365
  31.9 1.4 collective-permute-start.5
  33.3 13.7 %collective-permute-done.5.refs_3_.refs_0_ = bf16[128,1024]{1,0:T(8,128)(2,1)S(1)} collective-permute-done((bf16[128,1024]{1,0:T(8,128)(2,1)S(1)}, bf16[128,1024]{1,0:T(8,128)(2,1)S(1)}, u32[]{:S(2)}, u32[]{:S(2)}) %collective-permute-start.5) | collective-permute-done | bytes 262176 | tf_op jit(solution)/shard_map/ppermute | solution.py:369
  47.1 0.7 copy-done.16
  47.8 0.8 shard_map.89.refs_0_
  48.6 0.0 collective-permute-start.8
  48.6 2.8 %collective-permute-start.6 = (bf16[128,1024]{1,0:T(8,128)(2,1)}, bf16[128,1024]{1,0:T(8,128)(2,1)S(1)}, u32[]{:S(2)}, u32[]{:S(2)}) collective-permute-start(bf16[128,1024]{1,0:T(8,128)(2,1)} %collective-permute-done.2.refs_2_), channel_id=1, source_target_pairs={{0,8},{8,0},{1,9},{9,1},{2,10},{10,2},{3,11},{11,3},{4,12},{12,4},... | collective-permute-start | bytes 786440 | tf_op jit(solution)/shard_map/ppermute | solution.py:369
  51.4 0.0 collective-permute-start.7
  51.4 2.0 %collective-permute-start.9 = (bf16[256,1024]{1,0:T(8,128)(2,1)}, bf16[256,1024]{1,0:T(8,128)(2,1)}, u32[]{:S(2)}, u32[]{:S(2)}) collective-permute-start(bf16[256,1024]{1,0:T(8,128)(2,1)} %shard_map.89.refs_0_), channel_id=1, source_target_pairs={{0,8},{8,0},{1,9},{9,1},{2,10},{10,2},{3,11},{11,3},{4,12},{12,4},... | collective-permute-start | bytes 1572872 | tf_op jit(solution)/shard_map/ppermute | solution.py:369
  53.4 21.1 %collective-permute-done.8.refs_1_ = bf16[256,1024]{1,0:T(8,128)(2,1)} collective-permute-done((bf16[256,1024]{1,0:T(8,128)(2,1)}, bf16[256,1024]{1,0:T(8,128)(2,1)}, u32[]{:S(2)}, u32[]{:S(2)}) %collective-permute-start.8) | collective-permute-done | bytes 524320 | tf_op jit(solution)/shard_map/ppermute | solution.py:369
  74.5 0.0 collective-permute-start.10
  74.5 0.0 all-to-all-done.received_ref
  74.5 3.2 %shard_map.86 = (bf16[256,1024]{1,0:T(8,128)(2,1)S(1)}, bf16[256,1024]{1,0:T(8,128)(2,1)S(1)}, bf16[256,1024]{1,0:T(8,128)(2,1)S(1)}, bf16[256,1024]{1,0:T(8,128)(2,1)}) custom-call(bf16[8,160,1024]{2,1,0:T(8,128)(2,1)S(1)} %all-to-all-done.received_ref), custom_call_target="tpu_custom_call" | custom-call | flops 2147483648 | bytes 6291456 | tf_op jit(solution)/shard_map/pallas_call | solution.py:221
  77.7 0.8 copy-done.6
  78.5 2.0 %collective-permute-start.11 = (bf16[256,1024]{1,0:T(8,128)(2,1)}, bf16[256,1024]{1,0:T(8,128)(2,1)}, u32[]{:S(2)}, u32[]{:S(2)}) collective-permute-start(bf16[256,1024]{1,0:T(8,128)(2,1)} %get-tuple-element.18), channel_id=1, source_target_pairs={{0,8},{8,0},{1,9},{9,1},{2,10},{10,2},{3,11},{11,3},{4,12},{12,4},... | collective-permute-start | bytes 1572872 | tf_op jit(solution)/shard_map/ppermute | solution.py:369
  80.5 0.0 collective-permute-done.6.refs_6_
  80.5 0.0 collective-permute-done.7.refs_7_
  80.6 0.7 copy-done.17
  81.2 5.5 %shard_map.87 = bf16[8,128,128]{2,1,0:T(8,128)(2,1)S(1)} custom-call(bf16[8,160,1024]{2,1,0:T(8,128)(2,1)S(1)} %all-to-all-done.received_ref, bf16[128,1024]{1,0:T(8,128)(2,1)} %copy-done.13, bf16[128,1024]{1,0:T(8,128)(2,1)} %copy-done.14, bf16[128,1024]{1,0:T(8,128)(2,1)} %collective-permute-done.2.refs_2_, bf16[128,1024]{1,0:T(8,128)(2,1)} %copy-done.16, ...), custom_call_target="tpu_custom_call" | custom-call | flops 2147483648 | bytes 6291456 | tf_op jit(solution)/shard_map/pallas_call | solution.py:284
  86.7 0.0 copy-done.12
  86.8 9.5 %all_to_all.20.parts_ref = bf16[8,128,128]{2,1,0:T(8,128)(2,1)S(1)} all-to-all(bf16[8,128,128]{2,1,0:T(8,128)(2,1)S(1)} %shard_map.87), channel_id=1, replica_groups=mesh['high'=2,'low'=2,'near'=2,'inner'=2,'outer'=2] {'inner','outer','ne..., dimensions={0} | all-to-all | bytes 524288 | tf_op jit(solution)/shard_map/all_to_all | solution.py:365
  96.2 0.7 shard_map.88
  97.0 0.7 copy-done.8
  97.7 3.4 %all-to-all-start.2 = ((bf16[8,128,128]{2,1,0:T(8,128)(2,1)}), bf16[8,128,128]{2,1,0:T(8,128)(2,1)S(1)}, u32[]{:S(2)}, u32[]{:S(2)}) async-start(bf16[8,128,128]{2,1,0:T(8,128)(2,1)} %copy-done.8), calls=%async_computation.2 | async-start | bytes 524288 | tf_op jit(solution)/shard_map/all_to_all | solution.py:365
  101.1 7.2 %collective-permute-done.11.refs_1_ = bf16[256,1024]{1,0:T(8,128)(2,1)} collective-permute-done((bf16[256,1024]{1,0:T(8,128)(2,1)}, bf16[256,1024]{1,0:T(8,128)(2,1)}, u32[]{:S(2)}, u32[]{:S(2)}) %collective-permute-start.11) | collective-permute-done | bytes 524320 | tf_op jit(solution)/shard_map/ppermute | solution.py:369
  108.3 1.2 shard_map.90.refs_4_
  109.5 0.0 copy-start.4
  109.5 0.8 copy-done.4
  110.3 0.0 collective-permute-done.9.refs_2_
  110.3 0.0 collective-permute-done.10.refs_3_
  110.3 0.0 all-to-all-done.2.hidden_ref
  110.3 6.0 %shard_map.91 = bf16[8,128,1024]{2,1,0:T(8,128)(2,1)S(1)} custom-call(bf16[8,160,1024]{2,1,0:T(8,128)(2,1)S(1)} %all-to-all-done.received_ref, bf16[8,128,128]{2,1,0:T(8,128)(2,1)S(1)} %all-to-all-done.2.hidden_ref, bf16[256,1024]{1,0:T(8,128)(2,1)} %shard_map.89.refs_0_, bf16[256,1024]{1,0:T(8,128)(2,1)} %collective-permute-done.8.refs_1_, ...), custom_call_target="tpu_custom_call" | custom-call | flops 2147483648 | bytes 6291456 | tf_op jit(solution)/shard_map/pallas_call | solution.py:344
  116.3 0.0 copy-start.1
  116.3 1.3 copy-done.1
  117.6 3.8 %all-to-all-start.3 = ((bf16[8,128,1024]{2,1,0:T(8,128)(2,1)}), bf16[8,128,1024]{2,1,0:T(8,128)(2,1)S(1)}, u32[]{:S(2)}, u32[]{:S(2)}) async-start(bf16[8,128,1024]{2,1,0:T(8,128)(2,1)} %copy-done.1), calls=%async_computation.3 | async-start | bytes 4194304 | tf_op jit(solution)/shard_map/all_to_all | solution.py:365
  121.4 0.1 collective-permute-start.12
  121.5 2.4 %collective-permute-start.13 = (bf16[256,1024]{1,0:T(8,128)(2,1)S(1)}, bf16[256,1024]{1,0:T(8,128)(2,1)S(1)}, u32[]{:S(2)}, u32[]{:S(2)}) collective-permute-start(bf16[256,1024]{1,0:T(8,128)(2,1)S(1)} %copy-done.5), channel_id=1, source_target_pairs={{0,16},{16,0},{1,17},{17,1},{2,18},{18,2},{3,19},{19,3},{4,20},{20... | collective-permute-start | bytes 1572872 | tf_op jit(solution)/shard_map/ppermute | solution.py:369
  123.8 22.8 %collective-permute-done.12 = bf16[256,1024]{1,0:T(8,128)(2,1)S(1)} collective-permute-done((bf16[256,1024]{1,0:T(8,128)(2,1)}, bf16[256,1024]{1,0:T(8,128)(2,1)S(1)}, u32[]{:S(2)}, u32[]{:S(2)}) %collective-permute-start.12) | collective-permute-done | bytes 524320 | tf_op jit(solution)/shard_map/ppermute | solution.py:369
  146.6 1.3 collective-permute-done.13
  148.0 0.3 add_convert_fusion
  148.3 1.7 %collective-permute-start.14 = (bf16[128,1024]{1,0:T(8,128)(2,1)S(1)}, bf16[128,1024]{1,0:T(8,128)(2,1)S(1)}, u32[]{:S(2)}, u32[]{:S(2)}) collective-permute-start(bf16[128,1024]{1,0:T(8,128)(2,1)S(1)} %slice.9), channel_id=1, source_target_pairs={{0,4},{4,0},{1,5},{5,1},{2,6},{6,2},{3,7},{7,3},{8,12},{12,8},{9,1... | collective-permute-start | bytes 786440 | tf_op jit(solution)/shard_map/ppermute | solution.py:369
  150.0 6.2 %collective-permute-done.14 = bf16[128,1024]{1,0:T(8,128)(2,1)S(1)} collective-permute-done((bf16[128,1024]{1,0:T(8,128)(2,1)S(1)}, bf16[128,1024]{1,0:T(8,128)(2,1)S(1)}, u32[]{:S(2)}, u32[]{:S(2)}) %collective-permute-start.14) | collective-permute-done | bytes 262176 | tf_op jit(solution)/shard_map/ppermute | solution.py:369
  156.3 0.8 pad_maximum_fusion
  157.1 0.0 all-to-all-done.3.parts_ref
  157.1 1.8 %shard_map.92 = bf16[128,8192]{1,0:T(8,128)(2,1)} custom-call(bf16[8,128,1024]{2,1,0:T(8,128)(2,1)S(1)} %all-to-all-done.3.parts_ref), custom_call_target="tpu_custom_call" | custom-call | tf_op jit(solution)/shard_map/pallas_call | solution.py:168
  (24 shorter events, 0.1 us)
Async XLA Ops:
  0.6 24.6 %copy-start.10 = (s32[128,2]{0,1:T(2,128)S(1)}, s32[128,2]{0,1:T(2,128)}, u32[]{:S(2)}) copy-start(s32[128,2]{0,1:T(2,128)} %param.8) | copy-start | bytes 3076
  0.6 24.6 %copy-start.11 = (bf16[128,2]{0,1:T(2,128)(2,1)S(1)}, bf16[128,2]{0,1:T(2,128)(2,1)}, u32[]{:S(2)}) copy-start(bf16[128,2]{0,1:T(2,128)(2,1)} %param.7) | copy-start | bytes 1540
  0.7 24.6 %copy-start = (bf16[128,8192]{1,0:T(8,128)(2,1)S(1)}, bf16[128,8192]{1,0:T(8,128)(2,1)}, u32[]{:S(2)}) copy-start(bf16[128,8192]{1,0:T(8,128)(2,1)} %tokens_ref.1) | copy-start | bytes 6291460
  0.7 24.6 %copy-start.9 = (bf16[128,128]{1,0:T(8,128)(2,1)S(1)}, bf16[128,128]{1,0:T(8,128)(2,1)}, u32[]{:S(2)}) copy-start(bf16[128,128]{1,0:T(8,128)(2,1)} %preact_ref.1) | copy-start | bytes 98308
  1.9 23.3 %copy-start.13 = (bf16[128,1024]{1,0:T(8,128)(2,1)}, bf16[128,1024]{1,0:T(8,128)(2,1)S(1)}, u32[]{:S(2)}) copy-start(bf16[128,1024]{1,0:T(8,128)(2,1)S(1)} %get-tuple-element.25.refs_0_) | copy-start | bytes 786436
  1.9 9.5 %collective-permute-start = (bf16[128,1024]{1,0:T(8,128)(2,1)S(1)}, bf16[128,1024]{1,0:T(8,128)(2,1)S(1)}, u32[]{:S(2)}, u32[]{:S(2)}) collective-permute-start(bf16[128,1024]{1,0:T(8,128)(2,1)S(1)} %get-tuple-element.26), channel_id=1, source_target_pairs={{0,4},{4,0},{1,5},{5,1},{2,6},{6,2},{3,7},{7,3},{8,12},{12,8},{9,1... | collective-permute-start | bytes 786440 | tf_op jit(solution)/shard_map/ppermute | solution.py:369
  4.9 14.5 %collective-permute-start.2 = (bf16[128,1024]{1,0:T(8,128)(2,1)S(1)}, bf16[128,1024]{1,0:T(8,128)(2,1)}, u32[]{:S(2)}, u32[]{:S(2)}) collective-permute-start(bf16[128,1024]{1,0:T(8,128)(2,1)S(1)} %get-tuple-element.25.refs_0_), channel_id=1, source_target_pairs={{0,16},{16,0},{1,17},{17,1},{2,18},{18,2},{3,19},{19,3},{4,20},{20... | collective-permute-start | bytes 786440 | tf_op jit(solution)/shard_map/ppermute | solution.py:369
  7.5 13.9 %collective-permute-start.3 = (bf16[128,1024]{1,0:T(8,128)(2,1)S(1)}, bf16[128,1024]{1,0:T(8,128)(2,1)}, u32[]{:S(2)}, u32[]{:S(2)}) collective-permute-start(bf16[128,1024]{1,0:T(8,128)(2,1)S(1)} %get-tuple-element.25.refs_0_), channel_id=1, source_target_pairs={{0,8},{8,0},{1,9},{9,1},{2,10},{10,2},{3,11},{11,3},{4,12},{12,4},... | collective-permute-start | bytes 786440 | tf_op jit(solution)/shard_map/ppermute | solution.py:369
  10.9 10.5 %collective-permute-start.1 = (bf16[128,1024]{1,0:T(8,128)(2,1)}, bf16[128,1024]{1,0:T(8,128)(2,1)S(1)}, u32[]{:S(2)}, u32[]{:S(2)}) collective-permute-start(bf16[128,1024]{1,0:T(8,128)(2,1)} %get-tuple-element.24), channel_id=1, source_target_pairs={{0,4},{4,0},{1,5},{5,1},{2,6},{6,2},{3,7},{7,3},{8,12},{12,8},{9,1... | collective-permute-start | bytes 786440 | tf_op jit(solution)/shard_map/ppermute | solution.py:369
  11.4 13.9 %copy-start.14 = (bf16[128,1024]{1,0:T(8,128)(2,1)}, bf16[128,1024]{1,0:T(8,128)(2,1)S(1)}, u32[]{:S(2)}) copy-start(bf16[128,1024]{1,0:T(8,128)(2,1)S(1)} %collective-permute-done.refs_0_.refs_1_) | copy-start | bytes 786436
  11.4 13.9 %collective-permute-start.4 = (bf16[128,1024]{1,0:T(8,128)(2,1)S(1)}, bf16[128,1024]{1,0:T(8,128)(2,1)}, u32[]{:S(2)}, u32[]{:S(2)}) collective-permute-start(bf16[128,1024]{1,0:T(8,128)(2,1)S(1)} %collective-permute-done.refs_0_.refs_1_), channel_id=1, source_target_pairs={{0,8},{8,0},{1,9},{9,1},{2,10},{10,2},{3,11},{11,3},{4,12},{12,4},... | collective-permute-start | bytes 786440 | tf_op jit(solution)/shard_map/ppermute | solution.py:369
  21.4 3.9 %copy-start.2 = (bf16[128,1024]{1,0:T(8,128)(2,1)}, bf16[128,1024]{1,0:T(8,128)(2,1)S(1)}, u32[]{:S(2)}) copy-start(bf16[128,1024]{1,0:T(8,128)(2,1)S(1)} %collective-permute-done.1.refs_1_.other_ref) | copy-start | bytes 786436
  28.2 3.8 %copy-start.15 = (bf16[128,1024]{1,0:T(8,128)(2,1)S(1)}, bf16[128,1024]{1,0:T(8,128)(2,1)}, u32[]{:S(2)}) copy-start(bf16[128,1024]{1,0:T(8,128)(2,1)} %copy-done.14) | copy-start | bytes 786436
  28.2 19.6 %copy-start.3 = (bf16[128,1024]{1,0:T(8,128)(2,1)S(1)}, bf16[128,1024]{1,0:T(8,128)(2,1)}, u32[]{:S(2)}) copy-start(bf16[128,1024]{1,0:T(8,128)(2,1)} %copy-done.2) | copy-start | bytes 786436
  28.2 46.4 %all-to-all-start = ((bf16[8,160,1024]{2,1,0:T(8,128)(2,1)}), bf16[8,160,1024]{2,1,0:T(8,128)(2,1)S(1)}, u32[]{:S(2)}, u32[]{:S(2)}) async-start(bf16[8,160,1024]{2,1,0:T(8,128)(2,1)} %get-tuple-element.12), calls=%async_computation | async-start | bytes 5242880 | tf_op jit(solution)/shard_map/all_to_all | solution.py:365
  31.9 15.1 %collective-permute-start.5 = (bf16[128,1024]{1,0:T(8,128)(2,1)S(1)}, bf16[128,1024]{1,0:T(8,128)(2,1)S(1)}, u32[]{:S(2)}, u32[]{:S(2)}) collective-permute-start(bf16[128,1024]{1,0:T(8,128)(2,1)S(1)} %copy-done.15), channel_id=1, source_target_pairs={{0,16},{16,0},{1,17},{17,1},{2,18},{18,2},{3,19},{19,3},{4,20},{20... | collective-permute-start | bytes 786440 | tf_op jit(solution)/shard_map/ppermute | solution.py:369
  47.1 0.7 copy-start.16
  48.6 25.9 %collective-permute-start.8 = (bf16[256,1024]{1,0:T(8,128)(2,1)}, bf16[256,1024]{1,0:T(8,128)(2,1)}, u32[]{:S(2)}, u32[]{:S(2)}) collective-permute-start(bf16[256,1024]{1,0:T(8,128)(2,1)} %shard_map.89.refs_0_), channel_id=1, source_target_pairs={{0,16},{16,0},{1,17},{17,1},{2,18},{18,2},{3,19},{19,3},{4,20},{20... | collective-permute-start | bytes 1572872 | tf_op jit(solution)/shard_map/ppermute | solution.py:369
  48.6 32.0 %collective-permute-start.6 = (bf16[128,1024]{1,0:T(8,128)(2,1)}, bf16[128,1024]{1,0:T(8,128)(2,1)S(1)}, u32[]{:S(2)}, u32[]{:S(2)}) collective-permute-start(bf16[128,1024]{1,0:T(8,128)(2,1)} %collective-permute-done.2.refs_2_), channel_id=1, source_target_pairs={{0,8},{8,0},{1,9},{9,1},{2,10},{10,2},{3,11},{11,3},{4,12},{12,4},... | collective-permute-start | bytes 786440 | tf_op jit(solution)/shard_map/ppermute | solution.py:369
  51.4 29.2 %collective-permute-start.7 = (bf16[128,1024]{1,0:T(8,128)(2,1)}, bf16[128,1024]{1,0:T(8,128)(2,1)}, u32[]{:S(2)}, u32[]{:S(2)}) collective-permute-start(bf16[128,1024]{1,0:T(8,128)(2,1)} %copy-done.16), channel_id=1, source_target_pairs={{0,8},{8,0},{1,9},{9,1},{2,10},{10,2},{3,11},{11,3},{4,12},{12,4},... | collective-permute-start | bytes 786440 | tf_op jit(solution)/shard_map/ppermute | solution.py:369
  51.4 58.8 %collective-permute-start.9 = (bf16[256,1024]{1,0:T(8,128)(2,1)}, bf16[256,1024]{1,0:T(8,128)(2,1)}, u32[]{:S(2)}, u32[]{:S(2)}) collective-permute-start(bf16[256,1024]{1,0:T(8,128)(2,1)} %shard_map.89.refs_0_), channel_id=1, source_target_pairs={{0,8},{8,0},{1,9},{9,1},{2,10},{10,2},{3,11},{11,3},{4,12},{12,4},... | collective-permute-start | bytes 1572872 | tf_op jit(solution)/shard_map/ppermute | solution.py:369
  74.5 35.8 %collective-permute-start.10 = (bf16[256,1024]{1,0:T(8,128)(2,1)}, bf16[256,1024]{1,0:T(8,128)(2,1)}, u32[]{:S(2)}, u32[]{:S(2)}) collective-permute-start(bf16[256,1024]{1,0:T(8,128)(2,1)} %collective-permute-done.8.refs_1_), channel_id=1, source_target_pairs={{0,8},{8,0},{1,9},{9,1},{2,10},{10,2},{3,11},{11,3},{4,12},{12,4},... | collective-permute-start | bytes 1572872 | tf_op jit(solution)/shard_map/ppermute | solution.py:369
  77.7 0.8 copy-start.6
  78.5 8.2 %copy-start.12 = (bf16[256,1024]{1,0:T(8,128)(2,1)}, bf16[256,1024]{1,0:T(8,128)(2,1)S(1)}, u32[]{:S(2)}) copy-start(bf16[256,1024]{1,0:T(8,128)(2,1)S(1)} %get-tuple-element.20) | copy-start | bytes 1572868
  78.5 29.8 %collective-permute-start.11 = (bf16[256,1024]{1,0:T(8,128)(2,1)}, bf16[256,1024]{1,0:T(8,128)(2,1)}, u32[]{:S(2)}, u32[]{:S(2)}) collective-permute-start(bf16[256,1024]{1,0:T(8,128)(2,1)} %get-tuple-element.18), channel_id=1, source_target_pairs={{0,8},{8,0},{1,9},{9,1},{2,10},{10,2},{3,11},{11,3},{4,12},{12,4},... | collective-permute-start | bytes 1572872 | tf_op jit(solution)/shard_map/ppermute | solution.py:369
  80.5 0.7 copy-start.17
  97.0 0.7 copy-start.8
  97.7 12.6 %all-to-all-start.2 = ((bf16[8,128,128]{2,1,0:T(8,128)(2,1)}), bf16[8,128,128]{2,1,0:T(8,128)(2,1)S(1)}, u32[]{:S(2)}, u32[]{:S(2)}) async-start(bf16[8,128,128]{2,1,0:T(8,128)(2,1)} %copy-done.8), calls=%async_computation.2 | async-start | bytes 524288 | tf_op jit(solution)/shard_map/all_to_all | solution.py:365
  109.5 0.8 copy-start.4
  116.3 1.3 copy-start.1
  117.6 3.8 %copy-start.5 = (bf16[256,1024]{1,0:T(8,128)(2,1)S(1)}, bf16[256,1024]{1,0:T(8,128)(2,1)}, u32[]{:S(2)}) copy-start(bf16[256,1024]{1,0:T(8,128)(2,1)} %copy-done.4) | copy-start | bytes 1572868
  117.6 30.4 %copy-start.7 = (bf16[256,1024]{1,0:T(8,128)(2,1)S(1)}, bf16[256,1024]{1,0:T(8,128)(2,1)}, u32[]{:S(2)}) copy-start(bf16[256,1024]{1,0:T(8,128)(2,1)} %copy-done.6) | copy-start | bytes 1572868
  117.6 39.5 %all-to-all-start.3 = ((bf16[8,128,1024]{2,1,0:T(8,128)(2,1)}), bf16[8,128,1024]{2,1,0:T(8,128)(2,1)S(1)}, u32[]{:S(2)}, u32[]{:S(2)}) async-start(bf16[8,128,1024]{2,1,0:T(8,128)(2,1)} %copy-done.1), calls=%async_computation.3 | async-start | bytes 4194304 | tf_op jit(solution)/shard_map/all_to_all | solution.py:365
  121.4 25.2 %collective-permute-start.12 = (bf16[256,1024]{1,0:T(8,128)(2,1)}, bf16[256,1024]{1,0:T(8,128)(2,1)S(1)}, u32[]{:S(2)}, u32[]{:S(2)}) collective-permute-start(bf16[256,1024]{1,0:T(8,128)(2,1)} %copy-done.12), channel_id=1, source_target_pairs={{0,8},{8,0},{1,9},{9,1},{2,10},{10,2},{3,11},{11,3},{4,12},{12,4},... | collective-permute-start | bytes 1572872 | tf_op jit(solution)/shard_map/ppermute | solution.py:369
  121.5 26.5 %collective-permute-start.13 = (bf16[256,1024]{1,0:T(8,128)(2,1)S(1)}, bf16[256,1024]{1,0:T(8,128)(2,1)S(1)}, u32[]{:S(2)}, u32[]{:S(2)}) collective-permute-start(bf16[256,1024]{1,0:T(8,128)(2,1)S(1)} %copy-done.5), channel_id=1, source_target_pairs={{0,16},{16,0},{1,17},{17,1},{2,18},{18,2},{3,19},{19,3},{4,20},{20... | collective-permute-start | bytes 1572872 | tf_op jit(solution)/shard_map/ppermute | solution.py:369
  148.3 7.9 %collective-permute-start.14 = (bf16[128,1024]{1,0:T(8,128)(2,1)S(1)}, bf16[128,1024]{1,0:T(8,128)(2,1)S(1)}, u32[]{:S(2)}, u32[]{:S(2)}) collective-permute-start(bf16[128,1024]{1,0:T(8,128)(2,1)S(1)} %slice.9), channel_id=1, source_target_pairs={{0,4},{4,0},{1,5},{5,1},{2,6},{6,2},{3,7},{7,3},{8,12},{12,8},{9,1... | collective-permute-start | bytes 786440 | tf_op jit(solution)/shard_map/ppermute | solution.py:369

commit v12 on v11

--- a/solution.py
+++ b/solution.py
@@ -72,6 +72,40 @@
         out_shape=jax.ShapeDtypeStruct((2 * own.shape[0], own.shape[1]), own.dtype),
         compiler_params=params(),
     )(own, other, *in_hbm(*before))
+
+
+def pass_on(value, before):
+    anywhere = pl.BlockSpec(memory_space=pl.ANY)
+    return pl.pallas_call(
+        lambda *refs: None,
+        in_specs=[anywhere] * (1 + len(before)),
+        out_specs=anywhere,
+        out_shape=jax.ShapeDtypeStruct(value.shape, value.dtype),
+        input_output_aliases={0: 0},
+        compiler_params=params(),
+    )(value, *before)
+
+
+def place_kernel(near_ref, kept_ref, passed_ref, before_ref, out_ref):
+    features = kept_ref.shape[1]
+    first = near_ref[0] == 0
+    kept, passed = kept_ref[...], passed_ref[...]
+    out_ref[:, 0:features] = jnp.where(first, kept, passed)
+    out_ref[:, features:] = jnp.where(first, passed, kept)
+
+
+def place_halves(near, kept, passed, before):
+    rows, features = kept.shape
+    return pl.pallas_call(
+        place_kernel,
+        in_specs=[
+            pl.BlockSpec(memory_space=pltpu.SMEM),
+            *[pl.BlockSpec(memory_space=pltpu.VMEM)] * 2,
+            pl.BlockSpec(memory_space=pl.ANY),
+        ],
+        out_shape=jax.ShapeDtypeStruct((rows, PAIR * features), kept.dtype),
+        compiler_params=params(),
+    )(near[None], kept, passed, *in_hbm(before))
 
 
 def add_kernel(count, *refs):
@@ -290,11 +324,11 @@
             *[pl.BlockSpec(memory_space=pl.ANY) for _ in before],
         ],
         out_specs=pl.BlockSpec((2, rows, wide), lambda i: (i, 0, 0)),
-        out_shape=jax.ShapeDtypeStruct((sources, rows, wide), jnp.bfloat16),
+        out_shape=pltpu.HBM((sources, rows, wide), jnp.bfloat16),
         scratch_shapes=[pltpu.VMEM((joined, features), jnp.bfloat16)],
         compiler_params=params(),
         cost_estimate=cost(sources * rows, features, joined),
-    )(received, *in_hbm(*pieces, *before))
+    )(received, *in_hbm(*pieces), *before)
 
 
 def hidden_kernel(parts_ref, activation_ref, scaled_ref, hidden_ref, gate_ref):
@@ -351,7 +385,7 @@
             *[pl.BlockSpec(memory_space=pl.ANY) for _ in before],
         ],
         out_specs=pl.BlockSpec((2, rows, features), lambda i: (i, 0, 0)),
-        out_shape=jax.ShapeDtypeStruct((sources, rows, features), jnp.bfloat16),
+        out_shape=pltpu.HBM((sources, rows, features), jnp.bfloat16),
         scratch_shapes=[
             pltpu.VMEM((joined, features), jnp.bfloat16),
             pltpu.VMEM((2 * rows, joined), jnp.bfloat16),
@@ -402,7 +436,6 @@
         up_own = stack(*up_halves, beside[1:])
         up_beside = swap(up_own, "high")
         up_low = swap(up_own, "low")
-        up_pieces = [up_own, up_beside, up_low, swap(up_beside, "low")]
     else:
         down_pieces = [lax.all_gather(stack(*down_halves, ()), FAR, tiled=True)]
         up_pieces = [lax.all_gather(stack(*up_halves, ()), FAR, tiled=True)]
@@ -416,6 +449,9 @@
         received, tok_count, wide, own_rows * PAIR * far_count, far_count if paired else 1, ()
     )
     projected = project(received, down_pieces, tok_count, wide, partial_value[:1])
+    if paired:
+        up_beside = pass_on(up_beside, (projected,))
+        up_pieces = [up_own, up_beside, up_low, swap(up_beside, "low")]
     parts = exchange(projected, GROUP)
     hidden_grad, gate_grads = pl.pallas_call(
         hidden_kernel,
@@ -428,17 +464,20 @@
     if paired:
         own, beside, low, low_beside = partial_value
         before = add_pairs([(beside, swap(low_beside, "low"))], ())
-        sums = add(own, swap(low, "low"), swap(before[0], "high"))
+        low = swap(low, "low")
+        passed, kept = [
+            add(own[at], low[at], swap(before[0][at], "high"))
+            for at in (slice(own_rows, None), slice(0, own_rows))
+        ]
     else:
         before = ()
         sums = lax.psum_scatter(partial_value[0], FAR, scatter_dimension=0, tiled=True)
+        kept, passed = sums[:own_rows], sums[own_rows:]
     rows_back = input_rows(received, exchange(hidden_grad, GROUP), up_pieces, before)
     input_grads = unpack_tokens(exchange(rows_back, GROUP))
 
-    kept, passed = sums[:own_rows], swap(sums[own_rows:], "near")
-    down_grads = jnp.concatenate(
-        [jnp.where(near == 0, kept, passed), jnp.where(near == 0, passed, kept)], axis=1
-    ).reshape(down_weight.shape)
+    down_grads = place_halves(near, kept, swap(passed, "near"), input_grads)
+    down_grads = down_grads.reshape(down_weight.shape)
     return (input_grads, gate_grads.T, down_grads)
 
 

time: 159 us -> 155 us (0.975)
  waiting for transfers between devices: 84.6 us -> 80.6 us
  Pallas kernels: 22.1 us -> 24.4 us
  local copies, waits for them, and re-layouts: 8.01 us -> 6.22 us
    ppermute x15 -> x16, waiting for transfers between devices: 84.6 us -> 67.8 us  [swap(): return lax.ppermute(value, axis, SWAP)]
    all_to_all x3, waiting for transfers between devices: 0.01 us -> 12.8 us  [exchange(): return lax.all_to_all(value, axes, split_axis=0, concat_axis=0, tiled=True)]
    unnamed x36 -> x38, local copies, waits for them, and re-layouts: 5 us -> 3.2 us
    ppermute x15 -> x16, starting transfers between devices: 21.7 us -> 21.8 us  [swap(): return lax.ppermute(value, axis, SWAP)]
  transfers between devices with their start and end apart: 18 -> 19, of which waited for: 9 -> 12; matrix products, arithmetic and copies ran while one was open for 2% -> 1% of each run, Pallas kernels for 7% -> 9%
where the time goes in v12:
time: 155 us
  waiting for transfers between devices  80.6 us (52%)
  starting transfers between devices  32.7 us (21%)
  Pallas kernels  24.4 us (16%)
  blocking collectives  9.47 us (6%)
  local copies, waits for them, and re-layouts  6.22 us (4%)
    ppermute x16, waiting for transfers between devices, swap(): return lax.ppermute(value, axis, SWAP)  67.8 us
    ppermute x16, starting transfers between devices, swap(): return lax.ppermute(value, axis, SWAP)  21.8 us
    all_to_all x3, waiting for transfers between devices, exchange(): return lax.all_to_all(value, axes, split_axis=0, concat_axis=0, tiled=True)  12.8 us
    all_to_all x3, starting transfers between devices, exchange(): return lax.all_to_all(value, axes, split_axis=0, concat_axis=0, tiled=True)  10.9 us
    all_to_all x1, blocking collectives, exchange(): return lax.all_to_all(value, axes, split_axis=0, concat_axis=0, tiled=True)  9.47 us
    pallas_call x1, Pallas kernels, input_rows(): pl.pallas_call(functools.partial(input_kernel, len(pieces)), grid=(source...  6.8 us
    pallas_call x1, Pallas kernels, project(): pl.pallas_call(functools.partial(project_kernel, len(pieces)), grid=(sour...  6.17 us
    unnamed x38, local copies, waits for them, and re-layouts  3.2 us
  transfers between devices with their start and end apart: 19, of which 12 were waited for; matrix products, arithmetic and copies ran while one was open for 1% of the time, Pallas kernels for 9%

profile of v12, /device:TPU:0, one launch (start us, length us, event | category | flops | bytes accessed | tf_op | source)
XLA Modules:
  0.0 154.6 jit_solution(9307933610770517284)
XLA Ops:
  0.6 0.0 copy-start.10
  0.6 0.0 copy-start.11
  0.7 0.0 copy-start.2
  0.7 0.0 copy-start.9
  0.7 1.2 constant_dynamic-slice_fusion.1
  1.9 0.0 copy-start.13
  1.9 3.0 %collective-permute-start = (bf16[128,1024]{1,0:T(8,128)(2,1)S(1)}, bf16[128,1024]{1,0:T(8,128)(2,1)S(1)}, u32[]{:S(2)}, u32[]{:S(2)}) collective-permute-start(bf16[128,1024]{1,0:T(8,128)(2,1)S(1)} %get-tuple-element.28), channel_id=1, source_target_pairs={{0,4},{4,0},{1,5},{5,1},{2,6},{6,2},{3,7},{7,3},{8,12},{12,8},{9,1... | collective-permute-start | bytes 786440 | tf_op jit(solution)/shard_map/ppermute | solution.py:403
  4.9 2.6 %collective-permute-start.2 = (bf16[128,1024]{1,0:T(8,128)(2,1)S(1)}, bf16[128,1024]{1,0:T(8,128)(2,1)S(1)}, u32[]{:S(2)}, u32[]{:S(2)}) collective-permute-start(bf16[128,1024]{1,0:T(8,128)(2,1)S(1)} %get-tuple-element.27.refs_0_), channel_id=1, source_target_pairs={{0,16},{16,0},{1,17},{17,1},{2,18},{18,2},{3,19},{19,3},{4,20},{20... | collective-permute-start | bytes 786440 | tf_op jit(solution)/shard_map/ppermute | solution.py:403
  7.5 1.6 %collective-permute-start.3 = (bf16[128,1024]{1,0:T(8,128)(2,1)S(1)}, bf16[128,1024]{1,0:T(8,128)(2,1)}, u32[]{:S(2)}, u32[]{:S(2)}) collective-permute-start(bf16[128,1024]{1,0:T(8,128)(2,1)S(1)} %get-tuple-element.27.refs_0_), channel_id=1, source_target_pairs={{0,8},{8,0},{1,9},{9,1},{2,10},{10,2},{3,11},{11,3},{4,12},{12,4},... | collective-permute-start | bytes 786440 | tf_op jit(solution)/shard_map/ppermute | solution.py:403
  9.1 1.8 %constant_dynamic-slice_fusion = (bf16[128,1024]{1,0:T(8,128)(2,1)S(1)}, bf16[128,1024]{1,0:T(8,128)(2,1)}) fusion(bf16[128,2048]{1,0:T(8,128)(2,1)} %bitcast.10, s32[]{:T(128)S(6)} %select_n.23, s32[]{:T(128)S(6)} %select_n.22), kind=kLoop, calls=%fused_computation.4 | loop fusion | bytes 1048584 | tf_op jit(solution)/shard_map/dynamic_slice | solution.py:421
  10.9 0.5 collective-permute-start.1
  11.4 0.0 collective-permute-done.refs_0_.refs_1_
  11.4 1.7 %collective-permute-start.4 = (bf16[128,1024]{1,0:T(8,128)(2,1)S(1)}, bf16[128,1024]{1,0:T(8,128)(2,1)}, u32[]{:S(2)}, u32[]{:S(2)}) collective-permute-start(bf16[128,1024]{1,0:T(8,128)(2,1)S(1)} %collective-permute-done.refs_0_.refs_1_), channel_id=1, source_target_pairs={{0,8},{8,0},{1,9},{9,1},{2,10},{10,2},{3,11},{11,3},{4,12},{12,4},... | collective-permute-start | bytes 786440 | tf_op jit(solution)/shard_map/ppermute | solution.py:403
  13.1 6.3 %collective-permute-done.2.refs_2_ = bf16[128,1024]{1,0:T(8,128)(2,1)S(1)} collective-permute-done((bf16[128,1024]{1,0:T(8,128)(2,1)S(1)}, bf16[128,1024]{1,0:T(8,128)(2,1)S(1)}, u32[]{:S(2)}, u32[]{:S(2)}) %collective-permute-start.2) | collective-permute-done | bytes 262176 | tf_op jit(solution)/shard_map/ppermute | solution.py:403
  19.3 2.1 %collective-permute-done.3.refs_3_.refs_4_ = bf16[128,1024]{1,0:T(8,128)(2,1)} collective-permute-done((bf16[128,1024]{1,0:T(8,128)(2,1)S(1)}, bf16[128,1024]{1,0:T(8,128)(2,1)}, u32[]{:S(2)}, u32[]{:S(2)}) %collective-permute-start.3) | collective-permute-done | bytes 262176 | tf_op jit(solution)/shard_map/ppermute | solution.py:403
  21.4 0.0 collective-permute-done.1.refs_1_.other_ref
  21.4 3.9 %collective-permute-done.4.refs_4_.refs_5_ = bf16[128,1024]{1,0:T(8,128)(2,1)} collective-permute-done((bf16[128,1024]{1,0:T(8,128)(2,1)S(1)}, bf16[128,1024]{1,0:T(8,128)(2,1)}, u32[]{:S(2)}, u32[]{:S(2)}) %collective-permute-start.4) | collective-permute-done | bytes 262176 | tf_op jit(solution)/shard_map/ppermute | solution.py:403
  25.2 0.0 copy-done.16
  25.3 2.9 %shard_map.85 = (bf16[8,160,1024]{2,1,0:T(8,128)(2,1)}, f32[128,128]{1,0:T(8,128)S(1)}, f32[128,128]{1,0:T(8,128)S(1)}) custom-call(s32[4]{0:T(128)S(1)} %fusion.2.far_ref, s32[2,128]{1,0:T(2,128)S(1)} %bitcast.7, bf16[2,128]{1,0:T(2,128)(2,1)S(1)} %bitcast.8, bf16[128,128]{1,0:T(8,128)(2,1)S(1)} %copy-done.9, bf16[128,8192]{1,0:T(8,128)(2,1)S(1)} %copy-done.2, ...), custom_call_target="tpu_custom_call" | custom-call | tf_op jit(solution)/shard_map/pallas_call | solution.py:175
  28.2 0.0 copy-done.13
  28.2 3.8 %all-to-all-start = ((bf16[8,160,1024]{2,1,0:T(8,128)(2,1)}), bf16[8,160,1024]{2,1,0:T(8,128)(2,1)S(1)}, u32[]{:S(2)}, u32[]{:S(2)}) async-start(bf16[8,160,1024]{2,1,0:T(8,128)(2,1)} %get-tuple-element.12), calls=%async_computation | async-start | bytes 5242880 | tf_op jit(solution)/shard_map/all_to_all | solution.py:399
  32.0 1.4 collective-permute-start.5
  33.4 13.7 %collective-permute-done.5.refs_3_.refs_0_ = bf16[128,1024]{1,0:T(8,128)(2,1)S(1)} collective-permute-done((bf16[128,1024]{1,0:T(8,128)(2,1)S(1)}, bf16[128,1024]{1,0:T(8,128)(2,1)S(1)}, u32[]{:S(2)}, u32[]{:S(2)}) %collective-permute-start.5) | collective-permute-done | bytes 262176 | tf_op jit(solution)/shard_map/ppermute | solution.py:403
  47.1 0.7 copy-done.17
  47.8 0.8 shard_map.89.refs_0_
  48.6 0.0 collective-permute-start.8
  48.7 2.8 %collective-permute-start.6 = (bf16[128,1024]{1,0:T(8,128)(2,1)}, bf16[128,1024]{1,0:T(8,128)(2,1)S(1)}, u32[]{:S(2)}, u32[]{:S(2)}) collective-permute-start(bf16[128,1024]{1,0:T(8,128)(2,1)} %copy-done.16), channel_id=1, source_target_pairs={{0,8},{8,0},{1,9},{9,1},{2,10},{10,2},{3,11},{11,3},{4,12},{12,4},... | collective-permute-start | bytes 786440 | tf_op jit(solution)/shard_map/ppermute | solution.py:403
  51.4 0.0 collective-permute-start.7
  51.5 2.0 %collective-permute-start.9 = (bf16[256,1024]{1,0:T(8,128)(2,1)}, bf16[256,1024]{1,0:T(8,128)(2,1)}, u32[]{:S(2)}, u32[]{:S(2)}) collective-permute-start(bf16[256,1024]{1,0:T(8,128)(2,1)} %shard_map.89.refs_0_), channel_id=1, source_target_pairs={{0,8},{8,0},{1,9},{9,1},{2,10},{10,2},{3,11},{11,3},{4,12},{12,4},... | collective-permute-start | bytes 1572872 | tf_op jit(solution)/shard_map/ppermute | solution.py:403
  53.5 9.8 %all-to-all-done.received_ref = bf16[8,160,1024]{2,1,0:T(8,128)(2,1)S(1)} async-done(((bf16[8,160,1024]{2,1,0:T(8,128)(2,1)}), bf16[8,160,1024]{2,1,0:T(8,128)(2,1)S(1)}, u32[]{:S(2)}, u32[]{:S(2)}) %all-to-all-start) | async-done | bytes 2621472 | tf_op jit(solution)/shard_map/all_to_all | solution.py:399
  63.3 3.2 %shard_map.86 = (bf16[256,1024]{1,0:T(8,128)(2,1)S(1)}, bf16[256,1024]{1,0:T(8,128)(2,1)S(1)}, bf16[256,1024]{1,0:T(8,128)(2,1)S(1)}, bf16[256,1024]{1,0:T(8,128)(2,1)}) custom-call(bf16[8,160,1024]{2,1,0:T(8,128)(2,1)S(1)} %all-to-all-done.received_ref), custom_call_target="tpu_custom_call" | custom-call | flops 2147483648 | bytes 6291456 | tf_op jit(solution)/shard_map/pallas_call | solution.py:255
  66.5 1.4 collective-permute-start.11
  67.9 0.0 collective-permute-done.6.refs_6_
  67.9 7.6 %collective-permute-done.7.refs_7_ = bf16[128,1024]{1,0:T(8,128)(2,1)} collective-permute-done((bf16[128,1024]{1,0:T(8,128)(2,1)}, bf16[128,1024]{1,0:T(8,128)(2,1)}, u32[]{:S(2)}, u32[]{:S(2)}) %collective-permute-start.7) | collective-permute-done | bytes 262176 | tf_op jit(solution)/shard_map/ppermute | solution.py:403
  75.5 0.0 copy-done.18
  75.5 6.2 %shard_map.87.refs_1_ = bf16[8,128,128]{2,1,0:T(8,128)(2,1)} custom-call(bf16[8,160,1024]{2,1,0:T(8,128)(2,1)S(1)} %all-to-all-done.received_ref, bf16[128,1024]{1,0:T(8,128)(2,1)} %copy-done.13, bf16[128,1024]{1,0:T(8,128)(2,1)} %copy-done.14, bf16[128,1024]{1,0:T(8,128)(2,1)} %copy-done.16, bf16[128,1024]{1,0:T(8,128)(2,1)} %copy-done.17, ...), custom_call_target="tpu_custom_call" | custom-call | flops 2147483648 | bytes 6291456 | tf_op jit(solution)/shard_map/pallas_call | solution.py:318
  81.7 0.0 collective-permute-done.8.refs_0_
  81.7 0.9 copy-done.5
  82.7 0.0 collective-permute-start.10
  82.7 9.5 %all_to_all.20.parts_ref = bf16[8,128,128]{2,1,0:T(8,128)(2,1)S(1)} all-to-all(bf16[8,128,128]{2,1,0:T(8,128)(2,1)S(1)} %copy-done.5), channel_id=1, replica_groups=mesh['high'=2,'low'=2,'near'=2,'inner'=2,'outer'=2] {'inner','outer','ne..., dimensions={0} | all-to-all | bytes 524288 | tf_op jit(solution)/shard_map/all_to_all | solution.py:399
  92.2 0.7 shard_map.88
  92.9 0.7 copy-done.8
  93.6 3.4 %all-to-all-start.2 = ((bf16[8,128,128]{2,1,0:T(8,128)(2,1)}), bf16[8,128,128]{2,1,0:T(8,128)(2,1)S(1)}, u32[]{:S(2)}, u32[]{:S(2)}) async-start(bf16[8,128,128]{2,1,0:T(8,128)(2,1)} %copy-done.8), calls=%async_computation.2 | async-start | bytes 524288 | tf_op jit(solution)/shard_map/all_to_all | solution.py:399
  97.0 1.0 collective-permute-done.11.refs_1_
  98.0 1.2 shard_map.91.refs_4_
  99.2 0.0 copy-start
  99.2 0.8 copy-done
  100.0 0.0 collective-permute-done.9.refs_2_
  100.0 3.0 %all-to-all-done.2.hidden_ref = bf16[8,128,128]{2,1,0:T(8,128)(2,1)S(1)} async-done(((bf16[8,128,128]{2,1,0:T(8,128)(2,1)}), bf16[8,128,128]{2,1,0:T(8,128)(2,1)S(1)}, u32[]{:S(2)}, u32[]{:S(2)}) %all-to-all-start.2) | async-done | bytes 262176 | tf_op jit(solution)/shard_map/all_to_all | solution.py:399
  103.0 5.4 %collective-permute-done.10.refs_3_ = bf16[256,1024]{1,0:T(8,128)(2,1)} collective-permute-done((bf16[256,1024]{1,0:T(8,128)(2,1)}, bf16[256,1024]{1,0:T(8,128)(2,1)}, u32[]{:S(2)}, u32[]{:S(2)}) %collective-permute-start.10) | collective-permute-done | bytes 524320 | tf_op jit(solution)/shard_map/ppermute | solution.py:403
  108.4 6.8 %shard_map.92 = bf16[8,128,1024]{2,1,0:T(8,128)(2,1)} custom-call(bf16[8,160,1024]{2,1,0:T(8,128)(2,1)S(1)} %all-to-all-done.received_ref, bf16[8,128,128]{2,1,0:T(8,128)(2,1)S(1)} %all-to-all-done.2.hidden_ref, bf16[256,1024]{1,0:T(8,128)(2,1)} %shard_map.89.refs_0_, bf16[256,1024]{1,0:T(8,128)(2,1)} %shard_map.90.refs_1_, ...), custom_call_target="tpu_custom_call" | custom-call | flops 2147483648 | bytes 6291456 | tf_op jit(solution)/shard_map/pallas_call | solution.py:378
  115.2 3.8 %all-to-all-start.3 = ((bf16[8,128,1024]{2,1,0:T(8,128)(2,1)}), bf16[8,128,1024]{2,1,0:T(8,128)(2,1)S(1)}, u32[]{:S(2)}, u32[]{:S(2)}) async-start(bf16[8,128,1024]{2,1,0:T(8,128)(2,1)} %shard_map.92), calls=%async_computation.3 | async-start | bytes 4194304 | tf_op jit(solution)/shard_map/all_to_all | solution.py:399
  118.9 0.1 collective-permute-start.12
  119.0 2.4 %collective-permute-start.13 = (bf16[128,1024]{1,0:T(8,128)(2,1)S(1)}, bf16[128,1024]{1,0:T(8,128)(2,1)S(1)}, u32[]{:S(2)}, u32[]{:S(2)}) collective-permute-start(bf16[128,1024]{1,0:T(8,128)(2,1)S(1)} %get-tuple-element.24), channel_id=1, source_target_pairs={{0,16},{16,0},{1,17},{17,1},{2,18},{18,2},{3,19},{19,3},{4,20},{20... | collective-permute-start | bytes 786440 | tf_op jit(solution)/shard_map/ppermute | solution.py:403
  121.5 0.6 collective-permute-start.14
  122.0 22.1 %collective-permute-done.12 = bf16[256,1024]{1,0:T(8,128)(2,1)S(1)} collective-permute-done((bf16[256,1024]{1,0:T(8,128)(2,1)}, bf16[256,1024]{1,0:T(8,128)(2,1)S(1)}, u32[]{:S(2)}, u32[]{:S(2)}) %collective-permute-start.12) | collective-permute-done | bytes 524320 | tf_op jit(solution)/shard_map/ppermute | solution.py:403
  144.1 0.0 collective-permute-done.13
  144.1 1.4 collective-permute-done.14
  145.6 0.3 add_convert_fusion
  145.8 1.7 %collective-permute-start.15 = (bf16[128,1024]{1,0:T(8,128)(2,1)S(1)}, bf16[128,1024]{1,0:T(8,128)(2,1)S(1)}, u32[]{:S(2)}, u32[]{:S(2)}) collective-permute-start(bf16[128,1024]{1,0:T(8,128)(2,1)S(1)} %get-tuple-element.21), channel_id=1, source_target_pairs={{0,4},{4,0},{1,5},{5,1},{2,6},{6,2},{3,7},{7,3},{8,12},{12,8},{9,1... | collective-permute-start | bytes 786440 | tf_op jit(solution)/shard_map/ppermute | solution.py:403
  147.6 0.0 all-to-all-done.3.parts_ref
  147.6 1.8 %shard_map.93.before_ref = bf16[128,8192]{1,0:T(8,128)(2,1)} custom-call(bf16[8,128,1024]{2,1,0:T(8,128)(2,1)S(1)} %all-to-all-done.3.parts_ref), custom_call_target="tpu_custom_call" | custom-call | tf_op jit(solution)/shard_map/pallas_call | solution.py:202
  149.4 4.4 %collective-permute-done.15.passed_ref = bf16[128,1024]{1,0:T(8,128)(2,1)S(1)} collective-permute-done((bf16[128,1024]{1,0:T(8,128)(2,1)S(1)}, bf16[128,1024]{1,0:T(8,128)(2,1)S(1)}, u32[]{:S(2)}, u32[]{:S(2)}) %collective-permute-start.15) | collective-permute-done | bytes 262176 | tf_op jit(solution)/shard_map/ppermute | solution.py:403
  153.8 0.8 shard_map.94
  (28 shorter events, 0.1 us)
Async XLA Ops:
  0.6 24.6 %copy-start.10 = (s32[128,2]{0,1:T(2,128)S(1)}, s32[128,2]{0,1:T(2,128)}, u32[]{:S(2)}) copy-start(s32[128,2]{0,1:T(2,128)} %param.8) | copy-start | bytes 3076
  0.6 24.6 %copy-start.11 = (bf16[128,2]{0,1:T(2,128)(2,1)S(1)}, bf16[128,2]{0,1:T(2,128)(2,1)}, u32[]{:S(2)}) copy-start(bf16[128,2]{0,1:T(2,128)(2,1)} %param.7) | copy-start | bytes 1540
  0.7 24.6 %copy-start.2 = (bf16[128,8192]{1,0:T(8,128)(2,1)S(1)}, bf16[128,8192]{1,0:T(8,128)(2,1)}, u32[]{:S(2)}) copy-start(bf16[128,8192]{1,0:T(8,128)(2,1)} %tokens_ref.1) | copy-start | bytes 6291460
  0.7 24.6 %copy-start.9 = (bf16[128,128]{1,0:T(8,128)(2,1)S(1)}, bf16[128,128]{1,0:T(8,128)(2,1)}, u32[]{:S(2)}) copy-start(bf16[128,128]{1,0:T(8,128)(2,1)} %preact_ref.1) | copy-start | bytes 98308
  1.9 26.3 %copy-start.13 = (bf16[128,1024]{1,0:T(8,128)(2,1)}, bf16[128,1024]{1,0:T(8,128)(2,1)S(1)}, u32[]{:S(2)}) copy-start(bf16[128,1024]{1,0:T(8,128)(2,1)S(1)} %get-tuple-element.27.refs_0_) | copy-start | bytes 786436
  1.9 9.5 %collective-permute-start = (bf16[128,1024]{1,0:T(8,128)(2,1)S(1)}, bf16[128,1024]{1,0:T(8,128)(2,1)S(1)}, u32[]{:S(2)}, u32[]{:S(2)}) collective-permute-start(bf16[128,1024]{1,0:T(8,128)(2,1)S(1)} %get-tuple-element.28), channel_id=1, source_target_pairs={{0,4},{4,0},{1,5},{5,1},{2,6},{6,2},{3,7},{7,3},{8,12},{12,8},{9,1... | collective-permute-start | bytes 786440 | tf_op jit(solution)/shard_map/ppermute | solution.py:403
  4.9 14.4 %collective-permute-start.2 = (bf16[128,1024]{1,0:T(8,128)(2,1)S(1)}, bf16[128,1024]{1,0:T(8,128)(2,1)S(1)}, u32[]{:S(2)}, u32[]{:S(2)}) collective-permute-start(bf16[128,1024]{1,0:T(8,128)(2,1)S(1)} %get-tuple-element.27.refs_0_), channel_id=1, source_target_pairs={{0,16},{16,0},{1,17},{17,1},{2,18},{18,2},{3,19},{19,3},{4,20},{20... | collective-permute-start | bytes 786440 | tf_op jit(solution)/shard_map/ppermute | solution.py:403
  7.5 13.9 %collective-permute-start.3 = (bf16[128,1024]{1,0:T(8,128)(2,1)S(1)}, bf16[128,1024]{1,0:T(8,128)(2,1)}, u32[]{:S(2)}, u32[]{:S(2)}) collective-permute-start(bf16[128,1024]{1,0:T(8,128)(2,1)S(1)} %get-tuple-element.27.refs_0_), channel_id=1, source_target_pairs={{0,8},{8,0},{1,9},{9,1},{2,10},{10,2},{3,11},{11,3},{4,12},{12,4},... | collective-permute-start | bytes 786440 | tf_op jit(solution)/shard_map/ppermute | solution.py:403
  10.9 10.5 %collective-permute-start.1 = (bf16[128,1024]{1,0:T(8,128)(2,1)}, bf16[128,1024]{1,0:T(8,128)(2,1)S(1)}, u32[]{:S(2)}, u32[]{:S(2)}) collective-permute-start(bf16[128,1024]{1,0:T(8,128)(2,1)} %get-tuple-element.26), channel_id=1, source_target_pairs={{0,4},{4,0},{1,5},{5,1},{2,6},{6,2},{3,7},{7,3},{8,12},{12,8},{9,1... | collective-permute-start | bytes 786440 | tf_op jit(solution)/shard_map/ppermute | solution.py:403
  11.4 13.9 %copy-start.14 = (bf16[128,1024]{1,0:T(8,128)(2,1)}, bf16[128,1024]{1,0:T(8,128)(2,1)S(1)}, u32[]{:S(2)}) copy-start(bf16[128,1024]{1,0:T(8,128)(2,1)S(1)} %collective-permute-done.refs_0_.refs_1_) | copy-start | bytes 786436
  11.4 13.9 %collective-permute-start.4 = (bf16[128,1024]{1,0:T(8,128)(2,1)S(1)}, bf16[128,1024]{1,0:T(8,128)(2,1)}, u32[]{:S(2)}, u32[]{:S(2)}) collective-permute-start(bf16[128,1024]{1,0:T(8,128)(2,1)S(1)} %collective-permute-done.refs_0_.refs_1_), channel_id=1, source_target_pairs={{0,8},{8,0},{1,9},{9,1},{2,10},{10,2},{3,11},{11,3},{4,12},{12,4},... | collective-permute-start | bytes 786440 | tf_op jit(solution)/shard_map/ppermute | solution.py:403
  19.3 5.9 %copy-start.16 = (bf16[128,1024]{1,0:T(8,128)(2,1)}, bf16[128,1024]{1,0:T(8,128)(2,1)S(1)}, u32[]{:S(2)}) copy-start(bf16[128,1024]{1,0:T(8,128)(2,1)S(1)} %collective-permute-done.2.refs_2_) | copy-start | bytes 786436
  21.4 3.9 %copy-start.3 = (bf16[128,1024]{1,0:T(8,128)(2,1)}, bf16[128,1024]{1,0:T(8,128)(2,1)S(1)}, u32[]{:S(2)}) copy-start(bf16[128,1024]{1,0:T(8,128)(2,1)S(1)} %collective-permute-done.1.refs_1_.other_ref) | copy-start | bytes 786436
  28.2 3.8 %copy-start.15 = (bf16[128,1024]{1,0:T(8,128)(2,1)S(1)}, bf16[128,1024]{1,0:T(8,128)(2,1)}, u32[]{:S(2)}) copy-start(bf16[128,1024]{1,0:T(8,128)(2,1)} %copy-done.14) | copy-start | bytes 786436
  28.2 19.6 %copy-start.4 = (bf16[128,1024]{1,0:T(8,128)(2,1)S(1)}, bf16[128,1024]{1,0:T(8,128)(2,1)}, u32[]{:S(2)}) copy-start(bf16[128,1024]{1,0:T(8,128)(2,1)} %copy-done.3) | copy-start | bytes 786436
  28.2 35.1 %all-to-all-start = ((bf16[8,160,1024]{2,1,0:T(8,128)(2,1)}), bf16[8,160,1024]{2,1,0:T(8,128)(2,1)S(1)}, u32[]{:S(2)}, u32[]{:S(2)}) async-start(bf16[8,160,1024]{2,1,0:T(8,128)(2,1)} %get-tuple-element.12), calls=%async_computation | async-start | bytes 5242880 | tf_op jit(solution)/shard_map/all_to_all | solution.py:399
  32.0 15.1 %collective-permute-start.5 = (bf16[128,1024]{1,0:T(8,128)(2,1)S(1)}, bf16[128,1024]{1,0:T(8,128)(2,1)S(1)}, u32[]{:S(2)}, u32[]{:S(2)}) collective-permute-start(bf16[128,1024]{1,0:T(8,128)(2,1)S(1)} %copy-done.15), channel_id=1, source_target_pairs={{0,16},{16,0},{1,17},{17,1},{2,18},{18,2},{3,19},{19,3},{4,20},{20... | collective-permute-start | bytes 786440 | tf_op jit(solution)/shard_map/ppermute | solution.py:403
  47.1 0.7 copy-start.17
  48.6 33.1 %collective-permute-start.8 = (bf16[256,1024]{1,0:T(8,128)(2,1)}, bf16[256,1024]{1,0:T(8,128)(2,1)}, u32[]{:S(2)}, u32[]{:S(2)}) collective-permute-start(bf16[256,1024]{1,0:T(8,128)(2,1)} %shard_map.89.refs_0_), channel_id=1, source_target_pairs={{0,16},{16,0},{1,17},{17,1},{2,18},{18,2},{3,19},{19,3},{4,20},{20... | collective-permute-start | bytes 1572872 | tf_op jit(solution)/shard_map/ppermute | solution.py:403
  48.7 19.3 %collective-permute-start.6 = (bf16[128,1024]{1,0:T(8,128)(2,1)}, bf16[128,1024]{1,0:T(8,128)(2,1)S(1)}, u32[]{:S(2)}, u32[]{:S(2)}) collective-permute-start(bf16[128,1024]{1,0:T(8,128)(2,1)} %copy-done.16), channel_id=1, source_target_pairs={{0,8},{8,0},{1,9},{9,1},{2,10},{10,2},{3,11},{11,3},{4,12},{12,4},... | collective-permute-start | bytes 786440 | tf_op jit(solution)/shard_map/ppermute | solution.py:403
  51.4 24.1 %collective-permute-start.7 = (bf16[128,1024]{1,0:T(8,128)(2,1)}, bf16[128,1024]{1,0:T(8,128)(2,1)}, u32[]{:S(2)}, u32[]{:S(2)}) collective-permute-start(bf16[128,1024]{1,0:T(8,128)(2,1)} %copy-done.17), channel_id=1, source_target_pairs={{0,8},{8,0},{1,9},{9,1},{2,10},{10,2},{3,11},{11,3},{4,12},{12,4},... | collective-permute-start | bytes 786440 | tf_op jit(solution)/shard_map/ppermute | solution.py:403
  51.5 48.5 %collective-permute-start.9 = (bf16[256,1024]{1,0:T(8,128)(2,1)}, bf16[256,1024]{1,0:T(8,128)(2,1)}, u32[]{:S(2)}, u32[]{:S(2)}) collective-permute-start(bf16[256,1024]{1,0:T(8,128)(2,1)} %shard_map.89.refs_0_), channel_id=1, source_target_pairs={{0,8},{8,0},{1,9},{9,1},{2,10},{10,2},{3,11},{11,3},{4,12},{12,4},... | collective-permute-start | bytes 1572872 | tf_op jit(solution)/shard_map/ppermute | solution.py:403
  66.5 15.2 %copy-start.6 = (bf16[256,1024]{1,0:T(8,128)(2,1)}, bf16[256,1024]{1,0:T(8,128)(2,1)S(1)}, u32[]{:S(2)}) copy-start(bf16[256,1024]{1,0:T(8,128)(2,1)S(1)} %get-tuple-element.13.refs_8_) | copy-start | bytes 1572868
  66.5 15.2 %copy-start.12 = (bf16[256,1024]{1,0:T(8,128)(2,1)}, bf16[256,1024]{1,0:T(8,128)(2,1)S(1)}, u32[]{:S(2)}) copy-start(bf16[256,1024]{1,0:T(8,128)(2,1)S(1)} %get-tuple-element.20) | copy-start | bytes 1572868
  66.5 31.5 %collective-permute-start.11 = (bf16[256,1024]{1,0:T(8,128)(2,1)}, bf16[256,1024]{1,0:T(8,128)(2,1)}, u32[]{:S(2)}, u32[]{:S(2)}) collective-permute-start(bf16[256,1024]{1,0:T(8,128)(2,1)} %get-tuple-element.18), channel_id=1, source_target_pairs={{0,8},{8,0},{1,9},{9,1},{2,10},{10,2},{3,11},{11,3},{4,12},{12,4},... | collective-permute-start | bytes 1572872 | tf_op jit(solution)/shard_map/ppermute | solution.py:403
  67.9 7.6 %copy-start.18 = (bf16[128,1024]{1,0:T(8,128)(2,1)}, bf16[128,1024]{1,0:T(8,128)(2,1)S(1)}, u32[]{:S(2)}) copy-start(bf16[128,1024]{1,0:T(8,128)(2,1)S(1)} %collective-permute-done.6.refs_6_) | copy-start | bytes 786436
  81.7 1.0 copy-start.5
  82.7 25.7 %collective-permute-start.10 = (bf16[256,1024]{1,0:T(8,128)(2,1)}, bf16[256,1024]{1,0:T(8,128)(2,1)}, u32[]{:S(2)}, u32[]{:S(2)}) collective-permute-start(bf16[256,1024]{1,0:T(8,128)(2,1)} %shard_map.90.refs_1_), channel_id=1, source_target_pairs={{0,8},{8,0},{1,9},{9,1},{2,10},{10,2},{3,11},{11,3},{4,12},{12,4},... | collective-permute-start | bytes 1572872 | tf_op jit(solution)/shard_map/ppermute | solution.py:403
  92.9 0.7 copy-start.8
  93.6 9.4 %all-to-all-start.2 = ((bf16[8,128,128]{2,1,0:T(8,128)(2,1)}), bf16[8,128,128]{2,1,0:T(8,128)(2,1)S(1)}, u32[]{:S(2)}, u32[]{:S(2)}) async-start(bf16[8,128,128]{2,1,0:T(8,128)(2,1)} %copy-done.8), calls=%async_computation.2 | async-start | bytes 524288 | tf_op jit(solution)/shard_map/all_to_all | solution.py:399
  99.2 0.8 copy-start
  115.2 3.8 %copy-start.1 = (bf16[256,1024]{1,0:T(8,128)(2,1)S(1)}, bf16[256,1024]{1,0:T(8,128)(2,1)}, u32[]{:S(2)}) copy-start(bf16[256,1024]{1,0:T(8,128)(2,1)} %copy-done) | copy-start | bytes 1572868
  115.2 30.4 %copy-start.7 = (bf16[256,1024]{1,0:T(8,128)(2,1)S(1)}, bf16[256,1024]{1,0:T(8,128)(2,1)}, u32[]{:S(2)}) copy-start(bf16[256,1024]{1,0:T(8,128)(2,1)} %copy-done.6) | copy-start | bytes 1572868
  115.2 32.4 %all-to-all-start.3 = ((bf16[8,128,1024]{2,1,0:T(8,128)(2,1)}), bf16[8,128,1024]{2,1,0:T(8,128)(2,1)S(1)}, u32[]{:S(2)}, u32[]{:S(2)}) async-start(bf16[8,128,1024]{2,1,0:T(8,128)(2,1)} %shard_map.92), calls=%async_computation.3 | async-start | bytes 4194304 | tf_op jit(solution)/shard_map/all_to_all | solution.py:399
  118.9 25.2 %collective-permute-start.12 = (bf16[256,1024]{1,0:T(8,128)(2,1)}, bf16[256,1024]{1,0:T(8,128)(2,1)S(1)}, u32[]{:S(2)}, u32[]{:S(2)}) collective-permute-start(bf16[256,1024]{1,0:T(8,128)(2,1)} %copy-done.12), channel_id=1, source_target_pairs={{0,8},{8,0},{1,9},{9,1},{2,10},{10,2},{3,11},{11,3},{4,12},{12,4},... | collective-permute-start | bytes 1572872 | tf_op jit(solution)/shard_map/ppermute | solution.py:403
  119.0 25.1 %collective-permute-start.13 = (bf16[128,1024]{1,0:T(8,128)(2,1)S(1)}, bf16[128,1024]{1,0:T(8,128)(2,1)S(1)}, u32[]{:S(2)}, u32[]{:S(2)}) collective-permute-start(bf16[128,1024]{1,0:T(8,128)(2,1)S(1)} %get-tuple-element.24), channel_id=1, source_target_pairs={{0,16},{16,0},{1,17},{17,1},{2,18},{18,2},{3,19},{19,3},{4,20},{20... | collective-permute-start | bytes 786440 | tf_op jit(solution)/shard_map/ppermute | solution.py:403
  121.5 24.1 %collective-permute-start.14 = (bf16[128,1024]{1,0:T(8,128)(2,1)S(1)}, bf16[128,1024]{1,0:T(8,128)(2,1)S(1)}, u32[]{:S(2)}, u32[]{:S(2)}) collective-permute-start(bf16[128,1024]{1,0:T(8,128)(2,1)S(1)} %get-tuple-element.23), channel_id=1, source_target_pairs={{0,16},{16,0},{1,17},{17,1},{2,18},{18,2},{3,19},{19,3},{4,20},{20... | collective-permute-start | bytes 786440 | tf_op jit(solution)/shard_map/ppermute | solution.py:403
  145.8 7.9 %collective-permute-start.15 = (bf16[128,1024]{1,0:T(8,128)(2,1)S(1)}, bf16[128,1024]{1,0:T(8,128)(2,1)S(1)}, u32[]{:S(2)}, u32[]{:S(2)}) collective-permute-start(bf16[128,1024]{1,0:T(8,128)(2,1)S(1)} %get-tuple-element.21), channel_id=1, source_target_pairs={{0,4},{4,0},{1,5},{5,1},{2,6},{6,2},{3,7},{7,3},{8,12},{12,8},{9,1... | collective-permute-start | bytes 786440 | tf_op jit(solution)/shard_map/ppermute | solution.py:403

commit v13 on v12

--- a/solution.py
+++ b/solution.py
@@ -80,10 +80,10 @@
         lambda *refs: None,
         in_specs=[anywhere] * (1 + len(before)),
         out_specs=anywhere,
-        out_shape=jax.ShapeDtypeStruct(value.shape, value.dtype),
+        out_shape=pltpu.HBM(value.shape, value.dtype),
         input_output_aliases={0: 0},
         compiler_params=params(),
-    )(value, *before)
+    )(*in_hbm(value), *before)
 
 
 def place_kernel(near_ref, kept_ref, passed_ref, before_ref, out_ref):
@@ -433,9 +433,9 @@
         low_beside = [swap(half, "low") for half in beside]
         down_pieces = [*down_halves, *beside, *low, *low_beside]
         first += [beside[0], *low]
-        up_own = stack(*up_halves, beside[1:])
+        up_low = swap(stack(*up_halves, ()), "low")
+        up_own = stack(*up_halves, (beside[1], up_low))
         up_beside = swap(up_own, "high")
-        up_low = swap(up_own, "low")
     else:
         down_pieces = [lax.all_gather(stack(*down_halves, ()), FAR, tiled=True)]
         up_pieces = [lax.all_gather(stack(*up_halves, ()), FAR, tiled=True)]
@@ -453,10 +453,15 @@
         up_beside = pass_on(up_beside, (projected,))
         up_pieces = [up_own, up_beside, up_low, swap(up_beside, "low")]
     parts = exchange(projected, GROUP)
+    gathered = pl.BlockSpec((members, tok_count, wide), lambda i: (0, 0, 0))
+    single = pl.BlockSpec((tok_count, wide), lambda i: (0, 0))
     hidden_grad, gate_grads = pl.pallas_call(
         hidden_kernel,
+        grid=(1,),
+        in_specs=[gathered, single, single],
+        out_specs=(gathered, pl.BlockSpec((2, tok_count), lambda i: (0, 0))),
         out_shape=(
-            jax.ShapeDtypeStruct((members, tok_count, wide), jnp.bfloat16),
+            pltpu.HBM((members, tok_count, wide), jnp.bfloat16),
             jax.ShapeDtypeStruct((2, tok_count), jnp.bfloat16),
         ),
         compiler_params=params(),

time: 155 us -> 157 us (1.013)
  starting transfers between devices: 32.7 us -> 37.1 us
  waiting for transfers between devices: 80.6 us -> 78.1 us
    ppermute x16, starting transfers between devices: 21.8 us -> 26.2 us  [swap(): return lax.ppermute(value, axis, SWAP)]
    all_to_all x3, waiting for transfers between devices: 12.8 us -> 8.6 us  [exchange(): return lax.all_to_all(value, axes, split_axis=0, concat_axis=0, tiled=True)]
    ppermute x16, waiting for transfers between devices: 67.8 us -> 69.4 us  [swap(): return lax.ppermute(value, axis, SWAP)]
    unnamed x38 -> x36, local copies, waits for them, and re-layouts: 3.2 us -> 2.6 us
where the time goes in v13:
time: 157 us; the launch traced here: 156 us
  waiting for transfers between devices  78.1 us (50%)
  starting transfers between devices  37.1 us (24%)
  Pallas kernels  24.5 us (16%)
  blocking collectives  9.67 us (6%)
  local copies, waits for them, and re-layouts  5.61 us (4%)
    ppermute x16, waiting for transfers between devices, swap(): return lax.ppermute(value, axis, SWAP)  69.4 us
    ppermute x16, starting transfers between devices, swap(): return lax.ppermute(value, axis, SWAP)  26.2 us
    all_to_all x3, starting transfers between devices, exchange(): return lax.all_to_all(value, axes, split_axis=0, concat_axis=0, tiled=True)  10.9 us
    all_to_all x1, blocking collectives, exchange(): return lax.all_to_all(value, axes, split_axis=0, concat_axis=0, tiled=True)  9.67 us
    all_to_all x3, waiting for transfers between devices, exchange(): return lax.all_to_all(value, axes, split_axis=0, concat_axis=0, tiled=True)  8.6 us
    pallas_call x1, Pallas kernels, input_rows(): pl.pallas_call(functools.partial(input_kernel, len(pieces)), grid=(source...  6.79 us
    pallas_call x1, Pallas kernels, project(): pl.pallas_call(functools.partial(project_kernel, len(pieces)), grid=(sour...  6.17 us
    pallas_call x1, Pallas kernels, down_partial(): pl.pallas_call(functools.partial(down_kernel, rows, wide, count), in_spec...  3.19 us
  transfers between devices with their start and end apart: 19, of which 12 were waited for; matrix products, arithmetic and copies ran while one was open for 1% of the time, Pallas kernels for 9%

profile of v13, /device:TPU:0, one launch (start us, length us, event | category | flops | bytes accessed | tf_op | source)
XLA Modules:
  0.0 156.0 jit_solution(15573614748074479)
XLA Ops:
  0.6 0.0 copy-start.9
  0.6 0.0 copy-start.10
  0.7 0.0 copy-start.4
  0.7 0.0 copy-start.8
  0.7 1.2 constant_dynamic-slice_fusion.1
  1.9 0.0 copy-start.13
  1.9 3.0 %collective-permute-start = (bf16[128,1024]{1,0:T(8,128)(2,1)S(1)}, bf16[128,1024]{1,0:T(8,128)(2,1)S(1)}, u32[]{:S(2)}, u32[]{:S(2)}) collective-permute-start(bf16[128,1024]{1,0:T(8,128)(2,1)S(1)} %get-tuple-element.28), channel_id=1, source_target_pairs={{0,4},{4,0},{1,5},{5,1},{2,6},{6,2},{3,7},{7,3},{8,12},{12,8},{9,1... | collective-permute-start | bytes 786440 | tf_op jit(solution)/shard_map/ppermute | solution.py:403
  4.9 2.6 %collective-permute-start.2 = (bf16[128,1024]{1,0:T(8,128)(2,1)S(1)}, bf16[128,1024]{1,0:T(8,128)(2,1)}, u32[]{:S(2)}, u32[]{:S(2)}) collective-permute-start(bf16[128,1024]{1,0:T(8,128)(2,1)S(1)} %get-tuple-element.27.refs_0_), channel_id=1, source_target_pairs={{0,16},{16,0},{1,17},{17,1},{2,18},{18,2},{3,19},{19,3},{4,20},{20... | collective-permute-start | bytes 786440 | tf_op jit(solution)/shard_map/ppermute | solution.py:403
  7.5 1.6 %collective-permute-start.3 = (bf16[128,1024]{1,0:T(8,128)(2,1)S(1)}, bf16[128,1024]{1,0:T(8,128)(2,1)}, u32[]{:S(2)}, u32[]{:S(2)}) collective-permute-start(bf16[128,1024]{1,0:T(8,128)(2,1)S(1)} %get-tuple-element.27.refs_0_), channel_id=1, source_target_pairs={{0,8},{8,0},{1,9},{9,1},{2,10},{10,2},{3,11},{11,3},{4,12},{12,4},... | collective-permute-start | bytes 786440 | tf_op jit(solution)/shard_map/ppermute | solution.py:403
  9.1 1.8 %constant_dynamic-slice_fusion = (bf16[128,1024]{1,0:T(8,128)(2,1)S(1)}, bf16[128,1024]{1,0:T(8,128)(2,1)}) fusion(bf16[128,2048]{1,0:T(8,128)(2,1)} %bitcast.10, s32[]{:T(128)S(6)} %select_n.23, s32[]{:T(128)S(6)} %select_n.22), kind=kLoop, calls=%fused_computation.4 | loop fusion | bytes 1048584 | tf_op jit(solution)/shard_map/dynamic_slice | solution.py:421
  10.9 0.5 collective-permute-start.1
  11.4 0.0 collective-permute-done.refs_0_.refs_1_
  11.4 1.7 %collective-permute-start.4 = (bf16[128,1024]{1,0:T(8,128)(2,1)S(1)}, bf16[128,1024]{1,0:T(8,128)(2,1)}, u32[]{:S(2)}, u32[]{:S(2)}) collective-permute-start(bf16[128,1024]{1,0:T(8,128)(2,1)S(1)} %collective-permute-done.refs_0_.refs_1_), channel_id=1, source_target_pairs={{0,8},{8,0},{1,9},{9,1},{2,10},{10,2},{3,11},{11,3},{4,12},{12,4},... | collective-permute-start | bytes 786440 | tf_op jit(solution)/shard_map/ppermute | solution.py:403
  13.1 6.4 %collective-permute-done.2.refs_2_ = bf16[128,1024]{1,0:T(8,128)(2,1)} collective-permute-done((bf16[128,1024]{1,0:T(8,128)(2,1)S(1)}, bf16[128,1024]{1,0:T(8,128)(2,1)}, u32[]{:S(2)}, u32[]{:S(2)}) %collective-permute-start.2) | collective-permute-done | bytes 262176 | tf_op jit(solution)/shard_map/ppermute | solution.py:403
  19.4 2.0 %collective-permute-done.3.refs_3_.refs_4_ = bf16[128,1024]{1,0:T(8,128)(2,1)} collective-permute-done((bf16[128,1024]{1,0:T(8,128)(2,1)S(1)}, bf16[128,1024]{1,0:T(8,128)(2,1)}, u32[]{:S(2)}, u32[]{:S(2)}) %collective-permute-start.3) | collective-permute-done | bytes 262176 | tf_op jit(solution)/shard_map/ppermute | solution.py:403
  21.4 0.0 collective-permute-done.1.refs_1_.other_ref
  21.4 3.9 %collective-permute-done.4.refs_4_.refs_5_ = bf16[128,1024]{1,0:T(8,128)(2,1)} collective-permute-done((bf16[128,1024]{1,0:T(8,128)(2,1)S(1)}, bf16[128,1024]{1,0:T(8,128)(2,1)}, u32[]{:S(2)}, u32[]{:S(2)}) %collective-permute-start.4) | collective-permute-done | bytes 262176 | tf_op jit(solution)/shard_map/ppermute | solution.py:403
  25.2 0.0 copy-done.13
  25.2 0.0 copy-done.14
  25.2 0.0 copy-done
  25.3 0.0 copy-done.9
  25.3 2.9 %shard_map.85 = (bf16[8,160,1024]{2,1,0:T(8,128)(2,1)}, f32[128,128]{1,0:T(8,128)S(1)}, f32[128,128]{1,0:T(8,128)S(1)}) custom-call(s32[4]{0:T(128)S(1)} %fusion.2.far_ref, s32[2,128]{1,0:T(2,128)S(1)} %bitcast.7, bf16[2,128]{1,0:T(2,128)(2,1)S(1)} %bitcast.8, bf16[128,128]{1,0:T(8,128)(2,1)S(1)} %copy-done.8, bf16[128,8192]{1,0:T(8,128)(2,1)S(1)} %copy-done.4, ...), custom_call_target="tpu_custom_call" | custom-call | tf_op jit(solution)/shard_map/pallas_call | solution.py:175
  28.2 3.8 %all-to-all-start = ((bf16[8,160,1024]{2,1,0:T(8,128)(2,1)}), bf16[8,160,1024]{2,1,0:T(8,128)(2,1)S(1)}, u32[]{:S(2)}, u32[]{:S(2)}) async-start(bf16[8,160,1024]{2,1,0:T(8,128)(2,1)} %get-tuple-element.12), calls=%async_computation | async-start | bytes 5242880 | tf_op jit(solution)/shard_map/all_to_all | solution.py:399
  32.0 1.5 collective-permute-start.8
  33.5 1.6 %collective-permute-start.5 = (bf16[128,1024]{1,0:T(8,128)(2,1)S(1)}, bf16[128,1024]{1,0:T(8,128)(2,1)S(1)}, u32[]{:S(2)}, u32[]{:S(2)}) collective-permute-start(bf16[128,1024]{1,0:T(8,128)(2,1)S(1)} %copy-done.15), channel_id=1, source_target_pairs={{0,16},{16,0},{1,17},{17,1},{2,18},{18,2},{3,19},{19,3},{4,20},{20... | collective-permute-start | bytes 786440 | tf_op jit(solution)/shard_map/ppermute | solution.py:403
  35.1 15.8 %collective-permute-done.5.refs_3_.refs_0_ = bf16[128,1024]{1,0:T(8,128)(2,1)S(1)} collective-permute-done((bf16[128,1024]{1,0:T(8,128)(2,1)S(1)}, bf16[128,1024]{1,0:T(8,128)(2,1)S(1)}, u32[]{:S(2)}, u32[]{:S(2)}) %collective-permute-start.5) | collective-permute-done | bytes 262176 | tf_op jit(solution)/shard_map/ppermute | solution.py:403
  50.9 1.0 collective-permute-done.8.refs_1_.refs_2_
  51.9 0.8 copy-done.12
  52.7 0.8 shard_map.90.refs_0_
  53.6 3.0 %collective-permute-start.9 = (bf16[256,1024]{1,0:T(8,128)(2,1)}, bf16[256,1024]{1,0:T(8,128)(2,1)}, u32[]{:S(2)}, u32[]{:S(2)}) collective-permute-start(bf16[256,1024]{1,0:T(8,128)(2,1)} %shard_map.90.refs_0_), channel_id=1, source_target_pairs={{0,16},{16,0},{1,17},{17,1},{2,18},{18,2},{3,19},{19,3},{4,20},{20... | collective-permute-start | bytes 1572872 | tf_op jit(solution)/shard_map/ppermute | solution.py:403
  56.6 0.0 collective-permute-start.6
  56.6 2.0 %collective-permute-start.7 = (bf16[128,1024]{1,0:T(8,128)(2,1)}, bf16[128,1024]{1,0:T(8,128)(2,1)}, u32[]{:S(2)}, u32[]{:S(2)}) collective-permute-start(bf16[128,1024]{1,0:T(8,128)(2,1)} %copy-done.16), channel_id=1, source_target_pairs={{0,8},{8,0},{1,9},{9,1},{2,10},{10,2},{3,11},{11,3},{4,12},{12,4},... | collective-permute-start | bytes 786440 | tf_op jit(solution)/shard_map/ppermute | solution.py:403
  58.6 4.6 %all-to-all-done.received_ref = bf16[8,160,1024]{2,1,0:T(8,128)(2,1)S(1)} async-done(((bf16[8,160,1024]{2,1,0:T(8,128)(2,1)}), bf16[8,160,1024]{2,1,0:T(8,128)(2,1)S(1)}, u32[]{:S(2)}, u32[]{:S(2)}) %all-to-all-start) | async-done | bytes 2621472 | tf_op jit(solution)/shard_map/all_to_all | solution.py:399
  63.3 3.2 %shard_map.86 = (bf16[256,1024]{1,0:T(8,128)(2,1)S(1)}, bf16[256,1024]{1,0:T(8,128)(2,1)S(1)}, bf16[256,1024]{1,0:T(8,128)(2,1)S(1)}, bf16[256,1024]{1,0:T(8,128)(2,1)}) custom-call(bf16[8,160,1024]{2,1,0:T(8,128)(2,1)S(1)} %all-to-all-done.received_ref), custom_call_target="tpu_custom_call" | custom-call | flops 2147483648 | bytes 6291456 | tf_op jit(solution)/shard_map/pallas_call | solution.py:255
  66.5 1.4 collective-permute-start.11
  67.9 7.0 %collective-permute-done.6.refs_6_ = bf16[128,1024]{1,0:T(8,128)(2,1)S(1)} collective-permute-done((bf16[128,1024]{1,0:T(8,128)(2,1)}, bf16[128,1024]{1,0:T(8,128)(2,1)S(1)}, u32[]{:S(2)}, u32[]{:S(2)}) %collective-permute-start.6) | collective-permute-done | bytes 262176 | tf_op jit(solution)/shard_map/ppermute | solution.py:403
  74.9 6.3 %collective-permute-done.7.refs_7_ = bf16[128,1024]{1,0:T(8,128)(2,1)} collective-permute-done((bf16[128,1024]{1,0:T(8,128)(2,1)}, bf16[128,1024]{1,0:T(8,128)(2,1)}, u32[]{:S(2)}, u32[]{:S(2)}) %collective-permute-start.7) | collective-permute-done | bytes 262176 | tf_op jit(solution)/shard_map/ppermute | solution.py:403
  81.2 6.2 %shard_map.87.refs_1_ = bf16[8,128,128]{2,1,0:T(8,128)(2,1)} custom-call(bf16[8,160,1024]{2,1,0:T(8,128)(2,1)S(1)} %all-to-all-done.received_ref, bf16[128,1024]{1,0:T(8,128)(2,1)} %copy-done.13, bf16[128,1024]{1,0:T(8,128)(2,1)} %copy-done.14, bf16[128,1024]{1,0:T(8,128)(2,1)} %collective-permute-done.2.refs_2_, bf16[128,1024]{1,0:T(8,128)(2,1)} %copy-done.16, ...), custom_call_target="tpu_custom_call" | custom-call | flops 2147483648 | bytes 6291456 | tf_op jit(solution)/shard_map/pallas_call | solution.py:318
  87.4 0.0 collective-permute-done.9.refs_0_
  87.4 0.9 copy-done.5
  88.4 1.8 %collective-permute-start.10 = (bf16[256,1024]{1,0:T(8,128)(2,1)}, bf16[256,1024]{1,0:T(8,128)(2,1)}, u32[]{:S(2)}, u32[]{:S(2)}) collective-permute-start(bf16[256,1024]{1,0:T(8,128)(2,1)} %shard_map.91.refs_1_), channel_id=1, source_target_pairs={{0,8},{8,0},{1,9},{9,1},{2,10},{10,2},{3,11},{11,3},{4,12},{12,4},... | collective-permute-start | bytes 1572872 | tf_op jit(solution)/shard_map/ppermute | solution.py:403
  90.2 9.7 %all_to_all.20.parts_ref = bf16[8,128,128]{2,1,0:T(8,128)(2,1)S(1)} all-to-all(bf16[8,128,128]{2,1,0:T(8,128)(2,1)S(1)} %copy-done.5), channel_id=1, replica_groups=mesh['high'=2,'low'=2,'near'=2,'inner'=2,'outer'=2] {'inner','outer','ne..., dimensions={0} | all-to-all | bytes 524288 | tf_op jit(solution)/shard_map/all_to_all | solution.py:399
  99.8 0.8 shard_map.88
  100.6 3.4 %all-to-all-start.2 = ((bf16[8,128,128]{2,1,0:T(8,128)(2,1)}), bf16[8,128,128]{2,1,0:T(8,128)(2,1)S(1)}, u32[]{:S(2)}, u32[]{:S(2)}) async-start(bf16[8,128,128]{2,1,0:T(8,128)(2,1)} %get-tuple-element.16), calls=%async_computation.2 | async-start | bytes 524288 | tf_op jit(solution)/shard_map/all_to_all | solution.py:399
  104.0 0.0 collective-permute-done.11.refs_1_
  104.0 1.2 shard_map.92.refs_4_
  105.2 0.0 copy-start.2
  105.2 0.8 copy-done.2
  106.0 4.0 %all-to-all-done.2.hidden_ref = bf16[8,128,128]{2,1,0:T(8,128)(2,1)S(1)} async-done(((bf16[8,128,128]{2,1,0:T(8,128)(2,1)}), bf16[8,128,128]{2,1,0:T(8,128)(2,1)S(1)}, u32[]{:S(2)}, u32[]{:S(2)}) %all-to-all-start.2) | async-done | bytes 262176 | tf_op jit(solution)/shard_map/all_to_all | solution.py:399
  109.9 0.0 collective-permute-done.10.refs_3_
  110.0 6.8 %shard_map.93 = bf16[8,128,1024]{2,1,0:T(8,128)(2,1)} custom-call(bf16[8,160,1024]{2,1,0:T(8,128)(2,1)S(1)} %all-to-all-done.received_ref, bf16[8,128,128]{2,1,0:T(8,128)(2,1)S(1)} %all-to-all-done.2.hidden_ref, bf16[256,1024]{1,0:T(8,128)(2,1)} %shard_map.90.refs_0_, bf16[256,1024]{1,0:T(8,128)(2,1)} %shard_map.91.refs_1_, bf16[256,1024]{1,0:T(8,128)(2,1)} %copy-done.12, ...), custom_call_target="tpu_custom_call" | custom-call | flops 2147483648 | bytes 6291456 | tf_op jit(solution)/shard_map/pallas_call | solution.py:378
  116.7 3.7 %all-to-all-start.3 = ((bf16[8,128,1024]{2,1,0:T(8,128)(2,1)}), bf16[8,128,1024]{2,1,0:T(8,128)(2,1)S(1)}, u32[]{:S(2)}, u32[]{:S(2)}) async-start(bf16[8,128,1024]{2,1,0:T(8,128)(2,1)} %shard_map.93), calls=%async_computation.3 | async-start | bytes 4194304 | tf_op jit(solution)/shard_map/all_to_all | solution.py:399
  120.5 0.7 collective-permute-start.12
  121.2 1.3 collective-permute-start.13
  122.6 1.7 %collective-permute-start.14 = (bf16[128,1024]{1,0:T(8,128)(2,1)S(1)}, bf16[128,1024]{1,0:T(8,128)(2,1)S(1)}, u32[]{:S(2)}, u32[]{:S(2)}) collective-permute-start(bf16[128,1024]{1,0:T(8,128)(2,1)S(1)} %get-tuple-element.23), channel_id=1, source_target_pairs={{0,16},{16,0},{1,17},{17,1},{2,18},{18,2},{3,19},{19,3},{4,20},{20... | collective-permute-start | bytes 786440 | tf_op jit(solution)/shard_map/ppermute | solution.py:403
  124.2 20.6 %collective-permute-done.12 = bf16[256,1024]{1,0:T(8,128)(2,1)S(1)} collective-permute-done((bf16[256,1024]{1,0:T(8,128)(2,1)}, bf16[256,1024]{1,0:T(8,128)(2,1)S(1)}, u32[]{:S(2)}, u32[]{:S(2)}) %collective-permute-start.12) | collective-permute-done | bytes 524320 | tf_op jit(solution)/shard_map/ppermute | solution.py:403
  144.9 0.0 collective-permute-done.13
  144.9 2.5 %collective-permute-done.14 = bf16[128,1024]{1,0:T(8,128)(2,1)S(1)} collective-permute-done((bf16[128,1024]{1,0:T(8,128)(2,1)S(1)}, bf16[128,1024]{1,0:T(8,128)(2,1)S(1)}, u32[]{:S(2)}, u32[]{:S(2)}) %collective-permute-start.14) | collective-permute-done | bytes 262176 | tf_op jit(solution)/shard_map/ppermute | solution.py:403
  147.4 0.3 add_convert_fusion
  147.6 1.7 %collective-permute-start.15 = (bf16[128,1024]{1,0:T(8,128)(2,1)S(1)}, bf16[128,1024]{1,0:T(8,128)(2,1)S(1)}, u32[]{:S(2)}, u32[]{:S(2)}) collective-permute-start(bf16[128,1024]{1,0:T(8,128)(2,1)S(1)} %get-tuple-element.21), channel_id=1, source_target_pairs={{0,4},{4,0},{1,5},{5,1},{2,6},{6,2},{3,7},{7,3},{8,12},{12,8},{9,1... | collective-permute-start | bytes 786440 | tf_op jit(solution)/shard_map/ppermute | solution.py:403
  149.4 0.0 all-to-all-done.3.parts_ref
  149.4 1.8 %shard_map.94.before_ref = bf16[128,8192]{1,0:T(8,128)(2,1)} custom-call(bf16[8,128,1024]{2,1,0:T(8,128)(2,1)S(1)} %all-to-all-done.3.parts_ref), custom_call_target="tpu_custom_call" | custom-call | tf_op jit(solution)/shard_map/pallas_call | solution.py:202
  151.2 3.9 %collective-permute-done.15.passed_ref = bf16[128,1024]{1,0:T(8,128)(2,1)S(1)} collective-permute-done((bf16[128,1024]{1,0:T(8,128)(2,1)S(1)}, bf16[128,1024]{1,0:T(8,128)(2,1)S(1)}, u32[]{:S(2)}, u32[]{:S(2)}) %collective-permute-start.15) | collective-permute-done | bytes 262176 | tf_op jit(solution)/shard_map/ppermute | solution.py:403
  155.2 0.8 shard_map.95
  (27 shorter events, 0.1 us)
Async XLA Ops:
  0.6 24.6 %copy-start.9 = (s32[128,2]{0,1:T(2,128)S(1)}, s32[128,2]{0,1:T(2,128)}, u32[]{:S(2)}) copy-start(s32[128,2]{0,1:T(2,128)} %param.8) | copy-start | bytes 3076
  0.6 24.6 %copy-start.10 = (bf16[128,2]{0,1:T(2,128)(2,1)S(1)}, bf16[128,2]{0,1:T(2,128)(2,1)}, u32[]{:S(2)}) copy-start(bf16[128,2]{0,1:T(2,128)(2,1)} %param.7) | copy-start | bytes 1540
  0.7 24.6 %copy-start.4 = (bf16[128,8192]{1,0:T(8,128)(2,1)S(1)}, bf16[128,8192]{1,0:T(8,128)(2,1)}, u32[]{:S(2)}) copy-start(bf16[128,8192]{1,0:T(8,128)(2,1)} %tokens_ref.1) | copy-start | bytes 6291460
  0.7 24.6 %copy-start.8 = (bf16[128,128]{1,0:T(8,128)(2,1)S(1)}, bf16[128,128]{1,0:T(8,128)(2,1)}, u32[]{:S(2)}) copy-start(bf16[128,128]{1,0:T(8,128)(2,1)} %preact_ref.1) | copy-start | bytes 98308
  1.9 23.3 %copy-start.13 = (bf16[128,1024]{1,0:T(8,128)(2,1)}, bf16[128,1024]{1,0:T(8,128)(2,1)S(1)}, u32[]{:S(2)}) copy-start(bf16[128,1024]{1,0:T(8,128)(2,1)S(1)} %get-tuple-element.27.refs_0_) | copy-start | bytes 786436
  1.9 9.5 %collective-permute-start = (bf16[128,1024]{1,0:T(8,128)(2,1)S(1)}, bf16[128,1024]{1,0:T(8,128)(2,1)S(1)}, u32[]{:S(2)}, u32[]{:S(2)}) collective-permute-start(bf16[128,1024]{1,0:T(8,128)(2,1)S(1)} %get-tuple-element.28), channel_id=1, source_target_pairs={{0,4},{4,0},{1,5},{5,1},{2,6},{6,2},{3,7},{7,3},{8,12},{12,8},{9,1... | collective-permute-start | bytes 786440 | tf_op jit(solution)/shard_map/ppermute | solution.py:403
  4.9 14.5 %collective-permute-start.2 = (bf16[128,1024]{1,0:T(8,128)(2,1)S(1)}, bf16[128,1024]{1,0:T(8,128)(2,1)}, u32[]{:S(2)}, u32[]{:S(2)}) collective-permute-start(bf16[128,1024]{1,0:T(8,128)(2,1)S(1)} %get-tuple-element.27.refs_0_), channel_id=1, source_target_pairs={{0,16},{16,0},{1,17},{17,1},{2,18},{18,2},{3,19},{19,3},{4,20},{20... | collective-permute-start | bytes 786440 | tf_op jit(solution)/shard_map/ppermute | solution.py:403
  7.5 13.9 %collective-permute-start.3 = (bf16[128,1024]{1,0:T(8,128)(2,1)S(1)}, bf16[128,1024]{1,0:T(8,128)(2,1)}, u32[]{:S(2)}, u32[]{:S(2)}) collective-permute-start(bf16[128,1024]{1,0:T(8,128)(2,1)S(1)} %get-tuple-element.27.refs_0_), channel_id=1, source_target_pairs={{0,8},{8,0},{1,9},{9,1},{2,10},{10,2},{3,11},{11,3},{4,12},{12,4},... | collective-permute-start | bytes 786440 | tf_op jit(solution)/shard_map/ppermute | solution.py:403
  10.9 10.5 %collective-permute-start.1 = (bf16[128,1024]{1,0:T(8,128)(2,1)}, bf16[128,1024]{1,0:T(8,128)(2,1)S(1)}, u32[]{:S(2)}, u32[]{:S(2)}) collective-permute-start(bf16[128,1024]{1,0:T(8,128)(2,1)} %get-tuple-element.26), channel_id=1, source_target_pairs={{0,4},{4,0},{1,5},{5,1},{2,6},{6,2},{3,7},{7,3},{8,12},{12,8},{9,1... | collective-permute-start | bytes 786440 | tf_op jit(solution)/shard_map/ppermute | solution.py:403
  11.4 13.9 %copy-start.14 = (bf16[128,1024]{1,0:T(8,128)(2,1)}, bf16[128,1024]{1,0:T(8,128)(2,1)S(1)}, u32[]{:S(2)}) copy-start(bf16[128,1024]{1,0:T(8,128)(2,1)S(1)} %collective-permute-done.refs_0_.refs_1_) | copy-start | bytes 786436
  11.4 13.9 %collective-permute-start.4 = (bf16[128,1024]{1,0:T(8,128)(2,1)S(1)}, bf16[128,1024]{1,0:T(8,128)(2,1)}, u32[]{:S(2)}, u32[]{:S(2)}) collective-permute-start(bf16[128,1024]{1,0:T(8,128)(2,1)S(1)} %collective-permute-done.refs_0_.refs_1_), channel_id=1, source_target_pairs={{0,8},{8,0},{1,9},{9,1},{2,10},{10,2},{3,11},{11,3},{4,12},{12,4},... | collective-permute-start | bytes 786440 | tf_op jit(solution)/shard_map/ppermute | solution.py:403
  21.4 3.9 %copy-start = (bf16[128,1024]{1,0:T(8,128)(2,1)}, bf16[128,1024]{1,0:T(8,128)(2,1)S(1)}, u32[]{:S(2)}) copy-start(bf16[128,1024]{1,0:T(8,128)(2,1)S(1)} %collective-permute-done.1.refs_1_.other_ref) | copy-start | bytes 786436
  28.2 3.8 %copy-start.1 = (bf16[128,1024]{1,0:T(8,128)(2,1)S(1)}, bf16[128,1024]{1,0:T(8,128)(2,1)}, u32[]{:S(2)}) copy-start(bf16[128,1024]{1,0:T(8,128)(2,1)} %copy-done) | copy-start | bytes 786436
  28.2 5.3 %copy-start.15 = (bf16[128,1024]{1,0:T(8,128)(2,1)S(1)}, bf16[128,1024]{1,0:T(8,128)(2,1)}, u32[]{:S(2)}) copy-start(bf16[128,1024]{1,0:T(8,128)(2,1)} %copy-done.14) | copy-start | bytes 786436
  28.2 35.1 %all-to-all-start = ((bf16[8,160,1024]{2,1,0:T(8,128)(2,1)}), bf16[8,160,1024]{2,1,0:T(8,128)(2,1)S(1)}, u32[]{:S(2)}, u32[]{:S(2)}) async-start(bf16[8,160,1024]{2,1,0:T(8,128)(2,1)} %get-tuple-element.12), calls=%async_computation | async-start | bytes 5242880 | tf_op jit(solution)/shard_map/all_to_all | solution.py:399
  32.0 19.9 %collective-permute-start.8 = (bf16[256,1024]{1,0:T(8,128)(2,1)S(1)}, bf16[256,1024]{1,0:T(8,128)(2,1)S(1)}, u32[]{:S(2)}, u32[]{:S(2)}) collective-permute-start(bf16[256,1024]{1,0:T(8,128)(2,1)S(1)} %shard_map.89), channel_id=1, source_target_pairs={{0,8},{8,0},{1,9},{9,1},{2,10},{10,2},{3,11},{11,3},{4,12},{12,4},... | collective-permute-start | bytes 1572872 | tf_op jit(solution)/shard_map/ppermute | solution.py:403
  33.5 17.4 %collective-permute-start.5 = (bf16[128,1024]{1,0:T(8,128)(2,1)S(1)}, bf16[128,1024]{1,0:T(8,128)(2,1)S(1)}, u32[]{:S(2)}, u32[]{:S(2)}) collective-permute-start(bf16[128,1024]{1,0:T(8,128)(2,1)S(1)} %copy-done.15), channel_id=1, source_target_pairs={{0,16},{16,0},{1,17},{17,1},{2,18},{18,2},{3,19},{19,3},{4,20},{20... | collective-permute-start | bytes 786440 | tf_op jit(solution)/shard_map/ppermute | solution.py:403
  50.9 1.0 copy-start.16
  51.9 0.8 copy-start.12
  53.6 33.8 %collective-permute-start.9 = (bf16[256,1024]{1,0:T(8,128)(2,1)}, bf16[256,1024]{1,0:T(8,128)(2,1)}, u32[]{:S(2)}, u32[]{:S(2)}) collective-permute-start(bf16[256,1024]{1,0:T(8,128)(2,1)} %shard_map.90.refs_0_), channel_id=1, source_target_pairs={{0,16},{16,0},{1,17},{17,1},{2,18},{18,2},{3,19},{19,3},{4,20},{20... | collective-permute-start | bytes 1572872 | tf_op jit(solution)/shard_map/ppermute | solution.py:403
  56.6 18.3 %collective-permute-start.6 = (bf16[128,1024]{1,0:T(8,128)(2,1)}, bf16[128,1024]{1,0:T(8,128)(2,1)S(1)}, u32[]{:S(2)}, u32[]{:S(2)}) collective-permute-start(bf16[128,1024]{1,0:T(8,128)(2,1)} %collective-permute-done.2.refs_2_), channel_id=1, source_target_pairs={{0,8},{8,0},{1,9},{9,1},{2,10},{10,2},{3,11},{11,3},{4,12},{12,4},... | collective-permute-start | bytes 786440 | tf_op jit(solution)/shard_map/ppermute | solution.py:403
  56.6 24.6 %collective-permute-start.7 = (bf16[128,1024]{1,0:T(8,128)(2,1)}, bf16[128,1024]{1,0:T(8,128)(2,1)}, u32[]{:S(2)}, u32[]{:S(2)}) collective-permute-start(bf16[128,1024]{1,0:T(8,128)(2,1)} %copy-done.16), channel_id=1, source_target_pairs={{0,8},{8,0},{1,9},{9,1},{2,10},{10,2},{3,11},{11,3},{4,12},{12,4},... | collective-permute-start | bytes 786440 | tf_op jit(solution)/shard_map/ppermute | solution.py:403
  66.5 20.9 %copy-start.6 = (bf16[256,1024]{1,0:T(8,128)(2,1)}, bf16[256,1024]{1,0:T(8,128)(2,1)S(1)}, u32[]{:S(2)}) copy-start(bf16[256,1024]{1,0:T(8,128)(2,1)S(1)} %get-tuple-element.13.refs_8_) | copy-start | bytes 1572868
  66.5 20.9 %copy-start.11 = (bf16[256,1024]{1,0:T(8,128)(2,1)}, bf16[256,1024]{1,0:T(8,128)(2,1)S(1)}, u32[]{:S(2)}) copy-start(bf16[256,1024]{1,0:T(8,128)(2,1)S(1)} %get-tuple-element.20) | copy-start | bytes 1572868
  66.5 37.5 %collective-permute-start.11 = (bf16[256,1024]{1,0:T(8,128)(2,1)}, bf16[256,1024]{1,0:T(8,128)(2,1)}, u32[]{:S(2)}, u32[]{:S(2)}) collective-permute-start(bf16[256,1024]{1,0:T(8,128)(2,1)} %get-tuple-element.18), channel_id=1, source_target_pairs={{0,8},{8,0},{1,9},{9,1},{2,10},{10,2},{3,11},{11,3},{4,12},{12,4},... | collective-permute-start | bytes 1572872 | tf_op jit(solution)/shard_map/ppermute | solution.py:403
  74.9 6.3 %copy-start.17 = (bf16[128,1024]{1,0:T(8,128)(2,1)}, bf16[128,1024]{1,0:T(8,128)(2,1)S(1)}, u32[]{:S(2)}) copy-start(bf16[128,1024]{1,0:T(8,128)(2,1)S(1)} %collective-permute-done.6.refs_6_) | copy-start | bytes 786436
  87.4 1.0 copy-start.5
  88.4 21.6 %collective-permute-start.10 = (bf16[256,1024]{1,0:T(8,128)(2,1)}, bf16[256,1024]{1,0:T(8,128)(2,1)}, u32[]{:S(2)}, u32[]{:S(2)}) collective-permute-start(bf16[256,1024]{1,0:T(8,128)(2,1)} %shard_map.91.refs_1_), channel_id=1, source_target_pairs={{0,8},{8,0},{1,9},{9,1},{2,10},{10,2},{3,11},{11,3},{4,12},{12,4},... | collective-permute-start | bytes 1572872 | tf_op jit(solution)/shard_map/ppermute | solution.py:403
  100.6 9.4 %all-to-all-start.2 = ((bf16[8,128,128]{2,1,0:T(8,128)(2,1)}), bf16[8,128,128]{2,1,0:T(8,128)(2,1)S(1)}, u32[]{:S(2)}, u32[]{:S(2)}) async-start(bf16[8,128,128]{2,1,0:T(8,128)(2,1)} %get-tuple-element.16), calls=%async_computation.2 | async-start | bytes 524288 | tf_op jit(solution)/shard_map/all_to_all | solution.py:399
  105.2 0.8 copy-start.2
  116.7 4.5 %copy-start.3 = (bf16[256,1024]{1,0:T(8,128)(2,1)S(1)}, bf16[256,1024]{1,0:T(8,128)(2,1)}, u32[]{:S(2)}) copy-start(bf16[256,1024]{1,0:T(8,128)(2,1)} %copy-done.2) | copy-start | bytes 1572868
  116.7 30.6 %copy-start.7 = (bf16[256,1024]{1,0:T(8,128)(2,1)S(1)}, bf16[256,1024]{1,0:T(8,128)(2,1)}, u32[]{:S(2)}) copy-start(bf16[256,1024]{1,0:T(8,128)(2,1)} %copy-done.6) | copy-start | bytes 1572868
  116.7 32.6 %all-to-all-start.3 = ((bf16[8,128,1024]{2,1,0:T(8,128)(2,1)}), bf16[8,128,1024]{2,1,0:T(8,128)(2,1)S(1)}, u32[]{:S(2)}, u32[]{:S(2)}) async-start(bf16[8,128,1024]{2,1,0:T(8,128)(2,1)} %shard_map.93), calls=%async_computation.3 | async-start | bytes 4194304 | tf_op jit(solution)/shard_map/all_to_all | solution.py:399
  120.5 24.4 %collective-permute-start.12 = (bf16[256,1024]{1,0:T(8,128)(2,1)}, bf16[256,1024]{1,0:T(8,128)(2,1)S(1)}, u32[]{:S(2)}, u32[]{:S(2)}) collective-permute-start(bf16[256,1024]{1,0:T(8,128)(2,1)} %copy-done.11), channel_id=1, source_target_pairs={{0,8},{8,0},{1,9},{9,1},{2,10},{10,2},{3,11},{11,3},{4,12},{12,4},... | collective-permute-start | bytes 1572872 | tf_op jit(solution)/shard_map/ppermute | solution.py:403
  121.2 23.6 %collective-permute-start.13 = (bf16[128,1024]{1,0:T(8,128)(2,1)S(1)}, bf16[128,1024]{1,0:T(8,128)(2,1)S(1)}, u32[]{:S(2)}, u32[]{:S(2)}) collective-permute-start(bf16[128,1024]{1,0:T(8,128)(2,1)S(1)} %get-tuple-element.24), channel_id=1, source_target_pairs={{0,16},{16,0},{1,17},{17,1},{2,18},{18,2},{3,19},{19,3},{4,20},{20... | collective-permute-start | bytes 786440 | tf_op jit(solution)/shard_map/ppermute | solution.py:403
  122.6 24.8 %collective-permute-start.14 = (bf16[128,1024]{1,0:T(8,128)(2,1)S(1)}, bf16[128,1024]{1,0:T(8,128)(2,1)S(1)}, u32[]{:S(2)}, u32[]{:S(2)}) collective-permute-start(bf16[128,1024]{1,0:T(8,128)(2,1)S(1)} %get-tuple-element.23), channel_id=1, source_target_pairs={{0,16},{16,0},{1,17},{17,1},{2,18},{18,2},{3,19},{19,3},{4,20},{20... | collective-permute-start | bytes 786440 | tf_op jit(solution)/shard_map/ppermute | solution.py:403
  147.6 7.5 %collective-permute-start.15 = (bf16[128,1024]{1,0:T(8,128)(2,1)S(1)}, bf16[128,1024]{1,0:T(8,128)(2,1)S(1)}, u32[]{:S(2)}, u32[]{:S(2)}) collective-permute-start(bf16[128,1024]{1,0:T(8,128)(2,1)S(1)} %get-tuple-element.21), channel_id=1, source_target_pairs={{0,4},{4,0},{1,5},{5,1},{2,6},{6,2},{3,7},{7,3},{8,12},{12,8},{9,1... | collective-permute-start | bytes 786440 | tf_op jit(solution)/shard_map/ppermute | solution.py:403

commit v14 on v13

--- a/solution.py
+++ b/solution.py
@@ -433,9 +433,9 @@
         low_beside = [swap(half, "low") for half in beside]
         down_pieces = [*down_halves, *beside, *low, *low_beside]
         first += [beside[0], *low]
-        up_low = swap(stack(*up_halves, ()), "low")
-        up_own = stack(*up_halves, (beside[1], up_low))
+        up_own = stack(*up_halves, (beside[1], low_beside[0]))
         up_beside = swap(up_own, "high")
+        up_low = swap(up_own, "low")
     else:
         down_pieces = [lax.all_gather(stack(*down_halves, ()), FAR, tiled=True)]
         up_pieces = [lax.all_gather(stack(*up_halves, ()), FAR, tiled=True)]

time: 157 us -> 148 us (0.943)
  waiting for transfers between devices: 78.1 us -> 70.4 us
    ppermute x16, waiting for transfers between devices: 69.4 us -> 55.8 us  [swap(): return lax.ppermute(value, axis, SWAP)]
    all_to_all x3, waiting for transfers between devices: 8.6 us -> 14.5 us  [exchange(): return lax.all_to_all(value, axes, split_axis=0, concat_axis=0, tiled=True)]
where the time goes in v14:
time: 148 us
  waiting for transfers between devices  70.4 us (48%)
  starting transfers between devices  35.7 us (24%)
  Pallas kernels  24.4 us (16%)
  blocking collectives  9.68 us (7%)
  local copies, waits for them, and re-layouts  6.31 us (4%)
    ppermute x16, waiting for transfers between devices, swap(): return lax.ppermute(value, axis, SWAP)  55.8 us
    ppermute x16, starting transfers between devices, swap(): return lax.ppermute(value, axis, SWAP)  24.8 us
    all_to_all x3, waiting for transfers between devices, exchange(): return lax.all_to_all(value, axes, split_axis=0, concat_axis=0, tiled=True)  14.5 us
    all_to_all x3, starting transfers between devices, exchange(): return lax.all_to_all(value, axes, split_axis=0, concat_axis=0, tiled=True)  11 us
    all_to_all x1, blocking collectives, exchange(): return lax.all_to_all(value, axes, split_axis=0, concat_axis=0, tiled=True)  9.68 us
    pallas_call x1, Pallas kernels, input_rows(): pl.pallas_call(functools.partial(input_kernel, len(pieces)), grid=(source...  6.79 us
    pallas_call x1, Pallas kernels, project(): pl.pallas_call(functools.partial(project_kernel, len(pieces)), grid=(sour...  6.17 us
    unnamed x36, local copies, waits for them, and re-layouts  3.3 us
  transfers between devices with their start and end apart: 19, of which 12 were waited for; matrix products, arithmetic and copies ran while one was open for 1% of the time, Pallas kernels for 9%

profile of v14, /device:TPU:0, one launch (start us, length us, event | category | flops | bytes accessed | tf_op | source)
XLA Modules:
  0.0 147.6 jit_solution(1234276611467115415)
XLA Ops:
  0.6 0.0 copy-start.9
  0.6 0.0 copy-start.10
  0.7 0.0 copy-start.2
  0.7 0.0 copy-start.8
  0.7 1.2 constant_dynamic-slice_fusion.1
  1.9 0.0 copy-start.12
  1.9 3.0 %collective-permute-start = (bf16[128,1024]{1,0:T(8,128)(2,1)S(1)}, bf16[128,1024]{1,0:T(8,128)(2,1)S(1)}, u32[]{:S(2)}, u32[]{:S(2)}) collective-permute-start(bf16[128,1024]{1,0:T(8,128)(2,1)S(1)} %get-tuple-element.28), channel_id=1, source_target_pairs={{0,4},{4,0},{1,5},{5,1},{2,6},{6,2},{3,7},{7,3},{8,12},{12,8},{9,1... | collective-permute-start | bytes 786440 | tf_op jit(solution)/shard_map/ppermute | solution.py:403
  4.9 2.6 %collective-permute-start.2 = (bf16[128,1024]{1,0:T(8,128)(2,1)S(1)}, bf16[128,1024]{1,0:T(8,128)(2,1)}, u32[]{:S(2)}, u32[]{:S(2)}) collective-permute-start(bf16[128,1024]{1,0:T(8,128)(2,1)S(1)} %get-tuple-element.27.refs_0_), channel_id=1, source_target_pairs={{0,16},{16,0},{1,17},{17,1},{2,18},{18,2},{3,19},{19,3},{4,20},{20... | collective-permute-start | bytes 786440 | tf_op jit(solution)/shard_map/ppermute | solution.py:403
  7.5 1.6 %collective-permute-start.3 = (bf16[128,1024]{1,0:T(8,128)(2,1)S(1)}, bf16[128,1024]{1,0:T(8,128)(2,1)}, u32[]{:S(2)}, u32[]{:S(2)}) collective-permute-start(bf16[128,1024]{1,0:T(8,128)(2,1)S(1)} %get-tuple-element.27.refs_0_), channel_id=1, source_target_pairs={{0,8},{8,0},{1,9},{9,1},{2,10},{10,2},{3,11},{11,3},{4,12},{12,4},... | collective-permute-start | bytes 786440 | tf_op jit(solution)/shard_map/ppermute | solution.py:403
  9.1 1.8 %constant_dynamic-slice_fusion = (bf16[128,1024]{1,0:T(8,128)(2,1)S(1)}, bf16[128,1024]{1,0:T(8,128)(2,1)}) fusion(bf16[128,2048]{1,0:T(8,128)(2,1)} %bitcast.10, s32[]{:T(128)S(6)} %select_n.23, s32[]{:T(128)S(6)} %select_n.22), kind=kLoop, calls=%fused_computation.4 | loop fusion | bytes 1048584 | tf_op jit(solution)/shard_map/dynamic_slice | solution.py:421
  10.9 0.5 collective-permute-start.1
  11.4 0.0 collective-permute-done.refs_0_.refs_1_
  11.4 1.7 %collective-permute-start.4 = (bf16[128,1024]{1,0:T(8,128)(2,1)S(1)}, bf16[128,1024]{1,0:T(8,128)(2,1)}, u32[]{:S(2)}, u32[]{:S(2)}) collective-permute-start(bf16[128,1024]{1,0:T(8,128)(2,1)S(1)} %collective-permute-done.refs_0_.refs_1_), channel_id=1, source_target_pairs={{0,8},{8,0},{1,9},{9,1},{2,10},{10,2},{3,11},{11,3},{4,12},{12,4},... | collective-permute-start | bytes 786440 | tf_op jit(solution)/shard_map/ppermute | solution.py:403
  13.1 6.4 %collective-permute-done.2.refs_2_ = bf16[128,1024]{1,0:T(8,128)(2,1)} collective-permute-done((bf16[128,1024]{1,0:T(8,128)(2,1)S(1)}, bf16[128,1024]{1,0:T(8,128)(2,1)}, u32[]{:S(2)}, u32[]{:S(2)}) %collective-permute-start.2) | collective-permute-done | bytes 262176 | tf_op jit(solution)/shard_map/ppermute | solution.py:403
  19.4 2.0 %collective-permute-done.3.refs_3_.refs_4_ = bf16[128,1024]{1,0:T(8,128)(2,1)} collective-permute-done((bf16[128,1024]{1,0:T(8,128)(2,1)S(1)}, bf16[128,1024]{1,0:T(8,128)(2,1)}, u32[]{:S(2)}, u32[]{:S(2)}) %collective-permute-start.3) | collective-permute-done | bytes 262176 | tf_op jit(solution)/shard_map/ppermute | solution.py:403
  21.4 0.0 collective-permute-done.1.refs_1_.other_ref
  21.4 3.9 %collective-permute-done.4.refs_4_.refs_5_ = bf16[128,1024]{1,0:T(8,128)(2,1)} collective-permute-done((bf16[128,1024]{1,0:T(8,128)(2,1)S(1)}, bf16[128,1024]{1,0:T(8,128)(2,1)}, u32[]{:S(2)}, u32[]{:S(2)}) %collective-permute-start.4) | collective-permute-done | bytes 262176 | tf_op jit(solution)/shard_map/ppermute | solution.py:403
  25.2 0.0 copy-done.12
  25.3 2.9 %shard_map.85 = (bf16[8,160,1024]{2,1,0:T(8,128)(2,1)}, f32[128,128]{1,0:T(8,128)S(1)}, f32[128,128]{1,0:T(8,128)S(1)}) custom-call(s32[4]{0:T(128)S(1)} %fusion.2.far_ref, s32[2,128]{1,0:T(2,128)S(1)} %bitcast.7, bf16[2,128]{1,0:T(2,128)(2,1)S(1)} %bitcast.8, bf16[128,128]{1,0:T(8,128)(2,1)S(1)} %copy-done.8, bf16[128,8192]{1,0:T(8,128)(2,1)S(1)} %copy-done.2, ...), custom_call_target="tpu_custom_call" | custom-call | tf_op jit(solution)/shard_map/pallas_call | solution.py:175
  28.2 3.8 %all-to-all-start = ((bf16[8,160,1024]{2,1,0:T(8,128)(2,1)}), bf16[8,160,1024]{2,1,0:T(8,128)(2,1)S(1)}, u32[]{:S(2)}, u32[]{:S(2)}) async-start(bf16[8,160,1024]{2,1,0:T(8,128)(2,1)} %get-tuple-element.12), calls=%async_computation | async-start | bytes 5242880 | tf_op jit(solution)/shard_map/all_to_all | solution.py:399
  31.9 1.4 collective-permute-start.5
  33.3 1.7 %collective-permute-start.6 = (bf16[128,1024]{1,0:T(8,128)(2,1)}, bf16[128,1024]{1,0:T(8,128)(2,1)S(1)}, u32[]{:S(2)}, u32[]{:S(2)}) collective-permute-start(bf16[128,1024]{1,0:T(8,128)(2,1)} %collective-permute-done.2.refs_2_), channel_id=1, source_target_pairs={{0,8},{8,0},{1,9},{9,1},{2,10},{10,2},{3,11},{11,3},{4,12},{12,4},... | collective-permute-start | bytes 786440 | tf_op jit(solution)/shard_map/ppermute | solution.py:403
  35.0 12.0 %collective-permute-done.5.refs_3_.refs_0_ = bf16[128,1024]{1,0:T(8,128)(2,1)S(1)} collective-permute-done((bf16[128,1024]{1,0:T(8,128)(2,1)S(1)}, bf16[128,1024]{1,0:T(8,128)(2,1)S(1)}, u32[]{:S(2)}, u32[]{:S(2)}) %collective-permute-start.5) | collective-permute-done | bytes 262176 | tf_op jit(solution)/shard_map/ppermute | solution.py:403
  47.1 0.0 collective-permute-done.6.refs_6_.refs_1_
  47.1 0.7 copy-done.15
  47.8 0.1 copy-done.16
  47.9 0.8 shard_map.89.refs_0_
  48.7 1.4 collective-permute-start.8
  50.1 1.9 %collective-permute-start.7 = (bf16[128,1024]{1,0:T(8,128)(2,1)}, bf16[128,1024]{1,0:T(8,128)(2,1)S(1)}, u32[]{:S(2)}, u32[]{:S(2)}) collective-permute-start(bf16[128,1024]{1,0:T(8,128)(2,1)} %copy-done.15), channel_id=1, source_target_pairs={{0,8},{8,0},{1,9},{9,1},{2,10},{10,2},{3,11},{11,3},{4,12},{12,4},... | collective-permute-start | bytes 786440 | tf_op jit(solution)/shard_map/ppermute | solution.py:403
  52.0 0.1 collective-permute-start.9
  52.1 11.1 %all-to-all-done.received_ref = bf16[8,160,1024]{2,1,0:T(8,128)(2,1)S(1)} async-done(((bf16[8,160,1024]{2,1,0:T(8,128)(2,1)}), bf16[8,160,1024]{2,1,0:T(8,128)(2,1)S(1)}, u32[]{:S(2)}, u32[]{:S(2)}) %all-to-all-start) | async-done | bytes 2621472 | tf_op jit(solution)/shard_map/all_to_all | solution.py:399
  63.3 3.2 %shard_map.86 = (bf16[256,1024]{1,0:T(8,128)(2,1)S(1)}, bf16[256,1024]{1,0:T(8,128)(2,1)S(1)}, bf16[256,1024]{1,0:T(8,128)(2,1)S(1)}, bf16[256,1024]{1,0:T(8,128)(2,1)}) custom-call(bf16[8,160,1024]{2,1,0:T(8,128)(2,1)S(1)} %all-to-all-done.received_ref), custom_call_target="tpu_custom_call" | custom-call | flops 2147483648 | bytes 6291456 | tf_op jit(solution)/shard_map/pallas_call | solution.py:255
  66.5 1.4 collective-permute-start.11
  67.9 0.6 collective-permute-done.7.refs_7_
  68.5 0.7 copy-done.17
  69.2 6.2 %shard_map.87.refs_1_ = bf16[8,128,128]{2,1,0:T(8,128)(2,1)} custom-call(bf16[8,160,1024]{2,1,0:T(8,128)(2,1)S(1)} %all-to-all-done.received_ref, bf16[128,1024]{1,0:T(8,128)(2,1)} %copy-done.12, bf16[128,1024]{1,0:T(8,128)(2,1)} %copy-done.13, bf16[128,1024]{1,0:T(8,128)(2,1)} %collective-permute-done.2.refs_2_, bf16[128,1024]{1,0:T(8,128)(2,1)} %copy-done.15, ...), custom_call_target="tpu_custom_call" | custom-call | flops 2147483648 | bytes 6291456 | tf_op jit(solution)/shard_map/pallas_call | solution.py:318
  75.4 0.0 copy-done.11
  75.4 0.0 collective-permute-done.8.refs_0_
  75.4 0.9 copy-done.3
  76.3 2.4 %collective-permute-start.10 = (bf16[256,1024]{1,0:T(8,128)(2,1)}, bf16[256,1024]{1,0:T(8,128)(2,1)}, u32[]{:S(2)}, u32[]{:S(2)}) collective-permute-start(bf16[256,1024]{1,0:T(8,128)(2,1)} %shard_map.90.refs_1_), channel_id=1, source_target_pairs={{0,8},{8,0},{1,9},{9,1},{2,10},{10,2},{3,11},{11,3},{4,12},{12,4},... | collective-permute-start | bytes 1572872 | tf_op jit(solution)/shard_map/ppermute | solution.py:403
  78.7 9.7 %all_to_all.20.parts_ref = bf16[8,128,128]{2,1,0:T(8,128)(2,1)S(1)} all-to-all(bf16[8,128,128]{2,1,0:T(8,128)(2,1)S(1)} %copy-done.3), channel_id=1, replica_groups=mesh['high'=2,'low'=2,'near'=2,'inner'=2,'outer'=2] {'inner','outer','ne..., dimensions={0} | all-to-all | bytes 524288 | tf_op jit(solution)/shard_map/all_to_all | solution.py:399
  88.4 0.8 shard_map.88
  89.1 3.4 %all-to-all-start.2 = ((bf16[8,128,128]{2,1,0:T(8,128)(2,1)}), bf16[8,128,128]{2,1,0:T(8,128)(2,1)S(1)}, u32[]{:S(2)}, u32[]{:S(2)}) async-start(bf16[8,128,128]{2,1,0:T(8,128)(2,1)} %get-tuple-element.16), calls=%async_computation.2 | async-start | bytes 524288 | tf_op jit(solution)/shard_map/all_to_all | solution.py:399
  92.6 0.6 collective-permute-done.11.refs_1_
  93.1 1.2 shard_map.91.refs_4_
  94.3 0.0 copy-start
  94.3 0.8 copy-done
  95.1 0.0 collective-permute-done.9.refs_2_
  95.1 3.4 %all-to-all-done.2.hidden_ref = bf16[8,128,128]{2,1,0:T(8,128)(2,1)S(1)} async-done(((bf16[8,128,128]{2,1,0:T(8,128)(2,1)}), bf16[8,128,128]{2,1,0:T(8,128)(2,1)S(1)}, u32[]{:S(2)}, u32[]{:S(2)}) %all-to-all-start.2) | async-done | bytes 262176 | tf_op jit(solution)/shard_map/all_to_all | solution.py:399
  98.5 4.3 %collective-permute-done.10.refs_3_ = bf16[256,1024]{1,0:T(8,128)(2,1)} collective-permute-done((bf16[256,1024]{1,0:T(8,128)(2,1)}, bf16[256,1024]{1,0:T(8,128)(2,1)}, u32[]{:S(2)}, u32[]{:S(2)}) %collective-permute-start.10) | collective-permute-done | bytes 524320 | tf_op jit(solution)/shard_map/ppermute | solution.py:403
  102.8 6.8 %shard_map.92 = bf16[8,128,1024]{2,1,0:T(8,128)(2,1)} custom-call(bf16[8,160,1024]{2,1,0:T(8,128)(2,1)S(1)} %all-to-all-done.received_ref, bf16[8,128,128]{2,1,0:T(8,128)(2,1)S(1)} %all-to-all-done.2.hidden_ref, bf16[256,1024]{1,0:T(8,128)(2,1)} %shard_map.89.refs_0_, bf16[256,1024]{1,0:T(8,128)(2,1)} %shard_map.90.refs_1_, ...), custom_call_target="tpu_custom_call" | custom-call | flops 2147483648 | bytes 6291456 | tf_op jit(solution)/shard_map/pallas_call | solution.py:378
  109.6 3.8 %all-to-all-start.3 = ((bf16[8,128,1024]{2,1,0:T(8,128)(2,1)}), bf16[8,128,1024]{2,1,0:T(8,128)(2,1)S(1)}, u32[]{:S(2)}, u32[]{:S(2)}) async-start(bf16[8,128,1024]{2,1,0:T(8,128)(2,1)} %shard_map.92), calls=%async_computation.3 | async-start | bytes 4194304 | tf_op jit(solution)/shard_map/all_to_all | solution.py:399
  113.4 0.4 collective-permute-start.12
  113.8 2.1 %collective-permute-start.13 = (bf16[128,1024]{1,0:T(8,128)(2,1)S(1)}, bf16[128,1024]{1,0:T(8,128)(2,1)S(1)}, u32[]{:S(2)}, u32[]{:S(2)}) collective-permute-start(bf16[128,1024]{1,0:T(8,128)(2,1)S(1)} %get-tuple-element.24), channel_id=1, source_target_pairs={{0,16},{16,0},{1,17},{17,1},{2,18},{18,2},{3,19},{19,3},{4,20},{20... | collective-permute-start | bytes 786440 | tf_op jit(solution)/shard_map/ppermute | solution.py:403
  116.0 0.8 collective-permute-start.14
  116.8 21.8 %collective-permute-done.12 = bf16[256,1024]{1,0:T(8,128)(2,1)S(1)} collective-permute-done((bf16[256,1024]{1,0:T(8,128)(2,1)}, bf16[256,1024]{1,0:T(8,128)(2,1)S(1)}, u32[]{:S(2)}, u32[]{:S(2)}) %collective-permute-start.12) | collective-permute-done | bytes 524320 | tf_op jit(solution)/shard_map/ppermute | solution.py:403
  138.6 0.0 collective-permute-done.13
  138.6 1.5 %collective-permute-done.14 = bf16[128,1024]{1,0:T(8,128)(2,1)S(1)} collective-permute-done((bf16[128,1024]{1,0:T(8,128)(2,1)S(1)}, bf16[128,1024]{1,0:T(8,128)(2,1)S(1)}, u32[]{:S(2)}, u32[]{:S(2)}) %collective-permute-start.14) | collective-permute-done | bytes 262176 | tf_op jit(solution)/shard_map/ppermute | solution.py:403
  140.1 0.3 add_convert_fusion
  140.4 1.7 %collective-permute-start.15 = (bf16[128,1024]{1,0:T(8,128)(2,1)S(1)}, bf16[128,1024]{1,0:T(8,128)(2,1)S(1)}, u32[]{:S(2)}, u32[]{:S(2)}) collective-permute-start(bf16[128,1024]{1,0:T(8,128)(2,1)S(1)} %get-tuple-element.21), channel_id=1, source_target_pairs={{0,4},{4,0},{1,5},{5,1},{2,6},{6,2},{3,7},{7,3},{8,12},{12,8},{9,1... | collective-permute-start | bytes 786440 | tf_op jit(solution)/shard_map/ppermute | solution.py:403
  142.1 0.0 all-to-all-done.3.parts_ref
  142.1 1.8 %shard_map.93.before_ref = bf16[128,8192]{1,0:T(8,128)(2,1)} custom-call(bf16[8,128,1024]{2,1,0:T(8,128)(2,1)S(1)} %all-to-all-done.3.parts_ref), custom_call_target="tpu_custom_call" | custom-call | tf_op jit(solution)/shard_map/pallas_call | solution.py:202
  143.9 2.9 %collective-permute-done.15.passed_ref = bf16[128,1024]{1,0:T(8,128)(2,1)S(1)} collective-permute-done((bf16[128,1024]{1,0:T(8,128)(2,1)S(1)}, bf16[128,1024]{1,0:T(8,128)(2,1)S(1)}, u32[]{:S(2)}, u32[]{:S(2)}) %collective-permute-start.15) | collective-permute-done | bytes 262176 | tf_op jit(solution)/shard_map/ppermute | solution.py:403
  146.8 0.8 shard_map.94
  (26 shorter events, 0.1 us)
Async XLA Ops:
  0.6 24.6 %copy-start.9 = (s32[128,2]{0,1:T(2,128)S(1)}, s32[128,2]{0,1:T(2,128)}, u32[]{:S(2)}) copy-start(s32[128,2]{0,1:T(2,128)} %param.8) | copy-start | bytes 3076
  0.6 24.6 %copy-start.10 = (bf16[128,2]{0,1:T(2,128)(2,1)S(1)}, bf16[128,2]{0,1:T(2,128)(2,1)}, u32[]{:S(2)}) copy-start(bf16[128,2]{0,1:T(2,128)(2,1)} %param.7) | copy-start | bytes 1540
  0.7 24.6 %copy-start.2 = (bf16[128,8192]{1,0:T(8,128)(2,1)S(1)}, bf16[128,8192]{1,0:T(8,128)(2,1)}, u32[]{:S(2)}) copy-start(bf16[128,8192]{1,0:T(8,128)(2,1)} %tokens_ref.1) | copy-start | bytes 6291460
  0.7 24.6 %copy-start.8 = (bf16[128,128]{1,0:T(8,128)(2,1)S(1)}, bf16[128,128]{1,0:T(8,128)(2,1)}, u32[]{:S(2)}) copy-start(bf16[128,128]{1,0:T(8,128)(2,1)} %preact_ref.1) | copy-start | bytes 98308
  1.9 23.3 %copy-start.12 = (bf16[128,1024]{1,0:T(8,128)(2,1)}, bf16[128,1024]{1,0:T(8,128)(2,1)S(1)}, u32[]{:S(2)}) copy-start(bf16[128,1024]{1,0:T(8,128)(2,1)S(1)} %get-tuple-element.27.refs_0_) | copy-start | bytes 786436
  1.9 9.5 %collective-permute-start = (bf16[128,1024]{1,0:T(8,128)(2,1)S(1)}, bf16[128,1024]{1,0:T(8,128)(2,1)S(1)}, u32[]{:S(2)}, u32[]{:S(2)}) collective-permute-start(bf16[128,1024]{1,0:T(8,128)(2,1)S(1)} %get-tuple-element.28), channel_id=1, source_target_pairs={{0,4},{4,0},{1,5},{5,1},{2,6},{6,2},{3,7},{7,3},{8,12},{12,8},{9,1... | collective-permute-start | bytes 786440 | tf_op jit(solution)/shard_map/ppermute | solution.py:403
  4.9 14.5 %collective-permute-start.2 = (bf16[128,1024]{1,0:T(8,128)(2,1)S(1)}, bf16[128,1024]{1,0:T(8,128)(2,1)}, u32[]{:S(2)}, u32[]{:S(2)}) collective-permute-start(bf16[128,1024]{1,0:T(8,128)(2,1)S(1)} %get-tuple-element.27.refs_0_), channel_id=1, source_target_pairs={{0,16},{16,0},{1,17},{17,1},{2,18},{18,2},{3,19},{19,3},{4,20},{20... | collective-permute-start | bytes 786440 | tf_op jit(solution)/shard_map/ppermute | solution.py:403
  7.5 13.9 %collective-permute-start.3 = (bf16[128,1024]{1,0:T(8,128)(2,1)S(1)}, bf16[128,1024]{1,0:T(8,128)(2,1)}, u32[]{:S(2)}, u32[]{:S(2)}) collective-permute-start(bf16[128,1024]{1,0:T(8,128)(2,1)S(1)} %get-tuple-element.27.refs_0_), channel_id=1, source_target_pairs={{0,8},{8,0},{1,9},{9,1},{2,10},{10,2},{3,11},{11,3},{4,12},{12,4},... | collective-permute-start | bytes 786440 | tf_op jit(solution)/shard_map/ppermute | solution.py:403
  10.9 10.5 %collective-permute-start.1 = (bf16[128,1024]{1,0:T(8,128)(2,1)}, bf16[128,1024]{1,0:T(8,128)(2,1)S(1)}, u32[]{:S(2)}, u32[]{:S(2)}) collective-permute-start(bf16[128,1024]{1,0:T(8,128)(2,1)} %get-tuple-element.26), channel_id=1, source_target_pairs={{0,4},{4,0},{1,5},{5,1},{2,6},{6,2},{3,7},{7,3},{8,12},{12,8},{9,1... | collective-permute-start | bytes 786440 | tf_op jit(solution)/shard_map/ppermute | solution.py:403
  11.4 13.9 %copy-start.13 = (bf16[128,1024]{1,0:T(8,128)(2,1)}, bf16[128,1024]{1,0:T(8,128)(2,1)S(1)}, u32[]{:S(2)}) copy-start(bf16[128,1024]{1,0:T(8,128)(2,1)S(1)} %collective-permute-done.refs_0_.refs_1_) | copy-start | bytes 786436
  11.4 13.9 %collective-permute-start.4 = (bf16[128,1024]{1,0:T(8,128)(2,1)S(1)}, bf16[128,1024]{1,0:T(8,128)(2,1)}, u32[]{:S(2)}, u32[]{:S(2)}) collective-permute-start(bf16[128,1024]{1,0:T(8,128)(2,1)S(1)} %collective-permute-done.refs_0_.refs_1_), channel_id=1, source_target_pairs={{0,8},{8,0},{1,9},{9,1},{2,10},{10,2},{3,11},{11,3},{4,12},{12,4},... | collective-permute-start | bytes 786440 | tf_op jit(solution)/shard_map/ppermute | solution.py:403
  21.4 3.9 %copy-start.4 = (bf16[128,1024]{1,0:T(8,128)(2,1)}, bf16[128,1024]{1,0:T(8,128)(2,1)S(1)}, u32[]{:S(2)}) copy-start(bf16[128,1024]{1,0:T(8,128)(2,1)S(1)} %collective-permute-done.1.refs_1_.other_ref) | copy-start | bytes 786436
  28.2 3.8 %copy-start.14 = (bf16[128,1024]{1,0:T(8,128)(2,1)S(1)}, bf16[128,1024]{1,0:T(8,128)(2,1)}, u32[]{:S(2)}) copy-start(bf16[128,1024]{1,0:T(8,128)(2,1)} %copy-done.13) | copy-start | bytes 786436
  28.2 19.7 %copy-start.5 = (bf16[128,1024]{1,0:T(8,128)(2,1)S(1)}, bf16[128,1024]{1,0:T(8,128)(2,1)}, u32[]{:S(2)}) copy-start(bf16[128,1024]{1,0:T(8,128)(2,1)} %copy-done.4) | copy-start | bytes 786436
  28.2 35.1 %all-to-all-start = ((bf16[8,160,1024]{2,1,0:T(8,128)(2,1)}), bf16[8,160,1024]{2,1,0:T(8,128)(2,1)S(1)}, u32[]{:S(2)}, u32[]{:S(2)}) async-start(bf16[8,160,1024]{2,1,0:T(8,128)(2,1)} %get-tuple-element.12), calls=%async_computation | async-start | bytes 5242880 | tf_op jit(solution)/shard_map/all_to_all | solution.py:399
  31.9 15.1 %collective-permute-start.5 = (bf16[128,1024]{1,0:T(8,128)(2,1)S(1)}, bf16[128,1024]{1,0:T(8,128)(2,1)S(1)}, u32[]{:S(2)}, u32[]{:S(2)}) collective-permute-start(bf16[128,1024]{1,0:T(8,128)(2,1)S(1)} %copy-done.14), channel_id=1, source_target_pairs={{0,16},{16,0},{1,17},{17,1},{2,18},{18,2},{3,19},{19,3},{4,20},{20... | collective-permute-start | bytes 786440 | tf_op jit(solution)/shard_map/ppermute | solution.py:403
  33.3 13.7 %collective-permute-start.6 = (bf16[128,1024]{1,0:T(8,128)(2,1)}, bf16[128,1024]{1,0:T(8,128)(2,1)S(1)}, u32[]{:S(2)}, u32[]{:S(2)}) collective-permute-start(bf16[128,1024]{1,0:T(8,128)(2,1)} %collective-permute-done.2.refs_2_), channel_id=1, source_target_pairs={{0,8},{8,0},{1,9},{9,1},{2,10},{10,2},{3,11},{11,3},{4,12},{12,4},... | collective-permute-start | bytes 786440 | tf_op jit(solution)/shard_map/ppermute | solution.py:403
  47.1 0.7 copy-start.15
  47.1 0.8 copy-start.16
  48.7 26.6 %collective-permute-start.8 = (bf16[256,1024]{1,0:T(8,128)(2,1)}, bf16[256,1024]{1,0:T(8,128)(2,1)}, u32[]{:S(2)}, u32[]{:S(2)}) collective-permute-start(bf16[256,1024]{1,0:T(8,128)(2,1)} %shard_map.89.refs_0_), channel_id=1, source_target_pairs={{0,16},{16,0},{1,17},{17,1},{2,18},{18,2},{3,19},{19,3},{4,20},{20... | collective-permute-start | bytes 1572872 | tf_op jit(solution)/shard_map/ppermute | solution.py:403
  50.1 18.4 %collective-permute-start.7 = (bf16[128,1024]{1,0:T(8,128)(2,1)}, bf16[128,1024]{1,0:T(8,128)(2,1)S(1)}, u32[]{:S(2)}, u32[]{:S(2)}) collective-permute-start(bf16[128,1024]{1,0:T(8,128)(2,1)} %copy-done.15), channel_id=1, source_target_pairs={{0,8},{8,0},{1,9},{9,1},{2,10},{10,2},{3,11},{11,3},{4,12},{12,4},... | collective-permute-start | bytes 786440 | tf_op jit(solution)/shard_map/ppermute | solution.py:403
  52.0 43.1 %collective-permute-start.9 = (bf16[256,1024]{1,0:T(8,128)(2,1)}, bf16[256,1024]{1,0:T(8,128)(2,1)}, u32[]{:S(2)}, u32[]{:S(2)}) collective-permute-start(bf16[256,1024]{1,0:T(8,128)(2,1)} %shard_map.89.refs_0_), channel_id=1, source_target_pairs={{0,8},{8,0},{1,9},{9,1},{2,10},{10,2},{3,11},{11,3},{4,12},{12,4},... | collective-permute-start | bytes 1572872 | tf_op jit(solution)/shard_map/ppermute | solution.py:403
  66.5 8.9 %copy-start.6 = (bf16[256,1024]{1,0:T(8,128)(2,1)}, bf16[256,1024]{1,0:T(8,128)(2,1)S(1)}, u32[]{:S(2)}) copy-start(bf16[256,1024]{1,0:T(8,128)(2,1)S(1)} %get-tuple-element.13.refs_8_) | copy-start | bytes 1572868
  66.5 8.9 %copy-start.11 = (bf16[256,1024]{1,0:T(8,128)(2,1)}, bf16[256,1024]{1,0:T(8,128)(2,1)S(1)}, u32[]{:S(2)}) copy-start(bf16[256,1024]{1,0:T(8,128)(2,1)S(1)} %get-tuple-element.20) | copy-start | bytes 1572868
  66.5 26.7 %collective-permute-start.11 = (bf16[256,1024]{1,0:T(8,128)(2,1)}, bf16[256,1024]{1,0:T(8,128)(2,1)}, u32[]{:S(2)}, u32[]{:S(2)}) collective-permute-start(bf16[256,1024]{1,0:T(8,128)(2,1)} %get-tuple-element.18), channel_id=1, source_target_pairs={{0,8},{8,0},{1,9},{9,1},{2,10},{10,2},{3,11},{11,3},{4,12},{12,4},... | collective-permute-start | bytes 1572872 | tf_op jit(solution)/shard_map/ppermute | solution.py:403
  68.5 0.7 copy-start.17
  75.4 1.0 copy-start.3
  76.3 26.5 %collective-permute-start.10 = (bf16[256,1024]{1,0:T(8,128)(2,1)}, bf16[256,1024]{1,0:T(8,128)(2,1)}, u32[]{:S(2)}, u32[]{:S(2)}) collective-permute-start(bf16[256,1024]{1,0:T(8,128)(2,1)} %shard_map.90.refs_1_), channel_id=1, source_target_pairs={{0,8},{8,0},{1,9},{9,1},{2,10},{10,2},{3,11},{11,3},{4,12},{12,4},... | collective-permute-start | bytes 1572872 | tf_op jit(solution)/shard_map/ppermute | solution.py:403
  89.1 9.4 %all-to-all-start.2 = ((bf16[8,128,128]{2,1,0:T(8,128)(2,1)}), bf16[8,128,128]{2,1,0:T(8,128)(2,1)S(1)}, u32[]{:S(2)}, u32[]{:S(2)}) async-start(bf16[8,128,128]{2,1,0:T(8,128)(2,1)} %get-tuple-element.16), calls=%async_computation.2 | async-start | bytes 524288 | tf_op jit(solution)/shard_map/all_to_all | solution.py:399
  94.3 0.8 copy-start
  109.6 4.2 %copy-start.1 = (bf16[256,1024]{1,0:T(8,128)(2,1)S(1)}, bf16[256,1024]{1,0:T(8,128)(2,1)}, u32[]{:S(2)}) copy-start(bf16[256,1024]{1,0:T(8,128)(2,1)} %copy-done) | copy-start | bytes 1572868
  109.6 30.5 %copy-start.7 = (bf16[256,1024]{1,0:T(8,128)(2,1)S(1)}, bf16[256,1024]{1,0:T(8,128)(2,1)}, u32[]{:S(2)}) copy-start(bf16[256,1024]{1,0:T(8,128)(2,1)} %copy-done.6) | copy-start | bytes 1572868
  109.6 32.5 %all-to-all-start.3 = ((bf16[8,128,1024]{2,1,0:T(8,128)(2,1)}), bf16[8,128,1024]{2,1,0:T(8,128)(2,1)S(1)}, u32[]{:S(2)}, u32[]{:S(2)}) async-start(bf16[8,128,1024]{2,1,0:T(8,128)(2,1)} %shard_map.92), calls=%async_computation.3 | async-start | bytes 4194304 | tf_op jit(solution)/shard_map/all_to_all | solution.py:399
  113.4 25.2 %collective-permute-start.12 = (bf16[256,1024]{1,0:T(8,128)(2,1)}, bf16[256,1024]{1,0:T(8,128)(2,1)S(1)}, u32[]{:S(2)}, u32[]{:S(2)}) collective-permute-start(bf16[256,1024]{1,0:T(8,128)(2,1)} %copy-done.11), channel_id=1, source_target_pairs={{0,8},{8,0},{1,9},{9,1},{2,10},{10,2},{3,11},{11,3},{4,12},{12,4},... | collective-permute-start | bytes 1572872 | tf_op jit(solution)/shard_map/ppermute | solution.py:403
  113.8 24.8 %collective-permute-start.13 = (bf16[128,1024]{1,0:T(8,128)(2,1)S(1)}, bf16[128,1024]{1,0:T(8,128)(2,1)S(1)}, u32[]{:S(2)}, u32[]{:S(2)}) collective-permute-start(bf16[128,1024]{1,0:T(8,128)(2,1)S(1)} %get-tuple-element.24), channel_id=1, source_target_pairs={{0,16},{16,0},{1,17},{17,1},{2,18},{18,2},{3,19},{19,3},{4,20},{20... | collective-permute-start | bytes 786440 | tf_op jit(solution)/shard_map/ppermute | solution.py:403
  116.0 24.1 %collective-permute-start.14 = (bf16[128,1024]{1,0:T(8,128)(2,1)S(1)}, bf16[128,1024]{1,0:T(8,128)(2,1)S(1)}, u32[]{:S(2)}, u32[]{:S(2)}) collective-permute-start(bf16[128,1024]{1,0:T(8,128)(2,1)S(1)} %get-tuple-element.23), channel_id=1, source_target_pairs={{0,16},{16,0},{1,17},{17,1},{2,18},{18,2},{3,19},{19,3},{4,20},{20... | collective-permute-start | bytes 786440 | tf_op jit(solution)/shard_map/ppermute | solution.py:403
  140.4 6.5 %collective-permute-start.15 = (bf16[128,1024]{1,0:T(8,128)(2,1)S(1)}, bf16[128,1024]{1,0:T(8,128)(2,1)S(1)}, u32[]{:S(2)}, u32[]{:S(2)}) collective-permute-start(bf16[128,1024]{1,0:T(8,128)(2,1)S(1)} %get-tuple-element.21), channel_id=1, source_target_pairs={{0,4},{4,0},{1,5},{5,1},{2,6},{6,2},{3,7},{7,3},{8,12},{12,8},{9,1... | collective-permute-start | bytes 786440 | tf_op jit(solution)/shard_map/ppermute | solution.py:403

commit v15 on v14

--- a/solution.py
+++ b/solution.py
@@ -331,7 +331,7 @@
     )(received, *in_hbm(*pieces), *before)
 
 
-def hidden_kernel(parts_ref, activation_ref, scaled_ref, hidden_ref, gate_ref):
+def hidden_kernel(parts_ref, activation_ref, scaled_ref, before_ref, hidden_ref, gate_ref):
     projected = parts_ref[0].astype(jnp.float32)
     for source in range(1, parts_ref.shape[0]):
         projected = projected + parts_ref[source].astype(jnp.float32)
@@ -445,10 +445,11 @@
     )
     received = exchange(packed, GROUP)
 
+    projected = project(received, down_pieces, tok_count, wide, ())
     partial_value = down_partial(
-        received, tok_count, wide, own_rows * PAIR * far_count, far_count if paired else 1, ()
-    )
-    projected = project(received, down_pieces, tok_count, wide, partial_value[:1])
+        received, tok_count, wide, own_rows * PAIR * far_count, far_count if paired else 1,
+        (projected,),
+    )
     if paired:
         up_beside = pass_on(up_beside, (projected,))
         up_pieces = [up_own, up_beside, up_low, swap(up_beside, "low")]
@@ -458,14 +459,14 @@
     hidden_grad, gate_grads = pl.pallas_call(
         hidden_kernel,
         grid=(1,),
-        in_specs=[gathered, single, single],
+        in_specs=[gathered, single, single, pl.BlockSpec(memory_space=pl.ANY)],
         out_specs=(gathered, pl.BlockSpec((2, tok_count), lambda i: (0, 0))),
         out_shape=(
             pltpu.HBM((members, tok_count, wide), jnp.bfloat16),
             jax.ShapeDtypeStruct((2, tok_count), jnp.bfloat16),
         ),
         compiler_params=params(),
-    )(parts, activation, scaled)
+    )(parts, activation, scaled, partial_value[0])
     if paired:
         own, beside, low, low_beside = partial_value
         before = add_pairs([(beside, swap(low_beside, "low"))], ())

time: 148 us -> 157 us (1.061)
  waiting for transfers between devices: 70.4 us -> 80.7 us
    ppermute x16, waiting for transfers between devices: 55.8 us -> 75.9 us  [swap(): return lax.ppermute(value, axis, SWAP)]
    all_to_all x3, waiting for transfers between devices: 14.5 us -> 4.82 us  [exchange(): return lax.all_to_all(value, axes, split_axis=0, concat_axis=0, tiled=True)]
where the time goes in v15:
time: 157 us; the launch traced here: 156 us
  waiting for transfers between devices  80.7 us (51%)
  starting transfers between devices  35.6 us (23%)
  Pallas kernels  24.4 us (16%)
  blocking collectives  8.56 us (5%)
  local copies, waits for them, and re-layouts  5.71 us (4%)
    ppermute x16, waiting for transfers between devices, swap(): return lax.ppermute(value, axis, SWAP)  75.9 us
    ppermute x16, starting transfers between devices, swap(): return lax.ppermute(value, axis, SWAP)  24.7 us
    all_to_all x3, starting transfers between devices, exchange(): return lax.all_to_all(value, axes, split_axis=0, concat_axis=0, tiled=True)  10.9 us
    all_to_all x1, blocking collectives, exchange(): return lax.all_to_all(value, axes, split_axis=0, concat_axis=0, tiled=True)  8.56 us
    pallas_call x1, Pallas kernels, input_rows(): pl.pallas_call(functools.partial(input_kernel, len(pieces)), grid=(source...  6.79 us
    pallas_call x1, Pallas kernels, project(): pl.pallas_call(functools.partial(project_kernel, len(pieces)), grid=(sour...  6.17 us
    all_to_all x3, waiting for transfers between devices, exchange(): return lax.all_to_all(value, axes, split_axis=0, concat_axis=0, tiled=True)  4.82 us
    pallas_call x1, Pallas kernels, down_partial(): pl.pallas_call(functools.partial(down_kernel, rows, wide, count), in_spec...  3.19 us
  transfers between devices with their start and end apart: 19, of which 12 were waited for; matrix products, arithmetic and copies ran while one was open for 1% of the time, Pallas kernels for 9%

profile of v15, /device:TPU:0, one launch (start us, length us, event | category | flops | bytes accessed | tf_op | source)
XLA Modules:
  0.0 156.2 jit_solution(15847163008035290807)
XLA Ops:
  0.6 0.0 copy-start.9
  0.6 0.0 copy-start.10
  0.7 0.0 copy-start.2
  0.7 0.0 copy-start.8
  0.7 1.2 constant_dynamic-slice_fusion.1
  1.9 3.0 %collective-permute-start = (bf16[128,1024]{1,0:T(8,128)(2,1)S(1)}, bf16[128,1024]{1,0:T(8,128)(2,1)S(1)}, u32[]{:S(2)}, u32[]{:S(2)}) collective-permute-start(bf16[128,1024]{1,0:T(8,128)(2,1)S(1)} %get-tuple-element.28), channel_id=1, source_target_pairs={{0,4},{4,0},{1,5},{5,1},{2,6},{6,2},{3,7},{7,3},{8,12},{12,8},{9,1... | collective-permute-start | bytes 786440 | tf_op jit(solution)/shard_map/ppermute | solution.py:403
  4.9 2.6 %collective-permute-start.2 = (bf16[128,1024]{1,0:T(8,128)(2,1)S(1)}, bf16[128,1024]{1,0:T(8,128)(2,1)}, u32[]{:S(2)}, u32[]{:S(2)}) collective-permute-start(bf16[128,1024]{1,0:T(8,128)(2,1)S(1)} %get-tuple-element.27.refs_0_), channel_id=1, source_target_pairs={{0,16},{16,0},{1,17},{17,1},{2,18},{18,2},{3,19},{19,3},{4,20},{20... | collective-permute-start | bytes 786440 | tf_op jit(solution)/shard_map/ppermute | solution.py:403
  7.5 1.6 %collective-permute-start.3 = (bf16[128,1024]{1,0:T(8,128)(2,1)S(1)}, bf16[128,1024]{1,0:T(8,128)(2,1)}, u32[]{:S(2)}, u32[]{:S(2)}) collective-permute-start(bf16[128,1024]{1,0:T(8,128)(2,1)S(1)} %get-tuple-element.27.refs_0_), channel_id=1, source_target_pairs={{0,8},{8,0},{1,9},{9,1},{2,10},{10,2},{3,11},{11,3},{4,12},{12,4},... | collective-permute-start | bytes 786440 | tf_op jit(solution)/shard_map/ppermute | solution.py:403
  9.1 1.8 %constant_dynamic-slice_fusion = (bf16[128,1024]{1,0:T(8,128)(2,1)S(1)}, bf16[128,1024]{1,0:T(8,128)(2,1)}) fusion(bf16[128,2048]{1,0:T(8,128)(2,1)} %bitcast.10, s32[]{:T(128)S(6)} %select_n.23, s32[]{:T(128)S(6)} %select_n.22), kind=kLoop, calls=%fused_computation.4 | loop fusion | bytes 1048584 | tf_op jit(solution)/shard_map/dynamic_slice | solution.py:421
  10.9 0.5 collective-permute-start.1
  11.4 0.0 collective-permute-done.refs_0_.refs_1_
  11.4 1.7 %collective-permute-start.4 = (bf16[128,1024]{1,0:T(8,128)(2,1)S(1)}, bf16[128,1024]{1,0:T(8,128)(2,1)}, u32[]{:S(2)}, u32[]{:S(2)}) collective-permute-start(bf16[128,1024]{1,0:T(8,128)(2,1)S(1)} %collective-permute-done.refs_0_.refs_1_), channel_id=1, source_target_pairs={{0,8},{8,0},{1,9},{9,1},{2,10},{10,2},{3,11},{11,3},{4,12},{12,4},... | collective-permute-start | bytes 786440 | tf_op jit(solution)/shard_map/ppermute | solution.py:403
  13.1 6.4 %collective-permute-done.2.refs_2_ = bf16[128,1024]{1,0:T(8,128)(2,1)} collective-permute-done((bf16[128,1024]{1,0:T(8,128)(2,1)S(1)}, bf16[128,1024]{1,0:T(8,128)(2,1)}, u32[]{:S(2)}, u32[]{:S(2)}) %collective-permute-start.2) | collective-permute-done | bytes 262176 | tf_op jit(solution)/shard_map/ppermute | solution.py:403
  19.4 2.0 %collective-permute-done.3.refs_3_.refs_4_ = bf16[128,1024]{1,0:T(8,128)(2,1)} collective-permute-done((bf16[128,1024]{1,0:T(8,128)(2,1)S(1)}, bf16[128,1024]{1,0:T(8,128)(2,1)}, u32[]{:S(2)}, u32[]{:S(2)}) %collective-permute-start.3) | collective-permute-done | bytes 262176 | tf_op jit(solution)/shard_map/ppermute | solution.py:403
  21.4 0.0 collective-permute-done.1.refs_1_.other_ref
  21.4 3.9 %collective-permute-done.4.refs_4_.refs_5_ = bf16[128,1024]{1,0:T(8,128)(2,1)} collective-permute-done((bf16[128,1024]{1,0:T(8,128)(2,1)S(1)}, bf16[128,1024]{1,0:T(8,128)(2,1)}, u32[]{:S(2)}, u32[]{:S(2)}) %collective-permute-start.4) | collective-permute-done | bytes 262176 | tf_op jit(solution)/shard_map/ppermute | solution.py:403
  25.2 0.0 copy-done.4
  25.3 2.9 %shard_map.85 = (bf16[8,160,1024]{2,1,0:T(8,128)(2,1)}, f32[128,128]{1,0:T(8,128)S(1)}, f32[128,128]{1,0:T(8,128)S(1)}) custom-call(s32[4]{0:T(128)S(1)} %fusion.2.far_ref, s32[2,128]{1,0:T(2,128)S(1)} %bitcast.7, bf16[2,128]{1,0:T(2,128)(2,1)S(1)} %bitcast.8, bf16[128,128]{1,0:T(8,128)(2,1)S(1)} %copy-done.8, bf16[128,8192]{1,0:T(8,128)(2,1)S(1)} %copy-done.2, ...), custom_call_target="tpu_custom_call" | custom-call | tf_op jit(solution)/shard_map/pallas_call | solution.py:175
  28.2 3.8 %all-to-all-start = ((bf16[8,160,1024]{2,1,0:T(8,128)(2,1)}), bf16[8,160,1024]{2,1,0:T(8,128)(2,1)S(1)}, u32[]{:S(2)}, u32[]{:S(2)}) async-start(bf16[8,160,1024]{2,1,0:T(8,128)(2,1)} %get-tuple-element.12), calls=%async_computation | async-start | bytes 5242880 | tf_op jit(solution)/shard_map/all_to_all | solution.py:399
  31.9 1.4 collective-permute-start.5
  33.3 1.7 %collective-permute-start.6 = (bf16[128,1024]{1,0:T(8,128)(2,1)}, bf16[128,1024]{1,0:T(8,128)(2,1)S(1)}, u32[]{:S(2)}, u32[]{:S(2)}) collective-permute-start(bf16[128,1024]{1,0:T(8,128)(2,1)} %collective-permute-done.2.refs_2_), channel_id=1, source_target_pairs={{0,8},{8,0},{1,9},{9,1},{2,10},{10,2},{3,11},{11,3},{4,12},{12,4},... | collective-permute-start | bytes 786440 | tf_op jit(solution)/shard_map/ppermute | solution.py:403
  35.0 12.0 %collective-permute-done.5.refs_3_.refs_0_ = bf16[128,1024]{1,0:T(8,128)(2,1)S(1)} collective-permute-done((bf16[128,1024]{1,0:T(8,128)(2,1)S(1)}, bf16[128,1024]{1,0:T(8,128)(2,1)S(1)}, u32[]{:S(2)}, u32[]{:S(2)}) %collective-permute-start.5) | collective-permute-done | bytes 262176 | tf_op jit(solution)/shard_map/ppermute | solution.py:403
  47.1 0.0 collective-permute-start.7
  47.1 0.0 collective-permute-done.6.refs_6_.refs_1_
  47.1 0.7 copy-done.15
  47.8 0.1 copy-done.16
  47.9 0.0 copy-done.5
  47.9 0.8 shard_map.89.refs_0_
  48.8 2.8 %collective-permute-start.8 = (bf16[256,1024]{1,0:T(8,128)(2,1)}, bf16[256,1024]{1,0:T(8,128)(2,1)}, u32[]{:S(2)}, u32[]{:S(2)}) collective-permute-start(bf16[256,1024]{1,0:T(8,128)(2,1)} %shard_map.89.refs_0_), channel_id=1, source_target_pairs={{0,16},{16,0},{1,17},{17,1},{2,18},{18,2},{3,19},{19,3},{4,20},{20... | collective-permute-start | bytes 1572872 | tf_op jit(solution)/shard_map/ppermute | solution.py:403
  51.5 6.9 %collective-permute-done.7.refs_7_ = bf16[128,1024]{1,0:T(8,128)(2,1)S(1)} collective-permute-done((bf16[128,1024]{1,0:T(8,128)(2,1)S(1)}, bf16[128,1024]{1,0:T(8,128)(2,1)S(1)}, u32[]{:S(2)}, u32[]{:S(2)}) %collective-permute-start.7) | collective-permute-done | bytes 262176 | tf_op jit(solution)/shard_map/ppermute | solution.py:403
  58.5 4.8 %all-to-all-done.received_ref = bf16[8,160,1024]{2,1,0:T(8,128)(2,1)S(1)} async-done(((bf16[8,160,1024]{2,1,0:T(8,128)(2,1)}), bf16[8,160,1024]{2,1,0:T(8,128)(2,1)S(1)}, u32[]{:S(2)}, u32[]{:S(2)}) %all-to-all-start) | async-done | bytes 2621472 | tf_op jit(solution)/shard_map/all_to_all | solution.py:399
  63.3 6.2 %shard_map.86.refs_0_.refs_1_ = bf16[8,128,128]{2,1,0:T(8,128)(2,1)} custom-call(bf16[8,160,1024]{2,1,0:T(8,128)(2,1)S(1)} %all-to-all-done.received_ref, bf16[128,1024]{1,0:T(8,128)(2,1)} %copy-done.12, bf16[128,1024]{1,0:T(8,128)(2,1)} %copy-done.13, bf16[128,1024]{1,0:T(8,128)(2,1)} %collective-permute-done.2.refs_2_, bf16[128,1024]{1,0:T(8,128)(2,1)} %copy-done.15, ...), custom_call_target="tpu_custom_call" | custom-call | flops 2147483648 | bytes 6291456 | tf_op jit(solution)/shard_map/pallas_call | solution.py:318
  69.4 3.2 %shard_map.87 = (bf16[256,1024]{1,0:T(8,128)(2,1)S(1)}, bf16[256,1024]{1,0:T(8,128)(2,1)S(1)}, bf16[256,1024]{1,0:T(8,128)(2,1)S(1)}, bf16[256,1024]{1,0:T(8,128)(2,1)}) custom-call(bf16[8,160,1024]{2,1,0:T(8,128)(2,1)S(1)} %all-to-all-done.received_ref, bf16[8,128,128]{2,1,0:T(8,128)(2,1)} %shard_map.86.refs_0_.refs_1_), custom_call_target="tpu_custom_call" | custom-call | flops 2147483648 | bytes 6291456 | tf_op jit(solution)/shard_map/pallas_call | solution.py:255
  72.6 1.4 collective-permute-start.11
  74.1 0.6 collective-permute-start.9
  74.7 0.3 collective-permute-done.8.refs_0_
  74.9 1.2 collective-permute-start.10
  76.2 8.6 %all_to_all.20.parts_ref = bf16[8,128,128]{2,1,0:T(8,128)(2,1)S(1)} all-to-all(bf16[8,128,128]{2,1,0:T(8,128)(2,1)S(1)} %copy-done.3), channel_id=1, replica_groups=mesh['high'=2,'low'=2,'near'=2,'inner'=2,'outer'=2] {'inner','outer','ne..., dimensions={0} | all-to-all | bytes 524288 | tf_op jit(solution)/shard_map/all_to_all | solution.py:399
  84.7 0.8 shard_map.88
  85.5 0.0 copy-done.11
  85.5 3.4 %all-to-all-start.2 = ((bf16[8,128,128]{2,1,0:T(8,128)(2,1)}), bf16[8,128,128]{2,1,0:T(8,128)(2,1)S(1)}, u32[]{:S(2)}, u32[]{:S(2)}) async-start(bf16[8,128,128]{2,1,0:T(8,128)(2,1)} %get-tuple-element.16), calls=%async_computation.2 | async-start | bytes 524288 | tf_op jit(solution)/shard_map/all_to_all | solution.py:399
  88.9 0.0 collective-permute-done.11.refs_1_
  88.9 0.0 copy-start.7
  88.9 1.0 copy-done.7
  90.0 1.2 shard_map.91.refs_4_
  91.1 0.0 copy-start
  91.2 0.8 copy-done
  91.9 7.0 %collective-permute-done.9.refs_2_ = bf16[256,1024]{1,0:T(8,128)(2,1)} collective-permute-done((bf16[256,1024]{1,0:T(8,128)(2,1)}, bf16[256,1024]{1,0:T(8,128)(2,1)}, u32[]{:S(2)}, u32[]{:S(2)}) %collective-permute-start.9) | collective-permute-done | bytes 524320 | tf_op jit(solution)/shard_map/ppermute | solution.py:403
  99.0 0.0 all-to-all-done.2.hidden_ref
  99.0 10.4 %collective-permute-done.10.refs_3_ = bf16[256,1024]{1,0:T(8,128)(2,1)} collective-permute-done((bf16[256,1024]{1,0:T(8,128)(2,1)}, bf16[256,1024]{1,0:T(8,128)(2,1)}, u32[]{:S(2)}, u32[]{:S(2)}) %collective-permute-start.10) | collective-permute-done | bytes 524320 | tf_op jit(solution)/shard_map/ppermute | solution.py:403
  109.4 6.8 %shard_map.92 = bf16[8,128,1024]{2,1,0:T(8,128)(2,1)} custom-call(bf16[8,160,1024]{2,1,0:T(8,128)(2,1)S(1)} %all-to-all-done.received_ref, bf16[8,128,128]{2,1,0:T(8,128)(2,1)S(1)} %all-to-all-done.2.hidden_ref, bf16[256,1024]{1,0:T(8,128)(2,1)} %shard_map.89.refs_0_, bf16[256,1024]{1,0:T(8,128)(2,1)} %shard_map.90.refs_1_, ...), custom_call_target="tpu_custom_call" | custom-call | flops 2147483648 | bytes 6291456 | tf_op jit(solution)/shard_map/pallas_call | solution.py:378
  116.2 3.7 %all-to-all-start.3 = ((bf16[8,128,1024]{2,1,0:T(8,128)(2,1)}), bf16[8,128,1024]{2,1,0:T(8,128)(2,1)S(1)}, u32[]{:S(2)}, u32[]{:S(2)}) async-start(bf16[8,128,1024]{2,1,0:T(8,128)(2,1)} %shard_map.92), calls=%async_computation.3 | async-start | bytes 4194304 | tf_op jit(solution)/shard_map/all_to_all | solution.py:399
  119.9 1.5 collective-permute-start.12
  121.4 1.6 %collective-permute-start.13 = (bf16[128,1024]{1,0:T(8,128)(2,1)S(1)}, bf16[128,1024]{1,0:T(8,128)(2,1)S(1)}, u32[]{:S(2)}, u32[]{:S(2)}) collective-permute-start(bf16[128,1024]{1,0:T(8,128)(2,1)S(1)} %get-tuple-element.24), channel_id=1, source_target_pairs={{0,16},{16,0},{1,17},{17,1},{2,18},{18,2},{3,19},{19,3},{4,20},{20... | collective-permute-start | bytes 786440 | tf_op jit(solution)/shard_map/ppermute | solution.py:403
  123.1 1.3 collective-permute-start.14
  124.4 20.0 %collective-permute-done.12 = bf16[256,1024]{1,0:T(8,128)(2,1)S(1)} collective-permute-done((bf16[256,1024]{1,0:T(8,128)(2,1)}, bf16[256,1024]{1,0:T(8,128)(2,1)S(1)}, u32[]{:S(2)}, u32[]{:S(2)}) %collective-permute-start.12) | collective-permute-done | bytes 524320 | tf_op jit(solution)/shard_map/ppermute | solution.py:403
  144.4 0.0 collective-permute-done.13
  144.5 3.1 %collective-permute-done.14 = bf16[128,1024]{1,0:T(8,128)(2,1)S(1)} collective-permute-done((bf16[128,1024]{1,0:T(8,128)(2,1)S(1)}, bf16[128,1024]{1,0:T(8,128)(2,1)S(1)}, u32[]{:S(2)}, u32[]{:S(2)}) %collective-permute-start.14) | collective-permute-done | bytes 262176 | tf_op jit(solution)/shard_map/ppermute | solution.py:403
  147.6 0.3 add_convert_fusion
  147.9 1.7 %collective-permute-start.15 = (bf16[128,1024]{1,0:T(8,128)(2,1)S(1)}, bf16[128,1024]{1,0:T(8,128)(2,1)S(1)}, u32[]{:S(2)}, u32[]{:S(2)}) collective-permute-start(bf16[128,1024]{1,0:T(8,128)(2,1)S(1)} %get-tuple-element.21), channel_id=1, source_target_pairs={{0,4},{4,0},{1,5},{5,1},{2,6},{6,2},{3,7},{7,3},{8,12},{12,8},{9,1... | collective-permute-start | bytes 786440 | tf_op jit(solution)/shard_map/ppermute | solution.py:403
  149.6 0.0 all-to-all-done.3.parts_ref
  149.6 1.8 %shard_map.93.before_ref = bf16[128,8192]{1,0:T(8,128)(2,1)} custom-call(bf16[8,128,1024]{2,1,0:T(8,128)(2,1)S(1)} %all-to-all-done.3.parts_ref), custom_call_target="tpu_custom_call" | custom-call | tf_op jit(solution)/shard_map/pallas_call | solution.py:202
  151.4 3.9 %collective-permute-done.15.passed_ref = bf16[128,1024]{1,0:T(8,128)(2,1)S(1)} collective-permute-done((bf16[128,1024]{1,0:T(8,128)(2,1)S(1)}, bf16[128,1024]{1,0:T(8,128)(2,1)S(1)}, u32[]{:S(2)}, u32[]{:S(2)}) %collective-permute-start.15) | collective-permute-done | bytes 262176 | tf_op jit(solution)/shard_map/ppermute | solution.py:403
  155.4 0.8 shard_map.94
  (26 shorter events, 0.1 us)
Async XLA Ops:
  0.6 24.6 %copy-start.9 = (s32[128,2]{0,1:T(2,128)S(1)}, s32[128,2]{0,1:T(2,128)}, u32[]{:S(2)}) copy-start(s32[128,2]{0,1:T(2,128)} %param.8) | copy-start | bytes 3076
  0.6 24.6 %copy-start.10 = (bf16[128,2]{0,1:T(2,128)(2,1)S(1)}, bf16[128,2]{0,1:T(2,128)(2,1)}, u32[]{:S(2)}) copy-start(bf16[128,2]{0,1:T(2,128)(2,1)} %param.7) | copy-start | bytes 1540
  0.7 24.6 %copy-start.2 = (bf16[128,8192]{1,0:T(8,128)(2,1)S(1)}, bf16[128,8192]{1,0:T(8,128)(2,1)}, u32[]{:S(2)}) copy-start(bf16[128,8192]{1,0:T(8,128)(2,1)} %tokens_ref.1) | copy-start | bytes 6291460
  0.7 24.6 %copy-start.8 = (bf16[128,128]{1,0:T(8,128)(2,1)S(1)}, bf16[128,128]{1,0:T(8,128)(2,1)}, u32[]{:S(2)}) copy-start(bf16[128,128]{1,0:T(8,128)(2,1)} %preact_ref.1) | copy-start | bytes 98308
  1.9 26.3 %copy-start.12 = (bf16[128,1024]{1,0:T(8,128)(2,1)}, bf16[128,1024]{1,0:T(8,128)(2,1)S(1)}, u32[]{:S(2)}) copy-start(bf16[128,1024]{1,0:T(8,128)(2,1)S(1)} %get-tuple-element.27.refs_0_) | copy-start | bytes 786436
  1.9 9.5 %collective-permute-start = (bf16[128,1024]{1,0:T(8,128)(2,1)S(1)}, bf16[128,1024]{1,0:T(8,128)(2,1)S(1)}, u32[]{:S(2)}, u32[]{:S(2)}) collective-permute-start(bf16[128,1024]{1,0:T(8,128)(2,1)S(1)} %get-tuple-element.28), channel_id=1, source_target_pairs={{0,4},{4,0},{1,5},{5,1},{2,6},{6,2},{3,7},{7,3},{8,12},{12,8},{9,1... | collective-permute-start | bytes 786440 | tf_op jit(solution)/shard_map/ppermute | solution.py:403
  4.9 14.5 %collective-permute-start.2 = (bf16[128,1024]{1,0:T(8,128)(2,1)S(1)}, bf16[128,1024]{1,0:T(8,128)(2,1)}, u32[]{:S(2)}, u32[]{:S(2)}) collective-permute-start(bf16[128,1024]{1,0:T(8,128)(2,1)S(1)} %get-tuple-element.27.refs_0_), channel_id=1, source_target_pairs={{0,16},{16,0},{1,17},{17,1},{2,18},{18,2},{3,19},{19,3},{4,20},{20... | collective-permute-start | bytes 786440 | tf_op jit(solution)/shard_map/ppermute | solution.py:403
  7.5 13.9 %collective-permute-start.3 = (bf16[128,1024]{1,0:T(8,128)(2,1)S(1)}, bf16[128,1024]{1,0:T(8,128)(2,1)}, u32[]{:S(2)}, u32[]{:S(2)}) collective-permute-start(bf16[128,1024]{1,0:T(8,128)(2,1)S(1)} %get-tuple-element.27.refs_0_), channel_id=1, source_target_pairs={{0,8},{8,0},{1,9},{9,1},{2,10},{10,2},{3,11},{11,3},{4,12},{12,4},... | collective-permute-start | bytes 786440 | tf_op jit(solution)/shard_map/ppermute | solution.py:403
  10.9 10.5 %collective-permute-start.1 = (bf16[128,1024]{1,0:T(8,128)(2,1)}, bf16[128,1024]{1,0:T(8,128)(2,1)S(1)}, u32[]{:S(2)}, u32[]{:S(2)}) collective-permute-start(bf16[128,1024]{1,0:T(8,128)(2,1)} %get-tuple-element.26), channel_id=1, source_target_pairs={{0,4},{4,0},{1,5},{5,1},{2,6},{6,2},{3,7},{7,3},{8,12},{12,8},{9,1... | collective-permute-start | bytes 786440 | tf_op jit(solution)/shard_map/ppermute | solution.py:403
  11.4 13.9 %copy-start.13 = (bf16[128,1024]{1,0:T(8,128)(2,1)}, bf16[128,1024]{1,0:T(8,128)(2,1)S(1)}, u32[]{:S(2)}) copy-start(bf16[128,1024]{1,0:T(8,128)(2,1)S(1)} %collective-permute-done.refs_0_.refs_1_) | copy-start | bytes 786436
  11.4 13.9 %collective-permute-start.4 = (bf16[128,1024]{1,0:T(8,128)(2,1)S(1)}, bf16[128,1024]{1,0:T(8,128)(2,1)}, u32[]{:S(2)}, u32[]{:S(2)}) collective-permute-start(bf16[128,1024]{1,0:T(8,128)(2,1)S(1)} %collective-permute-done.refs_0_.refs_1_), channel_id=1, source_target_pairs={{0,8},{8,0},{1,9},{9,1},{2,10},{10,2},{3,11},{11,3},{4,12},{12,4},... | collective-permute-start | bytes 786440 | tf_op jit(solution)/shard_map/ppermute | solution.py:403
  21.4 3.9 %copy-start.4 = (bf16[128,1024]{1,0:T(8,128)(2,1)}, bf16[128,1024]{1,0:T(8,128)(2,1)S(1)}, u32[]{:S(2)}) copy-start(bf16[128,1024]{1,0:T(8,128)(2,1)S(1)} %collective-permute-done.1.refs_1_.other_ref) | copy-start | bytes 786436
  28.2 3.8 %copy-start.14 = (bf16[128,1024]{1,0:T(8,128)(2,1)S(1)}, bf16[128,1024]{1,0:T(8,128)(2,1)}, u32[]{:S(2)}) copy-start(bf16[128,1024]{1,0:T(8,128)(2,1)} %copy-done.13) | copy-start | bytes 786436
  28.2 19.8 %copy-start.5 = (bf16[128,1024]{1,0:T(8,128)(2,1)S(1)}, bf16[128,1024]{1,0:T(8,128)(2,1)}, u32[]{:S(2)}) copy-start(bf16[128,1024]{1,0:T(8,128)(2,1)} %copy-done.4) | copy-start | bytes 786436
  28.2 35.1 %all-to-all-start = ((bf16[8,160,1024]{2,1,0:T(8,128)(2,1)}), bf16[8,160,1024]{2,1,0:T(8,128)(2,1)S(1)}, u32[]{:S(2)}, u32[]{:S(2)}) async-start(bf16[8,160,1024]{2,1,0:T(8,128)(2,1)} %get-tuple-element.12), calls=%async_computation | async-start | bytes 5242880 | tf_op jit(solution)/shard_map/all_to_all | solution.py:399
  31.9 15.1 %collective-permute-start.5 = (bf16[128,1024]{1,0:T(8,128)(2,1)S(1)}, bf16[128,1024]{1,0:T(8,128)(2,1)S(1)}, u32[]{:S(2)}, u32[]{:S(2)}) collective-permute-start(bf16[128,1024]{1,0:T(8,128)(2,1)S(1)} %copy-done.14), channel_id=1, source_target_pairs={{0,16},{16,0},{1,17},{17,1},{2,18},{18,2},{3,19},{19,3},{4,20},{20... | collective-permute-start | bytes 786440 | tf_op jit(solution)/shard_map/ppermute | solution.py:403
  33.3 13.7 %collective-permute-start.6 = (bf16[128,1024]{1,0:T(8,128)(2,1)}, bf16[128,1024]{1,0:T(8,128)(2,1)S(1)}, u32[]{:S(2)}, u32[]{:S(2)}) collective-permute-start(bf16[128,1024]{1,0:T(8,128)(2,1)} %collective-permute-done.2.refs_2_), channel_id=1, source_target_pairs={{0,8},{8,0},{1,9},{9,1},{2,10},{10,2},{3,11},{11,3},{4,12},{12,4},... | collective-permute-start | bytes 786440 | tf_op jit(solution)/shard_map/ppermute | solution.py:403
  47.1 0.7 copy-start.15
  47.1 11.4 %collective-permute-start.7 = (bf16[128,1024]{1,0:T(8,128)(2,1)S(1)}, bf16[128,1024]{1,0:T(8,128)(2,1)S(1)}, u32[]{:S(2)}, u32[]{:S(2)}) collective-permute-start(bf16[128,1024]{1,0:T(8,128)(2,1)S(1)} %collective-permute-done.5.refs_3_.refs_0_), channel_id=1, source_target_pairs={{0,8},{8,0},{1,9},{9,1},{2,10},{10,2},{3,11},{11,3},{4,12},{12,4},... | collective-permute-start | bytes 786440 | tf_op jit(solution)/shard_map/ppermute | solution.py:403
  47.1 0.8 copy-start.16
  48.8 26.2 %collective-permute-start.8 = (bf16[256,1024]{1,0:T(8,128)(2,1)}, bf16[256,1024]{1,0:T(8,128)(2,1)}, u32[]{:S(2)}, u32[]{:S(2)}) collective-permute-start(bf16[256,1024]{1,0:T(8,128)(2,1)} %shard_map.89.refs_0_), channel_id=1, source_target_pairs={{0,16},{16,0},{1,17},{17,1},{2,18},{18,2},{3,19},{19,3},{4,20},{20... | collective-permute-start | bytes 1572872 | tf_op jit(solution)/shard_map/ppermute | solution.py:403
  58.4 4.8 %copy-start.17 = (bf16[128,1024]{1,0:T(8,128)(2,1)}, bf16[128,1024]{1,0:T(8,128)(2,1)S(1)}, u32[]{:S(2)}) copy-start(bf16[128,1024]{1,0:T(8,128)(2,1)S(1)} %collective-permute-done.7.refs_7_) | copy-start | bytes 786436
  69.4 5.5 %copy-start.3 = (bf16[8,128,128]{2,1,0:T(8,128)(2,1)S(1)}, bf16[8,128,128]{2,1,0:T(8,128)(2,1)}, u32[]{:S(2)}) copy-start(bf16[8,128,128]{2,1,0:T(8,128)(2,1)} %shard_map.86.refs_0_.refs_1_) | copy-start | bytes 786436
  72.6 2.3 %copy-start.6 = (bf16[256,1024]{1,0:T(8,128)(2,1)}, bf16[256,1024]{1,0:T(8,128)(2,1)S(1)}, u32[]{:S(2)}) copy-start(bf16[256,1024]{1,0:T(8,128)(2,1)S(1)} %get-tuple-element.17.refs_0_) | copy-start | bytes 1572868
  72.6 12.9 %copy-start.11 = (bf16[256,1024]{1,0:T(8,128)(2,1)}, bf16[256,1024]{1,0:T(8,128)(2,1)S(1)}, u32[]{:S(2)}) copy-start(bf16[256,1024]{1,0:T(8,128)(2,1)S(1)} %get-tuple-element.20) | copy-start | bytes 1572868
  72.6 16.3 %collective-permute-start.11 = (bf16[256,1024]{1,0:T(8,128)(2,1)}, bf16[256,1024]{1,0:T(8,128)(2,1)}, u32[]{:S(2)}, u32[]{:S(2)}) collective-permute-start(bf16[256,1024]{1,0:T(8,128)(2,1)} %get-tuple-element.18), channel_id=1, source_target_pairs={{0,8},{8,0},{1,9},{9,1},{2,10},{10,2},{3,11},{11,3},{4,12},{12,4},... | collective-permute-start | bytes 1572872 | tf_op jit(solution)/shard_map/ppermute | solution.py:403
  74.1 24.9 %collective-permute-start.9 = (bf16[256,1024]{1,0:T(8,128)(2,1)}, bf16[256,1024]{1,0:T(8,128)(2,1)}, u32[]{:S(2)}, u32[]{:S(2)}) collective-permute-start(bf16[256,1024]{1,0:T(8,128)(2,1)} %shard_map.89.refs_0_), channel_id=1, source_target_pairs={{0,8},{8,0},{1,9},{9,1},{2,10},{10,2},{3,11},{11,3},{4,12},{12,4},... | collective-permute-start | bytes 1572872 | tf_op jit(solution)/shard_map/ppermute | solution.py:403
  74.9 34.4 %collective-permute-start.10 = (bf16[256,1024]{1,0:T(8,128)(2,1)}, bf16[256,1024]{1,0:T(8,128)(2,1)}, u32[]{:S(2)}, u32[]{:S(2)}) collective-permute-start(bf16[256,1024]{1,0:T(8,128)(2,1)} %shard_map.90.refs_1_), channel_id=1, source_target_pairs={{0,8},{8,0},{1,9},{9,1},{2,10},{10,2},{3,11},{11,3},{4,12},{12,4},... | collective-permute-start | bytes 1572872 | tf_op jit(solution)/shard_map/ppermute | solution.py:403
  85.5 13.5 %all-to-all-start.2 = ((bf16[8,128,128]{2,1,0:T(8,128)(2,1)}), bf16[8,128,128]{2,1,0:T(8,128)(2,1)S(1)}, u32[]{:S(2)}, u32[]{:S(2)}) async-start(bf16[8,128,128]{2,1,0:T(8,128)(2,1)} %get-tuple-element.16), calls=%async_computation.2 | async-start | bytes 524288 | tf_op jit(solution)/shard_map/all_to_all | solution.py:399
  88.9 1.0 copy-start.7
  91.1 0.8 copy-start
  116.2 5.3 %copy-start.1 = (bf16[256,1024]{1,0:T(8,128)(2,1)S(1)}, bf16[256,1024]{1,0:T(8,128)(2,1)}, u32[]{:S(2)}) copy-start(bf16[256,1024]{1,0:T(8,128)(2,1)} %copy-done) | copy-start | bytes 1572868
  116.2 33.4 %all-to-all-start.3 = ((bf16[8,128,1024]{2,1,0:T(8,128)(2,1)}), bf16[8,128,1024]{2,1,0:T(8,128)(2,1)S(1)}, u32[]{:S(2)}, u32[]{:S(2)}) async-start(bf16[8,128,1024]{2,1,0:T(8,128)(2,1)} %shard_map.92), calls=%async_computation.3 | async-start | bytes 4194304 | tf_op jit(solution)/shard_map/all_to_all | solution.py:399
  119.9 24.6 %collective-permute-start.12 = (bf16[256,1024]{1,0:T(8,128)(2,1)}, bf16[256,1024]{1,0:T(8,128)(2,1)S(1)}, u32[]{:S(2)}, u32[]{:S(2)}) collective-permute-start(bf16[256,1024]{1,0:T(8,128)(2,1)} %copy-done.11), channel_id=1, source_target_pairs={{0,8},{8,0},{1,9},{9,1},{2,10},{10,2},{3,11},{11,3},{4,12},{12,4},... | collective-permute-start | bytes 1572872 | tf_op jit(solution)/shard_map/ppermute | solution.py:403
  121.4 23.0 %collective-permute-start.13 = (bf16[128,1024]{1,0:T(8,128)(2,1)S(1)}, bf16[128,1024]{1,0:T(8,128)(2,1)S(1)}, u32[]{:S(2)}, u32[]{:S(2)}) collective-permute-start(bf16[128,1024]{1,0:T(8,128)(2,1)S(1)} %get-tuple-element.24), channel_id=1, source_target_pairs={{0,16},{16,0},{1,17},{17,1},{2,18},{18,2},{3,19},{19,3},{4,20},{20... | collective-permute-start | bytes 786440 | tf_op jit(solution)/shard_map/ppermute | solution.py:403
  123.1 24.5 %collective-permute-start.14 = (bf16[128,1024]{1,0:T(8,128)(2,1)S(1)}, bf16[128,1024]{1,0:T(8,128)(2,1)S(1)}, u32[]{:S(2)}, u32[]{:S(2)}) collective-permute-start(bf16[128,1024]{1,0:T(8,128)(2,1)S(1)} %get-tuple-element.23), channel_id=1, source_target_pairs={{0,16},{16,0},{1,17},{17,1},{2,18},{18,2},{3,19},{19,3},{4,20},{20... | collective-permute-start | bytes 786440 | tf_op jit(solution)/shard_map/ppermute | solution.py:403
  147.9 7.5 %collective-permute-start.15 = (bf16[128,1024]{1,0:T(8,128)(2,1)S(1)}, bf16[128,1024]{1,0:T(8,128)(2,1)S(1)}, u32[]{:S(2)}, u32[]{:S(2)}) collective-permute-start(bf16[128,1024]{1,0:T(8,128)(2,1)S(1)} %get-tuple-element.21), channel_id=1, source_target_pairs={{0,4},{4,0},{1,5},{5,1},{2,6},{6,2},{3,7},{7,3},{8,12},{12,8},{9,1... | collective-permute-start | bytes 786440 | tf_op jit(solution)/shard_map/ppermute | solution.py:403

commit v16 on v13

--- a/solution.py
+++ b/solution.py
@@ -434,7 +434,7 @@
         down_pieces = [*down_halves, *beside, *low, *low_beside]
         first += [beside[0], *low]
         up_low = swap(stack(*up_halves, ()), "low")
-        up_own = stack(*up_halves, (beside[1], up_low))
+        up_own = stack(*up_halves, (beside[1], low_beside[0], up_low))
         up_beside = swap(up_own, "high")
     else:
         down_pieces = [lax.all_gather(stack(*down_halves, ()), FAR, tiled=True)]

time: 157 us -> 155 us (0.987)
  starting transfers between devices: 37.1 us -> 35.4 us
    all_to_all x3, waiting for transfers between devices: 8.6 us -> 4.33 us  [exchange(): return lax.all_to_all(value, axes, split_axis=0, concat_axis=0, tiled=True)]
    ppermute x16, waiting for transfers between devices: 69.4 us -> 72.6 us  [swap(): return lax.ppermute(value, axis, SWAP)]
    ppermute x16, starting transfers between devices: 26.2 us -> 24.5 us  [swap(): return lax.ppermute(value, axis, SWAP)]
    unnamed x36 -> x38, local copies, waits for them, and re-layouts: 2.6 us -> 3.99 us
  transfers between devices with their start and end apart: 19 -> 19, of which waited for: 12 -> 11; matrix products, arithmetic and copies ran while one was open for 1% -> 1% of each run, Pallas kernels for 9% -> 9%
where the time goes in v16:
time: 155 us
  waiting for transfers between devices  76.9 us (50%)
  starting transfers between devices  35.4 us (23%)
  Pallas kernels  24.5 us (16%)
  blocking collectives  9.69 us (6%)
  local copies, waits for them, and re-layouts  7 us (5%)
    ppermute x16, waiting for transfers between devices, swap(): return lax.ppermute(value, axis, SWAP)  72.6 us
    ppermute x16, starting transfers between devices, swap(): return lax.ppermute(value, axis, SWAP)  24.5 us
    all_to_all x3, starting transfers between devices, exchange(): return lax.all_to_all(value, axes, split_axis=0, concat_axis=0, tiled=True)  10.9 us
    all_to_all x1, blocking collectives, exchange(): return lax.all_to_all(value, axes, split_axis=0, concat_axis=0, tiled=True)  9.69 us
    pallas_call x1, Pallas kernels, input_rows(): pl.pallas_call(functools.partial(input_kernel, len(pieces)), grid=(source...  6.79 us
    pallas_call x1, Pallas kernels, project(): pl.pallas_call(functools.partial(project_kernel, len(pieces)), grid=(sour...  6.17 us
    all_to_all x3, waiting for transfers between devices, exchange(): return lax.all_to_all(value, axes, split_axis=0, concat_axis=0, tiled=True)  4.33 us
    unnamed x38, local copies, waits for them, and re-layouts  3.99 us
  transfers between devices with their start and end apart: 19, of which 11 were waited for; matrix products, arithmetic and copies ran while one was open for 1% of the time, Pallas kernels for 9%

profile of v16, /device:TPU:0, one launch (start us, length us, event | category | flops | bytes accessed | tf_op | source)
XLA Modules:
  0.0 154.6 jit_solution(4442364570328688636)
XLA Ops:
  0.7 1.2 constant_dynamic-slice_fusion.1
  1.9 3.0 %collective-permute-start = (bf16[128,1024]{1,0:T(8,128)(2,1)S(1)}, bf16[128,1024]{1,0:T(8,128)(2,1)S(1)}, u32[]{:S(2)}, u32[]{:S(2)}) collective-permute-start(bf16[128,1024]{1,0:T(8,128)(2,1)S(1)} %get-tuple-element.28), channel_id=1, source_target_pairs={{0,4},{4,0},{1,5},{5,1},{2,6},{6,2},{3,7},{7,3},{8,12},{12,8},{9,1... | collective-permute-start | bytes 786440 | tf_op jit(solution)/shard_map/ppermute | solution.py:403
  4.9 2.6 %collective-permute-start.2 = (bf16[128,1024]{1,0:T(8,128)(2,1)S(1)}, bf16[128,1024]{1,0:T(8,128)(2,1)}, u32[]{:S(2)}, u32[]{:S(2)}) collective-permute-start(bf16[128,1024]{1,0:T(8,128)(2,1)S(1)} %get-tuple-element.27.refs_0_), channel_id=1, source_target_pairs={{0,16},{16,0},{1,17},{17,1},{2,18},{18,2},{3,19},{19,3},{4,20},{20... | collective-permute-start | bytes 786440 | tf_op jit(solution)/shard_map/ppermute | solution.py:403
  7.5 1.6 %collective-permute-start.3 = (bf16[128,1024]{1,0:T(8,128)(2,1)S(1)}, bf16[128,1024]{1,0:T(8,128)(2,1)}, u32[]{:S(2)}, u32[]{:S(2)}) collective-permute-start(bf16[128,1024]{1,0:T(8,128)(2,1)S(1)} %get-tuple-element.27.refs_0_), channel_id=1, source_target_pairs={{0,8},{8,0},{1,9},{9,1},{2,10},{10,2},{3,11},{11,3},{4,12},{12,4},... | collective-permute-start | bytes 786440 | tf_op jit(solution)/shard_map/ppermute | solution.py:403
  9.1 1.8 %constant_dynamic-slice_fusion = (bf16[128,1024]{1,0:T(8,128)(2,1)S(1)}, bf16[128,1024]{1,0:T(8,128)(2,1)}) fusion(bf16[128,2048]{1,0:T(8,128)(2,1)} %bitcast.10, s32[]{:T(128)S(6)} %select_n.23, s32[]{:T(128)S(6)} %select_n.22), kind=kLoop, calls=%fused_computation.4 | loop fusion | bytes 1048584 | tf_op jit(solution)/shard_map/dynamic_slice | solution.py:421
  10.9 0.5 collective-permute-start.1
  11.4 0.0 collective-permute-done.refs_0_.refs_1_
  11.4 1.7 %collective-permute-start.4 = (bf16[128,1024]{1,0:T(8,128)(2,1)S(1)}, bf16[128,1024]{1,0:T(8,128)(2,1)}, u32[]{:S(2)}, u32[]{:S(2)}) collective-permute-start(bf16[128,1024]{1,0:T(8,128)(2,1)S(1)} %collective-permute-done.refs_0_.refs_1_), channel_id=1, source_target_pairs={{0,8},{8,0},{1,9},{9,1},{2,10},{10,2},{3,11},{11,3},{4,12},{12,4},... | collective-permute-start | bytes 786440 | tf_op jit(solution)/shard_map/ppermute | solution.py:403
  13.1 6.4 %collective-permute-done.2.refs_2_ = bf16[128,1024]{1,0:T(8,128)(2,1)} collective-permute-done((bf16[128,1024]{1,0:T(8,128)(2,1)S(1)}, bf16[128,1024]{1,0:T(8,128)(2,1)}, u32[]{:S(2)}, u32[]{:S(2)}) %collective-permute-start.2) | collective-permute-done | bytes 262176 | tf_op jit(solution)/shard_map/ppermute | solution.py:403
  19.4 2.0 %collective-permute-done.3.refs_3_.refs_4_ = bf16[128,1024]{1,0:T(8,128)(2,1)} collective-permute-done((bf16[128,1024]{1,0:T(8,128)(2,1)S(1)}, bf16[128,1024]{1,0:T(8,128)(2,1)}, u32[]{:S(2)}, u32[]{:S(2)}) %collective-permute-start.3) | collective-permute-done | bytes 262176 | tf_op jit(solution)/shard_map/ppermute | solution.py:403
  21.4 0.0 collective-permute-done.1.refs_1_.other_ref
  21.4 3.9 %collective-permute-done.4.refs_4_.refs_5_ = bf16[128,1024]{1,0:T(8,128)(2,1)} collective-permute-done((bf16[128,1024]{1,0:T(8,128)(2,1)S(1)}, bf16[128,1024]{1,0:T(8,128)(2,1)}, u32[]{:S(2)}, u32[]{:S(2)}) %collective-permute-start.4) | collective-permute-done | bytes 262176 | tf_op jit(solution)/shard_map/ppermute | solution.py:403
  25.3 0.0 copy-done.9
  25.3 0.0 copy-done.10
  25.3 0.0 copy-done.4
  25.3 0.0 copy-done.8
  25.3 2.9 %shard_map.85 = (bf16[8,160,1024]{2,1,0:T(8,128)(2,1)}, f32[128,128]{1,0:T(8,128)S(1)}, f32[128,128]{1,0:T(8,128)S(1)}) custom-call(s32[4]{0:T(128)S(1)} %fusion.2.far_ref, s32[2,128]{1,0:T(2,128)S(1)} %bitcast.7, bf16[2,128]{1,0:T(2,128)(2,1)S(1)} %bitcast.8, bf16[128,128]{1,0:T(8,128)(2,1)S(1)} %copy-done.8, bf16[128,8192]{1,0:T(8,128)(2,1)S(1)} %copy-done.4, ...), custom_call_target="tpu_custom_call" | custom-call | tf_op jit(solution)/shard_map/pallas_call | solution.py:175
  28.2 3.8 %all-to-all-start = ((bf16[8,160,1024]{2,1,0:T(8,128)(2,1)}), bf16[8,160,1024]{2,1,0:T(8,128)(2,1)S(1)}, u32[]{:S(2)}, u32[]{:S(2)}) async-start(bf16[8,160,1024]{2,1,0:T(8,128)(2,1)} %get-tuple-element.12), calls=%async_computation | async-start | bytes 5242880 | tf_op jit(solution)/shard_map/all_to_all | solution.py:399
  32.0 1.5 collective-permute-start.8
  33.5 1.6 %collective-permute-start.5 = (bf16[128,1024]{1,0:T(8,128)(2,1)S(1)}, bf16[128,1024]{1,0:T(8,128)(2,1)S(1)}, u32[]{:S(2)}, u32[]{:S(2)}) collective-permute-start(bf16[128,1024]{1,0:T(8,128)(2,1)S(1)} %copy-done.15), channel_id=1, source_target_pairs={{0,16},{16,0},{1,17},{17,1},{2,18},{18,2},{3,19},{19,3},{4,20},{20... | collective-permute-start | bytes 786440 | tf_op jit(solution)/shard_map/ppermute | solution.py:403
  35.1 0.3 collective-permute-start.6
  35.4 15.9 %collective-permute-done.5.refs_3_.refs_0_ = bf16[128,1024]{1,0:T(8,128)(2,1)S(1)} collective-permute-done((bf16[128,1024]{1,0:T(8,128)(2,1)S(1)}, bf16[128,1024]{1,0:T(8,128)(2,1)S(1)}, u32[]{:S(2)}, u32[]{:S(2)}) %collective-permute-start.5) | collective-permute-done | bytes 262176 | tf_op jit(solution)/shard_map/ppermute | solution.py:403
  51.4 6.2 %collective-permute-done.6.refs_6_.refs_1_ = bf16[128,1024]{1,0:T(8,128)(2,1)S(1)} collective-permute-done((bf16[128,1024]{1,0:T(8,128)(2,1)}, bf16[128,1024]{1,0:T(8,128)(2,1)S(1)}, u32[]{:S(2)}, u32[]{:S(2)}) %collective-permute-start.6) | collective-permute-done | bytes 262176 | tf_op jit(solution)/shard_map/ppermute | solution.py:403
  57.6 0.0 collective-permute-done.8.refs_2_
  57.6 0.7 copy-done.17
  58.3 0.8 copy-done.12
  59.1 0.8 shard_map.90.refs_0_
  59.9 1.3 collective-permute-start.9
  61.2 1.7 %collective-permute-start.7 = (bf16[128,1024]{1,0:T(8,128)(2,1)}, bf16[128,1024]{1,0:T(8,128)(2,1)S(1)}, u32[]{:S(2)}, u32[]{:S(2)}) collective-permute-start(bf16[128,1024]{1,0:T(8,128)(2,1)} %copy-done.16), channel_id=1, source_target_pairs={{0,8},{8,0},{1,9},{9,1},{2,10},{10,2},{3,11},{11,3},{4,12},{12,4},... | collective-permute-start | bytes 786440 | tf_op jit(solution)/shard_map/ppermute | solution.py:403
  62.9 0.3 all-to-all-done.received_ref
  63.3 3.2 %shard_map.86 = (bf16[256,1024]{1,0:T(8,128)(2,1)S(1)}, bf16[256,1024]{1,0:T(8,128)(2,1)S(1)}, bf16[256,1024]{1,0:T(8,128)(2,1)S(1)}, bf16[256,1024]{1,0:T(8,128)(2,1)}) custom-call(bf16[8,160,1024]{2,1,0:T(8,128)(2,1)S(1)} %all-to-all-done.received_ref), custom_call_target="tpu_custom_call" | custom-call | flops 2147483648 | bytes 6291456 | tf_op jit(solution)/shard_map/pallas_call | solution.py:255
  66.5 1.4 collective-permute-start.11
  67.9 11.7 %collective-permute-done.7.refs_7_ = bf16[128,1024]{1,0:T(8,128)(2,1)S(1)} collective-permute-done((bf16[128,1024]{1,0:T(8,128)(2,1)}, bf16[128,1024]{1,0:T(8,128)(2,1)S(1)}, u32[]{:S(2)}, u32[]{:S(2)}) %collective-permute-start.7) | collective-permute-done | bytes 262176 | tf_op jit(solution)/shard_map/ppermute | solution.py:403
  79.6 0.7 copy-done.18
  80.3 6.2 %shard_map.87.refs_1_ = bf16[8,128,128]{2,1,0:T(8,128)(2,1)} custom-call(bf16[8,160,1024]{2,1,0:T(8,128)(2,1)S(1)} %all-to-all-done.received_ref, bf16[128,1024]{1,0:T(8,128)(2,1)} %copy-done.13, bf16[128,1024]{1,0:T(8,128)(2,1)} %copy-done.14, bf16[128,1024]{1,0:T(8,128)(2,1)} %collective-permute-done.2.refs_2_, bf16[128,1024]{1,0:T(8,128)(2,1)} %copy-done.16, ...), custom_call_target="tpu_custom_call" | custom-call | flops 2147483648 | bytes 6291456 | tf_op jit(solution)/shard_map/pallas_call | solution.py:318
  86.4 0.0 copy-done.6
  86.4 0.0 collective-permute-done.9.refs_0_
  86.4 0.0 copy-start.5
  86.5 0.9 copy-done.5
  87.4 2.4 %collective-permute-start.10 = (bf16[256,1024]{1,0:T(8,128)(2,1)}, bf16[256,1024]{1,0:T(8,128)(2,1)}, u32[]{:S(2)}, u32[]{:S(2)}) collective-permute-start(bf16[256,1024]{1,0:T(8,128)(2,1)} %shard_map.91.refs_1_), channel_id=1, source_target_pairs={{0,8},{8,0},{1,9},{9,1},{2,10},{10,2},{3,11},{11,3},{4,12},{12,4},... | collective-permute-start | bytes 1572872 | tf_op jit(solution)/shard_map/ppermute | solution.py:403
  89.8 9.7 %all_to_all.20.parts_ref = bf16[8,128,128]{2,1,0:T(8,128)(2,1)S(1)} all-to-all(bf16[8,128,128]{2,1,0:T(8,128)(2,1)S(1)} %copy-done.5), channel_id=1, replica_groups=mesh['high'=2,'low'=2,'near'=2,'inner'=2,'outer'=2] {'inner','outer','ne..., dimensions={0} | all-to-all | bytes 524288 | tf_op jit(solution)/shard_map/all_to_all | solution.py:399
  99.5 0.8 shard_map.88
  100.2 3.4 %all-to-all-start.2 = ((bf16[8,128,128]{2,1,0:T(8,128)(2,1)}), bf16[8,128,128]{2,1,0:T(8,128)(2,1)S(1)}, u32[]{:S(2)}, u32[]{:S(2)}) async-start(bf16[8,128,128]{2,1,0:T(8,128)(2,1)} %get-tuple-element.16), calls=%async_computation.2 | async-start | bytes 524288 | tf_op jit(solution)/shard_map/all_to_all | solution.py:399
  103.6 0.0 collective-permute-done.11.refs_1_
  103.6 1.2 shard_map.92.refs_4_
  104.8 0.0 copy-start.2
  104.8 0.8 copy-done.2
  105.6 4.0 %all-to-all-done.2.hidden_ref = bf16[8,128,128]{2,1,0:T(8,128)(2,1)S(1)} async-done(((bf16[8,128,128]{2,1,0:T(8,128)(2,1)}), bf16[8,128,128]{2,1,0:T(8,128)(2,1)S(1)}, u32[]{:S(2)}, u32[]{:S(2)}) %all-to-all-start.2) | async-done | bytes 262176 | tf_op jit(solution)/shard_map/all_to_all | solution.py:399
  109.6 0.0 collective-permute-done.10.refs_3_
  109.6 6.8 %shard_map.93 = bf16[8,128,1024]{2,1,0:T(8,128)(2,1)} custom-call(bf16[8,160,1024]{2,1,0:T(8,128)(2,1)S(1)} %all-to-all-done.received_ref, bf16[8,128,128]{2,1,0:T(8,128)(2,1)S(1)} %all-to-all-done.2.hidden_ref, bf16[256,1024]{1,0:T(8,128)(2,1)} %shard_map.90.refs_0_, bf16[256,1024]{1,0:T(8,128)(2,1)} %shard_map.91.refs_1_, bf16[256,1024]{1,0:T(8,128)(2,1)} %copy-done.12, ...), custom_call_target="tpu_custom_call" | custom-call | flops 2147483648 | bytes 6291456 | tf_op jit(solution)/shard_map/pallas_call | solution.py:378
  116.4 3.7 %all-to-all-start.3 = ((bf16[8,128,1024]{2,1,0:T(8,128)(2,1)}), bf16[8,128,1024]{2,1,0:T(8,128)(2,1)S(1)}, u32[]{:S(2)}, u32[]{:S(2)}) async-start(bf16[8,128,1024]{2,1,0:T(8,128)(2,1)} %shard_map.93), calls=%async_computation.3 | async-start | bytes 4194304 | tf_op jit(solution)/shard_map/all_to_all | solution.py:399
  120.1 0.1 collective-permute-start.12
  120.2 0.0 copy-done.3
  120.3 3.0 %collective-permute-start.13 = (bf16[128,1024]{1,0:T(8,128)(2,1)S(1)}, bf16[128,1024]{1,0:T(8,128)(2,1)S(1)}, u32[]{:S(2)}, u32[]{:S(2)}) collective-permute-start(bf16[128,1024]{1,0:T(8,128)(2,1)S(1)} %get-tuple-element.24), channel_id=1, source_target_pairs={{0,16},{16,0},{1,17},{17,1},{2,18},{18,2},{3,19},{19,3},{4,20},{20... | collective-permute-start | bytes 786440 | tf_op jit(solution)/shard_map/ppermute | solution.py:403
  123.3 0.1 collective-permute-start.14
  123.4 22.3 %collective-permute-done.12 = bf16[256,1024]{1,0:T(8,128)(2,1)S(1)} collective-permute-done((bf16[256,1024]{1,0:T(8,128)(2,1)}, bf16[256,1024]{1,0:T(8,128)(2,1)S(1)}, u32[]{:S(2)}, u32[]{:S(2)}) %collective-permute-start.12) | collective-permute-done | bytes 524320 | tf_op jit(solution)/shard_map/ppermute | solution.py:403
  145.7 0.0 collective-permute-done.13
  145.7 1.0 collective-permute-done.14
  146.7 0.3 add_convert_fusion
  147.0 1.7 %collective-permute-start.15 = (bf16[128,1024]{1,0:T(8,128)(2,1)S(1)}, bf16[128,1024]{1,0:T(8,128)(2,1)S(1)}, u32[]{:S(2)}, u32[]{:S(2)}) collective-permute-start(bf16[128,1024]{1,0:T(8,128)(2,1)S(1)} %get-tuple-element.21), channel_id=1, source_target_pairs={{0,4},{4,0},{1,5},{5,1},{2,6},{6,2},{3,7},{7,3},{8,12},{12,8},{9,1... | collective-permute-start | bytes 786440 | tf_op jit(solution)/shard_map/ppermute | solution.py:403
  148.7 0.0 all-to-all-done.3.parts_ref
  148.7 1.8 %shard_map.94.before_ref = bf16[128,8192]{1,0:T(8,128)(2,1)} custom-call(bf16[8,128,1024]{2,1,0:T(8,128)(2,1)S(1)} %all-to-all-done.3.parts_ref), custom_call_target="tpu_custom_call" | custom-call | tf_op jit(solution)/shard_map/pallas_call | solution.py:202
  150.6 3.2 %collective-permute-done.15.passed_ref = bf16[128,1024]{1,0:T(8,128)(2,1)S(1)} collective-permute-done((bf16[128,1024]{1,0:T(8,128)(2,1)S(1)}, bf16[128,1024]{1,0:T(8,128)(2,1)S(1)}, u32[]{:S(2)}, u32[]{:S(2)}) %collective-permute-start.15) | collective-permute-done | bytes 262176 | tf_op jit(solution)/shard_map/ppermute | solution.py:403
  153.8 0.8 shard_map.95
  (29 shorter events, 0.1 us)
Async XLA Ops:
  0.6 24.6 %copy-start.9 = (s32[128,2]{0,1:T(2,128)S(1)}, s32[128,2]{0,1:T(2,128)}, u32[]{:S(2)}) copy-start(s32[128,2]{0,1:T(2,128)} %param.8) | copy-start | bytes 3076
  0.6 24.6 %copy-start.10 = (bf16[128,2]{0,1:T(2,128)(2,1)S(1)}, bf16[128,2]{0,1:T(2,128)(2,1)}, u32[]{:S(2)}) copy-start(bf16[128,2]{0,1:T(2,128)(2,1)} %param.7) | copy-start | bytes 1540
  0.7 24.6 %copy-start.4 = (bf16[128,8192]{1,0:T(8,128)(2,1)S(1)}, bf16[128,8192]{1,0:T(8,128)(2,1)}, u32[]{:S(2)}) copy-start(bf16[128,8192]{1,0:T(8,128)(2,1)} %tokens_ref.1) | copy-start | bytes 6291460
  0.7 24.6 %copy-start.8 = (bf16[128,128]{1,0:T(8,128)(2,1)S(1)}, bf16[128,128]{1,0:T(8,128)(2,1)}, u32[]{:S(2)}) copy-start(bf16[128,128]{1,0:T(8,128)(2,1)} %preact_ref.1) | copy-start | bytes 98308
  1.9 23.3 %copy-start.13 = (bf16[128,1024]{1,0:T(8,128)(2,1)}, bf16[128,1024]{1,0:T(8,128)(2,1)S(1)}, u32[]{:S(2)}) copy-start(bf16[128,1024]{1,0:T(8,128)(2,1)S(1)} %get-tuple-element.27.refs_0_) | copy-start | bytes 786436
  1.9 9.5 %collective-permute-start = (bf16[128,1024]{1,0:T(8,128)(2,1)S(1)}, bf16[128,1024]{1,0:T(8,128)(2,1)S(1)}, u32[]{:S(2)}, u32[]{:S(2)}) collective-permute-start(bf16[128,1024]{1,0:T(8,128)(2,1)S(1)} %get-tuple-element.28), channel_id=1, source_target_pairs={{0,4},{4,0},{1,5},{5,1},{2,6},{6,2},{3,7},{7,3},{8,12},{12,8},{9,1... | collective-permute-start | bytes 786440 | tf_op jit(solution)/shard_map/ppermute | solution.py:403
  4.9 14.5 %collective-permute-start.2 = (bf16[128,1024]{1,0:T(8,128)(2,1)S(1)}, bf16[128,1024]{1,0:T(8,128)(2,1)}, u32[]{:S(2)}, u32[]{:S(2)}) collective-permute-start(bf16[128,1024]{1,0:T(8,128)(2,1)S(1)} %get-tuple-element.27.refs_0_), channel_id=1, source_target_pairs={{0,16},{16,0},{1,17},{17,1},{2,18},{18,2},{3,19},{19,3},{4,20},{20... | collective-permute-start | bytes 786440 | tf_op jit(solution)/shard_map/ppermute | solution.py:403
  7.5 13.9 %collective-permute-start.3 = (bf16[128,1024]{1,0:T(8,128)(2,1)S(1)}, bf16[128,1024]{1,0:T(8,128)(2,1)}, u32[]{:S(2)}, u32[]{:S(2)}) collective-permute-start(bf16[128,1024]{1,0:T(8,128)(2,1)S(1)} %get-tuple-element.27.refs_0_), channel_id=1, source_target_pairs={{0,8},{8,0},{1,9},{9,1},{2,10},{10,2},{3,11},{11,3},{4,12},{12,4},... | collective-permute-start | bytes 786440 | tf_op jit(solution)/shard_map/ppermute | solution.py:403
  10.9 10.5 %collective-permute-start.1 = (bf16[128,1024]{1,0:T(8,128)(2,1)}, bf16[128,1024]{1,0:T(8,128)(2,1)S(1)}, u32[]{:S(2)}, u32[]{:S(2)}) collective-permute-start(bf16[128,1024]{1,0:T(8,128)(2,1)} %get-tuple-element.26), channel_id=1, source_target_pairs={{0,4},{4,0},{1,5},{5,1},{2,6},{6,2},{3,7},{7,3},{8,12},{12,8},{9,1... | collective-permute-start | bytes 786440 | tf_op jit(solution)/shard_map/ppermute | solution.py:403
  11.4 13.9 %copy-start.14 = (bf16[128,1024]{1,0:T(8,128)(2,1)}, bf16[128,1024]{1,0:T(8,128)(2,1)S(1)}, u32[]{:S(2)}) copy-start(bf16[128,1024]{1,0:T(8,128)(2,1)S(1)} %collective-permute-done.refs_0_.refs_1_) | copy-start | bytes 786436
  11.4 13.9 %collective-permute-start.4 = (bf16[128,1024]{1,0:T(8,128)(2,1)S(1)}, bf16[128,1024]{1,0:T(8,128)(2,1)}, u32[]{:S(2)}, u32[]{:S(2)}) collective-permute-start(bf16[128,1024]{1,0:T(8,128)(2,1)S(1)} %collective-permute-done.refs_0_.refs_1_), channel_id=1, source_target_pairs={{0,8},{8,0},{1,9},{9,1},{2,10},{10,2},{3,11},{11,3},{4,12},{12,4},... | collective-permute-start | bytes 786440 | tf_op jit(solution)/shard_map/ppermute | solution.py:403
  21.4 3.9 %copy-start = (bf16[128,1024]{1,0:T(8,128)(2,1)}, bf16[128,1024]{1,0:T(8,128)(2,1)S(1)}, u32[]{:S(2)}) copy-start(bf16[128,1024]{1,0:T(8,128)(2,1)S(1)} %collective-permute-done.1.refs_1_.other_ref) | copy-start | bytes 786436
  28.2 3.8 %copy-start.1 = (bf16[128,1024]{1,0:T(8,128)(2,1)S(1)}, bf16[128,1024]{1,0:T(8,128)(2,1)}, u32[]{:S(2)}) copy-start(bf16[128,1024]{1,0:T(8,128)(2,1)} %copy-done) | copy-start | bytes 786436
  28.2 5.3 %copy-start.15 = (bf16[128,1024]{1,0:T(8,128)(2,1)S(1)}, bf16[128,1024]{1,0:T(8,128)(2,1)}, u32[]{:S(2)}) copy-start(bf16[128,1024]{1,0:T(8,128)(2,1)} %copy-done.14) | copy-start | bytes 786436
  28.2 35.1 %all-to-all-start = ((bf16[8,160,1024]{2,1,0:T(8,128)(2,1)}), bf16[8,160,1024]{2,1,0:T(8,128)(2,1)S(1)}, u32[]{:S(2)}, u32[]{:S(2)}) async-start(bf16[8,160,1024]{2,1,0:T(8,128)(2,1)} %get-tuple-element.12), calls=%async_computation | async-start | bytes 5242880 | tf_op jit(solution)/shard_map/all_to_all | solution.py:399
  32.0 25.6 %collective-permute-start.8 = (bf16[256,1024]{1,0:T(8,128)(2,1)S(1)}, bf16[256,1024]{1,0:T(8,128)(2,1)S(1)}, u32[]{:S(2)}, u32[]{:S(2)}) collective-permute-start(bf16[256,1024]{1,0:T(8,128)(2,1)S(1)} %shard_map.89), channel_id=1, source_target_pairs={{0,8},{8,0},{1,9},{9,1},{2,10},{10,2},{3,11},{11,3},{4,12},{12,4},... | collective-permute-start | bytes 1572872 | tf_op jit(solution)/shard_map/ppermute | solution.py:403
  33.5 17.9 %collective-permute-start.5 = (bf16[128,1024]{1,0:T(8,128)(2,1)S(1)}, bf16[128,1024]{1,0:T(8,128)(2,1)S(1)}, u32[]{:S(2)}, u32[]{:S(2)}) collective-permute-start(bf16[128,1024]{1,0:T(8,128)(2,1)S(1)} %copy-done.15), channel_id=1, source_target_pairs={{0,16},{16,0},{1,17},{17,1},{2,18},{18,2},{3,19},{19,3},{4,20},{20... | collective-permute-start | bytes 786440 | tf_op jit(solution)/shard_map/ppermute | solution.py:403
  35.1 22.5 %collective-permute-start.6 = (bf16[128,1024]{1,0:T(8,128)(2,1)}, bf16[128,1024]{1,0:T(8,128)(2,1)S(1)}, u32[]{:S(2)}, u32[]{:S(2)}) collective-permute-start(bf16[128,1024]{1,0:T(8,128)(2,1)} %collective-permute-done.2.refs_2_), channel_id=1, source_target_pairs={{0,8},{8,0},{1,9},{9,1},{2,10},{10,2},{3,11},{11,3},{4,12},{12,4},... | collective-permute-start | bytes 786440 | tf_op jit(solution)/shard_map/ppermute | solution.py:403
  51.4 6.2 %copy-start.16 = (bf16[128,1024]{1,0:T(8,128)(2,1)}, bf16[128,1024]{1,0:T(8,128)(2,1)S(1)}, u32[]{:S(2)}) copy-start(bf16[128,1024]{1,0:T(8,128)(2,1)S(1)} %collective-permute-done.5.refs_3_.refs_0_) | copy-start | bytes 786436
  57.6 0.7 copy-start.17
  58.3 0.8 copy-start.12
  59.9 26.5 %collective-permute-start.9 = (bf16[256,1024]{1,0:T(8,128)(2,1)}, bf16[256,1024]{1,0:T(8,128)(2,1)}, u32[]{:S(2)}, u32[]{:S(2)}) collective-permute-start(bf16[256,1024]{1,0:T(8,128)(2,1)} %shard_map.90.refs_0_), channel_id=1, source_target_pairs={{0,16},{16,0},{1,17},{17,1},{2,18},{18,2},{3,19},{19,3},{4,20},{20... | collective-permute-start | bytes 1572872 | tf_op jit(solution)/shard_map/ppermute | solution.py:403
  61.2 18.3 %collective-permute-start.7 = (bf16[128,1024]{1,0:T(8,128)(2,1)}, bf16[128,1024]{1,0:T(8,128)(2,1)S(1)}, u32[]{:S(2)}, u32[]{:S(2)}) collective-permute-start(bf16[128,1024]{1,0:T(8,128)(2,1)} %copy-done.16), channel_id=1, source_target_pairs={{0,8},{8,0},{1,9},{9,1},{2,10},{10,2},{3,11},{11,3},{4,12},{12,4},... | collective-permute-start | bytes 786440 | tf_op jit(solution)/shard_map/ppermute | solution.py:403
  66.5 20.0 %copy-start.6 = (bf16[256,1024]{1,0:T(8,128)(2,1)}, bf16[256,1024]{1,0:T(8,128)(2,1)S(1)}, u32[]{:S(2)}) copy-start(bf16[256,1024]{1,0:T(8,128)(2,1)S(1)} %get-tuple-element.13.refs_8_) | copy-start | bytes 1572868
  66.5 20.0 %copy-start.11 = (bf16[256,1024]{1,0:T(8,128)(2,1)}, bf16[256,1024]{1,0:T(8,128)(2,1)S(1)}, u32[]{:S(2)}) copy-start(bf16[256,1024]{1,0:T(8,128)(2,1)S(1)} %get-tuple-element.20) | copy-start | bytes 1572868
  66.5 37.2 %collective-permute-start.11 = (bf16[256,1024]{1,0:T(8,128)(2,1)}, bf16[256,1024]{1,0:T(8,128)(2,1)}, u32[]{:S(2)}, u32[]{:S(2)}) collective-permute-start(bf16[256,1024]{1,0:T(8,128)(2,1)} %get-tuple-element.18), channel_id=1, source_target_pairs={{0,8},{8,0},{1,9},{9,1},{2,10},{10,2},{3,11},{11,3},{4,12},{12,4},... | collective-permute-start | bytes 1572872 | tf_op jit(solution)/shard_map/ppermute | solution.py:403
  79.6 0.7 copy-start.18
  86.4 1.0 copy-start.5
  87.4 22.2 %collective-permute-start.10 = (bf16[256,1024]{1,0:T(8,128)(2,1)}, bf16[256,1024]{1,0:T(8,128)(2,1)}, u32[]{:S(2)}, u32[]{:S(2)}) collective-permute-start(bf16[256,1024]{1,0:T(8,128)(2,1)} %shard_map.91.refs_1_), channel_id=1, source_target_pairs={{0,8},{8,0},{1,9},{9,1},{2,10},{10,2},{3,11},{11,3},{4,12},{12,4},... | collective-permute-start | bytes 1572872 | tf_op jit(solution)/shard_map/ppermute | solution.py:403
  100.2 9.4 %all-to-all-start.2 = ((bf16[8,128,128]{2,1,0:T(8,128)(2,1)}), bf16[8,128,128]{2,1,0:T(8,128)(2,1)S(1)}, u32[]{:S(2)}, u32[]{:S(2)}) async-start(bf16[8,128,128]{2,1,0:T(8,128)(2,1)} %get-tuple-element.16), calls=%async_computation.2 | async-start | bytes 524288 | tf_op jit(solution)/shard_map/all_to_all | solution.py:399
  104.8 0.8 copy-start.2
  116.4 3.8 %copy-start.3 = (bf16[256,1024]{1,0:T(8,128)(2,1)S(1)}, bf16[256,1024]{1,0:T(8,128)(2,1)}, u32[]{:S(2)}) copy-start(bf16[256,1024]{1,0:T(8,128)(2,1)} %copy-done.2) | copy-start | bytes 1572868
  116.4 30.4 %copy-start.7 = (bf16[256,1024]{1,0:T(8,128)(2,1)S(1)}, bf16[256,1024]{1,0:T(8,128)(2,1)}, u32[]{:S(2)}) copy-start(bf16[256,1024]{1,0:T(8,128)(2,1)} %copy-done.6) | copy-start | bytes 1572868
  116.4 32.4 %all-to-all-start.3 = ((bf16[8,128,1024]{2,1,0:T(8,128)(2,1)}), bf16[8,128,1024]{2,1,0:T(8,128)(2,1)S(1)}, u32[]{:S(2)}, u32[]{:S(2)}) async-start(bf16[8,128,1024]{2,1,0:T(8,128)(2,1)} %shard_map.93), calls=%async_computation.3 | async-start | bytes 4194304 | tf_op jit(solution)/shard_map/all_to_all | solution.py:399
  120.1 25.6 %collective-permute-start.12 = (bf16[256,1024]{1,0:T(8,128)(2,1)}, bf16[256,1024]{1,0:T(8,128)(2,1)S(1)}, u32[]{:S(2)}, u32[]{:S(2)}) collective-permute-start(bf16[256,1024]{1,0:T(8,128)(2,1)} %copy-done.11), channel_id=1, source_target_pairs={{0,8},{8,0},{1,9},{9,1},{2,10},{10,2},{3,11},{11,3},{4,12},{12,4},... | collective-permute-start | bytes 1572872 | tf_op jit(solution)/shard_map/ppermute | solution.py:403
  120.3 25.4 %collective-permute-start.13 = (bf16[128,1024]{1,0:T(8,128)(2,1)S(1)}, bf16[128,1024]{1,0:T(8,128)(2,1)S(1)}, u32[]{:S(2)}, u32[]{:S(2)}) collective-permute-start(bf16[128,1024]{1,0:T(8,128)(2,1)S(1)} %get-tuple-element.24), channel_id=1, source_target_pairs={{0,16},{16,0},{1,17},{17,1},{2,18},{18,2},{3,19},{19,3},{4,20},{20... | collective-permute-start | bytes 786440 | tf_op jit(solution)/shard_map/ppermute | solution.py:403
  123.3 23.4 %collective-permute-start.14 = (bf16[128,1024]{1,0:T(8,128)(2,1)S(1)}, bf16[128,1024]{1,0:T(8,128)(2,1)S(1)}, u32[]{:S(2)}, u32[]{:S(2)}) collective-permute-start(bf16[128,1024]{1,0:T(8,128)(2,1)S(1)} %get-tuple-element.23), channel_id=1, source_target_pairs={{0,16},{16,0},{1,17},{17,1},{2,18},{18,2},{3,19},{19,3},{4,20},{20... | collective-permute-start | bytes 786440 | tf_op jit(solution)/shard_map/ppermute | solution.py:403
  147.0 6.8 %collective-permute-start.15 = (bf16[128,1024]{1,0:T(8,128)(2,1)S(1)}, bf16[128,1024]{1,0:T(8,128)(2,1)S(1)}, u32[]{:S(2)}, u32[]{:S(2)}) collective-permute-start(bf16[128,1024]{1,0:T(8,128)(2,1)S(1)} %get-tuple-element.21), channel_id=1, source_target_pairs={{0,4},{4,0},{1,5},{5,1},{2,6},{6,2},{3,7},{7,3},{8,12},{12,8},{9,1... | collective-permute-start | bytes 786440 | tf_op jit(solution)/shard_map/ppermute | solution.py:403
